TPU v7x, 32 devices: a whole 2x2x4 slice. The times are simulated.
32 devices in a mesh: grp: 2 (over x), ad: 16 (over z, y, core).
Axes of the slice: x: 2, y: 2, z: 4, core: 2. Of those that a mesh axis runs over, the one named last changes fastest.
Arguments:
- tokens: bfloat16 [8192, 8192], P(('grp', 'ad')), parts along dimension 0, may hold values from -6 to 6
- value_weight: bfloat16 [8192, 512], replicated, may hold values from -0.0625 to 0.0625
- adapt_down: bfloat16 [512, 8192, 16], P(('grp', 'ad')), parts along dimension 0, may hold values from -0.0625 to 0.0625
- adapt_up: bfloat16 [512, 16, 512], P(('grp', 'ad')), parts along dimension 0, may hold values from -1.5 to 1.5
- tenant_ids: int32 [8192, 1], P(('grp', 'ad')), parts along dimension 0, may hold values from 0 to 255; in each aligned block of 256 rows (0 to 255, 256 to 511, ...) at most 2 rows name the same one
- tenant_slot: int32 [512], P('grp'), parts along dimension 0, may hold values from 0 to 255, each once
Outputs:
- values_out: bfloat16 [8192, 512], P(('grp', 'ad')), parts along dimension 0
There are 2 independent parts, one for each index of `grp`. A program takes and returns all parts, laid end to end along the dimension named above; an argument that names none is the same for every part. Nothing has to cross between parts.
Inputs may be any that keep to these rules, and one draw needn't show every extreme that they name: `tenant_ids`: among the rows of one device no tenant appears more than 2 times, and some tenant appears exactly 2 times. `tenant_slot`: each slot holds exactly one tenant.
All inputs are finite; a program needn't handle non-finite values.
Results may differ from a plain program's by a relative error of at most 0.0049.
Values may be sent and summed in bfloat16 or wider, within the bound.
No kernel may reach another device: no remote copies, remote signals or barrier semaphores. Data moves between devices by JAX's collectives and lax.ppermute only.
A program may use at most 128 MiB of HBM per device.

v0:
```python
import jax
import jax.numpy as jnp
from jax import lax
from jax.sharding import PartitionSpec as P

TENANTS = 256
CAP = 2


def on_device(tokens, value_weight, adapt_down, adapt_up, tenant_ids, tenant_slot):
    row_count = tokens.shape[0]
    owner_count = lax.axis_size("ad")
    local_count = adapt_down.shape[0]
    out_width = adapt_up.shape[2]
    slot_total = TENANTS * CAP
    tenant = tenant_ids[:, 0]
    tenant_match = tenant[:, None] == jnp.arange(TENANTS, dtype=jnp.int32)[None, :]
    slot_index = jnp.sum(jnp.where(tenant_match, tenant_slot[None, :], 0), axis=1)
    row_order = jnp.arange(row_count, dtype=jnp.int32)
    earlier = (slot_index[:, None] == slot_index[None, :]) & (
        row_order[None, :] < row_order[:, None]
    )
    position = jnp.sum(earlier.astype(jnp.int32), axis=1)
    target_slot = slot_index * CAP + position
    slot_hits = target_slot[:, None] == jnp.arange(slot_total, dtype=jnp.int32)[None, :]
    source_row = jnp.sum(jnp.where(slot_hits, row_order[:, None], 0), axis=0)
    filled = jnp.any(slot_hits, axis=0)
    base_value = jnp.dot(tokens, value_weight, preferred_element_type=jnp.float32)
    outgoing = jnp.where(filled[:, None], tokens[source_row], jnp.zeros((), tokens.dtype))
    outgoing = outgoing.reshape(owner_count, local_count * CAP, tokens.shape[1])
    arrived = lax.all_to_all(outgoing, "ad", split_axis=0, concat_axis=0, tiled=True)
    tenant_blocks = arrived.reshape(owner_count, local_count, CAP, tokens.shape[1])
    low_rank = jnp.einsum(
        "slcd,ldr->slcr", tenant_blocks, adapt_down, preferred_element_type=jnp.float32
    ).astype(jnp.bfloat16)
    delta_rows = jnp.einsum(
        "slcr,lre->slce", low_rank, adapt_up, preferred_element_type=jnp.float32
    ).astype(jnp.bfloat16)
    returned_rows = lax.all_to_all(
        delta_rows.reshape(owner_count, local_count * CAP, out_width),
        "ad",
        split_axis=0,
        concat_axis=0,
        tiled=True,
    )
    adapter_delta = returned_rows.reshape(slot_total, out_width)[target_slot]
    return (base_value + adapter_delta.astype(jnp.float32)).astype(jnp.bfloat16)


def solution(mesh):
    placed = (
        P(("grp", "ad"), None),
        P(),
        P(("grp", "ad"), None, None),
        P(("grp", "ad"), None, None),
        P(("grp", "ad"), None),
        P("grp"),
    )
    return jax.shard_map(
        on_device, mesh=mesh, in_specs=placed, out_specs=P(("grp", "ad"), None), check_vma=False
    )
```

profile of v0, /device:TPU:0, one launch (start us, length us, event | category | flops | bytes accessed | tf_op | source)
XLA Modules:
  0.0 264.9 jit_solution(856243796005701239)
XLA Ops:
  0.0 0.0 copy-start
  0.0 0.9 select_reduce_fusion.1
  0.9 0.2 convert_reduce_fusion
  1.1 0.1 select_reduce_fusion
  1.3 0.2 fusion.11
  1.4 0.1 broadcast_in_dim.52
  1.5 18.2 %gather_fusion = bf16[512,8192]{1,0:T(8,128)(2,1)} fusion(bf16[256,8192]{1,0:T(8,128)(2,1)} %param.6, s32[1024]{0:T(1024)S(1)} %pad_clamp_fusion.1), kind=kCustom, calls=%fused_computation | custom fusion | bytes 16779264 | tf_op jit(solution)/shard_map/gather | solution.py:29
  19.7 7.2 %broadcast_select_fusion = bf16[16,32,8192]{2,1,0:T(8,128)(2,1)} fusion(bf16[16,32,8192]{2,1,0:T(8,128)(2,1)} %bitcast.34, pred[16,32]{1,0:T(8,128)(4,1)S(1)} %broadcast_in_dim.52), kind=kLoop, calls=%fused_computation.2 | loop fusion | flops 4194304 | bytes 16777728 | tf_op jit(solution)/shard_map/jit(_where)/select_n | solution.py:29
  26.9 189.6 %all_to_all.10 = bf16[16,32,8192]{2,1,0:T(8,128)(2,1)} all-to-all(bf16[16,32,8192]{2,1,0:T(8,128)(2,1)} %broadcast_select_fusion), channel_id=1, replica_groups=mesh['grp'=2,'ad'=16] {'ad'}, dimensions={0} | all-to-all | bytes 16777216 | tf_op jit(solution)/shard_map/all_to_all | solution.py:31
  216.6 11.2 %copy.16 = bf16[16,32,8192]{2,0,1:T(8,128)(2,1)} copy(bf16[16,32,8192]{2,1,0:T(8,128)(2,1)} %all_to_all.10) | data formatting | bytes 16777216 | tf_op jit(solution)/shard_map/all_to_all | solution.py:31
  227.8 0.0 copy-done
  227.8 7.0 %convolution_convert_fusion = bf16[16,16,2,512]{3,1,2,0:T(8,128)(2,1)S(1)} fusion(bf16[16,16,2,8192]{3,0,2,1:T(8,128)(2,1)} %bitcast.36, bf16[16,8192,16]{1,2,0:T(8,128)(2,1)} %param.8, bf16[16,16,512]{2,1,0:T(8,128)(2,1)S(1)} %copy-done), kind=kOutput, calls=%fused_computation.5 | convolution fusion | flops 142876672 | bytes 13369344 | tf_op jit(solution)/shard_map/slcr,lre->slce/dot_general | solution.py:36
  234.8 1.1 copy.17
  235.9 5.7 %all-to-all-start.1 = ((bf16[16,32,512]{2,1,0:T(8,128)(2,1)}), bf16[16,32,512]{2,1,0:T(8,128)(2,1)S(1)}, u32[]{:S(2)}, u32[]{:S(2)}) async-start(bf16[16,32,512]{2,1,0:T(8,128)(2,1)} %copy.17), calls=%async_computation.1 | async-start | bytes 1048576 | tf_op jit(solution)/shard_map/all_to_all | solution.py:39
  241.6 14.4 %all-to-all-done.1 = bf16[16,32,512]{2,1,0:T(8,128)(2,1)S(1)} async-done(((bf16[16,32,512]{2,1,0:T(8,128)(2,1)}), bf16[16,32,512]{2,1,0:T(8,128)(2,1)S(1)}, u32[]{:S(2)}, u32[]{:S(2)}) %all-to-all-start.1) | async-done | bytes 524320 | tf_op jit(solution)/shard_map/all_to_all | solution.py:39
  256.0 1.2 gather_fusion.1
  257.2 7.7 %fusion.2 = bf16[256,512]{1,0:T(8,128)(2,1)} fusion(bf16[256,8192]{1,0:T(8,128)(2,1)} %param.6, bf16[8192,512]{1,0:T(8,128)(2,1)} %param.7, bf16[256,512]{1,0:T(8,128)(2,1)S(1)} %gather_fusion.1), kind=kOutput, calls=%fused_computation.7 | convolution fusion | flops 2147876864 | bytes 13107200 | tf_op jit(solution)/shard_map/dot_general | solution.py:28
  (5 shorter events, 0.0 us)
Async XLA Ops:
  0.0 227.8 %copy-start = (bf16[16,16,512]{2,1,0:T(8,128)(2,1)S(1)}, bf16[16,16,512]{2,1,0:T(8,128)(2,1)}, u32[]{:S(2)}) copy-start(bf16[16,16,512]{2,1,0:T(8,128)(2,1)} %param.9) | copy-start | bytes 786436
  235.9 20.2 %all-to-all-start.1 = ((bf16[16,32,512]{2,1,0:T(8,128)(2,1)}), bf16[16,32,512]{2,1,0:T(8,128)(2,1)S(1)}, u32[]{:S(2)}, u32[]{:S(2)}) async-start(bf16[16,32,512]{2,1,0:T(8,128)(2,1)} %copy.17), calls=%async_computation.1 | async-start | bytes 1048576 | tf_op jit(solution)/shard_map/all_to_all | solution.py:39
where the time goes:
time: 265 us
  blocking collectives  190 us (72%)
  local copies, waits for them, and re-layouts  31.7 us (12%)
  matrix products  14.7 us (6%)
  waiting for transfers between devices  14.4 us (5%)
  other arithmetic  8.64 us (3%)
  starting transfers between devices  5.69 us (2%)
    all_to_all x1, blocking collectives, on_device(): lax.all_to_all(outgoing, 'ad', split_axis=0, concat_axis=0, tiled=True)  190 us
    gather x1, local copies, waits for them, and re-layouts, on_device(): tokens[source_row]  18.2 us
    all_to_all x1, waiting for transfers between devices, on_device(): lax.all_to_all(delta_rows.reshape(owner_count, local_count * CAP, out_wid...  14.4 us
    all_to_all x1, local copies, waits for them, and re-layouts, on_device(): lax.all_to_all(outgoing, 'ad', split_axis=0, concat_axis=0, tiled=True)  11.2 us
    dot_general x1, matrix products, on_device(): jnp.dot(tokens, value_weight, preferred_element_type=jnp.float32)  7.69 us
    select_n x1, other arithmetic, on_device(): jnp.where(filled[:, None], tokens[source_row], jnp.zeros((), tokens.dtype))  7.22 us
    dot_general x1, matrix products, on_device(): jnp.einsum('slcr,lre->slce', low_rank, adapt_up, preferred_element_type=j...  7.02 us
    all_to_all x1, starting transfers between devices, on_device(): lax.all_to_all(delta_rows.reshape(owner_count, local_count * CAP, out_wid...  5.69 us
  transfers between devices with their start and end apart: 1, of which 1 were waited for; matrix products, arithmetic and copies ran while one was open for 0% of the time, Pallas kernels for 0%

commit v1 on v0

v1 whole, which is shorter than its diff:
```python
import functools

import jax
import jax.numpy as jnp
from jax import lax
from jax.experimental import pallas as pl
from jax.experimental.pallas import tpu as pltpu
from jax.sharding import PartitionSpec as P

TENANTS = 256
CAP = 2
PLANE = 4
SPARE = 12
NOTE = 128
STEP = 1024
FIRST = (1, 2, 3)
REST = (4, 8, 5, 9, 6, 10, 7, 11, 12, 13, 14, 15)
GROUPS = ((0, 1, 2, 3), (4, 8, 5, 9), (6, 10, 7, 11), (12, 13), (14, 15))
VMEM = pl.BlockSpec(memory_space=pltpu.VMEM)
SMEM = pl.BlockSpec(memory_space=pltpu.SMEM)


def exchange(tokens, slot, owner, place, room, down, up):
    count = lax.axis_size("ad")
    local, depth, rank = down.shape
    width = up.shape[2]
    at = jnp.where((place >= 0) & (place < room), owner * room + place, -1)
    hits = at[None, :] == jnp.arange(count * room, dtype=jnp.int32)[:, None]
    slots = jnp.sum(jnp.where(hits, slot[None, :] + 1, 0), axis=1) - 1
    pick = hits.astype(jnp.bfloat16)
    sent = jnp.dot(pick, tokens, preferred_element_type=jnp.float32).astype(jnp.bfloat16)
    got = lax.all_to_all(
        sent.reshape(count, room, depth), "ad", split_axis=0, concat_axis=0, tiled=True
    ).reshape(count * room, depth)
    got_slots = lax.all_to_all(
        slots.reshape(count, room), "ad", split_axis=0, concat_axis=0, tiled=True
    ).reshape(count * room)
    low_rank = jnp.einsum("td,ldr->tlr", got, down, preferred_element_type=jnp.float32)
    own = (got_slots - lax.axis_index("ad") * local)[:, None] == jnp.arange(local)[None, :]
    low_rank = jnp.where(own[:, :, None], low_rank, 0.0).astype(jnp.bfloat16)
    delta = jnp.dot(
        low_rank.reshape(count * room, local * rank),
        up.reshape(local * rank, width),
        preferred_element_type=jnp.float32,
    ).astype(jnp.bfloat16)
    back = lax.all_to_all(
        delta.reshape(count, room, width), "ad", split_axis=0, concat_axis=0, tiled=True
    )
    return jnp.dot(
        pick.T, back.reshape(count * room, width), preferred_element_type=jnp.float32
    )


def one_hot(at, starts, size):
    ids = [lax.broadcasted_iota(jnp.int32, (size, at.shape[1]), 0) + s for s in starts]
    return (jnp.concatenate(ids, axis=0) == at).astype(jnp.float32).astype(jnp.bfloat16)


def pack_over_body(main_rows, planes, at_ref, info_ref, tokens_ref, *outs):
    at = at_ref[...]
    half = tokens_ref.shape[1] // 2
    row = lax.broadcasted_iota(jnp.int32, (2 * SPARE, at.shape[1]), 0)
    upper = row >= SPARE
    ids = jnp.where(upper, row - SPARE, row)
    ids = jnp.concatenate([ids + main_rows + b * SPARE for b in range(planes)], axis=0)
    upper = jnp.concatenate([upper] * planes, axis=0)
    hit = ids == at
    left = (hit & ~upper).astype(jnp.float32).astype(jnp.bfloat16)
    right = (hit & upper).astype(jnp.float32).astype(jnp.bfloat16)
    both = hit.astype(jnp.float32).astype(jnp.bfloat16)

    def put(value, columns):
        for b in range(planes):
            outs[b][:, columns] = value[2 * SPARE * b : 2 * SPARE * (b + 1)].astype(jnp.bfloat16)

    for c in range(0, half, STEP):
        put(
            jnp.dot(left, tokens_ref[:, c : c + STEP], preferred_element_type=jnp.float32)
            + jnp.dot(
                right, tokens_ref[:, half + c : half + c + STEP], preferred_element_type=jnp.float32
            ),
            slice(c, c + STEP),
        )
    put(
        jnp.dot(both, info_ref[...], preferred_element_type=jnp.float32), slice(half, half + NOTE)
    )


def pack_body(starts, at_ref, info_ref, tokens_ref, *outs):
    depth = tokens_ref.shape[1]
    size = outs[0].shape[0]
    pick = one_hot(at_ref[...], starts, size)

    def put(value, columns):
        for j, out in enumerate(outs):
            out[:, columns] = value[size * j : size * (j + 1)].astype(jnp.bfloat16)

    for c in range(0, depth, STEP):
        put(
            jnp.dot(pick, tokens_ref[:, c : c + STEP], preferred_element_type=jnp.float32),
            slice(c, c + STEP),
        )
    put(
        jnp.dot(pick, info_ref[...], preferred_element_type=jnp.float32), slice(depth, depth + NOTE)
    )


def low_delta(low, note, first, rank, up):
    column = lax.broadcasted_iota(jnp.int32, low.shape, 1) // rank + (first + 1)
    low = jnp.where(note.astype(jnp.float32) == column.astype(jnp.float32), low, 0.0)
    return jnp.dot(low.astype(jnp.bfloat16), up, preferred_element_type=jnp.float32)


def adapt_body(keys, rank, first_ref, down_ref, up_ref, *refs):
    rows_refs, over_refs = refs[: len(keys)], refs[len(keys) : -len(keys)]
    outs = refs[-len(keys) :]
    depth = down_ref.shape[1]
    size = rows_refs[0].shape[0]
    low = jnp.zeros((size * len(keys), down_ref.shape[0]), jnp.float32)
    for c in range(0, depth, STEP):
        rows = jnp.concatenate([r[:, c : c + STEP] for r in rows_refs], axis=0)
        low += lax.dot_general(
            rows,
            down_ref[:, c : c + STEP],
            (((1,), (1,)), ((), ())),
            preferred_element_type=jnp.float32,
        )
    note = jnp.concatenate([r[:, depth : depth + NOTE] for r in rows_refs], axis=0)[:, :1]
    delta = low_delta(low, note, first_ref[0], rank, up_ref[...]).astype(jnp.bfloat16)
    for j, k in enumerate(keys):
        outs[j][:size] = delta[size * j : size * (j + 1)]
        outs[j][size:] = over_refs[k % PLANE][16 * (k // PLANE) : 16 * (k // PLANE + 1)]


def adapt_over_body(planes, rank, first_ref, down_ref, up_ref, *refs):
    rows_refs, outs = refs[:PLANE], refs[PLANE:]
    half = down_ref.shape[1] // 2
    for rows_ref, out in zip(rows_refs, outs, strict=True):
        shape = (rows_ref.shape[0], down_ref.shape[0])
        low0, low1 = jnp.zeros(shape, jnp.float32), jnp.zeros(shape, jnp.float32)
        for c in range(0, half, STEP):
            rows = rows_ref[:, c : c + STEP]
            dims = (((1,), (1,)), ((), ()))
            low0 += lax.dot_general(
                rows, down_ref[:, c : c + STEP], dims, preferred_element_type=jnp.float32
            )
            low1 += lax.dot_general(
                rows,
                down_ref[:, half + c : half + c + STEP],
                dims,
                preferred_element_type=jnp.float32,
            )
        note = rows_ref[:, half : half + NOTE].astype(jnp.float32)
        zeros = jnp.zeros((16 - SPARE, shape[1]), jnp.float32)
        no_note = jnp.zeros((16 - SPARE, NOTE), jnp.float32)
        lows, notes = [], []
        for b in range(planes):
            s = 2 * SPARE * b
            lows += [low0[s : s + SPARE] + low1[s + SPARE : s + 2 * SPARE], zeros]
            notes += [note[s : s + SPARE], no_note]
        low = jnp.concatenate(lows, axis=0)
        note = jnp.concatenate(notes, axis=0)[:, :1]
        out[...] = low_delta(low, note, first_ref[0], rank, up_ref[...]).astype(jnp.bfloat16)


def final_body(room, main_rows, at_ref, base_ref, *refs):
    *backs, out = refs
    back = jnp.concatenate([b[...] for b in backs], axis=0)
    size = backs[0].shape[0]
    shape = (back.shape[0], at_ref.shape[1])
    row = lax.broadcasted_iota(jnp.int32, shape, 0)
    k, i = row // size, row % size
    spare = main_rows + (k // PLANE) * SPARE + (i - room)
    came = jnp.where(i < room, k * room + i, jnp.where(i < room + SPARE, spare, -2))
    pick = (came == at_ref[...]).astype(jnp.float32).astype(jnp.bfloat16)
    delta = lax.dot_general(
        pick, back, (((0,), (0,)), ((), ())), preferred_element_type=jnp.float32
    )
    out[...] = (base_ref[...] + delta).astype(jnp.bfloat16)


def call(body, outs, args, specs, flops, moved):
    return pl.pallas_call(
        body,
        in_specs=specs,
        out_specs=[VMEM] * len(outs),
        out_shape=[jax.ShapeDtypeStruct(s, jnp.bfloat16) for s in outs],
        compiler_params=pltpu.CompilerParams(vmem_limit_bytes=40 * 2**20),
        cost_estimate=pl.CostEstimate(flops=flops, bytes_accessed=moved, transcendentals=0),
    )(*args)


def swap(x, k):
    count = lax.axis_size("ad")
    return lax.ppermute(x, "ad", [(s, s ^ k) for s in range(count)])


def on_device(tokens, value_weight, adapt_down, adapt_up, tenant_ids, tenant_slot):
    row_count, depth = tokens.shape
    count = lax.axis_size("ad")
    me = lax.axis_index("ad")
    local, _, rank = adapt_down.shape
    width = adapt_up.shape[2]
    tenant = tenant_ids[:, 0]
    tenant_match = tenant[:, None] == jnp.arange(TENANTS, dtype=jnp.int32)[None, :]
    slot = jnp.sum(jnp.where(tenant_match, tenant_slot[None, :], 0), axis=1)
    owner = slot // local
    order = jnp.arange(row_count, dtype=jnp.int32)
    before = order[None, :] < order[:, None]
    place = jnp.sum(((owner[:, None] == owner[None, :]) & before).astype(jnp.int32), axis=1)
    base_value = jnp.dot(tokens, value_weight, preferred_element_type=jnp.float32)
    room = row_count // count
    planes = count // PLANE
    if count != 16 or room != 16:
        delta = exchange(tokens, slot, owner, place, CAP * local, adapt_down, adapt_up)
        return (base_value + delta).astype(jnp.bfloat16)

    block = owner ^ me
    plane = block // PLANE
    over = place >= room
    over_place = jnp.sum(
        (over[None, :] & (plane[:, None] == plane[None, :]) & before).astype(jnp.int32), axis=1
    )
    main_rows = count * room
    left = over & (over_place >= SPARE)
    at = jnp.where(over, main_rows + plane * SPARE + over_place, block * room + place)
    at = jnp.where(left, -1, at)[None, :]
    info = jnp.where(jnp.arange(NOTE)[None, :] == 0, slot[:, None] + 1, 0).astype(jnp.bfloat16)
    some_left = jnp.max(left.astype(jnp.int32))

    spare = call(
        functools.partial(pack_over_body, main_rows, planes),
        [(2 * SPARE, depth // 2 + NOTE)] * planes,
        (at, info, tokens),
        [VMEM] * 3,
        2 * 96 * row_count * depth,
        6 * 2**20,
    )
    blocks = {}
    for keys in (FIRST, (0,) + REST):
        made = call(
            functools.partial(pack_body, [k * room for k in keys]),
            [(room, depth + NOTE)] * len(keys),
            (at, info, tokens),
            [VMEM] * 3,
            2 * len(keys) * room * row_count * depth,
            8 * 2**20,
        )
        blocks.update(zip(keys, made, strict=True))

    along = jnp.concatenate(
        [spare[0]] + [swap(spare[b], b * PLANE) for b in range(1, planes)], axis=0
    )
    shared = [along] + [swap(along, a) for a in range(1, PLANE)]

    got = {0: blocks[0]}
    for k in FIRST + REST:
        got[k] = swap(blocks[k], k)

    seen = some_left
    for g in range(1, lax.axis_size("grp")):
        groups = lax.axis_size("grp")
        other = lax.ppermute(some_left, "grp", [(s, (s + g) % groups) for s in range(groups)])
        seen = jnp.maximum(seen, other)
    step = 1
    while step < count:
        seen = jnp.maximum(seen, swap(seen, step))
        step *= 2

    first = (me * local).reshape(1)
    down = adapt_down.transpose(0, 2, 1).reshape(local * rank, depth)
    up = adapt_up.reshape(local * rank, width)
    over_delta = call(
        functools.partial(adapt_over_body, planes, rank),
        [(16 * planes, width)] * PLANE,
        (first, down, up, *shared),
        [SMEM] + [VMEM] * 6,
        2 * 384 * depth * local * rank,
        6 * 2**20,
    )
    back = {}
    for keys in GROUPS:
        made = call(
            functools.partial(adapt_body, keys, rank),
            [(room + 16, width)] * len(keys),
            (first, down, up, *[got[k] for k in keys], *over_delta),
            [SMEM] + [VMEM] * (2 + len(keys) + PLANE),
            2 * room * len(keys) * depth * local * rank,
            6 * 2**20,
        )
        for k, rows in zip(keys, made, strict=True):
            back[k] = swap(rows, k) if k else rows
    back = [back[k] for k in range(count)]

    def finish(base):
        return call(
            functools.partial(final_body, room, main_rows),
            [(row_count, width)],
            (at, base, *back),
            [VMEM] * (2 + count),
            2 * row_count * width * 512,
            2**20,
        )[0]

    def more():
        extra = exchange(
            tokens,
            slot,
            owner,
            jnp.where(left, place - room, -1),
            CAP * local - room,
            adapt_down,
            adapt_up,
        )
        return finish(base_value + extra)

    return lax.cond(seen > 0, more, lambda: finish(base_value))


def solution(mesh):
    placed = (
        P(("grp", "ad"), None),
        P(),
        P(("grp", "ad"), None, None),
        P(("grp", "ad"), None, None),
        P(("grp", "ad"), None),
        P("grp"),
    )
    return jax.shard_map(
        on_device, mesh=mesh, in_specs=placed, out_specs=P(("grp", "ad"), None), check_vma=False
    )
```

time: 265 us -> 203 us (0.77)
  blocking collectives: 190 us -> 0 us
  starting transfers between devices: 5.69 us -> 77.5 us
  waiting for transfers between devices: 14.4 us -> 71.2 us
  Pallas kernels: 0 us -> 27.4 us
  local copies, waits for them, and re-layouts: 31.7 us -> 13.8 us
  matrix products: 14.7 us -> 5.88 us
  other arithmetic: 8.64 us -> 2.27 us
  between operations: 0.06 us -> 4.37 us
    all_to_all x1 -> x0, blocking collectives: 190 us -> none  [on_device(): lax.all_to_all(outgoing, 'ad', split_axis=0, concat_axis=0, tiled=True)]
    ppermute x0 -> x41, starting transfers between devices: none -> 77.5 us  [the longest x40 74.6 us: swap(): return lax.ppermute(x, 'ad', [(s, s ^ k) for s in range(count)])]
    ppermute x0 -> x41, waiting for transfers between devices: none -> 71.2 us  [the longest x40 71.2 us: swap(): return lax.ppermute(x, 'ad', [(s, s ^ k) for s in range(count)])]
    pallas_call x0 -> x10, Pallas kernels: none -> 27.4 us  [call(): pl.pallas_call(body, in_specs=specs, out_specs=[VMEM] * len(outs), out_sh...]
    gather x2 -> x0, local copies, waits for them, and re-layouts: 19.3 us -> none  [the longest x1 18.2 us: on_device(): tokens[source_row]]
    all_to_all x1 -> x0, waiting for transfers between devices: 14.4 us -> none  [on_device(): lax.all_to_all(delta_rows.reshape(owner_count, local_count * CAP, out_wid...]
    unnamed x2 -> x75, local copies, waits for them, and re-layouts: 0.01 us -> 13.8 us
    all_to_all x1 -> x0, local copies, waits for them, and re-layouts: 11.2 us -> none  [on_device(): lax.all_to_all(outgoing, 'ad', split_axis=0, concat_axis=0, tiled=True)]
  transfers between devices with their start and end apart: 1 -> 41, of which waited for: 1 -> 14; matrix products, arithmetic and copies ran while one was open for 0% -> 3% of each run, Pallas kernels for 0% -> 13%
where the time goes in v1:
time: 203 us; the launch traced here: 202 us
  starting transfers between devices  77.5 us (38%)
  waiting for transfers between devices  71.2 us (35%)
  Pallas kernels  27.4 us (13%)
  local copies, waits for them, and re-layouts  13.8 us (7%)
  matrix products  5.88 us (3%)
  between operations  4.37 us (2%)
  other arithmetic  2.27 us (1%)
    ppermute x40, starting transfers between devices, swap(): return lax.ppermute(x, 'ad', [(s, s ^ k) for s in range(count)])  74.6 us
    ppermute x40, waiting for transfers between devices, swap(): return lax.ppermute(x, 'ad', [(s, s ^ k) for s in range(count)])  71.2 us
    pallas_call x10, Pallas kernels, call(): pl.pallas_call(body, in_specs=specs, out_specs=[VMEM] * len(outs), out_sh...  27.4 us
    unnamed x75, local copies, waits for them, and re-layouts  13.8 us
    dot_general x1, matrix products, on_device(): jnp.dot(tokens, value_weight, preferred_element_type=jnp.float32)  5.88 us
  transfers between devices with their start and end apart: 41, of which 14 were waited for; matrix products, arithmetic and copies ran while one was open for 3% of the time, Pallas kernels for 13%

profile of v1, /device:TPU:0, one launch (start us, length us, event | category | flops | bytes accessed | tf_op | source)
XLA Modules:
  0.0 202.4 jit_solution(14320681443108784558)
XLA Ops:
  2.2 2.9 %collective-permute-start = (s32[]{:T(128)}, s32[]{:T(128)}, u32[]{:S(2)}, u32[]{:S(2)}) collective-permute-start(s32[]{:T(128)} %get-tuple-element.242), channel_id=1, source_target_pairs={{0,16},{16,0},{1,17},{17,1},{2,18},{18,2},{3,19},{19,3},{4,20},{20... | collective-permute-start | bytes 20 | tf_op jit(solution)/shard_map/ppermute | solution.py:263
  5.2 3.7 %shard_map.67 = (bf16[16,8320]{1,0:T(8,128)(2,1)S(1)}, bf16[16,8320]{1,0:T(8,128)(2,1)S(1)}, bf16[16,8320]{1,0:T(8,128)(2,1)}) custom-call(s32[1,256]{1,0:T(1,128)S(1)} %and_select_fusion.4.at_ref, bf16[256,128]{1,0:T(8,128)(2,1)S(1)} %select_convert_fusion.2.info_ref, bf16[256,8192]{1,0:T(8,128)(2,1)} %tokens_ref.5), custom_call_target="tpu_custom_call" | custom-call | flops 201326592 | bytes 8388608 | tf_op jit(solution)/shard_map/pallas_call | solution.py:183
  25.2 2.9 %collective-permute-start.2 = (s32[]{:T(128)}, s32[]{:T(128)}, u32[]{:S(2)}, u32[]{:S(2)}) collective-permute-start(s32[]{:T(128)} %max.16), channel_id=1, source_target_pairs={{0,2},{1,3},{2,0},{3,1},{4,6},{5,7},{6,4},{7,5},{8,10},{9,11},{10,... | collective-permute-start | bytes 20 | tf_op jit(solution)/shard_map/ppermute | solution.py:195
  33.0 2.6 %collective-permute-start.9 = (bf16[24,4224]{1,0:T(8,128)(2,1)}, bf16[24,4224]{1,0:T(8,128)(2,1)S(1)}, u32[]{:S(2)}, u32[]{:S(2)}) collective-permute-start(bf16[24,4224]{1,0:T(8,128)(2,1)} %copy-done.29), channel_id=1, source_target_pairs={{0,8},{1,9},{2,10},{3,11},{4,12},{5,13},{6,14},{7,15},{8,0},{9,1},... | collective-permute-start | bytes 608264 | tf_op jit(solution)/shard_map/ppermute | solution.py:195
  37.6 11.0 %collective-permute-done.9 = bf16[24,4224]{1,0:T(8,128)(2,1)S(1)} collective-permute-done((bf16[24,4224]{1,0:T(8,128)(2,1)}, bf16[24,4224]{1,0:T(8,128)(2,1)S(1)}, u32[]{:S(2)}, u32[]{:S(2)}) %collective-permute-start.9) | collective-permute-done | bytes 202784 | tf_op jit(solution)/shard_map/ppermute | solution.py:195
  49.0 6.2 %collective-permute-start.4 = (s32[]{:T(128)}, s32[]{:T(128)}, u32[]{:S(2)}, u32[]{:S(2)}) collective-permute-start(s32[]{:T(128)} %max.18), channel_id=1, source_target_pairs={{0,8},{1,9},{2,10},{3,11},{4,12},{5,13},{6,14},{7,15},{8,0},{9,1},... | collective-permute-start | bytes 20 | tf_op jit(solution)/shard_map/ppermute | solution.py:195
  58.2 2.9 %collective-permute-start.18 = (bf16[16,8320]{1,0:T(8,128)(2,1)}, bf16[16,8320]{1,0:T(8,128)(2,1)S(1)}, u32[]{:S(2)}, u32[]{:S(2)}) collective-permute-start(bf16[16,8320]{1,0:T(8,128)(2,1)} %copy-done.28), channel_id=1, source_target_pairs={{0,8},{1,9},{2,10},{3,11},{4,12},{5,13},{6,14},{7,15},{8,0},{9,1},... | collective-permute-start | bytes 798728 | tf_op jit(solution)/shard_map/ppermute | solution.py:195
  61.9 12.2 %collective-permute-done.18.refs_1_ = bf16[16,8320]{1,0:T(8,128)(2,1)S(1)} collective-permute-done((bf16[16,8320]{1,0:T(8,128)(2,1)}, bf16[16,8320]{1,0:T(8,128)(2,1)S(1)}, u32[]{:S(2)}, u32[]{:S(2)}) %collective-permute-start.18) | collective-permute-done | bytes 266272 | tf_op jit(solution)/shard_map/ppermute | solution.py:195
  77.5 10.7 %collective-permute-done.20.refs_3_ = bf16[16,8320]{1,0:T(8,128)(2,1)S(1)} collective-permute-done((bf16[16,8320]{1,0:T(8,128)(2,1)}, bf16[16,8320]{1,0:T(8,128)(2,1)S(1)}, u32[]{:S(2)}, u32[]{:S(2)}) %collective-permute-start.20) | collective-permute-done | bytes 266272 | tf_op jit(solution)/shard_map/ppermute | solution.py:195
  93.1 12.1 %collective-permute-done.24.refs_1_ = bf16[16,8320]{1,0:T(8,128)(2,1)S(1)} collective-permute-done((bf16[16,8320]{1,0:T(8,128)(2,1)}, bf16[16,8320]{1,0:T(8,128)(2,1)S(1)}, u32[]{:S(2)}, u32[]{:S(2)}) %collective-permute-start.24) | collective-permute-done | bytes 266272 | tf_op jit(solution)/shard_map/ppermute | solution.py:195
  111.0 2.4 %collective-permute-start.37 = (bf16[16,8320]{1,0:T(8,128)(2,1)}, bf16[16,8320]{1,0:T(8,128)(2,1)}, u32[]{:S(2)}, u32[]{:S(2)}) collective-permute-start(bf16[16,8320]{1,0:T(8,128)(2,1)} %copy-done.19), channel_id=1, source_target_pairs={{0,14},{1,15},{2,12},{3,13},{4,10},{5,11},{6,8},{7,9},{8,6},{9,7},... | collective-permute-start | bytes 798728 | tf_op jit(solution)/shard_map/ppermute | solution.py:195
  113.4 2.7 %collective-permute-start.38 = (bf16[16,8320]{1,0:T(8,128)(2,1)}, bf16[16,8320]{1,0:T(8,128)(2,1)}, u32[]{:S(2)}, u32[]{:S(2)}) collective-permute-start(bf16[16,8320]{1,0:T(8,128)(2,1)} %copy-done.18), channel_id=1, source_target_pairs={{0,15},{1,14},{2,13},{3,12},{4,11},{5,10},{6,9},{7,8},{8,7},{9,6},... | collective-permute-start | bytes 798728 | tf_op jit(solution)/shard_map/ppermute | solution.py:195
  116.1 8.1 %shard_map.69 = (bf16[64,512]{1,0:T(8,128)(2,1)S(1)}, bf16[64,512]{1,0:T(8,128)(2,1)S(1)}, bf16[64,512]{1,0:T(8,128)(2,1)S(1)}, bf16[64,512]{1,0:T(8,128)(2,1)S(1)}) custom-call(s32[1]{0:T(128)} %bitcast.12.first_ref, bf16[256,8192]{1,0:T(8,128)(2,1)} %bitcast.28, bf16[256,512]{1,0:T(8,128)(2,1)} %bitcast.36, ...), custom_call_target="tpu_custom_call" | custom-call | flops 1610612736 | bytes 6291456 | tf_op jit(solution)/shard_map/pallas_call | solution.py:183
  124.3 2.6 %shard_map.70 = (bf16[32,512]{1,0:T(8,128)(2,1)S(1)}, bf16[32,512]{1,0:T(8,128)(2,1)S(1)}, bf16[32,512]{1,0:T(8,128)(2,1)S(1)}, bf16[32,512]{1,0:T(8,128)(2,1)S(1)}) custom-call(s32[1]{0:T(128)} %bitcast.12.first_ref, bf16[256,8192]{1,0:T(8,128)(2,1)S(1)} %bitcast.29, bf16[256,512]{1,0:T(8,128)(2,1)S(1)} %bitcast.37, bf16[16,8320]{1,0:T(8,128)(2,1)S(1)} %copy-done.3, ...), custom_call_target="tpu_custom_call" | custom-call | flops 268435456 | bytes 6291456 | tf_op jit(solution)/shard_map/pallas_call | solution.py:183
  128.6 14.2 %collective-permute-done.26.refs_3_ = bf16[16,8320]{1,0:T(8,128)(2,1)} collective-permute-done((bf16[16,8320]{1,0:T(8,128)(2,1)}, bf16[16,8320]{1,0:T(8,128)(2,1)}, u32[]{:S(2)}, u32[]{:S(2)}) %collective-permute-start.26) | collective-permute-done | bytes 266272 | tf_op jit(solution)/shard_map/ppermute | solution.py:195
  144.7 15.9 %collective-permute-start.21 = (bf16[32,512]{1,0:T(8,128)(2,1)S(1)}, bf16[32,512]{1,0:T(8,128)(2,1)S(1)}, u32[]{:S(2)}, u32[]{:S(2)}) collective-permute-start(bf16[32,512]{1,0:T(8,128)(2,1)S(1)} %get-tuple-element.221), channel_id=1, source_target_pairs={{0,4},{1,5},{2,6},{3,7},{4,0},{5,1},{6,2},{7,3},{8,12},{9,13},{10,... | collective-permute-start | bytes 98312 | tf_op jit(solution)/shard_map/ppermute | solution.py:195
  160.6 5.4 %collective-permute-start.22 = (bf16[32,512]{1,0:T(8,128)(2,1)S(1)}, bf16[32,512]{1,0:T(8,128)(2,1)S(1)}, u32[]{:S(2)}, u32[]{:S(2)}) collective-permute-start(bf16[32,512]{1,0:T(8,128)(2,1)S(1)} %get-tuple-element.222), channel_id=1, source_target_pairs={{0,5},{1,4},{2,7},{3,6},{4,1},{5,0},{6,3},{7,2},{8,13},{9,12},{10,... | collective-permute-start | bytes 98312 | tf_op jit(solution)/shard_map/ppermute | solution.py:195
  166.0 2.5 %shard_map.72 = (bf16[32,512]{1,0:T(8,128)(2,1)S(1)}, bf16[32,512]{1,0:T(8,128)(2,1)S(1)}, bf16[32,512]{1,0:T(8,128)(2,1)S(1)}, bf16[32,512]{1,0:T(8,128)(2,1)S(1)}) custom-call(s32[1]{0:T(128)} %bitcast.12.first_ref, bf16[256,8192]{1,0:T(8,128)(2,1)S(1)} %bitcast.31, bf16[256,512]{1,0:T(8,128)(2,1)S(1)} %bitcast.39, bf16[16,8320]{1,0:T(8,128)(2,1)S(1)} %copy-done.7, ...), custom_call_target="tpu_custom_call" | custom-call | flops 268435456 | bytes 6291456 | tf_op jit(solution)/shard_map/pallas_call | solution.py:183
  175.9 5.9 %fusion.10 = f32[256,512]{1,0:T(8,128)S(1)} fusion(bf16[256,8192]{1,0:T(8,128)(2,1)S(1)} %copy-done.32, bf16[8192,512]{1,0:T(8,128)(2,1)} %param.9), kind=kOutput, calls=%fused_computation.57 | convolution fusion | flops 2147483648 | bytes 13107200 | tf_op jit(solution)/shard_map/dot_general | solution.py:211
  181.8 2.6 %shard_map.73 = (bf16[32,512]{1,0:T(8,128)(2,1)S(1)}, bf16[32,512]{1,0:T(8,128)(2,1)S(1)}) custom-call(s32[1]{0:T(128)} %bitcast.12.first_ref, bf16[256,8192]{1,0:T(8,128)(2,1)S(1)} %bitcast.32, bf16[256,512]{1,0:T(8,128)(2,1)S(1)} %bitcast.40, bf16[16,8320]{1,0:T(8,128)(2,1)} %collective-permute-done.33.refs_0_, ...), custom_call_target="tpu_custom_call" | custom-call | flops 134217728 | bytes 6291456 | tf_op jit(solution)/shard_map/pallas_call | solution.py:183
  184.4 2.6 %shard_map.74 = (bf16[32,512]{1,0:T(8,128)(2,1)S(1)}, bf16[32,512]{1,0:T(8,128)(2,1)S(1)}) custom-call(s32[1]{0:T(128)} %bitcast.12.first_ref, bf16[256,8192]{1,0:T(8,128)(2,1)S(1)} %bitcast.33, bf16[256,512]{1,0:T(8,128)(2,1)S(1)} %bitcast.41, bf16[16,8320]{1,0:T(8,128)(2,1)} %collective-permute-done.37.refs_0_, ...), custom_call_target="tpu_custom_call" | custom-call | flops 134217728 | bytes 6291456 | tf_op jit(solution)/shard_map/pallas_call | solution.py:183
  188.7 2.5 %collective-permute-start.35 = (bf16[32,512]{1,0:T(8,128)(2,1)S(1)}, bf16[32,512]{1,0:T(8,128)(2,1)S(1)}, u32[]{:S(2)}, u32[]{:S(2)}) collective-permute-start(bf16[32,512]{1,0:T(8,128)(2,1)S(1)} %get-tuple-element.235), channel_id=1, source_target_pairs={{0,12},{1,13},{2,14},{3,15},{4,8},{5,9},{6,10},{7,11},{8,4},{9,5},... | collective-permute-start | bytes 98312 | tf_op jit(solution)/shard_map/ppermute | solution.py:195
  192.1 3.1 %collective-permute-start.39 = (bf16[32,512]{1,0:T(8,128)(2,1)S(1)}, bf16[32,512]{1,0:T(8,128)(2,1)S(1)}, u32[]{:S(2)}, u32[]{:S(2)}) collective-permute-start(bf16[32,512]{1,0:T(8,128)(2,1)S(1)} %get-tuple-element.239), channel_id=1, source_target_pairs={{0,14},{1,15},{2,12},{3,13},{4,10},{5,11},{6,8},{7,9},{8,6},{9,7},... | collective-permute-start | bytes 98312 | tf_op jit(solution)/shard_map/ppermute | solution.py:195
  198.8 2.6 %collective-permute-done.40 = bf16[32,512]{1,0:T(8,128)(2,1)S(1)} collective-permute-done((bf16[32,512]{1,0:T(8,128)(2,1)S(1)}, bf16[32,512]{1,0:T(8,128)(2,1)S(1)}, u32[]{:S(2)}, u32[]{:S(2)}) %collective-permute-start.40) | collective-permute-done | bytes 32800 | tf_op jit(solution)/shard_map/ppermute | solution.py:195
  (157 shorter events, 57.9 us)
Async XLA Ops:
  2.2 19.9 %collective-permute-start = (s32[]{:T(128)}, s32[]{:T(128)}, u32[]{:S(2)}, u32[]{:S(2)}) collective-permute-start(s32[]{:T(128)} %get-tuple-element.242), channel_id=1, source_target_pairs={{0,16},{16,0},{1,17},{17,1},{2,18},{18,2},{3,19},{19,3},{4,20},{20... | collective-permute-start | bytes 20 | tf_op jit(solution)/shard_map/ppermute | solution.py:263
  9.0 46.6 %collective-permute-start.5 = (bf16[16,8320]{1,0:T(8,128)(2,1)S(1)}, bf16[16,8320]{1,0:T(8,128)(2,1)S(1)}, u32[]{:S(2)}, u32[]{:S(2)}) collective-permute-start(bf16[16,8320]{1,0:T(8,128)(2,1)S(1)} %get-tuple-element.202), channel_id=1, source_target_pairs={{0,1},{1,0},{2,3},{3,2},{4,5},{5,4},{6,7},{7,6},{8,9},{9,8},{10,11... | collective-permute-start | bytes 798728 | tf_op jit(solution)/shard_map/ppermute | solution.py:195
  9.0 48.2 %collective-permute-start.6 = (bf16[16,8320]{1,0:T(8,128)(2,1)S(1)}, bf16[16,8320]{1,0:T(8,128)(2,1)S(1)}, u32[]{:S(2)}, u32[]{:S(2)}) collective-permute-start(bf16[16,8320]{1,0:T(8,128)(2,1)S(1)} %get-tuple-element.203), channel_id=1, source_target_pairs={{0,2},{1,3},{2,0},{3,1},{4,6},{5,7},{6,4},{7,5},{8,10},{9,11},{10,... | collective-permute-start | bytes 798728 | tf_op jit(solution)/shard_map/ppermute | solution.py:195
  10.5 47.7 %collective-permute-start.7 = (bf16[16,8320]{1,0:T(8,128)(2,1)}, bf16[16,8320]{1,0:T(8,128)(2,1)}, u32[]{:S(2)}, u32[]{:S(2)}) collective-permute-start(bf16[16,8320]{1,0:T(8,128)(2,1)} %get-tuple-element.204), channel_id=1, source_target_pairs={{0,3},{1,2},{2,1},{3,0},{4,7},{5,6},{6,5},{7,4},{8,11},{9,10},{10,... | collective-permute-start | bytes 798728 | tf_op jit(solution)/shard_map/ppermute | solution.py:195
  13.0 23.3 %collective-permute-start.8 = (bf16[24,4224]{1,0:T(8,128)(2,1)}, bf16[24,4224]{1,0:T(8,128)(2,1)}, u32[]{:S(2)}, u32[]{:S(2)}) collective-permute-start(bf16[24,4224]{1,0:T(8,128)(2,1)} %get-tuple-element.206), channel_id=1, source_target_pairs={{0,4},{1,5},{2,6},{3,7},{4,0},{5,1},{6,2},{7,3},{8,12},{9,13},{10,... | collective-permute-start | bytes 608264 | tf_op jit(solution)/shard_map/ppermute | solution.py:195
  55.6 54.4 %collective-permute-start.11 = (bf16[96,4224]{1,0:T(8,128)(2,1)S(1)}, bf16[96,4224]{1,0:T(8,128)(2,1)S(1)}, u32[]{:S(2)}, u32[]{:S(2)}) collective-permute-start(bf16[96,4224]{1,0:T(8,128)(2,1)S(1)} %constant_dynamic-update-slice_fusion.refs_0_), channel_id=1, source_target_pairs={{0,1},{1,0},{2,3},{3,2},{4,5},{5,4},{6,7},{7,6},{8,9},{9,8},{10,11... | collective-permute-start | bytes 2433032 | tf_op jit(solution)/shard_map/ppermute | solution.py:195
  55.6 55.4 %collective-permute-start.12 = (bf16[96,4224]{1,0:T(8,128)(2,1)S(1)}, bf16[96,4224]{1,0:T(8,128)(2,1)S(1)}, u32[]{:S(2)}, u32[]{:S(2)}) collective-permute-start(bf16[96,4224]{1,0:T(8,128)(2,1)S(1)} %constant_dynamic-update-slice_fusion.refs_0_), channel_id=1, source_target_pairs={{0,2},{1,3},{2,0},{3,1},{4,6},{5,7},{6,4},{7,5},{8,10},{9,11},{10,... | collective-permute-start | bytes 2433032 | tf_op jit(solution)/shard_map/ppermute | solution.py:195
  57.9 55.5 %collective-permute-start.13 = (bf16[96,4224]{1,0:T(8,128)(2,1)S(1)}, bf16[96,4224]{1,0:T(8,128)(2,1)S(1)}, u32[]{:S(2)}, u32[]{:S(2)}) collective-permute-start(bf16[96,4224]{1,0:T(8,128)(2,1)S(1)} %constant_dynamic-update-slice_fusion.refs_0_), channel_id=1, source_target_pairs={{0,3},{1,2},{2,1},{3,0},{4,7},{5,6},{6,5},{7,4},{8,11},{9,10},{10,... | collective-permute-start | bytes 2433032 | tf_op jit(solution)/shard_map/ppermute | solution.py:195
  58.2 15.8 %collective-permute-start.18 = (bf16[16,8320]{1,0:T(8,128)(2,1)}, bf16[16,8320]{1,0:T(8,128)(2,1)S(1)}, u32[]{:S(2)}, u32[]{:S(2)}) collective-permute-start(bf16[16,8320]{1,0:T(8,128)(2,1)} %copy-done.28), channel_id=1, source_target_pairs={{0,8},{1,9},{2,10},{3,11},{4,12},{5,13},{6,14},{7,15},{8,0},{9,1},... | collective-permute-start | bytes 798728 | tf_op jit(solution)/shard_map/ppermute | solution.py:195
  89.0 16.2 %collective-permute-start.24 = (bf16[16,8320]{1,0:T(8,128)(2,1)}, bf16[16,8320]{1,0:T(8,128)(2,1)S(1)}, u32[]{:S(2)}, u32[]{:S(2)}) collective-permute-start(bf16[16,8320]{1,0:T(8,128)(2,1)} %copy-done.24), channel_id=1, source_target_pairs={{0,10},{1,11},{2,8},{3,9},{4,14},{5,15},{6,12},{7,13},{8,2},{9,3},... | collective-permute-start | bytes 798728 | tf_op jit(solution)/shard_map/ppermute | solution.py:195
  105.9 36.9 %collective-permute-start.26 = (bf16[16,8320]{1,0:T(8,128)(2,1)}, bf16[16,8320]{1,0:T(8,128)(2,1)}, u32[]{:S(2)}, u32[]{:S(2)}) collective-permute-start(bf16[16,8320]{1,0:T(8,128)(2,1)} %copy-done.22), channel_id=1, source_target_pairs={{0,11},{1,10},{2,9},{3,8},{4,15},{5,14},{6,13},{7,12},{8,3},{9,2},... | collective-permute-start | bytes 798728 | tf_op jit(solution)/shard_map/ppermute | solution.py:195
  108.1 34.9 %collective-permute-start.33 = (bf16[16,8320]{1,0:T(8,128)(2,1)}, bf16[16,8320]{1,0:T(8,128)(2,1)}, u32[]{:S(2)}, u32[]{:S(2)}) collective-permute-start(bf16[16,8320]{1,0:T(8,128)(2,1)} %copy-done.21), channel_id=1, source_target_pairs={{0,12},{1,13},{2,14},{3,15},{4,8},{5,9},{6,10},{7,11},{8,4},{9,5},... | collective-permute-start | bytes 798728 | tf_op jit(solution)/shard_map/ppermute | solution.py:195
  109.9 34.2 %collective-permute-start.34 = (bf16[16,8320]{1,0:T(8,128)(2,1)}, bf16[16,8320]{1,0:T(8,128)(2,1)}, u32[]{:S(2)}, u32[]{:S(2)}) collective-permute-start(bf16[16,8320]{1,0:T(8,128)(2,1)} %copy-done.20), channel_id=1, source_target_pairs={{0,13},{1,12},{2,15},{3,14},{4,9},{5,8},{6,11},{7,10},{8,5},{9,4},... | collective-permute-start | bytes 798728 | tf_op jit(solution)/shard_map/ppermute | solution.py:195
  111.0 33.7 %collective-permute-start.37 = (bf16[16,8320]{1,0:T(8,128)(2,1)}, bf16[16,8320]{1,0:T(8,128)(2,1)}, u32[]{:S(2)}, u32[]{:S(2)}) collective-permute-start(bf16[16,8320]{1,0:T(8,128)(2,1)} %copy-done.19), channel_id=1, source_target_pairs={{0,14},{1,15},{2,12},{3,13},{4,10},{5,11},{6,8},{7,9},{8,6},{9,7},... | collective-permute-start | bytes 798728 | tf_op jit(solution)/shard_map/ppermute | solution.py:195
  113.4 47.2 %collective-permute-start.38 = (bf16[16,8320]{1,0:T(8,128)(2,1)}, bf16[16,8320]{1,0:T(8,128)(2,1)}, u32[]{:S(2)}, u32[]{:S(2)}) collective-permute-start(bf16[16,8320]{1,0:T(8,128)(2,1)} %copy-done.18), channel_id=1, source_target_pairs={{0,15},{1,14},{2,13},{3,12},{4,11},{5,10},{6,9},{7,8},{8,7},{9,6},... | collective-permute-start | bytes 798728 | tf_op jit(solution)/shard_map/ppermute | solution.py:195
  142.8 25.7 %collective-permute-start.14 = (bf16[32,512]{1,0:T(8,128)(2,1)S(1)}, bf16[32,512]{1,0:T(8,128)(2,1)S(1)}, u32[]{:S(2)}, u32[]{:S(2)}) collective-permute-start(bf16[32,512]{1,0:T(8,128)(2,1)S(1)} %get-tuple-element.214), channel_id=1, source_target_pairs={{0,1},{1,0},{2,3},{3,2},{4,5},{5,4},{6,7},{7,6},{8,9},{9,8},{10,11... | collective-permute-start | bytes 98312 | tf_op jit(solution)/shard_map/ppermute | solution.py:195
  142.9 26.7 %collective-permute-start.15 = (bf16[32,512]{1,0:T(8,128)(2,1)S(1)}, bf16[32,512]{1,0:T(8,128)(2,1)S(1)}, u32[]{:S(2)}, u32[]{:S(2)}) collective-permute-start(bf16[32,512]{1,0:T(8,128)(2,1)S(1)} %get-tuple-element.215), channel_id=1, source_target_pairs={{0,2},{1,3},{2,0},{3,1},{4,6},{5,7},{6,4},{7,5},{8,10},{9,11},{10,... | collective-permute-start | bytes 98312 | tf_op jit(solution)/shard_map/ppermute | solution.py:195
  144.2 27.1 %collective-permute-start.16 = (bf16[32,512]{1,0:T(8,128)(2,1)S(1)}, bf16[32,512]{1,0:T(8,128)(2,1)S(1)}, u32[]{:S(2)}, u32[]{:S(2)}) collective-permute-start(bf16[32,512]{1,0:T(8,128)(2,1)S(1)} %get-tuple-element.216), channel_id=1, source_target_pairs={{0,3},{1,2},{2,1},{3,0},{4,7},{5,6},{6,5},{7,4},{8,11},{9,10},{10,... | collective-permute-start | bytes 98312 | tf_op jit(solution)/shard_map/ppermute | solution.py:195
  144.7 27.8 %collective-permute-start.21 = (bf16[32,512]{1,0:T(8,128)(2,1)S(1)}, bf16[32,512]{1,0:T(8,128)(2,1)S(1)}, u32[]{:S(2)}, u32[]{:S(2)}) collective-permute-start(bf16[32,512]{1,0:T(8,128)(2,1)S(1)} %get-tuple-element.221), channel_id=1, source_target_pairs={{0,4},{1,5},{2,6},{3,7},{4,0},{5,1},{6,2},{7,3},{8,12},{9,13},{10,... | collective-permute-start | bytes 98312 | tf_op jit(solution)/shard_map/ppermute | solution.py:195
  168.5 18.5 %collective-permute-start.27 = (bf16[32,512]{1,0:T(8,128)(2,1)S(1)}, bf16[32,512]{1,0:T(8,128)(2,1)S(1)}, u32[]{:S(2)}, u32[]{:S(2)}) collective-permute-start(bf16[32,512]{1,0:T(8,128)(2,1)S(1)} %get-tuple-element.227), channel_id=1, source_target_pairs={{0,6},{1,7},{2,4},{3,5},{4,2},{5,3},{6,0},{7,1},{8,14},{9,15},{10,... | collective-permute-start | bytes 98312 | tf_op jit(solution)/shard_map/ppermute | solution.py:195
  169.6 19.1 %collective-permute-start.28 = (bf16[32,512]{1,0:T(8,128)(2,1)S(1)}, bf16[32,512]{1,0:T(8,128)(2,1)S(1)}, u32[]{:S(2)}, u32[]{:S(2)}) collective-permute-start(bf16[32,512]{1,0:T(8,128)(2,1)S(1)} %get-tuple-element.228), channel_id=1, source_target_pairs={{0,7},{1,6},{2,5},{3,4},{4,3},{5,2},{6,1},{7,0},{8,15},{9,14},{10,... | collective-permute-start | bytes 98312 | tf_op jit(solution)/shard_map/ppermute | solution.py:195
  171.3 19.9 %collective-permute-start.29 = (bf16[32,512]{1,0:T(8,128)(2,1)S(1)}, bf16[32,512]{1,0:T(8,128)(2,1)S(1)}, u32[]{:S(2)}, u32[]{:S(2)}) collective-permute-start(bf16[32,512]{1,0:T(8,128)(2,1)S(1)} %get-tuple-element.229), channel_id=1, source_target_pairs={{0,8},{1,9},{2,10},{3,11},{4,12},{5,13},{6,14},{7,15},{8,0},{9,1},... | collective-permute-start | bytes 98312 | tf_op jit(solution)/shard_map/ppermute | solution.py:195
  172.4 19.7 %collective-permute-start.30 = (bf16[32,512]{1,0:T(8,128)(2,1)S(1)}, bf16[32,512]{1,0:T(8,128)(2,1)S(1)}, u32[]{:S(2)}, u32[]{:S(2)}) collective-permute-start(bf16[32,512]{1,0:T(8,128)(2,1)S(1)} %get-tuple-element.230), channel_id=1, source_target_pairs={{0,9},{1,8},{2,11},{3,10},{4,13},{5,12},{6,15},{7,14},{8,1},{9,0},... | collective-permute-start | bytes 98312 | tf_op jit(solution)/shard_map/ppermute | solution.py:195
  173.9 21.4 %collective-permute-start.31 = (bf16[32,512]{1,0:T(8,128)(2,1)S(1)}, bf16[32,512]{1,0:T(8,128)(2,1)S(1)}, u32[]{:S(2)}, u32[]{:S(2)}) collective-permute-start(bf16[32,512]{1,0:T(8,128)(2,1)S(1)} %get-tuple-element.231), channel_id=1, source_target_pairs={{0,10},{1,11},{2,8},{3,9},{4,14},{5,15},{6,12},{7,13},{8,2},{9,3},... | collective-permute-start | bytes 98312 | tf_op jit(solution)/shard_map/ppermute | solution.py:195
  (53 other events, 548.6 us)

commit v2 on v1

--- a/solution.py
+++ b/solution.py
@@ -13,9 +13,6 @@
 SPARE = 12
 NOTE = 128
 STEP = 1024
-FIRST = (1, 2, 3)
-REST = (4, 8, 5, 9, 6, 10, 7, 11, 12, 13, 14, 15)
-GROUPS = ((0, 1, 2, 3), (4, 8, 5, 9), (6, 10, 7, 11), (12, 13), (14, 15))
 VMEM = pl.BlockSpec(memory_space=pltpu.VMEM)
 SMEM = pl.BlockSpec(memory_space=pltpu.SMEM)
 
@@ -51,11 +48,6 @@
     )
 
 
-def one_hot(at, starts, size):
-    ids = [lax.broadcasted_iota(jnp.int32, (size, at.shape[1]), 0) + s for s in starts]
-    return (jnp.concatenate(ids, axis=0) == at).astype(jnp.float32).astype(jnp.bfloat16)
-
-
 def pack_over_body(main_rows, planes, at_ref, info_ref, tokens_ref, *outs):
     at = at_ref[...]
     half = tokens_ref.shape[1] // 2
@@ -86,23 +78,20 @@
     )
 
 
-def pack_body(starts, at_ref, info_ref, tokens_ref, *outs):
+def pack_body(flag_ref, at_ref, info_ref, tokens_ref, out):
     depth = tokens_ref.shape[1]
-    size = outs[0].shape[0]
-    pick = one_hot(at_ref[...], starts, size)
-
-    def put(value, columns):
-        for j, out in enumerate(outs):
-            out[:, columns] = value[size * j : size * (j + 1)].astype(jnp.bfloat16)
-
+    shape = (out.shape[0], at_ref.shape[1])
+    pick = lax.broadcasted_iota(jnp.int32, shape, 0) == at_ref[...]
+    pick = pick.astype(jnp.float32).astype(jnp.bfloat16)
     for c in range(0, depth, STEP):
-        put(
-            jnp.dot(pick, tokens_ref[:, c : c + STEP], preferred_element_type=jnp.float32),
-            slice(c, c + STEP),
-        )
-    put(
-        jnp.dot(pick, info_ref[...], preferred_element_type=jnp.float32), slice(depth, depth + NOTE)
-    )
+        out[:, c : c + STEP] = jnp.dot(
+            pick, tokens_ref[:, c : c + STEP], preferred_element_type=jnp.float32
+        ).astype(jnp.bfloat16)
+    note = jnp.dot(pick, info_ref[...], preferred_element_type=jnp.float32)
+    flag = jnp.where(
+        lax.broadcasted_iota(jnp.int32, note.shape, 1) == 1, flag_ref[0].astype(jnp.float32), 0.0
+    )
+    out[:, depth : depth + NOTE] = (note + flag).astype(jnp.bfloat16)
 
 
 def low_delta(low, note, first, rank, up):
@@ -111,25 +100,20 @@
     return jnp.dot(low.astype(jnp.bfloat16), up, preferred_element_type=jnp.float32)
 
 
-def adapt_body(keys, rank, first_ref, down_ref, up_ref, *refs):
-    rows_refs, over_refs = refs[: len(keys)], refs[len(keys) : -len(keys)]
-    outs = refs[-len(keys) :]
+def adapt_body(rank, first_ref, down_ref, up_ref, rows_ref, out, flag_out):
     depth = down_ref.shape[1]
-    size = rows_refs[0].shape[0]
-    low = jnp.zeros((size * len(keys), down_ref.shape[0]), jnp.float32)
+    low = jnp.zeros((rows_ref.shape[0], down_ref.shape[0]), jnp.float32)
     for c in range(0, depth, STEP):
-        rows = jnp.concatenate([r[:, c : c + STEP] for r in rows_refs], axis=0)
         low += lax.dot_general(
-            rows,
+            rows_ref[:, c : c + STEP],
             down_ref[:, c : c + STEP],
             (((1,), (1,)), ((), ())),
             preferred_element_type=jnp.float32,
         )
-    note = jnp.concatenate([r[:, depth : depth + NOTE] for r in rows_refs], axis=0)[:, :1]
-    delta = low_delta(low, note, first_ref[0], rank, up_ref[...]).astype(jnp.bfloat16)
-    for j, k in enumerate(keys):
-        outs[j][:size] = delta[size * j : size * (j + 1)]
-        outs[j][size:] = over_refs[k % PLANE][16 * (k // PLANE) : 16 * (k // PLANE + 1)]
+    note = rows_ref[:, depth : depth + NOTE].astype(jnp.float32)
+    out[...] = low_delta(low, note[:, :1], first_ref[0], rank, up_ref[...]).astype(jnp.bfloat16)
+    most = jnp.max(note, axis=0, keepdims=True)
+    flag_out[...] = jnp.broadcast_to(most, flag_out.shape).astype(jnp.bfloat16)
 
 
 def adapt_over_body(planes, rank, first_ref, down_ref, up_ref, *refs):
@@ -163,16 +147,15 @@
         out[...] = low_delta(low, note, first_ref[0], rank, up_ref[...]).astype(jnp.bfloat16)
 
 
-def final_body(room, main_rows, at_ref, base_ref, *refs):
-    *backs, out = refs
-    back = jnp.concatenate([b[...] for b in backs], axis=0)
-    size = backs[0].shape[0]
-    shape = (back.shape[0], at_ref.shape[1])
-    row = lax.broadcasted_iota(jnp.int32, shape, 0)
-    k, i = row // size, row % size
-    spare = main_rows + (k // PLANE) * SPARE + (i - room)
-    came = jnp.where(i < room, k * room + i, jnp.where(i < room + SPARE, spare, -2))
-    pick = (came == at_ref[...]).astype(jnp.float32).astype(jnp.bfloat16)
+def final_body(at_ref, base_ref, back_ref, *refs):
+    *overs, out = refs
+    back = jnp.concatenate([back_ref[...]] + [o[...] for o in overs], axis=0)
+    main_rows, size = back_ref.shape[0], overs[0].shape[0]
+    row = lax.broadcasted_iota(jnp.int32, (back.shape[0], at_ref.shape[1]), 0)
+    b, i = (row - main_rows) // size, (row - main_rows) % size
+    spare = jnp.where(i < SPARE, main_rows + b * SPARE + i, -2)
+    pick = jnp.where(row < main_rows, row, spare) == at_ref[...]
+    pick = pick.astype(jnp.float32).astype(jnp.bfloat16)
     delta = lax.dot_general(
         pick, back, (((0,), (0,)), ((), ())), preferred_element_type=jnp.float32
     )
@@ -215,18 +198,17 @@
         delta = exchange(tokens, slot, owner, place, CAP * local, adapt_down, adapt_up)
         return (base_value + delta).astype(jnp.bfloat16)
 
-    block = owner ^ me
-    plane = block // PLANE
+    plane = (owner ^ me) // PLANE
     over = place >= room
     over_place = jnp.sum(
         (over[None, :] & (plane[:, None] == plane[None, :]) & before).astype(jnp.int32), axis=1
     )
     main_rows = count * room
     left = over & (over_place >= SPARE)
-    at = jnp.where(over, main_rows + plane * SPARE + over_place, block * room + place)
+    at = jnp.where(over, main_rows + plane * SPARE + over_place, owner * room + place)
     at = jnp.where(left, -1, at)[None, :]
     info = jnp.where(jnp.arange(NOTE)[None, :] == 0, slot[:, None] + 1, 0).astype(jnp.bfloat16)
-    some_left = jnp.max(left.astype(jnp.int32))
+    some_left = jnp.max(left.astype(jnp.int32)).reshape(1)
 
     spare = call(
         functools.partial(pack_over_body, main_rows, planes),
@@ -236,40 +218,27 @@
         2 * 96 * row_count * depth,
         6 * 2**20,
     )
-    blocks = {}
-    for keys in (FIRST, (0,) + REST):
-        made = call(
-            functools.partial(pack_body, [k * room for k in keys]),
-            [(room, depth + NOTE)] * len(keys),
-            (at, info, tokens),
-            [VMEM] * 3,
-            2 * len(keys) * room * row_count * depth,
-            8 * 2**20,
-        )
-        blocks.update(zip(keys, made, strict=True))
-
-    along = jnp.concatenate(
-        [spare[0]] + [swap(spare[b], b * PLANE) for b in range(1, planes)], axis=0
-    )
-    shared = [along] + [swap(along, a) for a in range(1, PLANE)]
-
-    got = {0: blocks[0]}
-    for k in FIRST + REST:
-        got[k] = swap(blocks[k], k)
-
-    seen = some_left
-    for g in range(1, lax.axis_size("grp")):
-        groups = lax.axis_size("grp")
-        other = lax.ppermute(some_left, "grp", [(s, (s + g) % groups) for s in range(groups)])
-        seen = jnp.maximum(seen, other)
-    step = 1
-    while step < count:
-        seen = jnp.maximum(seen, swap(seen, step))
-        step *= 2
+    blocks = call(
+        pack_body,
+        [(main_rows, depth + NOTE)],
+        (some_left, at, info, tokens),
+        [SMEM] + [VMEM] * 3,
+        2 * main_rows * row_count * depth,
+        8 * 2**20,
+    )[0]
+
+    got = lax.all_to_all(
+        blocks.reshape(count, room, depth + NOTE), "ad", split_axis=0, concat_axis=0, tiled=True
+    ).reshape(main_rows, depth + NOTE)
 
     first = (me * local).reshape(1)
     down = adapt_down.transpose(0, 2, 1).reshape(local * rank, depth)
     up = adapt_up.reshape(local * rank, width)
+
+    along = jnp.concatenate(
+        [spare[0]] + [swap(spare[b], b * PLANE) for b in range(1, planes)], axis=0
+    )
+    shared = [along] + [swap(along, a) for a in range(1, PLANE)]
     over_delta = call(
         functools.partial(adapt_over_body, planes, rank),
         [(16 * planes, width)] * PLANE,
@@ -278,27 +247,39 @@
         2 * 384 * depth * local * rank,
         6 * 2**20,
     )
-    back = {}
-    for keys in GROUPS:
-        made = call(
-            functools.partial(adapt_body, keys, rank),
-            [(room + 16, width)] * len(keys),
-            (first, down, up, *[got[k] for k in keys], *over_delta),
-            [SMEM] + [VMEM] * (2 + len(keys) + PLANE),
-            2 * room * len(keys) * depth * local * rank,
-            6 * 2**20,
-        )
-        for k, rows in zip(keys, made, strict=True):
-            back[k] = swap(rows, k) if k else rows
-    back = [back[k] for k in range(count)]
+    over_sum = over_delta[0]
+    for a in range(1, PLANE):
+        over_sum = over_sum + swap(over_delta[a], a)
+    over_back = [over_sum[:16]]
+    for b in range(1, planes):
+        over_back.append(swap(over_sum[16 * b : 16 * (b + 1)], b * PLANE))
+
+    delta, flags = call(
+        functools.partial(adapt_body, rank),
+        [(main_rows, width), (16, NOTE)],
+        (first, down, up, got),
+        [SMEM] + [VMEM] * 3,
+        2 * main_rows * depth * local * rank,
+        8 * 2**20,
+    )
+    back = lax.all_to_all(
+        delta.reshape(count, room, width), "ad", split_axis=0, concat_axis=0, tiled=True
+    ).reshape(main_rows, width)
+
+    some_left = flags[0, 1].astype(jnp.int32)
+    seen = some_left
+    groups = lax.axis_size("grp")
+    for g in range(1, groups):
+        other = lax.ppermute(some_left, "grp", [(s, (s + g) % groups) for s in range(groups)])
+        seen = jnp.maximum(seen, other)
 
     def finish(base):
         return call(
-            functools.partial(final_body, room, main_rows),
+            final_body,
             [(row_count, width)],
-            (at, base, *back),
-            [VMEM] * (2 + count),
-            2 * row_count * width * 512,
+            (at, base, back, *over_back),
+            [VMEM] * (3 + planes),
+            2 * row_count * width * 320,
             2**20,
         )[0]
 

time: 203 us -> 195 us (0.961)
  waiting for transfers between devices: 71.2 us -> 131 us
  starting transfers between devices: 77.5 us -> 29.9 us
  local copies, waits for them, and re-layouts: 13.8 us -> 3.48 us
  Pallas kernels: 27.4 us -> 19 us
  between operations: 4.37 us -> 1.59 us
    ppermute x40 -> x12, starting transfers between devices: 74.6 us -> 12.8 us  [swap(): return lax.ppermute(x, 'ad', [(s, s ^ k) for s in range(count)])]
    ppermute x40 -> x12, waiting for transfers between devices: 71.2 us -> 131 us  [swap(): return lax.ppermute(x, 'ad', [(s, s ^ k) for s in range(count)])]
    all_to_all x0 -> x2, starting transfers between devices: none -> 14.2 us  [the longest x1 7.43 us: on_device(): lax.all_to_all(blocks.reshape(count, room, depth + NOTE), 'ad', split_axi...]
    unnamed x75 -> x11, local copies, waits for them, and re-layouts: 13.8 us -> 2.79 us
    pallas_call x10 -> x5, Pallas kernels: 27.4 us -> 19 us  [call(): pl.pallas_call(body, in_specs=specs, out_specs=[VMEM] * len(outs), out_sh...]
  transfers between devices with their start and end apart: 41 -> 15, of which waited for: 14 -> 6; matrix products, arithmetic and copies ran while one was open for 3% -> 4% of each run, Pallas kernels for 13% -> 7%
where the time goes in v2:
time: 195 us; the launch traced here: 194 us
  waiting for transfers between devices  131 us (67%)
  starting transfers between devices  29.9 us (15%)
  Pallas kernels  19 us (10%)
  matrix products  6.97 us (4%)
  local copies, waits for them, and re-layouts  3.48 us (2%)
  other arithmetic  2.06 us (1%)
    ppermute x12, waiting for transfers between devices, swap(): return lax.ppermute(x, 'ad', [(s, s ^ k) for s in range(count)])  131 us
    pallas_call x5, Pallas kernels, call(): pl.pallas_call(body, in_specs=specs, out_specs=[VMEM] * len(outs), out_sh...  19 us
    ppermute x12, starting transfers between devices, swap(): return lax.ppermute(x, 'ad', [(s, s ^ k) for s in range(count)])  12.8 us
    all_to_all x1, starting transfers between devices, on_device(): lax.all_to_all(blocks.reshape(count, room, depth + NOTE), 'ad', split_axi...  7.43 us
    dot_general x1, matrix products, on_device(): jnp.dot(tokens, value_weight, preferred_element_type=jnp.float32)  6.97 us
    all_to_all x1, starting transfers between devices, on_device(): lax.all_to_all(delta.reshape(count, room, width), 'ad', split_axis=0, con...  6.79 us
  transfers between devices with their start and end apart: 15, of which 6 were waited for; matrix products, arithmetic and copies ran while one was open for 4% of the time, Pallas kernels for 7%

profile of v2, /device:TPU:0, one launch (start us, length us, event | category | flops | bytes accessed | tf_op | source)
XLA Modules:
  0.0 194.4 jit_solution(3744270212327016408)
XLA Ops:
  0.0 0.9 select_reduce_fusion.1
  2.1 4.1 %shard_map.66 = bf16[256,8320]{1,0:T(8,128)(2,1)S(1)} custom-call(s32[1]{0:T(128)} %bitcast.13.flag_ref, s32[1,256]{1,0:T(1,128)S(1)} %and_select_fusion.4.at_ref, bf16[256,128]{1,0:T(8,128)(2,1)S(1)} %select_convert_fusion.2.info_ref, bf16[256,8192]{1,0:T(8,128)(2,1)} %tokens_ref.3), custom_call_target="tpu_custom_call" | custom-call | flops 1073741824 | bytes 8388608 | tf_op jit(solution)/shard_map/pallas_call | solution.py:166
  6.2 2.0 %copy-done = bf16[256,8320]{1,0:T(8,128)(2,1)} copy-done((bf16[256,8320]{1,0:T(8,128)(2,1)}, bf16[256,8320]{1,0:T(8,128)(2,1)S(1)}, u32[]{:S(2)}) %copy-start) | copy-done | bytes 4259864
  8.2 7.4 %all-to-all-start.3 = ((bf16[16,16,8320]{2,1,0:T(8,128)(2,1)}), bf16[16,16,8320]{2,1,0:T(8,128)(2,1)}, u32[]{:S(2)}, u32[]{:S(2)}) async-start(bf16[16,16,8320]{2,1,0:T(8,128)(2,1)} %bitcast.35), calls=%async_computation.3 | async-start | bytes 8519680 | tf_op jit(solution)/shard_map/all_to_all | solution.py:230
  15.7 3.0 %shard_map.68 = (bf16[24,4224]{1,0:T(8,128)(2,1)S(1)}, bf16[24,4224]{1,0:T(8,128)(2,1)S(1)}, bf16[24,4224]{1,0:T(8,128)(2,1)S(1)}, bf16[24,4224]{1,0:T(8,128)(2,1)S(1)}) custom-call(s32[1,256]{1,0:T(1,128)S(1)} %and_select_fusion.4.at_ref, bf16[256,128]{1,0:T(8,128)(2,1)S(1)} %select_convert_fusion.2.info_ref, bf16[256,8192]{1,0:T(8,128)(2,1)} %tokens_ref.3), custom_call_target="tpu_custom_call" | custom-call | flops 402653184 | bytes 6291456 | tf_op jit(solution)/shard_map/pallas_call | solution.py:166
  18.7 1.9 %collective-permute-start.1 = (bf16[24,4224]{1,0:T(8,128)(2,1)S(1)}, bf16[24,4224]{1,0:T(8,128)(2,1)S(1)}, u32[]{:S(2)}, u32[]{:S(2)}) collective-permute-start(bf16[24,4224]{1,0:T(8,128)(2,1)S(1)} %get-tuple-element.108), channel_id=1, source_target_pairs={{0,4},{1,5},{2,6},{3,7},{4,0},{5,1},{6,2},{7,3},{8,12},{9,13},{10,... | collective-permute-start | bytes 608264 | tf_op jit(solution)/shard_map/ppermute | solution.py:178
  20.6 2.4 %collective-permute-start.2 = (bf16[24,4224]{1,0:T(8,128)(2,1)S(1)}, bf16[24,4224]{1,0:T(8,128)(2,1)S(1)}, u32[]{:S(2)}, u32[]{:S(2)}) collective-permute-start(bf16[24,4224]{1,0:T(8,128)(2,1)S(1)} %get-tuple-element.109), channel_id=1, source_target_pairs={{0,8},{1,9},{2,10},{3,11},{4,12},{5,13},{6,14},{7,15},{8,0},{9,1},... | collective-permute-start | bytes 608264 | tf_op jit(solution)/shard_map/ppermute | solution.py:178
  23.2 66.6 %collective-permute-done.1 = bf16[24,4224]{1,0:T(8,128)(2,1)S(1)} collective-permute-done((bf16[24,4224]{1,0:T(8,128)(2,1)S(1)}, bf16[24,4224]{1,0:T(8,128)(2,1)S(1)}, u32[]{:S(2)}, u32[]{:S(2)}) %collective-permute-start.1) | collective-permute-done | bytes 202784 | tf_op jit(solution)/shard_map/ppermute | solution.py:178
  89.8 34.8 %collective-permute-done.2 = bf16[24,4224]{1,0:T(8,128)(2,1)S(1)} collective-permute-done((bf16[24,4224]{1,0:T(8,128)(2,1)S(1)}, bf16[24,4224]{1,0:T(8,128)(2,1)S(1)}, u32[]{:S(2)}, u32[]{:S(2)}) %collective-permute-start.2) | collective-permute-done | bytes 202784 | tf_op jit(solution)/shard_map/ppermute | solution.py:178
  124.8 1.5 collective-permute-start.5
  126.6 7.0 %fusion.11 = f32[256,512]{1,0:T(8,128)S(1)} fusion(bf16[256,8192]{1,0:T(8,128)(2,1)} %tokens_ref.3, bf16[8192,512]{1,0:T(8,128)(2,1)} %param.9), kind=kOutput, calls=%fused_computation.60 | convolution fusion | flops 2147483648 | bytes 13107200 | tf_op jit(solution)/shard_map/dot_general | solution.py:194
  133.6 12.1 %collective-permute-done.5.refs_2_ = bf16[96,4224]{1,0:T(8,128)(2,1)S(1)} collective-permute-done((bf16[96,4224]{1,0:T(8,128)(2,1)S(1)}, bf16[96,4224]{1,0:T(8,128)(2,1)S(1)}, u32[]{:S(2)}, u32[]{:S(2)}) %collective-permute-start.5) | collective-permute-done | bytes 811040 | tf_op jit(solution)/shard_map/ppermute | solution.py:178
  145.7 16.5 %collective-permute-done.6.refs_3_ = bf16[96,4224]{1,0:T(8,128)(2,1)S(1)} collective-permute-done((bf16[96,4224]{1,0:T(8,128)(2,1)S(1)}, bf16[96,4224]{1,0:T(8,128)(2,1)S(1)}, u32[]{:S(2)}, u32[]{:S(2)}) %collective-permute-start.6) | collective-permute-done | bytes 811040 | tf_op jit(solution)/shard_map/ppermute | solution.py:178
  162.2 5.8 %shard_map.69 = (bf16[64,512]{1,0:T(8,128)(2,1)S(1)}, bf16[64,512]{1,0:T(8,128)(2,1)S(1)}, bf16[64,512]{1,0:T(8,128)(2,1)S(1)}, bf16[64,512]{1,0:T(8,128)(2,1)S(1)}) custom-call(s32[1]{0:T(128)} %bitcast.8.first_ref, bf16[256,8192]{1,0:T(8,128)(2,1)S(1)} %bitcast.38, bf16[256,512]{1,0:T(8,128)(2,1)S(1)} %bitcast.42, ...), custom_call_target="tpu_custom_call" | custom-call | flops 1610612736 | bytes 6291456 | tf_op jit(solution)/shard_map/pallas_call | solution.py:166
  167.9 1.4 collective-permute-start.9
  169.9 5.7 %shard_map.67 = (bf16[256,512]{1,0:T(8,128)(2,1)}, bf16[16,128]{1,0:T(8,128)(2,1)S(1)}) custom-call(s32[1]{0:T(128)} %bitcast.8.first_ref, bf16[256,8192]{1,0:T(8,128)(2,1)} %bitcast.37, bf16[256,512]{1,0:T(8,128)(2,1)S(1)} %bitcast.43, bf16[256,8320]{1,0:T(8,128)(2,1)} %bitcast.18.rows_ref), custom_call_target="tpu_custom_call" | custom-call | flops 1073741824 | bytes 8388608 | tf_op jit(solution)/shard_map/pallas_call | solution.py:166
  175.7 6.8 %all-to-all-start.4 = ((bf16[16,16,512]{2,1,0:T(8,128)(2,1)}), bf16[16,16,512]{2,1,0:T(8,128)(2,1)S(1)}, u32[]{:S(2)}, u32[]{:S(2)}) async-start(bf16[16,16,512]{2,1,0:T(8,128)(2,1)} %bitcast.21), calls=%async_computation.4 | async-start | bytes 524288 | tf_op jit(solution)/shard_map/all_to_all | solution.py:265
  182.5 2.0 %collective-permute-start.10 = (bf16[16,512]{1,0:T(8,128)(2,1)S(1)}, bf16[16,512]{1,0:T(8,128)(2,1)S(1)}, u32[]{:S(2)}, u32[]{:S(2)}) collective-permute-start(bf16[16,512]{1,0:T(8,128)(2,1)S(1)} %get-tuple-element.124), channel_id=1, source_target_pairs={{0,4},{1,5},{2,6},{3,7},{4,0},{5,1},{6,2},{7,3},{8,12},{9,13},{10,... | collective-permute-start | bytes 49160 | tf_op jit(solution)/shard_map/ppermute | solution.py:178
  184.5 2.4 %collective-permute-start.11 = (bf16[16,512]{1,0:T(8,128)(2,1)S(1)}, bf16[16,512]{1,0:T(8,128)(2,1)S(1)}, u32[]{:S(2)}, u32[]{:S(2)}) collective-permute-start(bf16[16,512]{1,0:T(8,128)(2,1)S(1)} %get-tuple-element.123), channel_id=1, source_target_pairs={{0,8},{1,9},{2,10},{3,11},{4,12},{5,13},{6,14},{7,15},{8,0},{9,1},... | collective-permute-start | bytes 49160 | tf_op jit(solution)/shard_map/ppermute | solution.py:178
  187.0 0.7 slice.15
  188.3 2.9 %collective-permute-start = (s32[]{:T(128)}, s32[]{:T(128)}, u32[]{:S(2)}, u32[]{:S(2)}) collective-permute-start(s32[]{:T(128)} %convert.1), channel_id=1, source_target_pairs={{0,16},{16,0},{1,17},{17,1},{2,18},{18,2},{3,19},{19,3},{4,20},{20... | collective-permute-start | bytes 20 | tf_op jit(solution)/shard_map/ppermute | solution.py:273
  191.2 0.7 collective-permute-done
  192.6 0.7 collective-permute-done.11
  193.7 0.7 copy-done.3
  (39 shorter events, 3.2 us)
Async XLA Ops:
  6.2 2.0 %copy-start = (bf16[256,8320]{1,0:T(8,128)(2,1)}, bf16[256,8320]{1,0:T(8,128)(2,1)S(1)}, u32[]{:S(2)}) copy-start(bf16[256,8320]{1,0:T(8,128)(2,1)S(1)} %shard_map.66) | copy-start | bytes 12779524
  8.2 161.7 %all-to-all-start.3 = ((bf16[16,16,8320]{2,1,0:T(8,128)(2,1)}), bf16[16,16,8320]{2,1,0:T(8,128)(2,1)}, u32[]{:S(2)}, u32[]{:S(2)}) async-start(bf16[16,16,8320]{2,1,0:T(8,128)(2,1)} %bitcast.35), calls=%async_computation.3 | async-start | bytes 8519680 | tf_op jit(solution)/shard_map/all_to_all | solution.py:230
  18.7 71.1 %collective-permute-start.1 = (bf16[24,4224]{1,0:T(8,128)(2,1)S(1)}, bf16[24,4224]{1,0:T(8,128)(2,1)S(1)}, u32[]{:S(2)}, u32[]{:S(2)}) collective-permute-start(bf16[24,4224]{1,0:T(8,128)(2,1)S(1)} %get-tuple-element.108), channel_id=1, source_target_pairs={{0,4},{1,5},{2,6},{3,7},{4,0},{5,1},{6,2},{7,3},{8,12},{9,13},{10,... | collective-permute-start | bytes 608264 | tf_op jit(solution)/shard_map/ppermute | solution.py:178
  20.6 104.0 %collective-permute-start.2 = (bf16[24,4224]{1,0:T(8,128)(2,1)S(1)}, bf16[24,4224]{1,0:T(8,128)(2,1)S(1)}, u32[]{:S(2)}, u32[]{:S(2)}) collective-permute-start(bf16[24,4224]{1,0:T(8,128)(2,1)S(1)} %get-tuple-element.109), channel_id=1, source_target_pairs={{0,8},{1,9},{2,10},{3,11},{4,12},{5,13},{6,14},{7,15},{8,0},{9,1},... | collective-permute-start | bytes 608264 | tf_op jit(solution)/shard_map/ppermute | solution.py:178
  23.0 101.6 %collective-permute-start.3 = (bf16[24,4224]{1,0:T(8,128)(2,1)S(1)}, bf16[24,4224]{1,0:T(8,128)(2,1)S(1)}, u32[]{:S(2)}, u32[]{:S(2)}) collective-permute-start(bf16[24,4224]{1,0:T(8,128)(2,1)S(1)} %get-tuple-element.110), channel_id=1, source_target_pairs={{0,12},{1,13},{2,14},{3,15},{4,8},{5,9},{6,10},{7,11},{8,4},{9,5},... | collective-permute-start | bytes 608264 | tf_op jit(solution)/shard_map/ppermute | solution.py:178
  124.6 37.5 %copy-start.1 = (bf16[16,8192,16]{1,2,0:T(8,128)(2,1)S(1)}, bf16[16,8192,16]{1,2,0:T(8,128)(2,1)}, u32[]{:S(2)}) copy-start(bf16[16,8192,16]{1,2,0:T(8,128)(2,1)} %param.10) | copy-start | bytes 12582916
  124.7 37.5 %copy-start.2 = (bf16[16,16,512]{2,1,0:T(8,128)(2,1)S(1)}, bf16[16,16,512]{2,1,0:T(8,128)(2,1)}, u32[]{:S(2)}) copy-start(bf16[16,16,512]{2,1,0:T(8,128)(2,1)} %param.11) | copy-start | bytes 786436
  124.7 8.9 %collective-permute-start.4 = (bf16[96,4224]{1,0:T(8,128)(2,1)S(1)}, bf16[96,4224]{1,0:T(8,128)(2,1)S(1)}, u32[]{:S(2)}, u32[]{:S(2)}) collective-permute-start(bf16[96,4224]{1,0:T(8,128)(2,1)S(1)} %constant_dynamic-update-slice_fusion.refs_0_), channel_id=1, source_target_pairs={{0,1},{1,0},{2,3},{3,2},{4,5},{5,4},{6,7},{7,6},{8,9},{9,8},{10,11... | collective-permute-start | bytes 2433032 | tf_op jit(solution)/shard_map/ppermute | solution.py:178
  124.8 20.9 %collective-permute-start.5 = (bf16[96,4224]{1,0:T(8,128)(2,1)S(1)}, bf16[96,4224]{1,0:T(8,128)(2,1)S(1)}, u32[]{:S(2)}, u32[]{:S(2)}) collective-permute-start(bf16[96,4224]{1,0:T(8,128)(2,1)S(1)} %constant_dynamic-update-slice_fusion.refs_0_), channel_id=1, source_target_pairs={{0,2},{1,3},{2,0},{3,1},{4,6},{5,7},{6,4},{7,5},{8,10},{9,11},{10,... | collective-permute-start | bytes 2433032 | tf_op jit(solution)/shard_map/ppermute | solution.py:178
  126.3 35.9 %collective-permute-start.6 = (bf16[96,4224]{1,0:T(8,128)(2,1)S(1)}, bf16[96,4224]{1,0:T(8,128)(2,1)S(1)}, u32[]{:S(2)}, u32[]{:S(2)}) collective-permute-start(bf16[96,4224]{1,0:T(8,128)(2,1)S(1)} %constant_dynamic-update-slice_fusion.refs_0_), channel_id=1, source_target_pairs={{0,3},{1,2},{2,1},{3,0},{4,7},{5,6},{6,5},{7,4},{8,11},{9,10},{10,... | collective-permute-start | bytes 2433032 | tf_op jit(solution)/shard_map/ppermute | solution.py:178
  167.9 14.5 %collective-permute-start.9 = (bf16[64,512]{1,0:T(8,128)(2,1)S(1)}, bf16[64,512]{1,0:T(8,128)(2,1)S(1)}, u32[]{:S(2)}, u32[]{:S(2)}) collective-permute-start(bf16[64,512]{1,0:T(8,128)(2,1)S(1)} %get-tuple-element.114), channel_id=1, source_target_pairs={{0,3},{1,2},{2,1},{3,0},{4,7},{5,6},{6,5},{7,4},{8,11},{9,10},{10,... | collective-permute-start | bytes 196616 | tf_op jit(solution)/shard_map/ppermute | solution.py:178
  169.3 13.1 %collective-permute-start.8 = (bf16[64,512]{1,0:T(8,128)(2,1)S(1)}, bf16[64,512]{1,0:T(8,128)(2,1)S(1)}, u32[]{:S(2)}, u32[]{:S(2)}) collective-permute-start(bf16[64,512]{1,0:T(8,128)(2,1)S(1)} %get-tuple-element.113), channel_id=1, source_target_pairs={{0,2},{1,3},{2,0},{3,1},{4,6},{5,7},{6,4},{7,5},{8,10},{9,11},{10,... | collective-permute-start | bytes 196616 | tf_op jit(solution)/shard_map/ppermute | solution.py:178
  169.9 12.6 %collective-permute-start.7 = (bf16[64,512]{1,0:T(8,128)(2,1)S(1)}, bf16[64,512]{1,0:T(8,128)(2,1)S(1)}, u32[]{:S(2)}, u32[]{:S(2)}) collective-permute-start(bf16[64,512]{1,0:T(8,128)(2,1)S(1)} %get-tuple-element.112), channel_id=1, source_target_pairs={{0,1},{1,0},{2,3},{3,2},{4,5},{5,4},{6,7},{7,6},{8,9},{9,8},{10,11... | collective-permute-start | bytes 196616 | tf_op jit(solution)/shard_map/ppermute | solution.py:178
  175.7 17.7 %all-to-all-start.4 = ((bf16[16,16,512]{2,1,0:T(8,128)(2,1)}), bf16[16,16,512]{2,1,0:T(8,128)(2,1)S(1)}, u32[]{:S(2)}, u32[]{:S(2)}) async-start(bf16[16,16,512]{2,1,0:T(8,128)(2,1)} %bitcast.21), calls=%async_computation.4 | async-start | bytes 524288 | tf_op jit(solution)/shard_map/all_to_all | solution.py:265
  182.5 10.1 %collective-permute-start.10 = (bf16[16,512]{1,0:T(8,128)(2,1)S(1)}, bf16[16,512]{1,0:T(8,128)(2,1)S(1)}, u32[]{:S(2)}, u32[]{:S(2)}) collective-permute-start(bf16[16,512]{1,0:T(8,128)(2,1)S(1)} %get-tuple-element.124), channel_id=1, source_target_pairs={{0,4},{1,5},{2,6},{3,7},{4,0},{5,1},{6,2},{7,3},{8,12},{9,13},{10,... | collective-permute-start | bytes 49160 | tf_op jit(solution)/shard_map/ppermute | solution.py:178
  184.5 8.8 %collective-permute-start.11 = (bf16[16,512]{1,0:T(8,128)(2,1)S(1)}, bf16[16,512]{1,0:T(8,128)(2,1)S(1)}, u32[]{:S(2)}, u32[]{:S(2)}) collective-permute-start(bf16[16,512]{1,0:T(8,128)(2,1)S(1)} %get-tuple-element.123), channel_id=1, source_target_pairs={{0,8},{1,9},{2,10},{3,11},{4,12},{5,13},{6,14},{7,15},{8,0},{9,1},... | collective-permute-start | bytes 49160 | tf_op jit(solution)/shard_map/ppermute | solution.py:178
  186.9 6.5 %collective-permute-start.12 = (bf16[16,512]{1,0:T(8,128)(2,1)S(1)}, bf16[16,512]{1,0:T(8,128)(2,1)S(1)}, u32[]{:S(2)}, u32[]{:S(2)}) collective-permute-start(bf16[16,512]{1,0:T(8,128)(2,1)S(1)} %get-tuple-element.122), channel_id=1, source_target_pairs={{0,12},{1,13},{2,14},{3,15},{4,8},{5,9},{6,10},{7,11},{8,4},{9,5},... | collective-permute-start | bytes 49160 | tf_op jit(solution)/shard_map/ppermute | solution.py:178
  188.3 3.6 %collective-permute-start = (s32[]{:T(128)}, s32[]{:T(128)}, u32[]{:S(2)}, u32[]{:S(2)}) collective-permute-start(s32[]{:T(128)} %convert.1), channel_id=1, source_target_pairs={{0,16},{16,0},{1,17},{17,1},{2,18},{18,2},{3,19},{19,3},{4,20},{20... | collective-permute-start | bytes 20 | tf_op jit(solution)/shard_map/ppermute | solution.py:273
  193.7 0.7 copy-start.3

commit v3 on v2

--- a/solution.py
+++ b/solution.py
@@ -13,6 +13,7 @@
 SPARE = 12
 NOTE = 128
 STEP = 1024
+WIDE = 1664
 VMEM = pl.BlockSpec(memory_space=pltpu.VMEM)
 SMEM = pl.BlockSpec(memory_space=pltpu.SMEM)
 
@@ -78,20 +79,47 @@
     )
 
 
-def pack_body(flag_ref, at_ref, info_ref, tokens_ref, out):
-    depth = tokens_ref.shape[1]
+def pack_body(last, flag_ref, at_ref, info_ref, tokens_ref, out):
     shape = (out.shape[0], at_ref.shape[1])
     pick = lax.broadcasted_iota(jnp.int32, shape, 0) == at_ref[...]
     pick = pick.astype(jnp.float32).astype(jnp.bfloat16)
-    for c in range(0, depth, STEP):
-        out[:, c : c + STEP] = jnp.dot(
-            pick, tokens_ref[:, c : c + STEP], preferred_element_type=jnp.float32
+
+    @pl.when(pl.program_id(0) < pl.num_programs(0) - 1)
+    def _():
+        out[...] = jnp.dot(
+            pick, tokens_ref[...], preferred_element_type=jnp.float32
         ).astype(jnp.bfloat16)
-    note = jnp.dot(pick, info_ref[...], preferred_element_type=jnp.float32)
-    flag = jnp.where(
-        lax.broadcasted_iota(jnp.int32, note.shape, 1) == 1, flag_ref[0].astype(jnp.float32), 0.0
-    )
-    out[:, depth : depth + NOTE] = (note + flag).astype(jnp.bfloat16)
+
+    @pl.when(pl.program_id(0) == pl.num_programs(0) - 1)
+    def _():
+        out[:, :last] = jnp.dot(
+            pick, tokens_ref[:, :last], preferred_element_type=jnp.float32
+        ).astype(jnp.bfloat16)
+        note = jnp.dot(pick, info_ref[...], preferred_element_type=jnp.float32)
+        column = lax.broadcasted_iota(jnp.int32, note.shape, 1)
+        flag = jnp.where(column == 1, flag_ref[0].astype(jnp.float32), 0.0)
+        out[:, last:] = (note + flag).astype(jnp.bfloat16)
+
+
+def pack(main_rows, some_left, at, info, tokens):
+    rows, depth = tokens.shape
+    steps = (depth + NOTE) // WIDE
+    return pl.pallas_call(
+        functools.partial(pack_body, WIDE - NOTE),
+        grid=(steps,),
+        in_specs=[
+            SMEM,
+            pl.BlockSpec(at.shape, lambda i: (0, 0)),
+            pl.BlockSpec(info.shape, lambda i: (0, 0)),
+            pl.BlockSpec((rows, WIDE), lambda i: (0, i)),
+        ],
+        out_specs=pl.BlockSpec((main_rows, WIDE), lambda i: (0, i)),
+        out_shape=jax.ShapeDtypeStruct((main_rows, depth + NOTE), jnp.bfloat16),
+        compiler_params=pltpu.CompilerParams(vmem_limit_bytes=56 * 2**20),
+        cost_estimate=pl.CostEstimate(
+            flops=2 * main_rows * rows * depth, bytes_accessed=8 * 2**20, transcendentals=0
+        ),
+    )(some_left, at, info, tokens)
 
 
 def low_delta(low, note, first, rank, up):
@@ -100,51 +128,92 @@
     return jnp.dot(low.astype(jnp.bfloat16), up, preferred_element_type=jnp.float32)
 
 
-def adapt_body(rank, first_ref, down_ref, up_ref, rows_ref, out, flag_out):
-    depth = down_ref.shape[1]
-    low = jnp.zeros((rows_ref.shape[0], down_ref.shape[0]), jnp.float32)
-    for c in range(0, depth, STEP):
-        low += lax.dot_general(
-            rows_ref[:, c : c + STEP],
-            down_ref[:, c : c + STEP],
+def adapt_body(rank, last, first_ref, down_ref, up_ref, rows_ref, out, flag_out, low_ref):
+    step = pl.program_id(0)
+
+    def product(columns):
+        return lax.dot_general(
+            rows_ref[:, columns],
+            down_ref[:, columns],
             (((1,), (1,)), ((), ())),
             preferred_element_type=jnp.float32,
         )
-    note = rows_ref[:, depth : depth + NOTE].astype(jnp.float32)
-    out[...] = low_delta(low, note[:, :1], first_ref[0], rank, up_ref[...]).astype(jnp.bfloat16)
-    most = jnp.max(note, axis=0, keepdims=True)
-    flag_out[...] = jnp.broadcast_to(most, flag_out.shape).astype(jnp.bfloat16)
+
+    @pl.when(step == 0)
+    def _():
+        low_ref[...] = product(slice(None))
+
+    @pl.when((step > 0) & (step < pl.num_programs(0) - 1))
+    def _():
+        low_ref[...] += product(slice(None))
+
+    @pl.when(step == pl.num_programs(0) - 1)
+    def _():
+        low = low_ref[...] + product(slice(0, last))
+        note = rows_ref[:, last:].astype(jnp.float32)
+        delta = low_delta(low, note[:, :1], first_ref[0], rank, up_ref[...])
+        out[...] = delta.astype(jnp.bfloat16)
+        most = jnp.max(note, axis=0, keepdims=True)
+        flag_out[...] = jnp.broadcast_to(most, flag_out.shape).astype(jnp.bfloat16)
+
+
+def adapt(rank, first, down, up, got):
+    rows, width = got.shape[0], up.shape[1]
+    return pl.pallas_call(
+        functools.partial(adapt_body, rank, WIDE - NOTE),
+        grid=(got.shape[1] // WIDE,),
+        in_specs=[
+            SMEM,
+            pl.BlockSpec((down.shape[0], WIDE), lambda i: (0, i)),
+            pl.BlockSpec(up.shape, lambda i: (0, 0)),
+            pl.BlockSpec((rows, WIDE), lambda i: (0, i)),
+        ],
+        out_specs=[
+            pl.BlockSpec((rows, width), lambda i: (0, 0)),
+            pl.BlockSpec((16, NOTE), lambda i: (0, 0)),
+        ],
+        out_shape=[
+            jax.ShapeDtypeStruct((rows, width), jnp.bfloat16),
+            jax.ShapeDtypeStruct((16, NOTE), jnp.bfloat16),
+        ],
+        scratch_shapes=[pltpu.VMEM((rows, down.shape[0]), jnp.float32)],
+        compiler_params=pltpu.CompilerParams(vmem_limit_bytes=24 * 2**20),
+        cost_estimate=pl.CostEstimate(
+            flops=2 * rows * down.size, bytes_accessed=8 * 2**20, transcendentals=0
+        ),
+    )(first, down, up, got)
 
 
 def adapt_over_body(planes, rank, first_ref, down_ref, up_ref, *refs):
     rows_refs, outs = refs[:PLANE], refs[PLANE:]
     half = down_ref.shape[1] // 2
-    for rows_ref, out in zip(rows_refs, outs, strict=True):
-        shape = (rows_ref.shape[0], down_ref.shape[0])
-        low0, low1 = jnp.zeros(shape, jnp.float32), jnp.zeros(shape, jnp.float32)
-        for c in range(0, half, STEP):
-            rows = rows_ref[:, c : c + STEP]
-            dims = (((1,), (1,)), ((), ()))
-            low0 += lax.dot_general(
-                rows, down_ref[:, c : c + STEP], dims, preferred_element_type=jnp.float32
-            )
-            low1 += lax.dot_general(
-                rows,
-                down_ref[:, half + c : half + c + STEP],
-                dims,
-                preferred_element_type=jnp.float32,
-            )
-        note = rows_ref[:, half : half + NOTE].astype(jnp.float32)
-        zeros = jnp.zeros((16 - SPARE, shape[1]), jnp.float32)
-        no_note = jnp.zeros((16 - SPARE, NOTE), jnp.float32)
-        lows, notes = [], []
+    each = rows_refs[0].shape[0]
+    shape = (PLANE * each, down_ref.shape[0])
+    dims = (((1,), (1,)), ((), ()))
+    low0, low1 = jnp.zeros(shape, jnp.float32), jnp.zeros(shape, jnp.float32)
+    for c in range(0, half, STEP):
+        rows = jnp.concatenate([r[:, c : c + STEP] for r in rows_refs], axis=0)
+        low0 += lax.dot_general(
+            rows, down_ref[:, c : c + STEP], dims, preferred_element_type=jnp.float32
+        )
+        low1 += lax.dot_general(
+            rows, down_ref[:, half + c : half + c + STEP], dims, preferred_element_type=jnp.float32
+        )
+    zeros = jnp.zeros((16 - SPARE, shape[1]), jnp.float32)
+    no_note = jnp.zeros((16 - SPARE, NOTE), jnp.float32)
+    lows, notes = [], []
+    for a in range(PLANE):
+        note = rows_refs[a][:, half : half + NOTE].astype(jnp.float32)
         for b in range(planes):
             s = 2 * SPARE * b
-            lows += [low0[s : s + SPARE] + low1[s + SPARE : s + 2 * SPARE], zeros]
+            m = a * each + s
+            lows += [low0[m : m + SPARE] + low1[m + SPARE : m + 2 * SPARE], zeros]
             notes += [note[s : s + SPARE], no_note]
-        low = jnp.concatenate(lows, axis=0)
-        note = jnp.concatenate(notes, axis=0)[:, :1]
-        out[...] = low_delta(low, note, first_ref[0], rank, up_ref[...]).astype(jnp.bfloat16)
+    low = jnp.concatenate(lows, axis=0)
+    note = jnp.concatenate(notes, axis=0)[:, :1]
+    delta = low_delta(low, note, first_ref[0], rank, up_ref[...]).astype(jnp.bfloat16)
+    for a, out in enumerate(outs):
+        out[...] = delta[16 * planes * a : 16 * planes * (a + 1)]
 
 
 def final_body(at_ref, base_ref, back_ref, *refs):
@@ -194,7 +263,7 @@
     base_value = jnp.dot(tokens, value_weight, preferred_element_type=jnp.float32)
     room = row_count // count
     planes = count // PLANE
-    if count != 16 or room != 16:
+    if count != 16 or room != 16 or (depth + NOTE) % WIDE:
         delta = exchange(tokens, slot, owner, place, CAP * local, adapt_down, adapt_up)
         return (base_value + delta).astype(jnp.bfloat16)
 
@@ -218,27 +287,21 @@
         2 * 96 * row_count * depth,
         6 * 2**20,
     )
-    blocks = call(
-        pack_body,
-        [(main_rows, depth + NOTE)],
-        (some_left, at, info, tokens),
-        [SMEM] + [VMEM] * 3,
-        2 * main_rows * row_count * depth,
-        8 * 2**20,
-    )[0]
-
+    blocks = pack(main_rows, some_left, at, info, tokens)
+
+    first = (me * local).reshape(1)
+    down = adapt_down.transpose(0, 2, 1).reshape(local * rank, depth)
+    up = adapt_up.reshape(local * rank, width)
+
+    along = jnp.concatenate(
+        [spare[0]] + [swap(spare[b], b * PLANE) for b in range(1, planes)], axis=0
+    )
+    shared = [along] + [swap(along, a) for a in range(1, PLANE)]
+    blocks, shared[1] = lax.optimization_barrier((blocks, shared[1]))
     got = lax.all_to_all(
         blocks.reshape(count, room, depth + NOTE), "ad", split_axis=0, concat_axis=0, tiled=True
     ).reshape(main_rows, depth + NOTE)
 
-    first = (me * local).reshape(1)
-    down = adapt_down.transpose(0, 2, 1).reshape(local * rank, depth)
-    up = adapt_up.reshape(local * rank, width)
-
-    along = jnp.concatenate(
-        [spare[0]] + [swap(spare[b], b * PLANE) for b in range(1, planes)], axis=0
-    )
-    shared = [along] + [swap(along, a) for a in range(1, PLANE)]
     over_delta = call(
         functools.partial(adapt_over_body, planes, rank),
         [(16 * planes, width)] * PLANE,
@@ -254,14 +317,7 @@
     for b in range(1, planes):
         over_back.append(swap(over_sum[16 * b : 16 * (b + 1)], b * PLANE))
 
-    delta, flags = call(
-        functools.partial(adapt_body, rank),
-        [(main_rows, width), (16, NOTE)],
-        (first, down, up, got),
-        [SMEM] + [VMEM] * 3,
-        2 * main_rows * depth * local * rank,
-        8 * 2**20,
-    )
+    delta, flags = adapt(rank, first, down, up, got)
     back = lax.all_to_all(
         delta.reshape(count, room, width), "ad", split_axis=0, concat_axis=0, tiled=True
     ).reshape(main_rows, width)

time: 195 us -> 158 us (0.81)
  waiting for transfers between devices: 131 us -> 90.4 us
  starting transfers between devices: 29.9 us -> 35.9 us
  local copies, waits for them, and re-layouts: 3.48 us -> 1.46 us
    ppermute x12, waiting for transfers between devices: 131 us -> 89.7 us  [swap(): return lax.ppermute(x, 'ad', [(s, s ^ k) for s in range(count)])]
    pallas_call x0 -> x2, Pallas kernels: none -> 14.1 us  [the longest x1 7.5 us: pack(): pl.pallas_call(functools.partial(pack_body, WIDE - NOTE), grid=(steps,),...]
    pallas_call x5 -> x3, Pallas kernels: 19 us -> 5.3 us  [call(): pl.pallas_call(body, in_specs=specs, out_specs=[VMEM] * len(outs), out_sh...]
    all_to_all x1, starting transfers between devices: 6.79 us -> 12 us  [on_device(): lax.all_to_all(delta.reshape(count, room, width), 'ad', split_axis=0, con...]
    unnamed x11, local copies, waits for them, and re-layouts: 2.79 us -> 0.77 us
  transfers between devices with their start and end apart: 15 -> 15, of which waited for: 6 -> 6; matrix products, arithmetic and copies ran while one was open for 4% -> 5% of each run, Pallas kernels for 7% -> 10%
where the time goes in v3:
time: 158 us
  waiting for transfers between devices  90.4 us (57%)
  starting transfers between devices  35.9 us (23%)
  Pallas kernels  19.4 us (12%)
  matrix products  6.97 us (4%)
  other arithmetic  2.12 us (1%)
  between operations  1.59 us (1%)
    ppermute x12, waiting for transfers between devices, swap(): return lax.ppermute(x, 'ad', [(s, s ^ k) for s in range(count)])  89.7 us
    ppermute x12, starting transfers between devices, swap(): return lax.ppermute(x, 'ad', [(s, s ^ k) for s in range(count)])  14.1 us
    all_to_all x1, starting transfers between devices, on_device(): lax.all_to_all(delta.reshape(count, room, width), 'ad', split_axis=0, con...  12 us
    pallas_call x1, Pallas kernels, pack(): pl.pallas_call(functools.partial(pack_body, WIDE - NOTE), grid=(steps,),...  7.5 us
    dot_general x1, matrix products, on_device(): jnp.dot(tokens, value_weight, preferred_element_type=jnp.float32)  6.97 us
    all_to_all x1, starting transfers between devices, on_device(): lax.all_to_all(blocks.reshape(count, room, depth + NOTE), 'ad', split_axi...  6.94 us
    pallas_call x1, Pallas kernels, adapt(): pl.pallas_call(functools.partial(adapt_body, rank, WIDE - NOTE), grid=(go...  6.57 us
    pallas_call x3, Pallas kernels, call(): pl.pallas_call(body, in_specs=specs, out_specs=[VMEM] * len(outs), out_sh...  5.3 us
  transfers between devices with their start and end apart: 15, of which 6 were waited for; matrix products, arithmetic and copies ran while one was open for 5% of the time, Pallas kernels for 10%

profile of v3, /device:TPU:0, one launch (start us, length us, event | category | flops | bytes accessed | tf_op | source)
XLA Modules:
  0.0 157.9 jit_solution(7223839349306079280)
XLA Ops:
  0.0 0.9 select_reduce_fusion.1
  1.4 3.0 %shard_map.67 = (bf16[24,4224]{1,0:T(8,128)(2,1)S(1)}, bf16[24,4224]{1,0:T(8,128)(2,1)S(1)}, bf16[24,4224]{1,0:T(8,128)(2,1)S(1)}, bf16[24,4224]{1,0:T(8,128)(2,1)S(1)}) custom-call(s32[1,256]{1,0:T(1,128)S(1)} %and_select_fusion.4.at_ref, bf16[256,128]{1,0:T(8,128)(2,1)S(1)} %select_convert_fusion.2.info_ref, bf16[256,8192]{1,0:T(8,128)(2,1)} %tokens_ref.3), custom_call_target="tpu_custom_call" | custom-call | flops 402653184 | bytes 6291456 | tf_op jit(solution)/shard_map/pallas_call | solution.py:235
  4.5 3.1 %collective-permute-start = (bf16[24,4224]{1,0:T(8,128)(2,1)S(1)}, bf16[24,4224]{1,0:T(8,128)(2,1)S(1)}, u32[]{:S(2)}, u32[]{:S(2)}) collective-permute-start(bf16[24,4224]{1,0:T(8,128)(2,1)S(1)} %get-tuple-element.108), channel_id=1, source_target_pairs={{0,4},{1,5},{2,6},{3,7},{4,0},{5,1},{6,2},{7,3},{8,12},{9,13},{10,... | collective-permute-start | bytes 608264 | tf_op jit(solution)/shard_map/ppermute | solution.py:247
  7.5 2.6 %collective-permute-start.1 = (bf16[24,4224]{1,0:T(8,128)(2,1)S(1)}, bf16[24,4224]{1,0:T(8,128)(2,1)S(1)}, u32[]{:S(2)}, u32[]{:S(2)}) collective-permute-start(bf16[24,4224]{1,0:T(8,128)(2,1)S(1)} %get-tuple-element.109), channel_id=1, source_target_pairs={{0,8},{1,9},{2,10},{3,11},{4,12},{5,13},{6,14},{7,15},{8,0},{9,1},... | collective-permute-start | bytes 608264 | tf_op jit(solution)/shard_map/ppermute | solution.py:247
  10.2 6.0 %collective-permute-done = bf16[24,4224]{1,0:T(8,128)(2,1)S(1)} collective-permute-done((bf16[24,4224]{1,0:T(8,128)(2,1)S(1)}, bf16[24,4224]{1,0:T(8,128)(2,1)S(1)}, u32[]{:S(2)}, u32[]{:S(2)}) %collective-permute-start) | collective-permute-done | bytes 202784 | tf_op jit(solution)/shard_map/ppermute | solution.py:247
  16.2 8.9 %collective-permute-done.1 = bf16[24,4224]{1,0:T(8,128)(2,1)S(1)} collective-permute-done((bf16[24,4224]{1,0:T(8,128)(2,1)S(1)}, bf16[24,4224]{1,0:T(8,128)(2,1)S(1)}, u32[]{:S(2)}, u32[]{:S(2)}) %collective-permute-start.1) | collective-permute-done | bytes 202784 | tf_op jit(solution)/shard_map/ppermute | solution.py:247
  25.2 0.7 convert_reduce_fusion.2
  25.9 7.5 %shard_map.66 = bf16[256,8320]{1,0:T(8,128)(2,1)} custom-call(s32[1]{0:T(128)} %bitcast.13.flag_ref, s32[1,256]{1,0:T(1,128)S(1)} %and_select_fusion.4.at_ref, bf16[256,128]{1,0:T(8,128)(2,1)} %copy-done, bf16[256,8192]{1,0:T(8,128)(2,1)} %tokens_ref.3), custom_call_target="tpu_custom_call" | custom-call | flops 1073741824 | bytes 8388608 | tf_op jit(solution)/shard_map/pallas_call | solution.py:107
  33.4 6.9 %all-to-all-start.3 = ((bf16[16,16,8320]{2,1,0:T(8,128)(2,1)}), bf16[16,16,8320]{2,1,0:T(8,128)(2,1)}, u32[]{:S(2)}, u32[]{:S(2)}) async-start(bf16[16,16,8320]{2,1,0:T(8,128)(2,1)} %bitcast.35), calls=%async_computation.3 | async-start | bytes 8519680 | tf_op jit(solution)/shard_map/all_to_all | solution.py:301
  40.4 1.9 %collective-permute-start.5 = (bf16[96,4224]{1,0:T(8,128)(2,1)S(1)}, bf16[96,4224]{1,0:T(8,128)(2,1)S(1)}, u32[]{:S(2)}, u32[]{:S(2)}) collective-permute-start(bf16[96,4224]{1,0:T(8,128)(2,1)S(1)} %constant_dynamic-update-slice_fusion.refs_0_), channel_id=1, source_target_pairs={{0,2},{1,3},{2,0},{3,1},{4,6},{5,7},{6,4},{7,5},{8,10},{9,11},{10,... | collective-permute-start | bytes 2433032 | tf_op jit(solution)/shard_map/ppermute | solution.py:247
  42.4 7.0 %fusion.11 = f32[256,512]{1,0:T(8,128)S(1)} fusion(bf16[256,8192]{1,0:T(8,128)(2,1)} %tokens_ref.3, bf16[8192,512]{1,0:T(8,128)(2,1)} %param.9), kind=kOutput, calls=%fused_computation.60 | convolution fusion | flops 2147483648 | bytes 13107200 | tf_op jit(solution)/shard_map/dot_general | solution.py:263
  49.3 46.2 %collective-permute-done.5.refs_2_ = bf16[96,4224]{1,0:T(8,128)(2,1)S(1)} collective-permute-done((bf16[96,4224]{1,0:T(8,128)(2,1)S(1)}, bf16[96,4224]{1,0:T(8,128)(2,1)S(1)}, u32[]{:S(2)}, u32[]{:S(2)}) %collective-permute-start.5) | collective-permute-done | bytes 811040 | tf_op jit(solution)/shard_map/ppermute | solution.py:247
  95.6 27.8 %collective-permute-done.6.refs_3_ = bf16[96,4224]{1,0:T(8,128)(2,1)S(1)} collective-permute-done((bf16[96,4224]{1,0:T(8,128)(2,1)S(1)}, bf16[96,4224]{1,0:T(8,128)(2,1)S(1)}, u32[]{:S(2)}, u32[]{:S(2)}) %collective-permute-start.6) | collective-permute-done | bytes 811040 | tf_op jit(solution)/shard_map/ppermute | solution.py:247
  123.4 2.0 %shard_map.69 = (bf16[64,512]{1,0:T(8,128)(2,1)S(1)}, bf16[64,512]{1,0:T(8,128)(2,1)S(1)}, bf16[64,512]{1,0:T(8,128)(2,1)S(1)}, bf16[64,512]{1,0:T(8,128)(2,1)S(1)}) custom-call(s32[1]{0:T(128)} %bitcast.8.first_ref, bf16[256,8192]{1,0:T(8,128)(2,1)S(1)} %bitcast.38, bf16[256,512]{1,0:T(8,128)(2,1)S(1)} %bitcast.42, ...), custom_call_target="tpu_custom_call" | custom-call | flops 1610612736 | bytes 6291456 | tf_op jit(solution)/shard_map/pallas_call | solution.py:235
  125.7 1.6 collective-permute-start.9
  127.3 6.6 %shard_map.68 = (bf16[256,512]{1,0:T(8,128)(2,1)}, bf16[16,128]{1,0:T(8,128)(2,1)S(1)}) custom-call(s32[1]{0:T(128)} %bitcast.8.first_ref, bf16[256,8192]{1,0:T(8,128)(2,1)} %bitcast.37, bf16[256,512]{1,0:T(8,128)(2,1)S(1)} %bitcast.43, bf16[256,8320]{1,0:T(8,128)(2,1)} %bitcast.18.rows_ref), custom_call_target="tpu_custom_call" | custom-call | flops 1073741824 | bytes 8388608 | tf_op jit(solution)/shard_map/pallas_call | solution.py:162
  133.9 12.0 %all-to-all-start.4 = ((bf16[16,16,512]{2,1,0:T(8,128)(2,1)}), bf16[16,16,512]{2,1,0:T(8,128)(2,1)S(1)}, u32[]{:S(2)}, u32[]{:S(2)}) async-start(bf16[16,16,512]{2,1,0:T(8,128)(2,1)} %bitcast.21), calls=%async_computation.4 | async-start | bytes 524288 | tf_op jit(solution)/shard_map/all_to_all | solution.py:321
  146.0 2.0 %collective-permute-start.10 = (bf16[16,512]{1,0:T(8,128)(2,1)S(1)}, bf16[16,512]{1,0:T(8,128)(2,1)S(1)}, u32[]{:S(2)}, u32[]{:S(2)}) collective-permute-start(bf16[16,512]{1,0:T(8,128)(2,1)S(1)} %get-tuple-element.128), channel_id=1, source_target_pairs={{0,4},{1,5},{2,6},{3,7},{4,0},{5,1},{6,2},{7,3},{8,12},{9,13},{10,... | collective-permute-start | bytes 49160 | tf_op jit(solution)/shard_map/ppermute | solution.py:247
  148.0 2.4 %collective-permute-start.11 = (bf16[16,512]{1,0:T(8,128)(2,1)S(1)}, bf16[16,512]{1,0:T(8,128)(2,1)S(1)}, u32[]{:S(2)}, u32[]{:S(2)}) collective-permute-start(bf16[16,512]{1,0:T(8,128)(2,1)S(1)} %get-tuple-element.127), channel_id=1, source_target_pairs={{0,8},{1,9},{2,10},{3,11},{4,12},{5,13},{6,14},{7,15},{8,0},{9,1},... | collective-permute-start | bytes 49160 | tf_op jit(solution)/shard_map/ppermute | solution.py:247
  150.5 0.7 slice.15
  151.8 2.9 %collective-permute-start.4 = (s32[]{:T(128)}, s32[]{:T(128)}, u32[]{:S(2)}, u32[]{:S(2)}) collective-permute-start(s32[]{:T(128)} %convert.1), channel_id=1, source_target_pairs={{0,16},{16,0},{1,17},{17,1},{2,18},{18,2},{3,19},{19,3},{4,20},{20... | collective-permute-start | bytes 20 | tf_op jit(solution)/shard_map/ppermute | solution.py:329
  154.7 0.7 collective-permute-done.4
  156.1 0.7 collective-permute-done.11
  157.2 0.7 copy-done.3
  (39 shorter events, 1.9 us)
Async XLA Ops:
  1.4 24.5 %copy-start = (bf16[256,128]{1,0:T(8,128)(2,1)}, bf16[256,128]{1,0:T(8,128)(2,1)S(1)}, u32[]{:S(2)}) copy-start(bf16[256,128]{1,0:T(8,128)(2,1)S(1)} %select_convert_fusion.2.info_ref) | copy-start | bytes 196612
  4.5 11.7 %collective-permute-start = (bf16[24,4224]{1,0:T(8,128)(2,1)S(1)}, bf16[24,4224]{1,0:T(8,128)(2,1)S(1)}, u32[]{:S(2)}, u32[]{:S(2)}) collective-permute-start(bf16[24,4224]{1,0:T(8,128)(2,1)S(1)} %get-tuple-element.108), channel_id=1, source_target_pairs={{0,4},{1,5},{2,6},{3,7},{4,0},{5,1},{6,2},{7,3},{8,12},{9,13},{10,... | collective-permute-start | bytes 608264 | tf_op jit(solution)/shard_map/ppermute | solution.py:247
  7.5 17.5 %collective-permute-start.1 = (bf16[24,4224]{1,0:T(8,128)(2,1)S(1)}, bf16[24,4224]{1,0:T(8,128)(2,1)S(1)}, u32[]{:S(2)}, u32[]{:S(2)}) collective-permute-start(bf16[24,4224]{1,0:T(8,128)(2,1)S(1)} %get-tuple-element.109), channel_id=1, source_target_pairs={{0,8},{1,9},{2,10},{3,11},{4,12},{5,13},{6,14},{7,15},{8,0},{9,1},... | collective-permute-start | bytes 608264 | tf_op jit(solution)/shard_map/ppermute | solution.py:247
  10.1 15.0 %collective-permute-start.2 = (bf16[24,4224]{1,0:T(8,128)(2,1)S(1)}, bf16[24,4224]{1,0:T(8,128)(2,1)S(1)}, u32[]{:S(2)}, u32[]{:S(2)}) collective-permute-start(bf16[24,4224]{1,0:T(8,128)(2,1)S(1)} %get-tuple-element.110), channel_id=1, source_target_pairs={{0,12},{1,13},{2,14},{3,15},{4,8},{5,9},{6,10},{7,11},{8,4},{9,5},... | collective-permute-start | bytes 608264 | tf_op jit(solution)/shard_map/ppermute | solution.py:247
  25.1 8.3 %collective-permute-start.3 = (bf16[96,4224]{1,0:T(8,128)(2,1)S(1)}, bf16[96,4224]{1,0:T(8,128)(2,1)S(1)}, u32[]{:S(2)}, u32[]{:S(2)}) collective-permute-start(bf16[96,4224]{1,0:T(8,128)(2,1)S(1)} %constant_dynamic-update-slice_fusion.refs_0_), channel_id=1, source_target_pairs={{0,1},{1,0},{2,3},{3,2},{4,5},{5,4},{6,7},{7,6},{8,9},{9,8},{10,11... | collective-permute-start | bytes 2433032 | tf_op jit(solution)/shard_map/ppermute | solution.py:247
  33.4 93.9 %all-to-all-start.3 = ((bf16[16,16,8320]{2,1,0:T(8,128)(2,1)}), bf16[16,16,8320]{2,1,0:T(8,128)(2,1)}, u32[]{:S(2)}, u32[]{:S(2)}) async-start(bf16[16,16,8320]{2,1,0:T(8,128)(2,1)} %bitcast.35), calls=%async_computation.3 | async-start | bytes 8519680 | tf_op jit(solution)/shard_map/all_to_all | solution.py:301
  40.4 83.0 %copy-start.1 = (bf16[16,8192,16]{1,2,0:T(8,128)(2,1)S(1)}, bf16[16,8192,16]{1,2,0:T(8,128)(2,1)}, u32[]{:S(2)}) copy-start(bf16[16,8192,16]{1,2,0:T(8,128)(2,1)} %param.10) | copy-start | bytes 12582916
  40.4 83.0 %copy-start.2 = (bf16[16,16,512]{2,1,0:T(8,128)(2,1)S(1)}, bf16[16,16,512]{2,1,0:T(8,128)(2,1)}, u32[]{:S(2)}) copy-start(bf16[16,16,512]{2,1,0:T(8,128)(2,1)} %param.11) | copy-start | bytes 786436
  40.4 55.1 %collective-permute-start.5 = (bf16[96,4224]{1,0:T(8,128)(2,1)S(1)}, bf16[96,4224]{1,0:T(8,128)(2,1)S(1)}, u32[]{:S(2)}, u32[]{:S(2)}) collective-permute-start(bf16[96,4224]{1,0:T(8,128)(2,1)S(1)} %constant_dynamic-update-slice_fusion.refs_0_), channel_id=1, source_target_pairs={{0,2},{1,3},{2,0},{3,1},{4,6},{5,7},{6,4},{7,5},{8,10},{9,11},{10,... | collective-permute-start | bytes 2433032 | tf_op jit(solution)/shard_map/ppermute | solution.py:247
  42.4 81.0 %collective-permute-start.6 = (bf16[96,4224]{1,0:T(8,128)(2,1)S(1)}, bf16[96,4224]{1,0:T(8,128)(2,1)S(1)}, u32[]{:S(2)}, u32[]{:S(2)}) collective-permute-start(bf16[96,4224]{1,0:T(8,128)(2,1)S(1)} %constant_dynamic-update-slice_fusion.refs_0_), channel_id=1, source_target_pairs={{0,3},{1,2},{2,1},{3,0},{4,7},{5,6},{6,5},{7,4},{8,11},{9,10},{10,... | collective-permute-start | bytes 2433032 | tf_op jit(solution)/shard_map/ppermute | solution.py:247
  125.4 20.5 %collective-permute-start.7 = (bf16[64,512]{1,0:T(8,128)(2,1)S(1)}, bf16[64,512]{1,0:T(8,128)(2,1)S(1)}, u32[]{:S(2)}, u32[]{:S(2)}) collective-permute-start(bf16[64,512]{1,0:T(8,128)(2,1)S(1)} %get-tuple-element.116), channel_id=1, source_target_pairs={{0,1},{1,0},{2,3},{3,2},{4,5},{5,4},{6,7},{7,6},{8,9},{9,8},{10,11... | collective-permute-start | bytes 196616 | tf_op jit(solution)/shard_map/ppermute | solution.py:247
  125.7 20.2 %collective-permute-start.8 = (bf16[64,512]{1,0:T(8,128)(2,1)S(1)}, bf16[64,512]{1,0:T(8,128)(2,1)S(1)}, u32[]{:S(2)}, u32[]{:S(2)}) collective-permute-start(bf16[64,512]{1,0:T(8,128)(2,1)S(1)} %get-tuple-element.117), channel_id=1, source_target_pairs={{0,2},{1,3},{2,0},{3,1},{4,6},{5,7},{6,4},{7,5},{8,10},{9,11},{10,... | collective-permute-start | bytes 196616 | tf_op jit(solution)/shard_map/ppermute | solution.py:247
  125.7 20.2 %collective-permute-start.9 = (bf16[64,512]{1,0:T(8,128)(2,1)S(1)}, bf16[64,512]{1,0:T(8,128)(2,1)S(1)}, u32[]{:S(2)}, u32[]{:S(2)}) collective-permute-start(bf16[64,512]{1,0:T(8,128)(2,1)S(1)} %get-tuple-element.118), channel_id=1, source_target_pairs={{0,3},{1,2},{2,1},{3,0},{4,7},{5,6},{6,5},{7,4},{8,11},{9,10},{10,... | collective-permute-start | bytes 196616 | tf_op jit(solution)/shard_map/ppermute | solution.py:247
  133.9 22.9 %all-to-all-start.4 = ((bf16[16,16,512]{2,1,0:T(8,128)(2,1)}), bf16[16,16,512]{2,1,0:T(8,128)(2,1)S(1)}, u32[]{:S(2)}, u32[]{:S(2)}) async-start(bf16[16,16,512]{2,1,0:T(8,128)(2,1)} %bitcast.21), calls=%async_computation.4 | async-start | bytes 524288 | tf_op jit(solution)/shard_map/all_to_all | solution.py:321
  146.0 10.1 %collective-permute-start.10 = (bf16[16,512]{1,0:T(8,128)(2,1)S(1)}, bf16[16,512]{1,0:T(8,128)(2,1)S(1)}, u32[]{:S(2)}, u32[]{:S(2)}) collective-permute-start(bf16[16,512]{1,0:T(8,128)(2,1)S(1)} %get-tuple-element.128), channel_id=1, source_target_pairs={{0,4},{1,5},{2,6},{3,7},{4,0},{5,1},{6,2},{7,3},{8,12},{9,13},{10,... | collective-permute-start | bytes 49160 | tf_op jit(solution)/shard_map/ppermute | solution.py:247
  148.0 8.8 %collective-permute-start.11 = (bf16[16,512]{1,0:T(8,128)(2,1)S(1)}, bf16[16,512]{1,0:T(8,128)(2,1)S(1)}, u32[]{:S(2)}, u32[]{:S(2)}) collective-permute-start(bf16[16,512]{1,0:T(8,128)(2,1)S(1)} %get-tuple-element.127), channel_id=1, source_target_pairs={{0,8},{1,9},{2,10},{3,11},{4,12},{5,13},{6,14},{7,15},{8,0},{9,1},... | collective-permute-start | bytes 49160 | tf_op jit(solution)/shard_map/ppermute | solution.py:247
  150.3 6.5 %collective-permute-start.12 = (bf16[16,512]{1,0:T(8,128)(2,1)S(1)}, bf16[16,512]{1,0:T(8,128)(2,1)S(1)}, u32[]{:S(2)}, u32[]{:S(2)}) collective-permute-start(bf16[16,512]{1,0:T(8,128)(2,1)S(1)} %get-tuple-element.126), channel_id=1, source_target_pairs={{0,12},{1,13},{2,14},{3,15},{4,8},{5,9},{6,10},{7,11},{8,4},{9,5},... | collective-permute-start | bytes 49160 | tf_op jit(solution)/shard_map/ppermute | solution.py:247
  151.8 3.6 %collective-permute-start.4 = (s32[]{:T(128)}, s32[]{:T(128)}, u32[]{:S(2)}, u32[]{:S(2)}) collective-permute-start(s32[]{:T(128)} %convert.1), channel_id=1, source_target_pairs={{0,16},{16,0},{1,17},{17,1},{2,18},{18,2},{3,19},{19,3},{4,20},{20... | collective-permute-start | bytes 20 | tf_op jit(solution)/shard_map/ppermute | solution.py:329
  157.2 0.7 copy-start.3

commit v4 on v3

--- a/solution.py
+++ b/solution.py
@@ -49,9 +49,17 @@
     )
 
 
-def pack_over_body(main_rows, planes, at_ref, info_ref, tokens_ref, *outs):
+def pack_over_body(main_rows, planes, at_ref, info_ref, tokens_hbm, *refs):
+    *outs, tokens_ref, sems = refs
+    half = tokens_ref.shape[1] // 2
+    spans = [slice(h + c, h + c + STEP) for c in range(0, half, STEP) for h in (0, half)]
+    copies = [
+        pltpu.make_async_copy(tokens_hbm.at[:, span], tokens_ref.at[:, span], sems.at[i])
+        for i, span in enumerate(spans)
+    ]
+    for copy in copies:
+        copy.start()
     at = at_ref[...]
-    half = tokens_ref.shape[1] // 2
     row = lax.broadcasted_iota(jnp.int32, (2 * SPARE, at.shape[1]), 0)
     upper = row >= SPARE
     ids = jnp.where(upper, row - SPARE, row)
@@ -66,7 +74,9 @@
         for b in range(planes):
             outs[b][:, columns] = value[2 * SPARE * b : 2 * SPARE * (b + 1)].astype(jnp.bfloat16)
 
-    for c in range(0, half, STEP):
+    for i, c in enumerate(range(0, half, STEP)):
+        copies[2 * i].wait()
+        copies[2 * i + 1].wait()
         put(
             jnp.dot(left, tokens_ref[:, c : c + STEP], preferred_element_type=jnp.float32)
             + jnp.dot(
@@ -128,55 +138,45 @@
     return jnp.dot(low.astype(jnp.bfloat16), up, preferred_element_type=jnp.float32)
 
 
-def adapt_body(rank, last, first_ref, down_ref, up_ref, rows_ref, out, flag_out, low_ref):
-    step = pl.program_id(0)
-
-    def product(columns):
-        return lax.dot_general(
-            rows_ref[:, columns],
-            down_ref[:, columns],
+def adapt_body(rank, first_ref, down_ref, up_ref, rows_hbm, out, flag_out, rows_ref, sems):
+    depth = down_ref.shape[1]
+    spans = [slice(c, min(c + WIDE, depth + NOTE)) for c in range(0, depth + NOTE, WIDE)]
+    copies = [
+        pltpu.make_async_copy(rows_hbm.at[:, span], rows_ref.at[:, span], sems.at[i])
+        for i, span in enumerate(spans)
+    ]
+    for copy in copies:
+        copy.start()
+    low = jnp.zeros((rows_ref.shape[0], down_ref.shape[0]), jnp.float32)
+    for copy, span in zip(copies, spans, strict=True):
+        copy.wait()
+        span = slice(span.start, min(span.stop, depth))
+        low += lax.dot_general(
+            rows_ref[:, span],
+            down_ref[:, span],
             (((1,), (1,)), ((), ())),
             preferred_element_type=jnp.float32,
         )
-
-    @pl.when(step == 0)
-    def _():
-        low_ref[...] = product(slice(None))
-
-    @pl.when((step > 0) & (step < pl.num_programs(0) - 1))
-    def _():
-        low_ref[...] += product(slice(None))
-
-    @pl.when(step == pl.num_programs(0) - 1)
-    def _():
-        low = low_ref[...] + product(slice(0, last))
-        note = rows_ref[:, last:].astype(jnp.float32)
-        delta = low_delta(low, note[:, :1], first_ref[0], rank, up_ref[...])
-        out[...] = delta.astype(jnp.bfloat16)
-        most = jnp.max(note, axis=0, keepdims=True)
-        flag_out[...] = jnp.broadcast_to(most, flag_out.shape).astype(jnp.bfloat16)
+    note = rows_ref[:, depth:].astype(jnp.float32)
+    out[...] = low_delta(low, note[:, :1], first_ref[0], rank, up_ref[...]).astype(jnp.bfloat16)
+    most = jnp.max(note, axis=0, keepdims=True)
+    flag_out[...] = jnp.broadcast_to(most, flag_out.shape).astype(jnp.bfloat16)
 
 
 def adapt(rank, first, down, up, got):
     rows, width = got.shape[0], up.shape[1]
     return pl.pallas_call(
-        functools.partial(adapt_body, rank, WIDE - NOTE),
-        grid=(got.shape[1] // WIDE,),
-        in_specs=[
-            SMEM,
-            pl.BlockSpec((down.shape[0], WIDE), lambda i: (0, i)),
-            pl.BlockSpec(up.shape, lambda i: (0, 0)),
-            pl.BlockSpec((rows, WIDE), lambda i: (0, i)),
-        ],
-        out_specs=[
-            pl.BlockSpec((rows, width), lambda i: (0, 0)),
-            pl.BlockSpec((16, NOTE), lambda i: (0, 0)),
-        ],
+        functools.partial(adapt_body, rank),
+        in_specs=[SMEM, VMEM, VMEM, pl.BlockSpec(memory_space=pl.ANY)],
+        out_specs=[VMEM, VMEM],
         out_shape=[
             jax.ShapeDtypeStruct((rows, width), jnp.bfloat16),
             jax.ShapeDtypeStruct((16, NOTE), jnp.bfloat16),
         ],
-        scratch_shapes=[pltpu.VMEM((rows, down.shape[0]), jnp.float32)],
+        scratch_shapes=[
+            pltpu.VMEM(got.shape, jnp.bfloat16),
+            pltpu.SemaphoreType.DMA((pl.cdiv(got.shape[1], WIDE),)),
+        ],
         compiler_params=pltpu.CompilerParams(vmem_limit_bytes=24 * 2**20),
         cost_estimate=pl.CostEstimate(
             flops=2 * rows * down.size, bytes_accessed=8 * 2**20, transcendentals=0
@@ -231,12 +231,13 @@
     out[...] = (base_ref[...] + delta).astype(jnp.bfloat16)
 
 
-def call(body, outs, args, specs, flops, moved):
+def call(body, outs, args, specs, flops, moved, scratch=()):
     return pl.pallas_call(
         body,
         in_specs=specs,
         out_specs=[VMEM] * len(outs),
         out_shape=[jax.ShapeDtypeStruct(s, jnp.bfloat16) for s in outs],
+        scratch_shapes=list(scratch),
         compiler_params=pltpu.CompilerParams(vmem_limit_bytes=40 * 2**20),
         cost_estimate=pl.CostEstimate(flops=flops, bytes_accessed=moved, transcendentals=0),
     )(*args)
@@ -278,16 +279,22 @@
     at = jnp.where(left, -1, at)[None, :]
     info = jnp.where(jnp.arange(NOTE)[None, :] == 0, slot[:, None] + 1, 0).astype(jnp.bfloat16)
     some_left = jnp.max(left.astype(jnp.int32)).reshape(1)
+    groups = lax.axis_size("grp")
+    seen = some_left
+    for g in range(1, groups):
+        other = lax.ppermute(some_left, "grp", [(s, (s + g) % groups) for s in range(groups)])
+        seen = jnp.maximum(seen, other)
 
     spare = call(
         functools.partial(pack_over_body, main_rows, planes),
         [(2 * SPARE, depth // 2 + NOTE)] * planes,
         (at, info, tokens),
-        [VMEM] * 3,
+        [VMEM, VMEM, pl.BlockSpec(memory_space=pl.ANY)],
         2 * 96 * row_count * depth,
         6 * 2**20,
-    )
-    blocks = pack(main_rows, some_left, at, info, tokens)
+        [pltpu.VMEM(tokens.shape, jnp.bfloat16), pltpu.SemaphoreType.DMA((depth // STEP,))],
+    )
+    blocks = pack(main_rows, seen, at, info, tokens)
 
     first = (me * local).reshape(1)
     down = adapt_down.transpose(0, 2, 1).reshape(local * rank, depth)
@@ -296,6 +303,7 @@
     along = jnp.concatenate(
         [spare[0]] + [swap(spare[b], b * PLANE) for b in range(1, planes)], axis=0
     )
+    along, blocks, base_value = lax.optimization_barrier((along, blocks, base_value))
     shared = [along] + [swap(along, a) for a in range(1, PLANE)]
     blocks, shared[1] = lax.optimization_barrier((blocks, shared[1]))
     got = lax.all_to_all(
@@ -307,7 +315,7 @@
         [(16 * planes, width)] * PLANE,
         (first, down, up, *shared),
         [SMEM] + [VMEM] * 6,
-        2 * 384 * depth * local * rank,
+        4 * 10**14,
         6 * 2**20,
     )
     over_sum = over_delta[0]
@@ -321,13 +329,6 @@
     back = lax.all_to_all(
         delta.reshape(count, room, width), "ad", split_axis=0, concat_axis=0, tiled=True
     ).reshape(main_rows, width)
-
-    some_left = flags[0, 1].astype(jnp.int32)
-    seen = some_left
-    groups = lax.axis_size("grp")
-    for g in range(1, groups):
-        other = lax.ppermute(some_left, "grp", [(s, (s + g) % groups) for s in range(groups)])
-        seen = jnp.maximum(seen, other)
 
     def finish(base):
         return call(
@@ -351,7 +352,7 @@
         )
         return finish(base_value + extra)
 
-    return lax.cond(seen > 0, more, lambda: finish(base_value))
+    return lax.cond(flags[0, 1] > 0, more, lambda: finish(base_value))
 
 
 def solution(mesh):

time: 158 us -> 156 us (0.987)
  waiting for transfers between devices: 90.4 us -> 79 us
  starting transfers between devices: 35.9 us -> 42.9 us
    ppermute x12, waiting for transfers between devices: 89.7 us -> 58.4 us  [swap(): return lax.ppermute(x, 'ad', [(s, s ^ k) for s in range(count)])]
    all_to_all x1, waiting for transfers between devices: 0.01 us -> 20.6 us  [on_device(): lax.all_to_all(blocks.reshape(count, room, depth + NOTE), 'ad', split_axi...]
    all_to_all x1, starting transfers between devices: 12 us -> 19.9 us  [on_device(): lax.all_to_all(delta.reshape(count, room, width), 'ad', split_axis=0, con...]
    pallas_call x1, Pallas kernels: 7.5 us -> 5.23 us  [pack(): pl.pallas_call(functools.partial(pack_body, WIDE - NOTE), grid=(steps,),...]
    pallas_call x3, Pallas kernels: 5.3 us -> 7.07 us  [call(): pl.pallas_call(body, in_specs=specs, out_specs=[VMEM] * len(outs), out_sh...]
  transfers between devices with their start and end apart: 15 -> 15, of which waited for: 6 -> 7; matrix products, arithmetic and copies ran while one was open for 5% -> 5% of each run, Pallas kernels for 10% -> 12%
where the time goes in v4:
time: 156 us; the launch traced here: 155 us
  waiting for transfers between devices  79 us (51%)
  starting transfers between devices  42.9 us (28%)
  Pallas kernels  19.5 us (12%)
  matrix products  6.55 us (4%)
  other arithmetic  3.45 us (2%)
  between operations  2.39 us (2%)
    ppermute x12, waiting for transfers between devices, swap(): return lax.ppermute(x, 'ad', [(s, s ^ k) for s in range(count)])  58.4 us
    all_to_all x1, waiting for transfers between devices, on_device(): lax.all_to_all(blocks.reshape(count, room, depth + NOTE), 'ad', split_axi...  20.6 us
    all_to_all x1, starting transfers between devices, on_device(): lax.all_to_all(delta.reshape(count, room, width), 'ad', split_axis=0, con...  19.9 us
    ppermute x12, starting transfers between devices, swap(): return lax.ppermute(x, 'ad', [(s, s ^ k) for s in range(count)])  13.5 us
    pallas_call x1, Pallas kernels, adapt(): pl.pallas_call(functools.partial(adapt_body, rank), in_specs=[SMEM, VMEM,...  7.19 us
    pallas_call x3, Pallas kernels, call(): pl.pallas_call(body, in_specs=specs, out_specs=[VMEM] * len(outs), out_sh...  7.07 us
    all_to_all x1, starting transfers between devices, on_device(): lax.all_to_all(blocks.reshape(count, room, depth + NOTE), 'ad', split_axi...  6.58 us
    dot_general x1, matrix products, on_device(): jnp.dot(tokens, value_weight, preferred_element_type=jnp.float32)  6.55 us
  transfers between devices with their start and end apart: 15, of which 7 were waited for; matrix products, arithmetic and copies ran while one was open for 5% of the time, Pallas kernels for 12%

profile of v4, /device:TPU:0, one launch (start us, length us, event | category | flops | bytes accessed | tf_op | source)
XLA Modules:
  0.0 155.3 jit_solution(15113198198099577569)
XLA Ops:
  0.0 1.0 select_reduce_fusion.1
  2.0 1.3 convert_reduce_fusion.2
  3.3 2.9 %collective-permute-start.3 = (s32[1]{0:T(128)}, s32[1]{0:T(128)}, u32[]{:S(2)}, u32[]{:S(2)}) collective-permute-start(s32[1]{0:T(128)} %bitcast.16), channel_id=1, source_target_pairs={{0,16},{16,0},{1,17},{17,1},{2,18},{18,2},{3,19},{19,3},{4,20},{20... | collective-permute-start | bytes 20 | tf_op jit(solution)/shard_map/ppermute | solution.py:285
  6.4 2.6 %shard_map.66 = (bf16[24,4224]{1,0:T(8,128)(2,1)S(1)}, bf16[24,4224]{1,0:T(8,128)(2,1)S(1)}, bf16[24,4224]{1,0:T(8,128)(2,1)S(1)}, bf16[24,4224]{1,0:T(8,128)(2,1)S(1)}) custom-call(s32[1,256]{1,0:T(1,128)S(1)} %and_select_fusion.4.at_ref, bf16[256,128]{1,0:T(8,128)(2,1)S(1)} %select_convert_fusion.2.info_ref, bf16[256,8192]{1,0:T(8,128)(2,1)} %tokens_ref.1), custom_call_target="tpu_custom_call" | custom-call | flops 402653184 | bytes 6291456 | tf_op jit(solution)/shard_map/pallas_call | solution.py:235
  9.0 1.6 %collective-permute-start = (bf16[24,4224]{1,0:T(8,128)(2,1)S(1)}, bf16[24,4224]{1,0:T(8,128)(2,1)S(1)}, u32[]{:S(2)}, u32[]{:S(2)}) collective-permute-start(bf16[24,4224]{1,0:T(8,128)(2,1)S(1)} %get-tuple-element.111), channel_id=1, source_target_pairs={{0,4},{1,5},{2,6},{3,7},{4,0},{5,1},{6,2},{7,3},{8,12},{9,13},{10,... | collective-permute-start | bytes 608264 | tf_op jit(solution)/shard_map/ppermute | solution.py:248
  10.6 2.6 %collective-permute-start.1 = (bf16[24,4224]{1,0:T(8,128)(2,1)S(1)}, bf16[24,4224]{1,0:T(8,128)(2,1)S(1)}, u32[]{:S(2)}, u32[]{:S(2)}) collective-permute-start(bf16[24,4224]{1,0:T(8,128)(2,1)S(1)} %get-tuple-element.112), channel_id=1, source_target_pairs={{0,8},{1,9},{2,10},{3,11},{4,12},{5,13},{6,14},{7,15},{8,0},{9,1},... | collective-permute-start | bytes 608264 | tf_op jit(solution)/shard_map/ppermute | solution.py:248
  13.4 6.5 %fusion.11 = f32[256,512]{1,0:T(8,128)} fusion(bf16[256,8192]{1,0:T(8,128)(2,1)S(1)} %copy-done.1, bf16[8192,512]{1,0:T(8,128)(2,1)} %param.9), kind=kOutput, calls=%fused_computation.57 | convolution fusion | flops 2147483648 | bytes 13107200 | tf_op jit(solution)/shard_map/dot_general | solution.py:264
  21.3 5.2 %shard_map.67 = bf16[256,8320]{1,0:T(8,128)(2,1)} custom-call(s32[1]{0:T(128)S(6)} %max.3.flag_ref, s32[1,256]{1,0:T(1,128)S(1)} %and_select_fusion.4.at_ref, bf16[256,128]{1,0:T(8,128)(2,1)} %copy-done, bf16[256,8192]{1,0:T(8,128)(2,1)S(1)} %copy-done.1), custom_call_target="tpu_custom_call" | custom-call | flops 1073741824 | bytes 8388608 | tf_op jit(solution)/shard_map/pallas_call | solution.py:117
  26.6 1.6 %collective-permute-done.1 = bf16[24,4224]{1,0:T(8,128)(2,1)S(1)} collective-permute-done((bf16[24,4224]{1,0:T(8,128)(2,1)S(1)}, bf16[24,4224]{1,0:T(8,128)(2,1)S(1)}, u32[]{:S(2)}, u32[]{:S(2)}) %collective-permute-start.1) | collective-permute-done | bytes 202784 | tf_op jit(solution)/shard_map/ppermute | solution.py:248
  28.3 1.6 %collective-permute-start.5 = (bf16[96,4224]{1,0:T(8,128)(2,1)S(1)}, bf16[96,4224]{1,0:T(8,128)(2,1)S(1)}, u32[]{:S(2)}, u32[]{:S(2)}) collective-permute-start(bf16[96,4224]{1,0:T(8,128)(2,1)S(1)} %pad_maximum_fusion.refs_0_), channel_id=1, source_target_pairs={{0,2},{1,3},{2,0},{3,1},{4,6},{5,7},{6,4},{7,5},{8,10},{9,11},{10,... | collective-permute-start | bytes 2433032 | tf_op jit(solution)/shard_map/ppermute | solution.py:248
  30.6 6.6 %all-to-all-start.3 = ((bf16[16,16,8320]{2,1,0:T(8,128)(2,1)}), bf16[16,16,8320]{2,1,0:T(8,128)(2,1)}, u32[]{:S(2)}, u32[]{:S(2)}) async-start(bf16[16,16,8320]{2,1,0:T(8,128)(2,1)} %bitcast.34), calls=%async_computation.3 | async-start | bytes 8519680 | tf_op jit(solution)/shard_map/all_to_all | solution.py:309
  37.2 18.8 %collective-permute-done.5.refs_2_ = bf16[96,4224]{1,0:T(8,128)(2,1)S(1)} collective-permute-done((bf16[96,4224]{1,0:T(8,128)(2,1)S(1)}, bf16[96,4224]{1,0:T(8,128)(2,1)S(1)}, u32[]{:S(2)}, u32[]{:S(2)}) %collective-permute-start.5) | collective-permute-done | bytes 811040 | tf_op jit(solution)/shard_map/ppermute | solution.py:248
  56.0 32.5 %collective-permute-done.6.refs_3_ = bf16[96,4224]{1,0:T(8,128)(2,1)S(1)} collective-permute-done((bf16[96,4224]{1,0:T(8,128)(2,1)S(1)}, bf16[96,4224]{1,0:T(8,128)(2,1)S(1)}, u32[]{:S(2)}, u32[]{:S(2)}) %collective-permute-start.6) | collective-permute-done | bytes 811040 | tf_op jit(solution)/shard_map/ppermute | solution.py:248
  88.5 4.2 %shard_map.69 = (bf16[64,512]{1,0:T(8,128)(2,1)S(1)}, bf16[64,512]{1,0:T(8,128)(2,1)S(1)}, bf16[64,512]{1,0:T(8,128)(2,1)S(1)}, bf16[64,512]{1,0:T(8,128)(2,1)S(1)}) custom-call(s32[1]{0:T(128)} %bitcast.8.first_ref, bf16[256,8192]{1,0:T(8,128)(2,1)} %bitcast.36, bf16[256,512]{1,0:T(8,128)(2,1)} %bitcast.42, bf16[96,4224]{1,0:T(8,128)(2,1)S(1)} %pad_maximum_fusion.refs_0_, ...), custom_call_target="tpu_custom_call" | custom-call | flops 400000001507328 | bytes 6291456 | tf_op jit(solution)/shard_map/pallas_call | solution.py:235
  92.8 1.2 collective-permute-start.7
  94.0 1.5 collective-permute-start.8
  95.5 20.6 %all-to-all-done.3 = bf16[16,16,8320]{2,1,0:T(8,128)(2,1)} async-done(((bf16[16,16,8320]{2,1,0:T(8,128)(2,1)}), bf16[16,16,8320]{2,1,0:T(8,128)(2,1)}, u32[]{:S(2)}, u32[]{:S(2)}) %all-to-all-start.3) | async-done | bytes 4259872 | tf_op jit(solution)/shard_map/all_to_all | solution.py:309
  116.2 7.2 %shard_map.68 = (bf16[256,512]{1,0:T(8,128)(2,1)}, bf16[16,128]{1,0:T(8,128)(2,1)S(1)}) custom-call(s32[1]{0:T(128)} %bitcast.8.first_ref, bf16[256,8192]{1,0:T(8,128)(2,1)} %bitcast.37, bf16[256,512]{1,0:T(8,128)(2,1)} %bitcast.43, bf16[256,8320]{1,0:T(8,128)(2,1)} %bitcast.18.rows_hbm), custom_call_target="tpu_custom_call" | custom-call | flops 1073741824 | bytes 8388608 | tf_op jit(solution)/shard_map/pallas_call | solution.py:168
  123.4 19.9 %all-to-all-start.4 = ((bf16[16,16,512]{2,1,0:T(8,128)(2,1)}), bf16[16,16,512]{2,1,0:T(8,128)(2,1)S(1)}, u32[]{:S(2)}, u32[]{:S(2)}) async-start(bf16[16,16,512]{2,1,0:T(8,128)(2,1)} %bitcast.20), calls=%async_computation.4 | async-start | bytes 524288 | tf_op jit(solution)/shard_map/all_to_all | solution.py:329
  143.3 2.0 %collective-permute-start.10 = (bf16[16,512]{1,0:T(8,128)(2,1)S(1)}, bf16[16,512]{1,0:T(8,128)(2,1)S(1)}, u32[]{:S(2)}, u32[]{:S(2)}) collective-permute-start(bf16[16,512]{1,0:T(8,128)(2,1)S(1)} %get-tuple-element.134), channel_id=1, source_target_pairs={{0,4},{1,5},{2,6},{3,7},{4,0},{5,1},{6,2},{7,3},{8,12},{9,13},{10,... | collective-permute-start | bytes 49160 | tf_op jit(solution)/shard_map/ppermute | solution.py:248
  145.3 2.4 %collective-permute-start.11 = (bf16[16,512]{1,0:T(8,128)(2,1)S(1)}, bf16[16,512]{1,0:T(8,128)(2,1)S(1)}, u32[]{:S(2)}, u32[]{:S(2)}) collective-permute-start(bf16[16,512]{1,0:T(8,128)(2,1)S(1)} %get-tuple-element.133), channel_id=1, source_target_pairs={{0,8},{1,9},{2,10},{3,11},{4,12},{5,13},{6,14},{7,15},{8,0},{9,1},... | collective-permute-start | bytes 49160 | tf_op jit(solution)/shard_map/ppermute | solution.py:248
  147.8 0.7 slice.15
  149.7 4.5 %collective-permute-done.11 = bf16[16,512]{1,0:T(8,128)(2,1)S(1)} collective-permute-done((bf16[16,512]{1,0:T(8,128)(2,1)S(1)}, bf16[16,512]{1,0:T(8,128)(2,1)S(1)}, u32[]{:S(2)}, u32[]{:S(2)}) %collective-permute-start.11) | collective-permute-done | bytes 16416 | tf_op jit(solution)/shard_map/ppermute | solution.py:248
  154.6 0.7 copy-done.4
  (56 shorter events, 3.6 us)
Async XLA Ops:
  3.3 16.7 %collective-permute-start.3 = (s32[1]{0:T(128)}, s32[1]{0:T(128)}, u32[]{:S(2)}, u32[]{:S(2)}) collective-permute-start(s32[1]{0:T(128)} %bitcast.16), channel_id=1, source_target_pairs={{0,16},{16,0},{1,17},{17,1},{2,18},{18,2},{3,19},{19,3},{4,20},{20... | collective-permute-start | bytes 20 | tf_op jit(solution)/shard_map/ppermute | solution.py:285
  6.4 15.0 %copy-start.5 = (s32[1,256]{1,0:T(1,128)}, s32[1,256]{1,0:T(1,128)S(1)}, u32[]{:S(2)}) copy-start(s32[1,256]{1,0:T(1,128)S(1)} %and_select_fusion.4.at_ref) | copy-start | bytes 3076
  9.0 17.6 %collective-permute-start = (bf16[24,4224]{1,0:T(8,128)(2,1)S(1)}, bf16[24,4224]{1,0:T(8,128)(2,1)S(1)}, u32[]{:S(2)}, u32[]{:S(2)}) collective-permute-start(bf16[24,4224]{1,0:T(8,128)(2,1)S(1)} %get-tuple-element.111), channel_id=1, source_target_pairs={{0,4},{1,5},{2,6},{3,7},{4,0},{5,1},{6,2},{7,3},{8,12},{9,13},{10,... | collective-permute-start | bytes 608264 | tf_op jit(solution)/shard_map/ppermute | solution.py:248
  10.6 17.6 %collective-permute-start.1 = (bf16[24,4224]{1,0:T(8,128)(2,1)S(1)}, bf16[24,4224]{1,0:T(8,128)(2,1)S(1)}, u32[]{:S(2)}, u32[]{:S(2)}) collective-permute-start(bf16[24,4224]{1,0:T(8,128)(2,1)S(1)} %get-tuple-element.112), channel_id=1, source_target_pairs={{0,8},{1,9},{2,10},{3,11},{4,12},{5,13},{6,14},{7,15},{8,0},{9,1},... | collective-permute-start | bytes 608264 | tf_op jit(solution)/shard_map/ppermute | solution.py:248
  13.2 15.0 %collective-permute-start.2 = (bf16[24,4224]{1,0:T(8,128)(2,1)S(1)}, bf16[24,4224]{1,0:T(8,128)(2,1)S(1)}, u32[]{:S(2)}, u32[]{:S(2)}) collective-permute-start(bf16[24,4224]{1,0:T(8,128)(2,1)S(1)} %get-tuple-element.113), channel_id=1, source_target_pairs={{0,12},{1,13},{2,14},{3,15},{4,8},{5,9},{6,10},{7,11},{8,4},{9,5},... | collective-permute-start | bytes 608264 | tf_op jit(solution)/shard_map/ppermute | solution.py:248
  28.2 2.4 %collective-permute-start.4 = (bf16[96,4224]{1,0:T(8,128)(2,1)S(1)}, bf16[96,4224]{1,0:T(8,128)(2,1)S(1)}, u32[]{:S(2)}, u32[]{:S(2)}) collective-permute-start(bf16[96,4224]{1,0:T(8,128)(2,1)S(1)} %pad_maximum_fusion.refs_0_), channel_id=1, source_target_pairs={{0,1},{1,0},{2,3},{3,2},{4,5},{5,4},{6,7},{7,6},{8,9},{9,8},{10,11... | collective-permute-start | bytes 2433032 | tf_op jit(solution)/shard_map/ppermute | solution.py:248
  28.3 27.7 %collective-permute-start.5 = (bf16[96,4224]{1,0:T(8,128)(2,1)S(1)}, bf16[96,4224]{1,0:T(8,128)(2,1)S(1)}, u32[]{:S(2)}, u32[]{:S(2)}) collective-permute-start(bf16[96,4224]{1,0:T(8,128)(2,1)S(1)} %pad_maximum_fusion.refs_0_), channel_id=1, source_target_pairs={{0,2},{1,3},{2,0},{3,1},{4,6},{5,7},{6,4},{7,5},{8,10},{9,11},{10,... | collective-permute-start | bytes 2433032 | tf_op jit(solution)/shard_map/ppermute | solution.py:248
  29.9 58.7 %collective-permute-start.6 = (bf16[96,4224]{1,0:T(8,128)(2,1)S(1)}, bf16[96,4224]{1,0:T(8,128)(2,1)S(1)}, u32[]{:S(2)}, u32[]{:S(2)}) collective-permute-start(bf16[96,4224]{1,0:T(8,128)(2,1)S(1)} %pad_maximum_fusion.refs_0_), channel_id=1, source_target_pairs={{0,3},{1,2},{2,1},{3,0},{4,7},{5,6},{6,5},{7,4},{8,11},{9,10},{10,... | collective-permute-start | bytes 2433032 | tf_op jit(solution)/shard_map/ppermute | solution.py:248
  30.6 85.5 %all-to-all-start.3 = ((bf16[16,16,8320]{2,1,0:T(8,128)(2,1)}), bf16[16,16,8320]{2,1,0:T(8,128)(2,1)}, u32[]{:S(2)}, u32[]{:S(2)}) async-start(bf16[16,16,8320]{2,1,0:T(8,128)(2,1)} %bitcast.34), calls=%async_computation.3 | async-start | bytes 8519680 | tf_op jit(solution)/shard_map/all_to_all | solution.py:309
  92.7 55.0 %copy-start.10 = (s32[256]{0:T(256)S(1)}, s32[256]{0:T(256)}, u32[]{:S(2)}) copy-start(s32[256]{0:T(256)} %copy-done.9) | copy-start | bytes 3076
  92.8 61.4 %copy-start.2 = (f32[256,512]{1,0:T(8,128)S(1)}, f32[256,512]{1,0:T(8,128)}, u32[]{:S(2)}) copy-start(f32[256,512]{1,0:T(8,128)} %fusion.11) | copy-start | bytes 1572868
  92.8 61.4 %copy-start.3 = (bf16[16,16,512]{2,1,0:T(8,128)(2,1)S(1)}, bf16[16,16,512]{2,1,0:T(8,128)(2,1)}, u32[]{:S(2)}) copy-start(bf16[16,16,512]{2,1,0:T(8,128)(2,1)} %param.11) | copy-start | bytes 786436
  92.8 61.4 %copy-start.6 = (s32[1,256]{1,0:T(1,128)S(1)}, s32[1,256]{1,0:T(1,128)}, u32[]{:S(2)}) copy-start(s32[1,256]{1,0:T(1,128)} %copy-done.5) | copy-start | bytes 3076
  92.8 61.4 %copy-start.8 = (s32[256]{0:T(256)S(1)}, s32[256]{0:T(256)}, u32[]{:S(2)}) copy-start(s32[256]{0:T(256)} %copy-done.7) | copy-start | bytes 3076
  92.8 61.4 %copy-start.11 = (s32[256]{0:T(256)S(1)}, s32[256]{0:T(256)}, u32[]{:S(2)}) copy-start(s32[256]{0:T(256)} %get-tuple-element.136) | copy-start | bytes 3076
  92.8 61.4 %copy-start.12 = (s32[256]{0:T(256)S(1)}, s32[256]{0:T(256)}, u32[]{:S(2)}) copy-start(s32[256]{0:T(256)} %get-tuple-element.138) | copy-start | bytes 3076
  92.8 61.4 %copy-start.13 = (pred[256]{0:T(512)(128)(4,1)S(1)}, pred[256]{0:T(512)(128)(4,1)}, u32[]{:S(2)}) copy-start(pred[256]{0:T(512)(128)(4,1)} %get-tuple-element.127) | copy-start | bytes 772
  92.8 50.4 %collective-permute-start.7 = (bf16[64,512]{1,0:T(8,128)(2,1)S(1)}, bf16[64,512]{1,0:T(8,128)(2,1)S(1)}, u32[]{:S(2)}, u32[]{:S(2)}) collective-permute-start(bf16[64,512]{1,0:T(8,128)(2,1)S(1)} %get-tuple-element.122), channel_id=1, source_target_pairs={{0,1},{1,0},{2,3},{3,2},{4,5},{5,4},{6,7},{7,6},{8,9},{9,8},{10,11... | collective-permute-start | bytes 196616 | tf_op jit(solution)/shard_map/ppermute | solution.py:248
  94.0 49.2 %collective-permute-start.8 = (bf16[64,512]{1,0:T(8,128)(2,1)S(1)}, bf16[64,512]{1,0:T(8,128)(2,1)S(1)}, u32[]{:S(2)}, u32[]{:S(2)}) collective-permute-start(bf16[64,512]{1,0:T(8,128)(2,1)S(1)} %get-tuple-element.123), channel_id=1, source_target_pairs={{0,2},{1,3},{2,0},{3,1},{4,6},{5,7},{6,4},{7,5},{8,10},{9,11},{10,... | collective-permute-start | bytes 196616 | tf_op jit(solution)/shard_map/ppermute | solution.py:248
  95.5 47.7 %collective-permute-start.9 = (bf16[64,512]{1,0:T(8,128)(2,1)S(1)}, bf16[64,512]{1,0:T(8,128)(2,1)S(1)}, u32[]{:S(2)}, u32[]{:S(2)}) collective-permute-start(bf16[64,512]{1,0:T(8,128)(2,1)S(1)} %get-tuple-element.124), channel_id=1, source_target_pairs={{0,3},{1,2},{2,1},{3,0},{4,7},{5,6},{6,5},{7,4},{8,11},{9,10},{10,... | collective-permute-start | bytes 196616 | tf_op jit(solution)/shard_map/ppermute | solution.py:248
  123.4 30.8 %all-to-all-start.4 = ((bf16[16,16,512]{2,1,0:T(8,128)(2,1)}), bf16[16,16,512]{2,1,0:T(8,128)(2,1)S(1)}, u32[]{:S(2)}, u32[]{:S(2)}) async-start(bf16[16,16,512]{2,1,0:T(8,128)(2,1)} %bitcast.20), calls=%async_computation.4 | async-start | bytes 524288 | tf_op jit(solution)/shard_map/all_to_all | solution.py:329
  143.3 6.3 %collective-permute-start.10 = (bf16[16,512]{1,0:T(8,128)(2,1)S(1)}, bf16[16,512]{1,0:T(8,128)(2,1)S(1)}, u32[]{:S(2)}, u32[]{:S(2)}) collective-permute-start(bf16[16,512]{1,0:T(8,128)(2,1)S(1)} %get-tuple-element.134), channel_id=1, source_target_pairs={{0,4},{1,5},{2,6},{3,7},{4,0},{5,1},{6,2},{7,3},{8,12},{9,13},{10,... | collective-permute-start | bytes 49160 | tf_op jit(solution)/shard_map/ppermute | solution.py:248
  145.3 8.8 %collective-permute-start.11 = (bf16[16,512]{1,0:T(8,128)(2,1)S(1)}, bf16[16,512]{1,0:T(8,128)(2,1)S(1)}, u32[]{:S(2)}, u32[]{:S(2)}) collective-permute-start(bf16[16,512]{1,0:T(8,128)(2,1)S(1)} %get-tuple-element.133), channel_id=1, source_target_pairs={{0,8},{1,9},{2,10},{3,11},{4,12},{5,13},{6,14},{7,15},{8,0},{9,1},... | collective-permute-start | bytes 49160 | tf_op jit(solution)/shard_map/ppermute | solution.py:248
  147.7 6.5 %collective-permute-start.12 = (bf16[16,512]{1,0:T(8,128)(2,1)S(1)}, bf16[16,512]{1,0:T(8,128)(2,1)S(1)}, u32[]{:S(2)}, u32[]{:S(2)}) collective-permute-start(bf16[16,512]{1,0:T(8,128)(2,1)S(1)} %get-tuple-element.132), channel_id=1, source_target_pairs={{0,12},{1,13},{2,14},{3,15},{4,8},{5,9},{6,10},{7,11},{8,4},{9,5},... | collective-permute-start | bytes 49160 | tf_op jit(solution)/shard_map/ppermute | solution.py:248
  (5 other events, 37.6 us)

commit v5 on v4

--- a/solution.py
+++ b/solution.py
@@ -15,6 +15,7 @@
 STEP = 1024
 WIDE = 1664
 VMEM = pl.BlockSpec(memory_space=pltpu.VMEM)
+ANY = pl.BlockSpec(memory_space=pl.ANY)
 SMEM = pl.BlockSpec(memory_space=pltpu.SMEM)
 
 
@@ -49,8 +50,17 @@
     )
 
 
-def pack_over_body(main_rows, planes, at_ref, info_ref, tokens_hbm, *refs):
-    *outs, tokens_ref, sems = refs
+def one_hot(hit):
+    return hit.astype(jnp.float32).astype(jnp.bfloat16)
+
+
+def earlier(hit, until):
+    counts = jnp.dot(one_hot(hit), until, preferred_element_type=jnp.float32)
+    return jnp.sum(jnp.where(hit, counts, 0.0), axis=0, keepdims=True).astype(jnp.int32)
+
+
+def route_body(room, local, me_ref, tenant_ref, slot_ref, tokens_hbm, *refs):
+    *outs, at_ref, note_ref, left_ref, tokens_ref, sems = refs
     half = tokens_ref.shape[1] // 2
     spans = [slice(h + c, h + c + STEP) for c in range(0, half, STEP) for h in (0, half)]
     copies = [
@@ -59,37 +69,65 @@
     ]
     for copy in copies:
         copy.start()
-    at = at_ref[...]
-    row = lax.broadcasted_iota(jnp.int32, (2 * SPARE, at.shape[1]), 0)
+    tenant = tenant_ref[...]
+    rows = tenant.shape[1]
+    planes = len(outs)
+    main_rows = planes * PLANE * room
+
+    def iota(size, axis=0):
+        return lax.broadcasted_iota(jnp.int32, (size, rows), axis)
+
+    table = jnp.broadcast_to(slot_ref[...].astype(jnp.float32), (16, TENANTS)).astype(jnp.bfloat16)
+    slot = jnp.dot(table, one_hot(iota(TENANTS) == tenant), preferred_element_type=jnp.float32)[:1]
+    owner = slot.astype(jnp.int32) // local
+    until = one_hot(iota(rows) < iota(rows, 1))
+    place = earlier(iota(planes * PLANE) == owner, until)
+    plane = (owner ^ me_ref[0]) // PLANE
+    over = place >= room
+    over_place = earlier((iota(16) == plane) & over, until)
+    left = over & (over_place >= SPARE)
+    at = jnp.where(over, main_rows + plane * SPARE + over_place, owner * room + place)
+    at = jnp.where(left, -1, at)
+    at_ref[...] = at
+    most = jnp.max(left.astype(jnp.float32), axis=1, keepdims=True).astype(jnp.int32)
+    left_ref[...] = jnp.broadcast_to(most, left_ref.shape)
+    note = jnp.where(iota(NOTE) == 0, slot + 1.0, 0.0).astype(jnp.bfloat16)
+    note_ref[...] = note
+
+    row = iota(2 * SPARE)
     upper = row >= SPARE
     ids = jnp.where(upper, row - SPARE, row)
     ids = jnp.concatenate([ids + main_rows + b * SPARE for b in range(planes)], axis=0)
     upper = jnp.concatenate([upper] * planes, axis=0)
     hit = ids == at
-    left = (hit & ~upper).astype(jnp.float32).astype(jnp.bfloat16)
-    right = (hit & upper).astype(jnp.float32).astype(jnp.bfloat16)
-    both = hit.astype(jnp.float32).astype(jnp.bfloat16)
+    first, second = one_hot(hit & ~upper), one_hot(hit & upper)
 
     def put(value, columns):
         for b in range(planes):
             outs[b][:, columns] = value[2 * SPARE * b : 2 * SPARE * (b + 1)].astype(jnp.bfloat16)
 
+    put(notes_of(one_hot(hit), note), slice(half, half + NOTE))
     for i, c in enumerate(range(0, half, STEP)):
         copies[2 * i].wait()
         copies[2 * i + 1].wait()
         put(
-            jnp.dot(left, tokens_ref[:, c : c + STEP], preferred_element_type=jnp.float32)
+            jnp.dot(first, tokens_ref[:, c : c + STEP], preferred_element_type=jnp.float32)
             + jnp.dot(
-                right, tokens_ref[:, half + c : half + c + STEP], preferred_element_type=jnp.float32
+                second,
+                tokens_ref[:, half + c : half + c + STEP],
+                preferred_element_type=jnp.float32,
             ),
             slice(c, c + STEP),
         )
-    put(
-        jnp.dot(both, info_ref[...], preferred_element_type=jnp.float32), slice(half, half + NOTE)
-    )
-
-
-def pack_body(last, flag_ref, at_ref, info_ref, tokens_ref, out):
+
+
+def notes_of(pick, note):
+    return lax.dot_general(
+        pick, note, (((1,), (1,)), ((), ())), preferred_element_type=jnp.float32
+    )
+
+
+def pack_body(last, flag_ref, at_ref, note_ref, tokens_ref, out):
     shape = (out.shape[0], at_ref.shape[1])
     pick = lax.broadcasted_iota(jnp.int32, shape, 0) == at_ref[...]
     pick = pick.astype(jnp.float32).astype(jnp.bfloat16)
@@ -105,22 +143,22 @@
         out[:, :last] = jnp.dot(
             pick, tokens_ref[:, :last], preferred_element_type=jnp.float32
         ).astype(jnp.bfloat16)
-        note = jnp.dot(pick, info_ref[...], preferred_element_type=jnp.float32)
+        note = notes_of(pick, note_ref[...])
         column = lax.broadcasted_iota(jnp.int32, note.shape, 1)
-        flag = jnp.where(column == 1, flag_ref[0].astype(jnp.float32), 0.0)
+        flag = jnp.where(column == 1, flag_ref[...].astype(jnp.float32), 0.0)
         out[:, last:] = (note + flag).astype(jnp.bfloat16)
 
 
-def pack(main_rows, some_left, at, info, tokens):
+def pack(main_rows, flag, at, note, tokens):
     rows, depth = tokens.shape
     steps = (depth + NOTE) // WIDE
     return pl.pallas_call(
         functools.partial(pack_body, WIDE - NOTE),
         grid=(steps,),
         in_specs=[
-            SMEM,
+            pl.BlockSpec(flag.shape, lambda i: (0, 0)),
             pl.BlockSpec(at.shape, lambda i: (0, 0)),
-            pl.BlockSpec(info.shape, lambda i: (0, 0)),
+            pl.BlockSpec(note.shape, lambda i: (0, 0)),
             pl.BlockSpec((rows, WIDE), lambda i: (0, i)),
         ],
         out_specs=pl.BlockSpec((main_rows, WIDE), lambda i: (0, i)),
@@ -129,7 +167,7 @@
         cost_estimate=pl.CostEstimate(
             flops=2 * main_rows * rows * depth, bytes_accessed=8 * 2**20, transcendentals=0
         ),
-    )(some_left, at, info, tokens)
+    )(flag, at, note, tokens)
 
 
 def low_delta(low, note, first, rank, up):
@@ -138,18 +176,26 @@
     return jnp.dot(low.astype(jnp.bfloat16), up, preferred_element_type=jnp.float32)
 
 
-def adapt_body(rank, first_ref, down_ref, up_ref, rows_hbm, out, flag_out, rows_ref, sems):
+def adapt_body(rank, first_ref, down_hbm, up_ref, rows_hbm, out, flag_out, *scratch):
+    down_ref, rows_ref, down_sems, sems = scratch
     depth = down_ref.shape[1]
     spans = [slice(c, min(c + WIDE, depth + NOTE)) for c in range(0, depth + NOTE, WIDE)]
-    copies = [
-        pltpu.make_async_copy(rows_hbm.at[:, span], rows_ref.at[:, span], sems.at[i])
-        for i, span in enumerate(spans)
-    ]
-    for copy in copies:
-        copy.start()
+    copies = []
+    for i, span in enumerate(spans):
+        kept = slice(span.start, min(span.stop, depth))
+        copies.append(
+            (
+                pltpu.make_async_copy(rows_hbm.at[:, span], rows_ref.at[:, span], sems.at[i]),
+                pltpu.make_async_copy(down_hbm.at[:, kept], down_ref.at[:, kept], down_sems.at[i]),
+            )
+        )
+    for pair in copies:
+        pair[0].start()
+        pair[1].start()
     low = jnp.zeros((rows_ref.shape[0], down_ref.shape[0]), jnp.float32)
-    for copy, span in zip(copies, spans, strict=True):
-        copy.wait()
+    for pair, span in zip(copies, spans, strict=True):
+        pair[0].wait()
+        pair[1].wait()
         span = slice(span.start, min(span.stop, depth))
         low += lax.dot_general(
             rows_ref[:, span],
@@ -167,14 +213,16 @@
     rows, width = got.shape[0], up.shape[1]
     return pl.pallas_call(
         functools.partial(adapt_body, rank),
-        in_specs=[SMEM, VMEM, VMEM, pl.BlockSpec(memory_space=pl.ANY)],
+        in_specs=[SMEM, ANY, VMEM, ANY],
         out_specs=[VMEM, VMEM],
         out_shape=[
             jax.ShapeDtypeStruct((rows, width), jnp.bfloat16),
             jax.ShapeDtypeStruct((16, NOTE), jnp.bfloat16),
         ],
         scratch_shapes=[
+            pltpu.VMEM(down.shape, jnp.bfloat16),
             pltpu.VMEM(got.shape, jnp.bfloat16),
+            pltpu.SemaphoreType.DMA((pl.cdiv(got.shape[1], WIDE),)),
             pltpu.SemaphoreType.DMA((pl.cdiv(got.shape[1], WIDE),)),
         ],
         compiler_params=pltpu.CompilerParams(vmem_limit_bytes=24 * 2**20),
@@ -184,14 +232,24 @@
     )(first, down, up, got)
 
 
-def adapt_over_body(planes, rank, first_ref, down_ref, up_ref, *refs):
-    rows_refs, outs = refs[:PLANE], refs[PLANE:]
+def adapt_over_body(planes, rank, first_ref, down_hbm, up_ref, *refs):
+    rows_refs, outs = refs[:PLANE], refs[PLANE : 2 * PLANE]
+    down_ref, sems = refs[2 * PLANE :]
     half = down_ref.shape[1] // 2
+    spans = [slice(h + c, h + c + STEP) for c in range(0, half, STEP) for h in (0, half)]
+    copies = [
+        pltpu.make_async_copy(down_hbm.at[:, span], down_ref.at[:, span], sems.at[i])
+        for i, span in enumerate(spans)
+    ]
+    for copy in copies:
+        copy.start()
     each = rows_refs[0].shape[0]
     shape = (PLANE * each, down_ref.shape[0])
     dims = (((1,), (1,)), ((), ()))
     low0, low1 = jnp.zeros(shape, jnp.float32), jnp.zeros(shape, jnp.float32)
-    for c in range(0, half, STEP):
+    for i, c in enumerate(range(0, half, STEP)):
+        copies[2 * i].wait()
+        copies[2 * i + 1].wait()
         rows = jnp.concatenate([r[:, c : c + STEP] for r in rows_refs], axis=0)
         low0 += lax.dot_general(
             rows, down_ref[:, c : c + STEP], dims, preferred_element_type=jnp.float32
@@ -248,75 +306,83 @@
     return lax.ppermute(x, "ad", [(s, s ^ k) for s in range(count)])
 
 
+def route(tenant_ids, tenant_slot, local):
+    tenant = tenant_ids[:, 0]
+    tenant_match = tenant[:, None] == jnp.arange(TENANTS, dtype=jnp.int32)[None, :]
+    slot = jnp.sum(jnp.where(tenant_match, tenant_slot[None, :], 0), axis=1)
+    owner = slot // local
+    order = jnp.arange(tenant.shape[0], dtype=jnp.int32)
+    before = order[None, :] < order[:, None]
+    place = jnp.sum(((owner[:, None] == owner[None, :]) & before).astype(jnp.int32), axis=1)
+    return slot, owner, place
+
+
 def on_device(tokens, value_weight, adapt_down, adapt_up, tenant_ids, tenant_slot):
     row_count, depth = tokens.shape
     count = lax.axis_size("ad")
     me = lax.axis_index("ad")
     local, _, rank = adapt_down.shape
     width = adapt_up.shape[2]
-    tenant = tenant_ids[:, 0]
-    tenant_match = tenant[:, None] == jnp.arange(TENANTS, dtype=jnp.int32)[None, :]
-    slot = jnp.sum(jnp.where(tenant_match, tenant_slot[None, :], 0), axis=1)
-    owner = slot // local
-    order = jnp.arange(row_count, dtype=jnp.int32)
-    before = order[None, :] < order[:, None]
-    place = jnp.sum(((owner[:, None] == owner[None, :]) & before).astype(jnp.int32), axis=1)
     base_value = jnp.dot(tokens, value_weight, preferred_element_type=jnp.float32)
     room = row_count // count
     planes = count // PLANE
-    if count != 16 or room != 16 or (depth + NOTE) % WIDE:
+    if count != 16 or room != 16 or (depth + NOTE) % WIDE or depth % (2 * STEP):
+        slot, owner, place = route(tenant_ids, tenant_slot, local)
         delta = exchange(tokens, slot, owner, place, CAP * local, adapt_down, adapt_up)
         return (base_value + delta).astype(jnp.bfloat16)
 
-    plane = (owner ^ me) // PLANE
-    over = place >= room
-    over_place = jnp.sum(
-        (over[None, :] & (plane[:, None] == plane[None, :]) & before).astype(jnp.int32), axis=1
-    )
     main_rows = count * room
-    left = over & (over_place >= SPARE)
-    at = jnp.where(over, main_rows + plane * SPARE + over_place, owner * room + place)
-    at = jnp.where(left, -1, at)[None, :]
-    info = jnp.where(jnp.arange(NOTE)[None, :] == 0, slot[:, None] + 1, 0).astype(jnp.bfloat16)
-    some_left = jnp.max(left.astype(jnp.int32)).reshape(1)
+    *spare, at, note, left = pl.pallas_call(
+        functools.partial(route_body, room, local),
+        in_specs=[SMEM, VMEM, VMEM, ANY],
+        out_specs=[VMEM] * (planes + 3),
+        out_shape=[jax.ShapeDtypeStruct((2 * SPARE, depth // 2 + NOTE), jnp.bfloat16)] * planes
+        + [
+            jax.ShapeDtypeStruct((1, row_count), jnp.int32),
+            jax.ShapeDtypeStruct((NOTE, row_count), jnp.bfloat16),
+            jax.ShapeDtypeStruct((1, NOTE), jnp.int32),
+        ],
+        scratch_shapes=[
+            pltpu.VMEM(tokens.shape, jnp.bfloat16),
+            pltpu.SemaphoreType.DMA((depth // STEP,)),
+        ],
+        compiler_params=pltpu.CompilerParams(vmem_limit_bytes=24 * 2**20),
+        cost_estimate=pl.CostEstimate(
+            flops=4 * 96 * row_count * depth, bytes_accessed=6 * 2**20, transcendentals=0
+        ),
+    )(me.reshape(1), tenant_ids.reshape(1, row_count), tenant_slot.reshape(1, TENANTS), tokens)
+
+    along = [spare[0]] + [swap(spare[b], b * PLANE) for b in range(1, planes)]
+
     groups = lax.axis_size("grp")
-    seen = some_left
+    along[1], left = lax.optimization_barrier((along[1], left))
+    flag = left
     for g in range(1, groups):
-        other = lax.ppermute(some_left, "grp", [(s, (s + g) % groups) for s in range(groups)])
-        seen = jnp.maximum(seen, other)
-
-    spare = call(
-        functools.partial(pack_over_body, main_rows, planes),
-        [(2 * SPARE, depth // 2 + NOTE)] * planes,
-        (at, info, tokens),
-        [VMEM, VMEM, pl.BlockSpec(memory_space=pl.ANY)],
-        2 * 96 * row_count * depth,
-        6 * 2**20,
-        [pltpu.VMEM(tokens.shape, jnp.bfloat16), pltpu.SemaphoreType.DMA((depth // STEP,))],
-    )
-    blocks = pack(main_rows, seen, at, info, tokens)
-
-    first = (me * local).reshape(1)
-    down = adapt_down.transpose(0, 2, 1).reshape(local * rank, depth)
-    up = adapt_up.reshape(local * rank, width)
-
-    along = jnp.concatenate(
-        [spare[0]] + [swap(spare[b], b * PLANE) for b in range(1, planes)], axis=0
-    )
+        other = lax.ppermute(left, "grp", [(s, (s + g) % groups) for s in range(groups)])
+        flag = jnp.maximum(flag, other)
+    blocks = pack(main_rows, flag, at, note, tokens)
+
+    along = jnp.concatenate(along, axis=0)
     along, blocks, base_value = lax.optimization_barrier((along, blocks, base_value))
     shared = [along] + [swap(along, a) for a in range(1, PLANE)]
+
     blocks, shared[1] = lax.optimization_barrier((blocks, shared[1]))
     got = lax.all_to_all(
         blocks.reshape(count, room, depth + NOTE), "ad", split_axis=0, concat_axis=0, tiled=True
     ).reshape(main_rows, depth + NOTE)
 
+    first = (me * local).reshape(1)
+    down = adapt_down.transpose(0, 2, 1).reshape(local * rank, depth)
+    up = adapt_up.reshape(local * rank, width)
+
     over_delta = call(
         functools.partial(adapt_over_body, planes, rank),
         [(16 * planes, width)] * PLANE,
         (first, down, up, *shared),
-        [SMEM] + [VMEM] * 6,
+        [SMEM, ANY] + [VMEM] * 5,
         4 * 10**14,
         6 * 2**20,
+        [pltpu.VMEM(down.shape, jnp.bfloat16), pltpu.SemaphoreType.DMA((depth // STEP,))],
     )
     over_sum = over_delta[0]
     for a in range(1, PLANE):
@@ -325,6 +391,7 @@
     for b in range(1, planes):
         over_back.append(swap(over_sum[16 * b : 16 * (b + 1)], b * PLANE))
 
+    got, *over_back = lax.optimization_barrier((got, *over_back))
     delta, flags = adapt(rank, first, down, up, got)
     back = lax.all_to_all(
         delta.reshape(count, room, width), "ad", split_axis=0, concat_axis=0, tiled=True
@@ -341,11 +408,12 @@
         )[0]
 
     def more():
+        slot, owner, place = route(tenant_ids, tenant_slot, local)
         extra = exchange(
             tokens,
             slot,
             owner,
-            jnp.where(left, place - room, -1),
+            jnp.where(at[0] < 0, place - room, -1),
             CAP * local - room,
             adapt_down,
             adapt_up,

time: 156 us -> 158 us (1.013)
  waiting for transfers between devices: 79 us -> 99.6 us
  starting transfers between devices: 42.9 us -> 29 us
  other arithmetic: 3.45 us -> 0.59 us
  between operations: 2.39 us -> 0.73 us
    ppermute x12, waiting for transfers between devices: 58.4 us -> 90.7 us  [swap(): return lax.ppermute(x, 'ad', [(s, s ^ k) for s in range(count)])]
    all_to_all x1, waiting for transfers between devices: 20.6 us -> 0.01 us  [on_device(): lax.all_to_all(blocks.reshape(count, room, depth + NOTE), 'ad', split_axi...]
    all_to_all x1, starting transfers between devices: 19.9 us -> 3.61 us  [on_device(): lax.all_to_all(delta.reshape(count, room, width), 'ad', split_axis=0, con...]
    all_to_all x1, waiting for transfers between devices: 0.01 us -> 8.88 us  [on_device(): lax.all_to_all(delta.reshape(count, room, width), 'ad', split_axis=0, con...]
    ppermute x12, starting transfers between devices: 13.5 us -> 16.7 us  [swap(): return lax.ppermute(x, 'ad', [(s, s ^ k) for s in range(count)])]
    pallas_call x3 -> x2, Pallas kernels: 7.07 us -> 4.27 us  [call(): pl.pallas_call(body, in_specs=specs, out_specs=[VMEM] * len(outs), out_sh...]
    pallas_call x1 -> x2, Pallas kernels: 7.19 us -> 9.39 us  [the longest x1 5.55 us: adapt(): pl.pallas_call(functools.partial(adapt_body, rank), in_specs=[SMEM, ANY,...]
  transfers between devices with their start and end apart: 15 -> 15, of which waited for: 7 -> 9; matrix products, arithmetic and copies ran while one was open for 5% -> 5% of each run, Pallas kernels for 12% -> 3%
where the time goes in v5:
time: 158 us; the launch traced here: 157 us
  waiting for transfers between devices  99.6 us (63%)
  starting transfers between devices  29 us (18%)
  Pallas kernels  18.9 us (12%)
  matrix products  6.55 us (4%)
  local copies, waits for them, and re-layouts  1.95 us (1%)
    ppermute x12, waiting for transfers between devices, swap(): return lax.ppermute(x, 'ad', [(s, s ^ k) for s in range(count)])  90.7 us
    ppermute x12, starting transfers between devices, swap(): return lax.ppermute(x, 'ad', [(s, s ^ k) for s in range(count)])  16.7 us
    all_to_all x1, waiting for transfers between devices, on_device(): lax.all_to_all(delta.reshape(count, room, width), 'ad', split_axis=0, con...  8.88 us
    all_to_all x1, starting transfers between devices, on_device(): lax.all_to_all(blocks.reshape(count, room, depth + NOTE), 'ad', split_axi...  7.01 us
    dot_general x1, matrix products, on_device(): jnp.dot(tokens, value_weight, preferred_element_type=jnp.float32)  6.55 us
    pallas_call x1, Pallas kernels, adapt(): pl.pallas_call(functools.partial(adapt_body, rank), in_specs=[SMEM, ANY,...  5.55 us
    pallas_call x1, Pallas kernels, pack(): pl.pallas_call(functools.partial(pack_body, WIDE - NOTE), grid=(steps,),...  5.19 us
    pallas_call x2, Pallas kernels, call(): pl.pallas_call(body, in_specs=specs, out_specs=[VMEM] * len(outs), out_sh...  4.27 us
  transfers between devices with their start and end apart: 15, of which 9 were waited for; matrix products, arithmetic and copies ran while one was open for 5% of the time, Pallas kernels for 3%

profile of v5, /device:TPU:0, one launch (start us, length us, event | category | flops | bytes accessed | tf_op | source)
XLA Modules:
  0.0 157.3 jit_solution(4182556097137506170)
XLA Ops:
  0.0 3.8 %shard_map.66 = (bf16[24,4224]{1,0:T(8,128)(2,1)S(1)}, bf16[24,4224]{1,0:T(8,128)(2,1)S(1)}, bf16[24,4224]{1,0:T(8,128)(2,1)S(1)}, bf16[24,4224]{1,0:T(8,128)(2,...) custom-call(s32[1]{0:T(128)} %bitcast.16.me_ref, s32[1,256]{1,0:T(1,128)} %bitcast.52, ...), custom_call_target="tpu_custom_call" | custom-call | flops 805306368 | bytes 6291456 | tf_op jit(solution)/shard_map/pallas_call | solution.py:335
  4.5 3.0 %collective-permute-start = (bf16[24,4224]{1,0:T(8,128)(2,1)S(1)}, bf16[24,4224]{1,0:T(8,128)(2,1)S(1)}, u32[]{:S(2)}, u32[]{:S(2)}) collective-permute-start(bf16[24,4224]{1,0:T(8,128)(2,1)S(1)} %get-tuple-element.91), channel_id=1, source_target_pairs={{0,4},{1,5},{2,6},{3,7},{4,0},{5,1},{6,2},{7,3},{8,12},{9,13},{10,... | collective-permute-start | bytes 608264 | tf_op jit(solution)/shard_map/ppermute | solution.py:306
  7.5 2.6 %collective-permute-start.1 = (bf16[24,4224]{1,0:T(8,128)(2,1)S(1)}, bf16[24,4224]{1,0:T(8,128)(2,1)S(1)}, u32[]{:S(2)}, u32[]{:S(2)}) collective-permute-start(bf16[24,4224]{1,0:T(8,128)(2,1)S(1)} %get-tuple-element.94), channel_id=1, source_target_pairs={{0,8},{1,9},{2,10},{3,11},{4,12},{5,13},{6,14},{7,15},{8,0},{9,1},... | collective-permute-start | bytes 608264 | tf_op jit(solution)/shard_map/ppermute | solution.py:306
  10.1 6.6 %fusion.9 = f32[256,512]{1,0:T(8,128)} fusion(bf16[256,8192]{1,0:T(8,128)(2,1)S(1)} %copy-done.1, bf16[8192,512]{1,0:T(8,128)(2,1)} %param.9), kind=kOutput, calls=%fused_computation.36 | convolution fusion | flops 2147483648 | bytes 13107200 | tf_op jit(solution)/shard_map/dot_general | solution.py:326
  16.7 1.7 %collective-permute-start.3 = (s32[1,128]{1,0:T(1,128)S(1)}, s32[1,128]{1,0:T(1,128)S(1)}, u32[]{:S(2)}, u32[]{:S(2)}) collective-permute-start(s32[1,128]{1,0:T(1,128)S(1)} %get-tuple-element.96), channel_id=1, source_target_pairs={{0,16},{16,0},{1,17},{17,1},{2,18},{18,2},{3,19},{19,3},{4,20},{20... | collective-permute-start | bytes 1544 | tf_op jit(solution)/shard_map/ppermute | solution.py:361
  18.4 6.7 %collective-permute-done.1 = bf16[24,4224]{1,0:T(8,128)(2,1)S(1)} collective-permute-done((bf16[24,4224]{1,0:T(8,128)(2,1)S(1)}, bf16[24,4224]{1,0:T(8,128)(2,1)S(1)}, u32[]{:S(2)}, u32[]{:S(2)}) %collective-permute-start.1) | collective-permute-done | bytes 202784 | tf_op jit(solution)/shard_map/ppermute | solution.py:306
  25.7 5.2 %shard_map.67 = bf16[256,8320]{1,0:T(8,128)(2,1)} custom-call(s32[1,128]{1,0:T(1,128)} %max.3.flag_ref, s32[1,256]{1,0:T(1,128)S(1)} %get-tuple-element.97.at_ref, bf16[128,256]{1,0:T(8,128)(2,1)} %copy-done, bf16[256,8192]{1,0:T(8,128)(2,1)S(1)} %copy-done.1), custom_call_target="tpu_custom_call" | custom-call | flops 1073741824 | bytes 8388608 | tf_op jit(solution)/shard_map/pallas_call | solution.py:155
  30.9 1.5 collective-permute-start.5
  33.2 7.0 %all-to-all-start.3 = ((bf16[16,16,8320]{2,1,0:T(8,128)(2,1)}), bf16[16,16,8320]{2,1,0:T(8,128)(2,1)}, u32[]{:S(2)}, u32[]{:S(2)}) async-start(bf16[16,16,8320]{2,1,0:T(8,128)(2,1)} %bitcast.36), calls=%async_computation.3 | async-start | bytes 8519680 | tf_op jit(solution)/shard_map/all_to_all | solution.py:370
  40.2 18.3 %collective-permute-done.5.refs_2_ = bf16[96,4224]{1,0:T(8,128)(2,1)S(1)} collective-permute-done((bf16[96,4224]{1,0:T(8,128)(2,1)S(1)}, bf16[96,4224]{1,0:T(8,128)(2,1)S(1)}, u32[]{:S(2)}, u32[]{:S(2)}) %collective-permute-start.5) | collective-permute-done | bytes 811040 | tf_op jit(solution)/shard_map/ppermute | solution.py:306
  58.5 32.7 %collective-permute-done.6.refs_3_ = bf16[96,4224]{1,0:T(8,128)(2,1)S(1)} collective-permute-done((bf16[96,4224]{1,0:T(8,128)(2,1)S(1)}, bf16[96,4224]{1,0:T(8,128)(2,1)S(1)}, u32[]{:S(2)}, u32[]{:S(2)}) %collective-permute-start.6) | collective-permute-done | bytes 811040 | tf_op jit(solution)/shard_map/ppermute | solution.py:306
  91.2 3.9 %shard_map.68 = (bf16[64,512]{1,0:T(8,128)(2,1)S(1)}, bf16[64,512]{1,0:T(8,128)(2,1)S(1)}, bf16[64,512]{1,0:T(8,128)(2,1)S(1)}, bf16[64,512]{1,0:T(8,128)(2,1)S(1)}) custom-call(s32[1]{0:T(128)} %bitcast.12.first_ref, bf16[256,8192]{1,0:T(8,128)(2,1)} %bitcast.38, bf16[256,512]{1,0:T(8,128)(2,1)S(1)} %bitcast.44, ...), custom_call_target="tpu_custom_call" | custom-call | flops 400000001507328 | bytes 6291456 | tf_op jit(solution)/shard_map/pallas_call | solution.py:293
  95.1 1.1 collective-permute-start.7
  96.2 1.5 collective-permute-start.8
  97.7 11.8 %collective-permute-done.8 = bf16[64,512]{1,0:T(8,128)(2,1)S(1)} collective-permute-done((bf16[64,512]{1,0:T(8,128)(2,1)S(1)}, bf16[64,512]{1,0:T(8,128)(2,1)S(1)}, u32[]{:S(2)}, u32[]{:S(2)}) %collective-permute-start.8) | collective-permute-done | bytes 65568 | tf_op jit(solution)/shard_map/ppermute | solution.py:306
  109.5 1.0 collective-permute-done.9
  110.6 4.1 %collective-permute-start.10 = (bf16[16,512]{1,0:T(8,128)(2,1)S(1)}, bf16[16,512]{1,0:T(8,128)(2,1)S(1)}, u32[]{:S(2)}, u32[]{:S(2)}) collective-permute-start(bf16[16,512]{1,0:T(8,128)(2,1)S(1)} %get-tuple-element.120), channel_id=1, source_target_pairs={{0,4},{1,5},{2,6},{3,7},{4,0},{5,1},{6,2},{7,3},{8,12},{9,13},{10,... | collective-permute-start | bytes 49160 | tf_op jit(solution)/shard_map/ppermute | solution.py:306
  114.7 1.1 collective-permute-start.11
  115.8 1.4 collective-permute-start.12
  117.2 1.8 %collective-permute-done.10 = bf16[16,512]{1,0:T(8,128)(2,1)S(1)} collective-permute-done((bf16[16,512]{1,0:T(8,128)(2,1)S(1)}, bf16[16,512]{1,0:T(8,128)(2,1)S(1)}, u32[]{:S(2)}, u32[]{:S(2)}) %collective-permute-start.10) | collective-permute-done | bytes 16416 | tf_op jit(solution)/shard_map/ppermute | solution.py:306
  119.0 17.9 %collective-permute-done.11 = bf16[16,512]{1,0:T(8,128)(2,1)S(1)} collective-permute-done((bf16[16,512]{1,0:T(8,128)(2,1)S(1)}, bf16[16,512]{1,0:T(8,128)(2,1)S(1)}, u32[]{:S(2)}, u32[]{:S(2)}) %collective-permute-start.11) | collective-permute-done | bytes 16416 | tf_op jit(solution)/shard_map/ppermute | solution.py:306
  137.0 5.5 %shard_map.69 = (bf16[256,512]{1,0:T(8,128)(2,1)}, bf16[16,128]{1,0:T(8,128)(2,1)S(1)}) custom-call(s32[1]{0:T(128)} %bitcast.12.first_ref, bf16[256,8192]{1,0:T(8,128)(2,1)} %bitcast.39, bf16[256,512]{1,0:T(8,128)(2,1)S(1)} %bitcast.45, bf16[256,8320]{1,0:T(8,128)(2,1)} %bitcast.20.rows_hbm), custom_call_target="tpu_custom_call" | custom-call | flops 1073741824 | bytes 8388608 | tf_op jit(solution)/shard_map/pallas_call | solution.py:214
  142.5 3.6 %all-to-all-start.4 = ((bf16[16,16,512]{2,1,0:T(8,128)(2,1)}), bf16[16,16,512]{2,1,0:T(8,128)(2,1)S(1)}, u32[]{:S(2)}, u32[]{:S(2)}) async-start(bf16[16,16,512]{2,1,0:T(8,128)(2,1)} %bitcast.23), calls=%async_computation.4 | async-start | bytes 524288 | tf_op jit(solution)/shard_map/all_to_all | solution.py:396
  147.3 8.9 %all-to-all-done.4 = bf16[16,16,512]{2,1,0:T(8,128)(2,1)S(1)} async-done(((bf16[16,16,512]{2,1,0:T(8,128)(2,1)}), bf16[16,16,512]{2,1,0:T(8,128)(2,1)S(1)}, u32[]{:S(2)}, u32[]{:S(2)}) %all-to-all-start.4) | async-done | bytes 262176 | tf_op jit(solution)/shard_map/all_to_all | solution.py:396
  (36 shorter events, 4.0 us)
Async XLA Ops:
  0.0 10.1 %copy-start.1 = (bf16[256,8192]{1,0:T(8,128)(2,1)S(1)}, bf16[256,8192]{1,0:T(8,128)(2,1)}, u32[]{:S(2)}) copy-start(bf16[256,8192]{1,0:T(8,128)(2,1)} %tokens_ref.1) | copy-start | bytes 12582916
  3.9 0.6 copy-start
  4.5 21.2 %copy-start.5 = (s32[1,256]{1,0:T(1,128)}, s32[1,256]{1,0:T(1,128)S(1)}, u32[]{:S(2)}) copy-start(s32[1,256]{1,0:T(1,128)S(1)} %get-tuple-element.97.at_ref) | copy-start | bytes 3076
  4.5 12.2 %collective-permute-start = (bf16[24,4224]{1,0:T(8,128)(2,1)S(1)}, bf16[24,4224]{1,0:T(8,128)(2,1)S(1)}, u32[]{:S(2)}, u32[]{:S(2)}) collective-permute-start(bf16[24,4224]{1,0:T(8,128)(2,1)S(1)} %get-tuple-element.91), channel_id=1, source_target_pairs={{0,4},{1,5},{2,6},{3,7},{4,0},{5,1},{6,2},{7,3},{8,12},{9,13},{10,... | collective-permute-start | bytes 608264 | tf_op jit(solution)/shard_map/ppermute | solution.py:306
  7.5 17.5 %collective-permute-start.1 = (bf16[24,4224]{1,0:T(8,128)(2,1)S(1)}, bf16[24,4224]{1,0:T(8,128)(2,1)S(1)}, u32[]{:S(2)}, u32[]{:S(2)}) collective-permute-start(bf16[24,4224]{1,0:T(8,128)(2,1)S(1)} %get-tuple-element.94), channel_id=1, source_target_pairs={{0,8},{1,9},{2,10},{3,11},{4,12},{5,13},{6,14},{7,15},{8,0},{9,1},... | collective-permute-start | bytes 608264 | tf_op jit(solution)/shard_map/ppermute | solution.py:306
  10.1 15.0 %collective-permute-start.2 = (bf16[24,4224]{1,0:T(8,128)(2,1)S(1)}, bf16[24,4224]{1,0:T(8,128)(2,1)S(1)}, u32[]{:S(2)}, u32[]{:S(2)}) collective-permute-start(bf16[24,4224]{1,0:T(8,128)(2,1)S(1)} %get-tuple-element.95), channel_id=1, source_target_pairs={{0,12},{1,13},{2,14},{3,15},{4,8},{5,9},{6,10},{7,11},{8,4},{9,5},... | collective-permute-start | bytes 608264 | tf_op jit(solution)/shard_map/ppermute | solution.py:306
  16.7 8.5 %collective-permute-start.3 = (s32[1,128]{1,0:T(1,128)S(1)}, s32[1,128]{1,0:T(1,128)S(1)}, u32[]{:S(2)}, u32[]{:S(2)}) collective-permute-start(s32[1,128]{1,0:T(1,128)S(1)} %get-tuple-element.96), channel_id=1, source_target_pairs={{0,16},{16,0},{1,17},{17,1},{2,18},{18,2},{3,19},{19,3},{4,20},{20... | collective-permute-start | bytes 1544 | tf_op jit(solution)/shard_map/ppermute | solution.py:361
  30.9 2.3 %collective-permute-start.4 = (bf16[96,4224]{1,0:T(8,128)(2,1)S(1)}, bf16[96,4224]{1,0:T(8,128)(2,1)S(1)}, u32[]{:S(2)}, u32[]{:S(2)}) collective-permute-start(bf16[96,4224]{1,0:T(8,128)(2,1)S(1)} %pad_maximum_fusion.refs_0_), channel_id=1, source_target_pairs={{0,1},{1,0},{2,3},{3,2},{4,5},{5,4},{6,7},{7,6},{8,9},{9,8},{10,11... | collective-permute-start | bytes 2433032 | tf_op jit(solution)/shard_map/ppermute | solution.py:306
  30.9 27.6 %collective-permute-start.5 = (bf16[96,4224]{1,0:T(8,128)(2,1)S(1)}, bf16[96,4224]{1,0:T(8,128)(2,1)S(1)}, u32[]{:S(2)}, u32[]{:S(2)}) collective-permute-start(bf16[96,4224]{1,0:T(8,128)(2,1)S(1)} %pad_maximum_fusion.refs_0_), channel_id=1, source_target_pairs={{0,2},{1,3},{2,0},{3,1},{4,6},{5,7},{6,4},{7,5},{8,10},{9,11},{10,... | collective-permute-start | bytes 2433032 | tf_op jit(solution)/shard_map/ppermute | solution.py:306
  32.4 58.8 %collective-permute-start.6 = (bf16[96,4224]{1,0:T(8,128)(2,1)S(1)}, bf16[96,4224]{1,0:T(8,128)(2,1)S(1)}, u32[]{:S(2)}, u32[]{:S(2)}) collective-permute-start(bf16[96,4224]{1,0:T(8,128)(2,1)S(1)} %pad_maximum_fusion.refs_0_), channel_id=1, source_target_pairs={{0,3},{1,2},{2,1},{3,0},{4,7},{5,6},{6,5},{7,4},{8,11},{9,10},{10,... | collective-permute-start | bytes 2433032 | tf_op jit(solution)/shard_map/ppermute | solution.py:306
  33.2 58.0 %copy-start.3 = (bf16[16,16,512]{2,1,0:T(8,128)(2,1)S(1)}, bf16[16,16,512]{2,1,0:T(8,128)(2,1)}, u32[]{:S(2)}) copy-start(bf16[16,16,512]{2,1,0:T(8,128)(2,1)} %param.11) | copy-start | bytes 786436
  33.2 103.8 %all-to-all-start.3 = ((bf16[16,16,8320]{2,1,0:T(8,128)(2,1)}), bf16[16,16,8320]{2,1,0:T(8,128)(2,1)}, u32[]{:S(2)}, u32[]{:S(2)}) async-start(bf16[16,16,8320]{2,1,0:T(8,128)(2,1)} %bitcast.36), calls=%async_computation.3 | async-start | bytes 8519680 | tf_op jit(solution)/shard_map/all_to_all | solution.py:370
  95.1 2.6 %collective-permute-start.7 = (bf16[64,512]{1,0:T(8,128)(2,1)S(1)}, bf16[64,512]{1,0:T(8,128)(2,1)S(1)}, u32[]{:S(2)}, u32[]{:S(2)}) collective-permute-start(bf16[64,512]{1,0:T(8,128)(2,1)S(1)} %get-tuple-element.104), channel_id=1, source_target_pairs={{0,1},{1,0},{2,3},{3,2},{4,5},{5,4},{6,7},{7,6},{8,9},{9,8},{10,11... | collective-permute-start | bytes 196616 | tf_op jit(solution)/shard_map/ppermute | solution.py:306
  96.2 13.3 %collective-permute-start.8 = (bf16[64,512]{1,0:T(8,128)(2,1)S(1)}, bf16[64,512]{1,0:T(8,128)(2,1)S(1)}, u32[]{:S(2)}, u32[]{:S(2)}) collective-permute-start(bf16[64,512]{1,0:T(8,128)(2,1)S(1)} %get-tuple-element.105), channel_id=1, source_target_pairs={{0,2},{1,3},{2,0},{3,1},{4,6},{5,7},{6,4},{7,5},{8,10},{9,11},{10,... | collective-permute-start | bytes 196616 | tf_op jit(solution)/shard_map/ppermute | solution.py:306
  97.7 12.8 %collective-permute-start.9 = (bf16[64,512]{1,0:T(8,128)(2,1)S(1)}, bf16[64,512]{1,0:T(8,128)(2,1)S(1)}, u32[]{:S(2)}, u32[]{:S(2)}) collective-permute-start(bf16[64,512]{1,0:T(8,128)(2,1)S(1)} %get-tuple-element.106), channel_id=1, source_target_pairs={{0,3},{1,2},{2,1},{3,0},{4,7},{5,6},{6,5},{7,4},{8,11},{9,10},{10,... | collective-permute-start | bytes 196616 | tf_op jit(solution)/shard_map/ppermute | solution.py:306
  110.5 45.7 %copy-start.2 = (f32[256,512]{1,0:T(8,128)S(1)}, f32[256,512]{1,0:T(8,128)}, u32[]{:S(2)}) copy-start(f32[256,512]{1,0:T(8,128)} %fusion.9) | copy-start | bytes 1572868
  110.5 45.7 %copy-start.6 = (s32[1,256]{1,0:T(1,128)S(1)}, s32[1,256]{1,0:T(1,128)}, u32[]{:S(2)}) copy-start(s32[1,256]{1,0:T(1,128)} %copy-done.5) | copy-start | bytes 3076
  110.6 45.7 %copy-start.7 = (s32[256,1]{0,1:T(1,128)S(1)}, s32[256,1]{0,1:T(1,128)}, u32[]{:S(2)}) copy-start(s32[256,1]{0,1:T(1,128)} %param.12) | copy-start | bytes 3076
  110.6 45.6 %copy-start.8 = (s32[256]{0:T(256)S(1)}, s32[256]{0:T(256)}, u32[]{:S(2)}) copy-start(s32[256]{0:T(256)} %param.13) | copy-start | bytes 3076
  110.6 8.4 %collective-permute-start.10 = (bf16[16,512]{1,0:T(8,128)(2,1)S(1)}, bf16[16,512]{1,0:T(8,128)(2,1)S(1)}, u32[]{:S(2)}, u32[]{:S(2)}) collective-permute-start(bf16[16,512]{1,0:T(8,128)(2,1)S(1)} %get-tuple-element.120), channel_id=1, source_target_pairs={{0,4},{1,5},{2,6},{3,7},{4,0},{5,1},{6,2},{7,3},{8,12},{9,13},{10,... | collective-permute-start | bytes 49160 | tf_op jit(solution)/shard_map/ppermute | solution.py:306
  114.7 22.3 %collective-permute-start.11 = (bf16[16,512]{1,0:T(8,128)(2,1)S(1)}, bf16[16,512]{1,0:T(8,128)(2,1)S(1)}, u32[]{:S(2)}, u32[]{:S(2)}) collective-permute-start(bf16[16,512]{1,0:T(8,128)(2,1)S(1)} %get-tuple-element.119), channel_id=1, source_target_pairs={{0,8},{1,9},{2,10},{3,11},{4,12},{5,13},{6,14},{7,15},{8,0},{9,1},... | collective-permute-start | bytes 49160 | tf_op jit(solution)/shard_map/ppermute | solution.py:306
  115.8 21.2 %collective-permute-start.12 = (bf16[16,512]{1,0:T(8,128)(2,1)S(1)}, bf16[16,512]{1,0:T(8,128)(2,1)S(1)}, u32[]{:S(2)}, u32[]{:S(2)}) collective-permute-start(bf16[16,512]{1,0:T(8,128)(2,1)S(1)} %get-tuple-element.118), channel_id=1, source_target_pairs={{0,12},{1,13},{2,14},{3,15},{4,8},{5,9},{6,10},{7,11},{8,4},{9,5},... | collective-permute-start | bytes 49160 | tf_op jit(solution)/shard_map/ppermute | solution.py:306
  142.5 13.7 %all-to-all-start.4 = ((bf16[16,16,512]{2,1,0:T(8,128)(2,1)}), bf16[16,16,512]{2,1,0:T(8,128)(2,1)S(1)}, u32[]{:S(2)}, u32[]{:S(2)}) async-start(bf16[16,16,512]{2,1,0:T(8,128)(2,1)} %bitcast.23), calls=%async_computation.4 | async-start | bytes 524288 | tf_op jit(solution)/shard_map/all_to_all | solution.py:396
  156.6 0.7 copy-start.4

commit v6 on v5

--- a/solution.py
+++ b/solution.py
@@ -354,19 +354,11 @@
 
     along = [spare[0]] + [swap(spare[b], b * PLANE) for b in range(1, planes)]
 
-    groups = lax.axis_size("grp")
-    along[1], left = lax.optimization_barrier((along[1], left))
-    flag = left
-    for g in range(1, groups):
-        other = lax.ppermute(left, "grp", [(s, (s + g) % groups) for s in range(groups)])
-        flag = jnp.maximum(flag, other)
-    blocks = pack(main_rows, flag, at, note, tokens)
+    blocks = pack(main_rows, left, at, note, tokens)
 
     along = jnp.concatenate(along, axis=0)
-    along, blocks, base_value = lax.optimization_barrier((along, blocks, base_value))
     shared = [along] + [swap(along, a) for a in range(1, PLANE)]
 
-    blocks, shared[1] = lax.optimization_barrier((blocks, shared[1]))
     got = lax.all_to_all(
         blocks.reshape(count, room, depth + NOTE), "ad", split_axis=0, concat_axis=0, tiled=True
     ).reshape(main_rows, depth + NOTE)
@@ -380,10 +372,11 @@
         [(16 * planes, width)] * PLANE,
         (first, down, up, *shared),
         [SMEM, ANY] + [VMEM] * 5,
-        4 * 10**14,
+        10**12,
         6 * 2**20,
         [pltpu.VMEM(down.shape, jnp.bfloat16), pltpu.SemaphoreType.DMA((depth // STEP,))],
     )
+    got, base_value, *over_delta = lax.optimization_barrier((got, base_value, *over_delta))
     over_sum = over_delta[0]
     for a in range(1, PLANE):
         over_sum = over_sum + swap(over_delta[a], a)
@@ -391,11 +384,17 @@
     for b in range(1, planes):
         over_back.append(swap(over_sum[16 * b : 16 * (b + 1)], b * PLANE))
 
-    got, *over_back = lax.optimization_barrier((got, *over_back))
     delta, flags = adapt(rank, first, down, up, got)
     back = lax.all_to_all(
         delta.reshape(count, room, width), "ad", split_axis=0, concat_axis=0, tiled=True
     ).reshape(main_rows, width)
+
+    groups = lax.axis_size("grp")
+    own = flags[0, 1].astype(jnp.int32)
+    seen = own
+    for g in range(1, groups):
+        other = lax.ppermute(own, "grp", [(s, (s + g) % groups) for s in range(groups)])
+        seen = jnp.maximum(seen, other)
 
     def finish(base):
         return call(
@@ -420,7 +419,7 @@
         )
         return finish(base_value + extra)
 
-    return lax.cond(flags[0, 1] > 0, more, lambda: finish(base_value))
+    return lax.cond(seen > 0, more, lambda: finish(base_value))
 
 
 def solution(mesh):

time: 158 us -> 145 us (0.918)
  waiting for transfers between devices: 99.6 us -> 74.7 us
  starting transfers between devices: 29 us -> 40.2 us
    ppermute x12, waiting for transfers between devices: 90.7 us -> 73.8 us  [swap(): return lax.ppermute(x, 'ad', [(s, s ^ k) for s in range(count)])]
    all_to_all x1, starting transfers between devices: 3.61 us -> 15.7 us  [on_device(): lax.all_to_all(delta.reshape(count, room, width), 'ad', split_axis=0, con...]
    all_to_all x1, waiting for transfers between devices: 8.88 us -> 0.01 us  [on_device(): lax.all_to_all(delta.reshape(count, room, width), 'ad', split_axis=0, con...]
  transfers between devices with their start and end apart: 15 -> 15, of which waited for: 9 -> 5; matrix products, arithmetic and copies ran while one was open for 5% -> 6% of each run, Pallas kernels for 3% -> 9%
where the time goes in v6:
time: 145 us
  waiting for transfers between devices  74.7 us (52%)
  starting transfers between devices  40.2 us (28%)
  Pallas kernels  17.8 us (12%)
  matrix products  7.81 us (5%)
  local copies, waits for them, and re-layouts  2.63 us (2%)
  between operations  1.53 us (1%)
    ppermute x12, waiting for transfers between devices, swap(): return lax.ppermute(x, 'ad', [(s, s ^ k) for s in range(count)])  73.8 us
    all_to_all x1, starting transfers between devices, on_device(): lax.all_to_all(delta.reshape(count, room, width), 'ad', split_axis=0, con...  15.7 us
    ppermute x12, starting transfers between devices, swap(): return lax.ppermute(x, 'ad', [(s, s ^ k) for s in range(count)])  15.5 us
    dot_general x1, matrix products, on_device(): jnp.dot(tokens, value_weight, preferred_element_type=jnp.float32)  7.81 us
    all_to_all x1, starting transfers between devices, on_device(): lax.all_to_all(blocks.reshape(count, room, depth + NOTE), 'ad', split_axi...  6.18 us
    pallas_call x1, Pallas kernels, adapt(): pl.pallas_call(functools.partial(adapt_body, rank), in_specs=[SMEM, ANY,...  5.55 us
    pallas_call x1, Pallas kernels, pack(): pl.pallas_call(functools.partial(pack_body, WIDE - NOTE), grid=(steps,),...  5.29 us
    pallas_call x1, Pallas kernels, on_device(): pl.pallas_call(functools.partial(route_body, room, local), in_specs=[SMEM...  3.84 us
  transfers between devices with their start and end apart: 15, of which 5 were waited for; matrix products, arithmetic and copies ran while one was open for 6% of the time, Pallas kernels for 9%

profile of v6, /device:TPU:0, one launch (start us, length us, event | category | flops | bytes accessed | tf_op | source)
XLA Modules:
  0.0 144.8 jit_solution(706420680701459445)
XLA Ops:
  0.0 3.8 %shard_map.66 = (bf16[24,4224]{1,0:T(8,128)(2,1)S(1)}, bf16[24,4224]{1,0:T(8,128)(2,1)S(1)}, bf16[24,4224]{1,0:T(8,128)(2,1)S(1)}, bf16[24,4224]{1,0:T(8,128)(2,...) custom-call(s32[1]{0:T(128)} %bitcast.16.me_ref, s32[1,256]{1,0:T(1,128)} %bitcast.53, ...), custom_call_target="tpu_custom_call" | custom-call | flops 805306368 | bytes 6291456 | tf_op jit(solution)/shard_map/pallas_call | solution.py:335
  3.9 0.6 copy-done
  4.5 0.6 copy-done.1
  5.1 3.0 %collective-permute-start = (bf16[24,4224]{1,0:T(8,128)(2,1)S(1)}, bf16[24,4224]{1,0:T(8,128)(2,1)S(1)}, u32[]{:S(2)}, u32[]{:S(2)}) collective-permute-start(bf16[24,4224]{1,0:T(8,128)(2,1)S(1)} %get-tuple-element.88), channel_id=1, source_target_pairs={{0,4},{1,5},{2,6},{3,7},{4,0},{5,1},{6,2},{7,3},{8,12},{9,13},{10,... | collective-permute-start | bytes 608264 | tf_op jit(solution)/shard_map/ppermute | solution.py:306
  8.1 2.6 %collective-permute-start.1 = (bf16[24,4224]{1,0:T(8,128)(2,1)S(1)}, bf16[24,4224]{1,0:T(8,128)(2,1)S(1)}, u32[]{:S(2)}, u32[]{:S(2)}) collective-permute-start(bf16[24,4224]{1,0:T(8,128)(2,1)S(1)} %get-tuple-element.89), channel_id=1, source_target_pairs={{0,8},{1,9},{2,10},{3,11},{4,12},{5,13},{6,14},{7,15},{8,0},{9,1},... | collective-permute-start | bytes 608264 | tf_op jit(solution)/shard_map/ppermute | solution.py:306
  10.7 5.3 %shard_map.67 = bf16[256,8320]{1,0:T(8,128)(2,1)} custom-call(s32[1,128]{1,0:T(1,128)} %copy-done.1, s32[1,256]{1,0:T(1,128)S(1)} %get-tuple-element.85.at_ref, bf16[128,256]{1,0:T(8,128)(2,1)} %copy-done, bf16[256,8192]{1,0:T(8,128)(2,1)S(1)} %copy-done.2), custom_call_target="tpu_custom_call" | custom-call | flops 1073741824 | bytes 8388608 | tf_op jit(solution)/shard_map/pallas_call | solution.py:155
  16.0 6.2 %all-to-all-start.3 = ((bf16[16,16,8320]{2,1,0:T(8,128)(2,1)}), bf16[16,16,8320]{2,1,0:T(8,128)(2,1)}, u32[]{:S(2)}, u32[]{:S(2)}) async-start(bf16[16,16,8320]{2,1,0:T(8,128)(2,1)} %bitcast.37), calls=%async_computation.3 | async-start | bytes 8519680 | tf_op jit(solution)/shard_map/all_to_all | solution.py:362
  22.2 3.4 %collective-permute-done.1 = bf16[24,4224]{1,0:T(8,128)(2,1)S(1)} collective-permute-done((bf16[24,4224]{1,0:T(8,128)(2,1)S(1)}, bf16[24,4224]{1,0:T(8,128)(2,1)S(1)}, u32[]{:S(2)}, u32[]{:S(2)}) %collective-permute-start.1) | collective-permute-done | bytes 202784 | tf_op jit(solution)/shard_map/ppermute | solution.py:306
  25.8 1.6 %collective-permute-start.4 = (bf16[96,4224]{1,0:T(8,128)(2,1)S(1)}, bf16[96,4224]{1,0:T(8,128)(2,1)S(1)}, u32[]{:S(2)}, u32[]{:S(2)}) collective-permute-start(bf16[96,4224]{1,0:T(8,128)(2,1)S(1)} %constant_dynamic-update-slice_fusion.refs_0_), channel_id=1, source_target_pairs={{0,2},{1,3},{2,0},{3,1},{4,6},{5,7},{6,4},{7,5},{8,10},{9,11},{10,... | collective-permute-start | bytes 2433032 | tf_op jit(solution)/shard_map/ppermute | solution.py:306
  27.7 7.8 %fusion.9 = f32[256,512]{1,0:T(8,128)} fusion(bf16[256,8192]{1,0:T(8,128)(2,1)} %tokens_ref.1, bf16[8192,512]{1,0:T(8,128)(2,1)} %param.9), kind=kOutput, calls=%fused_computation.39 | convolution fusion | flops 2147483648 | bytes 13107200 | tf_op jit(solution)/shard_map/dot_general | solution.py:326
  35.5 41.8 %collective-permute-done.4.refs_2_ = bf16[96,4224]{1,0:T(8,128)(2,1)S(1)} collective-permute-done((bf16[96,4224]{1,0:T(8,128)(2,1)S(1)}, bf16[96,4224]{1,0:T(8,128)(2,1)S(1)}, u32[]{:S(2)}, u32[]{:S(2)}) %collective-permute-start.4) | collective-permute-done | bytes 811040 | tf_op jit(solution)/shard_map/ppermute | solution.py:306
  77.3 27.8 %collective-permute-done.5.refs_3_ = bf16[96,4224]{1,0:T(8,128)(2,1)S(1)} collective-permute-done((bf16[96,4224]{1,0:T(8,128)(2,1)S(1)}, bf16[96,4224]{1,0:T(8,128)(2,1)S(1)}, u32[]{:S(2)}, u32[]{:S(2)}) %collective-permute-start.5) | collective-permute-done | bytes 811040 | tf_op jit(solution)/shard_map/ppermute | solution.py:306
  105.1 2.8 %shard_map.68 = (bf16[64,512]{1,0:T(8,128)(2,1)S(1)}, bf16[64,512]{1,0:T(8,128)(2,1)S(1)}, bf16[64,512]{1,0:T(8,128)(2,1)S(1)}, bf16[64,512]{1,0:T(8,128)(2,1)S(1)}) custom-call(s32[1]{0:T(128)} %bitcast.12.first_ref, bf16[256,8192]{1,0:T(8,128)(2,1)S(1)} %bitcast.40, bf16[256,512]{1,0:T(8,128)(2,1)S(1)} %bitcast.45, ...), custom_call_target="tpu_custom_call" | custom-call | flops 999999995904 | bytes 6291456 | tf_op jit(solution)/shard_map/pallas_call | solution.py:293
  108.0 0.4 collective-permute-start.7
  108.4 3.1 %collective-permute-start.8 = (bf16[64,512]{1,0:T(8,128)(2,1)S(1)}, bf16[64,512]{1,0:T(8,128)(2,1)S(1)}, u32[]{:S(2)}, u32[]{:S(2)}) collective-permute-start(bf16[64,512]{1,0:T(8,128)(2,1)S(1)} %get-tuple-element.101), channel_id=1, source_target_pairs={{0,2},{1,3},{2,0},{3,1},{4,6},{5,7},{6,4},{7,5},{8,10},{9,11},{10,... | collective-permute-start | bytes 196616 | tf_op jit(solution)/shard_map/ppermute | solution.py:306
  111.5 5.5 %shard_map.69 = (bf16[256,512]{1,0:T(8,128)(2,1)}, bf16[16,128]{1,0:T(8,128)(2,1)S(1)}) custom-call(s32[1]{0:T(128)} %bitcast.12.first_ref, bf16[256,8192]{1,0:T(8,128)(2,1)} %bitcast.39, bf16[256,512]{1,0:T(8,128)(2,1)S(1)} %bitcast.46, bf16[256,8320]{1,0:T(8,128)(2,1)} %bitcast.20.rows_hbm), custom_call_target="tpu_custom_call" | custom-call | flops 1073741824 | bytes 8388608 | tf_op jit(solution)/shard_map/pallas_call | solution.py:214
  117.1 15.7 %all-to-all-start.4 = ((bf16[16,16,512]{2,1,0:T(8,128)(2,1)}), bf16[16,16,512]{2,1,0:T(8,128)(2,1)S(1)}, u32[]{:S(2)}, u32[]{:S(2)}) async-start(bf16[16,16,512]{2,1,0:T(8,128)(2,1)} %bitcast.24), calls=%async_computation.4 | async-start | bytes 524288 | tf_op jit(solution)/shard_map/all_to_all | solution.py:388
  132.9 2.0 %collective-permute-start.10 = (bf16[16,512]{1,0:T(8,128)(2,1)S(1)}, bf16[16,512]{1,0:T(8,128)(2,1)S(1)}, u32[]{:S(2)}, u32[]{:S(2)}) collective-permute-start(bf16[16,512]{1,0:T(8,128)(2,1)S(1)} %get-tuple-element.108), channel_id=1, source_target_pairs={{0,4},{1,5},{2,6},{3,7},{4,0},{5,1},{6,2},{7,3},{8,12},{9,13},{10,... | collective-permute-start | bytes 49160 | tf_op jit(solution)/shard_map/ppermute | solution.py:306
  134.9 2.4 %collective-permute-start.11 = (bf16[16,512]{1,0:T(8,128)(2,1)S(1)}, bf16[16,512]{1,0:T(8,128)(2,1)S(1)}, u32[]{:S(2)}, u32[]{:S(2)}) collective-permute-start(bf16[16,512]{1,0:T(8,128)(2,1)S(1)} %get-tuple-element.107), channel_id=1, source_target_pairs={{0,8},{1,9},{2,10},{3,11},{4,12},{5,13},{6,14},{7,15},{8,0},{9,1},... | collective-permute-start | bytes 49160 | tf_op jit(solution)/shard_map/ppermute | solution.py:306
  137.3 0.6 slice.15
  138.6 2.9 %collective-permute-start.6 = (s32[]{:T(128)}, s32[]{:T(128)}, u32[]{:S(2)}, u32[]{:S(2)}) collective-permute-start(s32[]{:T(128)} %convert.1), channel_id=1, source_target_pairs={{0,16},{16,0},{1,17},{17,1},{2,18},{18,2},{3,19},{19,3},{4,20},{20... | collective-permute-start | bytes 20 | tf_op jit(solution)/shard_map/ppermute | solution.py:396
  141.4 0.8 collective-permute-done.6
  142.9 0.7 collective-permute-done.11
  144.1 0.7 copy-done.6
  (42 shorter events, 1.3 us)
Async XLA Ops:
  0.0 10.7 %copy-start.2 = (bf16[256,8192]{1,0:T(8,128)(2,1)S(1)}, bf16[256,8192]{1,0:T(8,128)(2,1)}, u32[]{:S(2)}) copy-start(bf16[256,8192]{1,0:T(8,128)(2,1)} %tokens_ref.1) | copy-start | bytes 12582916
  5.1 10.9 %copy-start.7 = (s32[1,256]{1,0:T(1,128)}, s32[1,256]{1,0:T(1,128)S(1)}, u32[]{:S(2)}) copy-start(s32[1,256]{1,0:T(1,128)S(1)} %get-tuple-element.85.at_ref) | copy-start | bytes 3076
  5.1 17.1 %collective-permute-start = (bf16[24,4224]{1,0:T(8,128)(2,1)S(1)}, bf16[24,4224]{1,0:T(8,128)(2,1)S(1)}, u32[]{:S(2)}, u32[]{:S(2)}) collective-permute-start(bf16[24,4224]{1,0:T(8,128)(2,1)S(1)} %get-tuple-element.88), channel_id=1, source_target_pairs={{0,4},{1,5},{2,6},{3,7},{4,0},{5,1},{6,2},{7,3},{8,12},{9,13},{10,... | collective-permute-start | bytes 608264 | tf_op jit(solution)/shard_map/ppermute | solution.py:306
  8.1 17.6 %collective-permute-start.1 = (bf16[24,4224]{1,0:T(8,128)(2,1)S(1)}, bf16[24,4224]{1,0:T(8,128)(2,1)S(1)}, u32[]{:S(2)}, u32[]{:S(2)}) collective-permute-start(bf16[24,4224]{1,0:T(8,128)(2,1)S(1)} %get-tuple-element.89), channel_id=1, source_target_pairs={{0,8},{1,9},{2,10},{3,11},{4,12},{5,13},{6,14},{7,15},{8,0},{9,1},... | collective-permute-start | bytes 608264 | tf_op jit(solution)/shard_map/ppermute | solution.py:306
  10.7 15.0 %collective-permute-start.2 = (bf16[24,4224]{1,0:T(8,128)(2,1)S(1)}, bf16[24,4224]{1,0:T(8,128)(2,1)S(1)}, u32[]{:S(2)}, u32[]{:S(2)}) collective-permute-start(bf16[24,4224]{1,0:T(8,128)(2,1)S(1)} %get-tuple-element.90), channel_id=1, source_target_pairs={{0,12},{1,13},{2,14},{3,15},{4,8},{5,9},{6,10},{7,11},{8,4},{9,5},... | collective-permute-start | bytes 608264 | tf_op jit(solution)/shard_map/ppermute | solution.py:306
  16.0 92.0 %all-to-all-start.3 = ((bf16[16,16,8320]{2,1,0:T(8,128)(2,1)}), bf16[16,16,8320]{2,1,0:T(8,128)(2,1)}, u32[]{:S(2)}, u32[]{:S(2)}) async-start(bf16[16,16,8320]{2,1,0:T(8,128)(2,1)} %bitcast.37), calls=%async_computation.3 | async-start | bytes 8519680 | tf_op jit(solution)/shard_map/all_to_all | solution.py:362
  25.7 79.4 %copy-start.3 = (bf16[16,8192,16]{1,2,0:T(8,128)(2,1)S(1)}, bf16[16,8192,16]{1,2,0:T(8,128)(2,1)}, u32[]{:S(2)}) copy-start(bf16[16,8192,16]{1,2,0:T(8,128)(2,1)} %param.10) | copy-start | bytes 12582916
  25.7 79.4 %copy-start.5 = (bf16[16,16,512]{2,1,0:T(8,128)(2,1)S(1)}, bf16[16,16,512]{2,1,0:T(8,128)(2,1)}, u32[]{:S(2)}) copy-start(bf16[16,16,512]{2,1,0:T(8,128)(2,1)} %param.11) | copy-start | bytes 786436
  25.7 9.8 %collective-permute-start.3 = (bf16[96,4224]{1,0:T(8,128)(2,1)S(1)}, bf16[96,4224]{1,0:T(8,128)(2,1)S(1)}, u32[]{:S(2)}, u32[]{:S(2)}) collective-permute-start(bf16[96,4224]{1,0:T(8,128)(2,1)S(1)} %constant_dynamic-update-slice_fusion.refs_0_), channel_id=1, source_target_pairs={{0,1},{1,0},{2,3},{3,2},{4,5},{5,4},{6,7},{7,6},{8,9},{9,8},{10,11... | collective-permute-start | bytes 2433032 | tf_op jit(solution)/shard_map/ppermute | solution.py:306
  25.8 51.5 %collective-permute-start.4 = (bf16[96,4224]{1,0:T(8,128)(2,1)S(1)}, bf16[96,4224]{1,0:T(8,128)(2,1)S(1)}, u32[]{:S(2)}, u32[]{:S(2)}) collective-permute-start(bf16[96,4224]{1,0:T(8,128)(2,1)S(1)} %constant_dynamic-update-slice_fusion.refs_0_), channel_id=1, source_target_pairs={{0,2},{1,3},{2,0},{3,1},{4,6},{5,7},{6,4},{7,5},{8,10},{9,11},{10,... | collective-permute-start | bytes 2433032 | tf_op jit(solution)/shard_map/ppermute | solution.py:306
  27.4 77.8 %collective-permute-start.5 = (bf16[96,4224]{1,0:T(8,128)(2,1)S(1)}, bf16[96,4224]{1,0:T(8,128)(2,1)S(1)}, u32[]{:S(2)}, u32[]{:S(2)}) collective-permute-start(bf16[96,4224]{1,0:T(8,128)(2,1)S(1)} %constant_dynamic-update-slice_fusion.refs_0_), channel_id=1, source_target_pairs={{0,3},{1,2},{2,1},{3,0},{4,7},{5,6},{6,5},{7,4},{8,11},{9,10},{10,... | collective-permute-start | bytes 2433032 | tf_op jit(solution)/shard_map/ppermute | solution.py:306
  108.0 35.7 %copy-start.4 = (f32[256,512]{1,0:T(8,128)S(1)}, f32[256,512]{1,0:T(8,128)}, u32[]{:S(2)}) copy-start(f32[256,512]{1,0:T(8,128)} %fusion.9) | copy-start | bytes 1572868
  108.0 35.7 %copy-start.8 = (s32[1,256]{1,0:T(1,128)S(1)}, s32[1,256]{1,0:T(1,128)}, u32[]{:S(2)}) copy-start(s32[1,256]{1,0:T(1,128)} %copy-done.7) | copy-start | bytes 3076
  108.0 35.7 %copy-start.9 = (s32[256,1]{0,1:T(1,128)S(1)}, s32[256,1]{0,1:T(1,128)}, u32[]{:S(2)}) copy-start(s32[256,1]{0,1:T(1,128)} %param.12) | copy-start | bytes 3076
  108.0 35.7 %copy-start.10 = (s32[256]{0:T(256)S(1)}, s32[256]{0:T(256)}, u32[]{:S(2)}) copy-start(s32[256]{0:T(256)} %param.13) | copy-start | bytes 3076
  108.0 24.8 %collective-permute-start.7 = (bf16[64,512]{1,0:T(8,128)(2,1)S(1)}, bf16[64,512]{1,0:T(8,128)(2,1)S(1)}, u32[]{:S(2)}, u32[]{:S(2)}) collective-permute-start(bf16[64,512]{1,0:T(8,128)(2,1)S(1)} %get-tuple-element.100), channel_id=1, source_target_pairs={{0,1},{1,0},{2,3},{3,2},{4,5},{5,4},{6,7},{7,6},{8,9},{9,8},{10,11... | collective-permute-start | bytes 196616 | tf_op jit(solution)/shard_map/ppermute | solution.py:306
  108.4 24.4 %collective-permute-start.8 = (bf16[64,512]{1,0:T(8,128)(2,1)S(1)}, bf16[64,512]{1,0:T(8,128)(2,1)S(1)}, u32[]{:S(2)}, u32[]{:S(2)}) collective-permute-start(bf16[64,512]{1,0:T(8,128)(2,1)S(1)} %get-tuple-element.101), channel_id=1, source_target_pairs={{0,2},{1,3},{2,0},{3,1},{4,6},{5,7},{6,4},{7,5},{8,10},{9,11},{10,... | collective-permute-start | bytes 196616 | tf_op jit(solution)/shard_map/ppermute | solution.py:306
  111.5 21.3 %collective-permute-start.9 = (bf16[64,512]{1,0:T(8,128)(2,1)S(1)}, bf16[64,512]{1,0:T(8,128)(2,1)S(1)}, u32[]{:S(2)}, u32[]{:S(2)}) collective-permute-start(bf16[64,512]{1,0:T(8,128)(2,1)S(1)} %get-tuple-element.102), channel_id=1, source_target_pairs={{0,3},{1,2},{2,1},{3,0},{4,7},{5,6},{6,5},{7,4},{8,11},{9,10},{10,... | collective-permute-start | bytes 196616 | tf_op jit(solution)/shard_map/ppermute | solution.py:306
  117.1 26.6 %all-to-all-start.4 = ((bf16[16,16,512]{2,1,0:T(8,128)(2,1)}), bf16[16,16,512]{2,1,0:T(8,128)(2,1)S(1)}, u32[]{:S(2)}, u32[]{:S(2)}) async-start(bf16[16,16,512]{2,1,0:T(8,128)(2,1)} %bitcast.24), calls=%async_computation.4 | async-start | bytes 524288 | tf_op jit(solution)/shard_map/all_to_all | solution.py:388
  132.9 10.1 %collective-permute-start.10 = (bf16[16,512]{1,0:T(8,128)(2,1)S(1)}, bf16[16,512]{1,0:T(8,128)(2,1)S(1)}, u32[]{:S(2)}, u32[]{:S(2)}) collective-permute-start(bf16[16,512]{1,0:T(8,128)(2,1)S(1)} %get-tuple-element.108), channel_id=1, source_target_pairs={{0,4},{1,5},{2,6},{3,7},{4,0},{5,1},{6,2},{7,3},{8,12},{9,13},{10,... | collective-permute-start | bytes 49160 | tf_op jit(solution)/shard_map/ppermute | solution.py:306
  134.9 8.8 %collective-permute-start.11 = (bf16[16,512]{1,0:T(8,128)(2,1)S(1)}, bf16[16,512]{1,0:T(8,128)(2,1)S(1)}, u32[]{:S(2)}, u32[]{:S(2)}) collective-permute-start(bf16[16,512]{1,0:T(8,128)(2,1)S(1)} %get-tuple-element.107), channel_id=1, source_target_pairs={{0,8},{1,9},{2,10},{3,11},{4,12},{5,13},{6,14},{7,15},{8,0},{9,1},... | collective-permute-start | bytes 49160 | tf_op jit(solution)/shard_map/ppermute | solution.py:306
  137.2 6.5 %collective-permute-start.12 = (bf16[16,512]{1,0:T(8,128)(2,1)S(1)}, bf16[16,512]{1,0:T(8,128)(2,1)S(1)}, u32[]{:S(2)}, u32[]{:S(2)}) collective-permute-start(bf16[16,512]{1,0:T(8,128)(2,1)S(1)} %get-tuple-element.106), channel_id=1, source_target_pairs={{0,12},{1,13},{2,14},{3,15},{4,8},{5,9},{6,10},{7,11},{8,4},{9,5},... | collective-permute-start | bytes 49160 | tf_op jit(solution)/shard_map/ppermute | solution.py:306
  138.6 3.7 %collective-permute-start.6 = (s32[]{:T(128)}, s32[]{:T(128)}, u32[]{:S(2)}, u32[]{:S(2)}) collective-permute-start(s32[]{:T(128)} %convert.1), channel_id=1, source_target_pairs={{0,16},{16,0},{1,17},{17,1},{2,18},{18,2},{3,19},{19,3},{4,20},{20... | collective-permute-start | bytes 20 | tf_op jit(solution)/shard_map/ppermute | solution.py:396
  144.1 0.7 copy-start.6
  (2 other events, 1.2 us)

commit v7 on v5

--- a/solution.py
+++ b/solution.py
@@ -127,47 +127,51 @@
     )
 
 
-def pack_body(last, flag_ref, at_ref, note_ref, tokens_ref, out):
-    shape = (out.shape[0], at_ref.shape[1])
-    pick = lax.broadcasted_iota(jnp.int32, shape, 0) == at_ref[...]
-    pick = pick.astype(jnp.float32).astype(jnp.bfloat16)
-
-    @pl.when(pl.program_id(0) < pl.num_programs(0) - 1)
-    def _():
-        out[...] = jnp.dot(
-            pick, tokens_ref[...], preferred_element_type=jnp.float32
+def pack_body(at_ref, note_ref, tokens_hbm, out_hbm, tokens_ref, out_ref, sems, out_sems):
+    depth = tokens_ref.shape[1]
+    spans = [slice(c, c + STEP) for c in range(0, depth, STEP)]
+    loads = [
+        pltpu.make_async_copy(tokens_hbm.at[:, span], tokens_ref.at[:, span], sems.at[i])
+        for i, span in enumerate(spans)
+    ]
+    for load in loads:
+        load.start()
+    pick = lax.broadcasted_iota(jnp.int32, (out_ref.shape[0], at_ref.shape[1]), 0) == at_ref[...]
+    pick = one_hot(pick)
+    out_ref[:, depth:] = notes_of(pick, note_ref[...]).astype(jnp.bfloat16)
+    stores = []
+    for i, span in enumerate(spans):
+        loads[i].wait()
+        out_ref[:, span] = jnp.dot(
+            pick, tokens_ref[:, span], preferred_element_type=jnp.float32
         ).astype(jnp.bfloat16)
-
-    @pl.when(pl.program_id(0) == pl.num_programs(0) - 1)
-    def _():
-        out[:, :last] = jnp.dot(
-            pick, tokens_ref[:, :last], preferred_element_type=jnp.float32
-        ).astype(jnp.bfloat16)
-        note = notes_of(pick, note_ref[...])
-        column = lax.broadcasted_iota(jnp.int32, note.shape, 1)
-        flag = jnp.where(column == 1, flag_ref[...].astype(jnp.float32), 0.0)
-        out[:, last:] = (note + flag).astype(jnp.bfloat16)
-
-
-def pack(main_rows, flag, at, note, tokens):
+        ready = slice(span.start, span.stop if i + 1 < len(spans) else depth + NOTE)
+        store = pltpu.make_async_copy(out_ref.at[:, ready], out_hbm.at[:, ready], out_sems.at[i])
+        store.start()
+        stores.append(store)
+    for store in stores:
+        store.wait()
+
+
+def pack(main_rows, at, note, tokens):
     rows, depth = tokens.shape
-    steps = (depth + NOTE) // WIDE
+    out = jax.ShapeDtypeStruct((main_rows, depth + NOTE), jnp.bfloat16)
     return pl.pallas_call(
-        functools.partial(pack_body, WIDE - NOTE),
-        grid=(steps,),
-        in_specs=[
-            pl.BlockSpec(flag.shape, lambda i: (0, 0)),
-            pl.BlockSpec(at.shape, lambda i: (0, 0)),
-            pl.BlockSpec(note.shape, lambda i: (0, 0)),
-            pl.BlockSpec((rows, WIDE), lambda i: (0, i)),
+        pack_body,
+        in_specs=[VMEM, VMEM, ANY],
+        out_specs=pl.BlockSpec(memory_space=pltpu.HBM),
+        out_shape=out,
+        scratch_shapes=[
+            pltpu.VMEM(tokens.shape, jnp.bfloat16),
+            pltpu.VMEM(out.shape, jnp.bfloat16),
+            pltpu.SemaphoreType.DMA((depth // STEP,)),
+            pltpu.SemaphoreType.DMA((depth // STEP,)),
         ],
-        out_specs=pl.BlockSpec((main_rows, WIDE), lambda i: (0, i)),
-        out_shape=jax.ShapeDtypeStruct((main_rows, depth + NOTE), jnp.bfloat16),
-        compiler_params=pltpu.CompilerParams(vmem_limit_bytes=56 * 2**20),
+        compiler_params=pltpu.CompilerParams(vmem_limit_bytes=52 * 2**20),
         cost_estimate=pl.CostEstimate(
             flops=2 * main_rows * rows * depth, bytes_accessed=8 * 2**20, transcendentals=0
         ),
-    )(flag, at, note, tokens)
+    )(at, note, tokens)
 
 
 def low_delta(low, note, first, rank, up):
@@ -176,7 +180,7 @@
     return jnp.dot(low.astype(jnp.bfloat16), up, preferred_element_type=jnp.float32)
 
 
-def adapt_body(rank, first_ref, down_hbm, up_ref, rows_hbm, out, flag_out, *scratch):
+def adapt_body(rank, first_ref, down_hbm, up_ref, rows_hbm, out, *scratch):
     down_ref, rows_ref, down_sems, sems = scratch
     depth = down_ref.shape[1]
     spans = [slice(c, min(c + WIDE, depth + NOTE)) for c in range(0, depth + NOTE, WIDE)]
@@ -205,8 +209,6 @@
         )
     note = rows_ref[:, depth:].astype(jnp.float32)
     out[...] = low_delta(low, note[:, :1], first_ref[0], rank, up_ref[...]).astype(jnp.bfloat16)
-    most = jnp.max(note, axis=0, keepdims=True)
-    flag_out[...] = jnp.broadcast_to(most, flag_out.shape).astype(jnp.bfloat16)
 
 
 def adapt(rank, first, down, up, got):
@@ -214,11 +216,8 @@
     return pl.pallas_call(
         functools.partial(adapt_body, rank),
         in_specs=[SMEM, ANY, VMEM, ANY],
-        out_specs=[VMEM, VMEM],
-        out_shape=[
-            jax.ShapeDtypeStruct((rows, width), jnp.bfloat16),
-            jax.ShapeDtypeStruct((16, NOTE), jnp.bfloat16),
-        ],
+        out_specs=VMEM,
+        out_shape=jax.ShapeDtypeStruct((rows, width), jnp.bfloat16),
         scratch_shapes=[
             pltpu.VMEM(down.shape, jnp.bfloat16),
             pltpu.VMEM(got.shape, jnp.bfloat16),
@@ -232,7 +231,7 @@
     )(first, down, up, got)
 
 
-def adapt_over_body(planes, rank, first_ref, down_hbm, up_ref, *refs):
+def adapt_over_body(planes, rank, first_ref, down_hbm, up_ref, flag_ref, *refs):
     rows_refs, outs = refs[:PLANE], refs[PLANE : 2 * PLANE]
     down_ref, sems = refs[2 * PLANE :]
     half = down_ref.shape[1] // 2
@@ -269,13 +268,18 @@
             notes += [note[s : s + SPARE], no_note]
     low = jnp.concatenate(lows, axis=0)
     note = jnp.concatenate(notes, axis=0)[:, :1]
-    delta = low_delta(low, note, first_ref[0], rank, up_ref[...]).astype(jnp.bfloat16)
+    delta = low_delta(low, note, first_ref[0], rank, up_ref[...])
+    row = lax.broadcasted_iota(jnp.int32, delta.shape, 0) % 16
+    flag = flag_ref[...][:, :1].astype(jnp.float32)
+    delta = jnp.where(row == SPARE, flag, delta).astype(jnp.bfloat16)
     for a, out in enumerate(outs):
         out[...] = delta[16 * planes * a : 16 * planes * (a + 1)]
 
 
 def final_body(at_ref, base_ref, back_ref, *refs):
-    *overs, out = refs
+    *overs, out, seen_ref = refs
+    seen = sum(o[...][SPARE:, :1].astype(jnp.float32) for o in overs)
+    seen_ref[0] = jnp.max(seen).astype(jnp.int32)
     back = jnp.concatenate([back_ref[...]] + [o[...] for o in overs], axis=0)
     main_rows, size = back_ref.shape[0], overs[0].shape[0]
     row = lax.broadcasted_iota(jnp.int32, (back.shape[0], at_ref.shape[1]), 0)
@@ -354,19 +358,18 @@
 
     along = [spare[0]] + [swap(spare[b], b * PLANE) for b in range(1, planes)]
 
+    blocks = pack(main_rows, at, note, tokens)
+
     groups = lax.axis_size("grp")
-    along[1], left = lax.optimization_barrier((along[1], left))
     flag = left
     for g in range(1, groups):
         other = lax.ppermute(left, "grp", [(s, (s + g) % groups) for s in range(groups)])
         flag = jnp.maximum(flag, other)
-    blocks = pack(main_rows, flag, at, note, tokens)
+
 
     along = jnp.concatenate(along, axis=0)
-    along, blocks, base_value = lax.optimization_barrier((along, blocks, base_value))
     shared = [along] + [swap(along, a) for a in range(1, PLANE)]
 
-    blocks, shared[1] = lax.optimization_barrier((blocks, shared[1]))
     got = lax.all_to_all(
         blocks.reshape(count, room, depth + NOTE), "ad", split_axis=0, concat_axis=0, tiled=True
     ).reshape(main_rows, depth + NOTE)
@@ -378,34 +381,37 @@
     over_delta = call(
         functools.partial(adapt_over_body, planes, rank),
         [(16 * planes, width)] * PLANE,
-        (first, down, up, *shared),
-        [SMEM, ANY] + [VMEM] * 5,
-        4 * 10**14,
+        (first, down, up, flag, *shared),
+        [SMEM, ANY] + [VMEM] * 6,
+        10**12,
         6 * 2**20,
         [pltpu.VMEM(down.shape, jnp.bfloat16), pltpu.SemaphoreType.DMA((depth // STEP,))],
     )
+    got, base_value = lax.optimization_barrier((got, base_value))
+    delta = adapt(rank, first, down, up, got)
+    delta, *over_delta = lax.optimization_barrier((delta, *over_delta))
     over_sum = over_delta[0]
     for a in range(1, PLANE):
         over_sum = over_sum + swap(over_delta[a], a)
     over_back = [over_sum[:16]]
     for b in range(1, planes):
         over_back.append(swap(over_sum[16 * b : 16 * (b + 1)], b * PLANE))
-
-    got, *over_back = lax.optimization_barrier((got, *over_back))
-    delta, flags = adapt(rank, first, down, up, got)
     back = lax.all_to_all(
         delta.reshape(count, room, width), "ad", split_axis=0, concat_axis=0, tiled=True
     ).reshape(main_rows, width)
 
     def finish(base):
-        return call(
+        return pl.pallas_call(
             final_body,
-            [(row_count, width)],
-            (at, base, back, *over_back),
-            [VMEM] * (3 + planes),
-            2 * row_count * width * 320,
-            2**20,
-        )[0]
+            in_specs=[VMEM] * (3 + planes),
+            out_specs=[VMEM, SMEM],
+            out_shape=[
+                jax.ShapeDtypeStruct((row_count, width), jnp.bfloat16),
+                jax.ShapeDtypeStruct((1,), jnp.int32),
+            ],
+        )(at, base, back, *over_back)
+
+    out, seen = finish(base_value)
 
     def more():
         slot, owner, place = route(tenant_ids, tenant_slot, local)
@@ -418,9 +424,9 @@
             adapt_down,
             adapt_up,
         )
-        return finish(base_value + extra)
-
-    return lax.cond(flags[0, 1] > 0, more, lambda: finish(base_value))
+        return finish(base_value + extra)[0]
+
+    return lax.cond(seen[0] > 0, more, lambda: out)
 
 
 def solution(mesh):

time: 158 us -> 195 us (1.23)
  waiting for transfers between devices: 99.6 us -> 137 us
    ppermute x12, waiting for transfers between devices: 90.7 us -> 137 us  [swap(): return lax.ppermute(x, 'ad', [(s, s ^ k) for s in range(count)])]
    all_to_all x1, waiting for transfers between devices: 8.88 us -> 0.01 us  [on_device(): lax.all_to_all(delta.reshape(count, room, width), 'ad', split_axis=0, con...]
    ppermute x12, starting transfers between devices: 16.7 us -> 12.7 us  [swap(): return lax.ppermute(x, 'ad', [(s, s ^ k) for s in range(count)])]
    all_to_all x1, starting transfers between devices: 3.61 us -> 6.79 us  [on_device(): lax.all_to_all(delta.reshape(count, room, width), 'ad', split_axis=0, con...]
    pallas_call x2 -> x1, Pallas kernels: 4.27 us -> 4.89 us  [call(): pl.pallas_call(body, in_specs=specs, out_specs=[VMEM] * len(outs), out_sh...]
    pallas_call x1 -> x2, Pallas kernels: 5.19 us -> 5.14 us  [the longest x1 4.09 us: pack(): pl.pallas_call(pack_body, in_specs=[VMEM, VMEM, ANY], out_specs=pl.BlockS...]
  transfers between devices with their start and end apart: 15 -> 15, of which waited for: 9 -> 6; matrix products, arithmetic and copies ran while one was open for 5% -> 4% of each run, Pallas kernels for 3% -> 3%
where the time goes in v7:
time: 195 us
  waiting for transfers between devices  137 us (70%)
  starting transfers between devices  28.5 us (15%)
  Pallas kernels  20.4 us (10%)
  matrix products  7.85 us (4%)
    ppermute x12, waiting for transfers between devices, swap(): return lax.ppermute(x, 'ad', [(s, s ^ k) for s in range(count)])  137 us
    ppermute x12, starting transfers between devices, swap(): return lax.ppermute(x, 'ad', [(s, s ^ k) for s in range(count)])  12.7 us
    dot_general x1, matrix products, on_device(): jnp.dot(tokens, value_weight, preferred_element_type=jnp.float32)  7.85 us
    all_to_all x1, starting transfers between devices, on_device(): lax.all_to_all(blocks.reshape(count, room, depth + NOTE), 'ad', split_axi...  7.45 us
    all_to_all x1, starting transfers between devices, on_device(): lax.all_to_all(delta.reshape(count, room, width), 'ad', split_axis=0, con...  6.79 us
    pallas_call x1, Pallas kernels, adapt(): pl.pallas_call(functools.partial(adapt_body, rank), in_specs=[SMEM, ANY,...  6.56 us
    pallas_call x1, Pallas kernels, call(): pl.pallas_call(body, in_specs=specs, out_specs=[VMEM] * len(outs), out_sh...  4.89 us
    pallas_call x1, Pallas kernels, pack(): pl.pallas_call(pack_body, in_specs=[VMEM, VMEM, ANY], out_specs=pl.BlockS...  4.09 us
  transfers between devices with their start and end apart: 15, of which 6 were waited for; matrix products, arithmetic and copies ran while one was open for 4% of the time, Pallas kernels for 3%

profile of v7, /device:TPU:0, one launch (start us, length us, event | category | flops | bytes accessed | tf_op | source)
XLA Modules:
  0.0 194.8 jit_solution(10656952777369490417)
XLA Ops:
  0.0 3.8 %shard_map.66 = (bf16[24,4224]{1,0:T(8,128)(2,1)S(1)}, bf16[24,4224]{1,0:T(8,128)(2,1)S(1)}, bf16[24,4224]{1,0:T(8,128)(2,1)S(1)}, bf16[24,4224]{1,0:T(8,128)(2,...) custom-call(s32[1]{0:T(128)} %bitcast.12.me_ref, s32[1,256]{1,0:T(1,128)} %bitcast.52, ...), custom_call_target="tpu_custom_call" | custom-call | flops 805306368 | bytes 6291456 | tf_op jit(solution)/shard_map/pallas_call | solution.py:339
  3.9 4.1 %shard_map.67 = bf16[256,8320]{1,0:T(8,128)(2,1)} custom-call(s32[1,256]{1,0:T(1,128)S(1)} %get-tuple-element.66.at_ref, bf16[128,256]{1,0:T(8,128)(2,1)S(1)} %get-tuple-element.67.note_ref, bf16[256,8192]{1,0:T(8,128)(2,1)S(1)} %copy-done), custom_call_target="tpu_custom_call" | custom-call | flops 1073741824 | bytes 8388608 | tf_op jit(solution)/shard_map/pallas_call | solution.py:159
  8.0 7.4 %all-to-all-start.3 = ((bf16[16,16,8320]{2,1,0:T(8,128)(2,1)}), bf16[16,16,8320]{2,1,0:T(8,128)(2,1)}, u32[]{:S(2)}, u32[]{:S(2)}) async-start(bf16[16,16,8320]{2,1,0:T(8,128)(2,1)} %bitcast.36), calls=%async_computation.3 | async-start | bytes 8519680 | tf_op jit(solution)/shard_map/all_to_all | solution.py:373
  15.4 1.5 collective-permute-start
  17.0 1.8 collective-permute-start.1
  18.8 2.4 %collective-permute-start.2 = (bf16[24,4224]{1,0:T(8,128)(2,1)S(1)}, bf16[24,4224]{1,0:T(8,128)(2,1)S(1)}, u32[]{:S(2)}, u32[]{:S(2)}) collective-permute-start(bf16[24,4224]{1,0:T(8,128)(2,1)S(1)} %get-tuple-element.73), channel_id=1, source_target_pairs={{0,8},{1,9},{2,10},{3,11},{4,12},{5,13},{6,14},{7,15},{8,0},{9,1},... | collective-permute-start | bytes 608264 | tf_op jit(solution)/shard_map/ppermute | solution.py:310
  21.2 0.2 collective-permute-start.3
  21.4 68.2 %collective-permute-done.1 = bf16[24,4224]{1,0:T(8,128)(2,1)S(1)} collective-permute-done((bf16[24,4224]{1,0:T(8,128)(2,1)S(1)}, bf16[24,4224]{1,0:T(8,128)(2,1)S(1)}, u32[]{:S(2)}, u32[]{:S(2)}) %collective-permute-start.1) | collective-permute-done | bytes 202784 | tf_op jit(solution)/shard_map/ppermute | solution.py:310
  89.6 34.8 %collective-permute-done.2 = bf16[24,4224]{1,0:T(8,128)(2,1)S(1)} collective-permute-done((bf16[24,4224]{1,0:T(8,128)(2,1)S(1)}, bf16[24,4224]{1,0:T(8,128)(2,1)S(1)}, u32[]{:S(2)}, u32[]{:S(2)}) %collective-permute-start.2) | collective-permute-done | bytes 202784 | tf_op jit(solution)/shard_map/ppermute | solution.py:310
  124.5 1.5 collective-permute-start.5
  126.0 0.3 collective-permute-start.6
  126.4 7.8 %fusion.9.base_ref = f32[256,512]{1,0:T(8,128)} fusion(bf16[256,8192]{1,0:T(8,128)(2,1)} %tokens_hbm.3, bf16[8192,512]{1,0:T(8,128)(2,1)} %param.9), kind=kOutput, calls=%fused_computation.39 | convolution fusion | flops 2147483648 | bytes 13107200 | tf_op jit(solution)/shard_map/dot_general | solution.py:330
  134.2 11.2 %collective-permute-done.5.refs_2_ = bf16[96,4224]{1,0:T(8,128)(2,1)S(1)} collective-permute-done((bf16[96,4224]{1,0:T(8,128)(2,1)S(1)}, bf16[96,4224]{1,0:T(8,128)(2,1)S(1)}, u32[]{:S(2)}, u32[]{:S(2)}) %collective-permute-start.5) | collective-permute-done | bytes 811040 | tf_op jit(solution)/shard_map/ppermute | solution.py:310
  145.4 16.5 %collective-permute-done.6.refs_3_ = bf16[96,4224]{1,0:T(8,128)(2,1)S(1)} collective-permute-done((bf16[96,4224]{1,0:T(8,128)(2,1)S(1)}, bf16[96,4224]{1,0:T(8,128)(2,1)S(1)}, u32[]{:S(2)}, u32[]{:S(2)}) %collective-permute-start.6) | collective-permute-done | bytes 811040 | tf_op jit(solution)/shard_map/ppermute | solution.py:310
  161.9 4.9 %shard_map.69 = (bf16[64,512]{1,0:T(8,128)(2,1)S(1)}, bf16[64,512]{1,0:T(8,128)(2,1)S(1)}, bf16[64,512]{1,0:T(8,128)(2,1)S(1)}, bf16[64,512]{1,0:T(8,128)(2,1)S(1)}) custom-call(s32[1]{0:T(128)} %bitcast.17.first_ref, bf16[256,8192]{1,0:T(8,128)(2,1)} %bitcast.38, bf16[256,512]{1,0:T(8,128)(2,1)} %bitcast.44, s32[1,128]{1,0:T(1,128)S(1)} %max.3.flag_ref, ...), custom_call_target="tpu_custom_call" | custom-call | flops 999999995904 | bytes 6291456 | tf_op jit(solution)/shard_map/pallas_call | solution.py:297
  166.9 6.6 %shard_map.68 = bf16[256,512]{1,0:T(8,128)(2,1)} custom-call(s32[1]{0:T(128)} %bitcast.17.first_ref, bf16[256,8192]{1,0:T(8,128)(2,1)} %bitcast.39, bf16[256,512]{1,0:T(8,128)(2,1)} %bitcast.45, bf16[256,8320]{1,0:T(8,128)(2,1)} %bitcast.16.rows_hbm), custom_call_target="tpu_custom_call" | custom-call | flops 1073741824 | bytes 8388608 | tf_op jit(solution)/shard_map/pallas_call | solution.py:216
  173.4 1.4 collective-permute-start.9
  174.8 0.6 collective-permute-start.8
  175.4 6.8 %all-to-all-start.4 = ((bf16[16,16,512]{2,1,0:T(8,128)(2,1)}), bf16[16,16,512]{2,1,0:T(8,128)(2,1)S(1)}, u32[]{:S(2)}, u32[]{:S(2)}) async-start(bf16[16,16,512]{2,1,0:T(8,128)(2,1)} %bitcast.22), calls=%async_computation.4 | async-start | bytes 524288 | tf_op jit(solution)/shard_map/all_to_all | solution.py:399
  182.3 2.0 %collective-permute-start.10 = (bf16[16,512]{1,0:T(8,128)(2,1)S(1)}, bf16[16,512]{1,0:T(8,128)(2,1)S(1)}, u32[]{:S(2)}, u32[]{:S(2)}) collective-permute-start(bf16[16,512]{1,0:T(8,128)(2,1)S(1)} %get-tuple-element.91), channel_id=1, source_target_pairs={{0,4},{1,5},{2,6},{3,7},{4,0},{5,1},{6,2},{7,3},{8,12},{9,13},{10,... | collective-permute-start | bytes 49160 | tf_op jit(solution)/shard_map/ppermute | solution.py:310
  184.3 2.4 %collective-permute-start.11 = (bf16[16,512]{1,0:T(8,128)(2,1)S(1)}, bf16[16,512]{1,0:T(8,128)(2,1)S(1)}, u32[]{:S(2)}, u32[]{:S(2)}) collective-permute-start(bf16[16,512]{1,0:T(8,128)(2,1)S(1)} %get-tuple-element.90), channel_id=1, source_target_pairs={{0,8},{1,9},{2,10},{3,11},{4,12},{5,13},{6,14},{7,15},{8,0},{9,1},... | collective-permute-start | bytes 49160 | tf_op jit(solution)/shard_map/ppermute | solution.py:310
  186.7 1.9 collective-permute-done.10.refs_1_
  188.6 4.5 %collective-permute-done.11.refs_2_ = bf16[16,512]{1,0:T(8,128)(2,1)S(1)} collective-permute-done((bf16[16,512]{1,0:T(8,128)(2,1)S(1)}, bf16[16,512]{1,0:T(8,128)(2,1)S(1)}, u32[]{:S(2)}, u32[]{:S(2)}) %collective-permute-start.11) | collective-permute-done | bytes 16416 | tf_op jit(solution)/shard_map/ppermute | solution.py:310
  193.1 1.1 shard_map.70
  (34 shorter events, 0.3 us)
Async XLA Ops:
  0.0 3.9 %copy-start = (bf16[256,8192]{1,0:T(8,128)(2,1)S(1)}, bf16[256,8192]{1,0:T(8,128)(2,1)}, u32[]{:S(2)}) copy-start(bf16[256,8192]{1,0:T(8,128)(2,1)} %tokens_hbm.3) | copy-start | bytes 12582916
  3.9 4.1 %copy-start.3 = (s32[1,256]{1,0:T(1,128)}, s32[1,256]{1,0:T(1,128)S(1)}, u32[]{:S(2)}) copy-start(s32[1,256]{1,0:T(1,128)S(1)} %get-tuple-element.66.at_ref) | copy-start | bytes 3076
  8.0 158.8 %all-to-all-start.3 = ((bf16[16,16,8320]{2,1,0:T(8,128)(2,1)}), bf16[16,16,8320]{2,1,0:T(8,128)(2,1)}, u32[]{:S(2)}, u32[]{:S(2)}) async-start(bf16[16,16,8320]{2,1,0:T(8,128)(2,1)} %bitcast.36), calls=%async_computation.3 | async-start | bytes 8519680 | tf_op jit(solution)/shard_map/all_to_all | solution.py:373
  15.4 118.8 %collective-permute-start = (s32[1,128]{1,0:T(1,128)S(1)}, s32[1,128]{1,0:T(1,128)S(1)}, u32[]{:S(2)}, u32[]{:S(2)}) collective-permute-start(s32[1,128]{1,0:T(1,128)S(1)} %get-tuple-element.70), channel_id=1, source_target_pairs={{0,16},{16,0},{1,17},{17,1},{2,18},{18,2},{3,19},{19,3},{4,20},{20... | collective-permute-start | bytes 1544 | tf_op jit(solution)/shard_map/ppermute | solution.py:366
  17.0 72.6 %collective-permute-start.1 = (bf16[24,4224]{1,0:T(8,128)(2,1)S(1)}, bf16[24,4224]{1,0:T(8,128)(2,1)S(1)}, u32[]{:S(2)}, u32[]{:S(2)}) collective-permute-start(bf16[24,4224]{1,0:T(8,128)(2,1)S(1)} %get-tuple-element.72), channel_id=1, source_target_pairs={{0,4},{1,5},{2,6},{3,7},{4,0},{5,1},{6,2},{7,3},{8,12},{9,13},{10,... | collective-permute-start | bytes 608264 | tf_op jit(solution)/shard_map/ppermute | solution.py:310
  18.8 105.6 %collective-permute-start.2 = (bf16[24,4224]{1,0:T(8,128)(2,1)S(1)}, bf16[24,4224]{1,0:T(8,128)(2,1)S(1)}, u32[]{:S(2)}, u32[]{:S(2)}) collective-permute-start(bf16[24,4224]{1,0:T(8,128)(2,1)S(1)} %get-tuple-element.73), channel_id=1, source_target_pairs={{0,8},{1,9},{2,10},{3,11},{4,12},{5,13},{6,14},{7,15},{8,0},{9,1},... | collective-permute-start | bytes 608264 | tf_op jit(solution)/shard_map/ppermute | solution.py:310
  21.2 103.2 %collective-permute-start.3 = (bf16[24,4224]{1,0:T(8,128)(2,1)S(1)}, bf16[24,4224]{1,0:T(8,128)(2,1)S(1)}, u32[]{:S(2)}, u32[]{:S(2)}) collective-permute-start(bf16[24,4224]{1,0:T(8,128)(2,1)S(1)} %get-tuple-element.74), channel_id=1, source_target_pairs={{0,12},{1,13},{2,14},{3,15},{4,8},{5,9},{6,10},{7,11},{8,4},{9,5},... | collective-permute-start | bytes 608264 | tf_op jit(solution)/shard_map/ppermute | solution.py:310
  124.4 9.8 %collective-permute-start.4 = (bf16[96,4224]{1,0:T(8,128)(2,1)S(1)}, bf16[96,4224]{1,0:T(8,128)(2,1)S(1)}, u32[]{:S(2)}, u32[]{:S(2)}) collective-permute-start(bf16[96,4224]{1,0:T(8,128)(2,1)S(1)} %constant_dynamic-update-slice_fusion.refs_0_), channel_id=1, source_target_pairs={{0,1},{1,0},{2,3},{3,2},{4,5},{5,4},{6,7},{7,6},{8,9},{9,8},{10,11... | collective-permute-start | bytes 2433032 | tf_op jit(solution)/shard_map/ppermute | solution.py:310
  124.5 20.9 %collective-permute-start.5 = (bf16[96,4224]{1,0:T(8,128)(2,1)S(1)}, bf16[96,4224]{1,0:T(8,128)(2,1)S(1)}, u32[]{:S(2)}, u32[]{:S(2)}) collective-permute-start(bf16[96,4224]{1,0:T(8,128)(2,1)S(1)} %constant_dynamic-update-slice_fusion.refs_0_), channel_id=1, source_target_pairs={{0,2},{1,3},{2,0},{3,1},{4,6},{5,7},{6,4},{7,5},{8,10},{9,11},{10,... | collective-permute-start | bytes 2433032 | tf_op jit(solution)/shard_map/ppermute | solution.py:310
  126.0 35.9 %collective-permute-start.6 = (bf16[96,4224]{1,0:T(8,128)(2,1)S(1)}, bf16[96,4224]{1,0:T(8,128)(2,1)S(1)}, u32[]{:S(2)}, u32[]{:S(2)}) collective-permute-start(bf16[96,4224]{1,0:T(8,128)(2,1)S(1)} %constant_dynamic-update-slice_fusion.refs_0_), channel_id=1, source_target_pairs={{0,3},{1,2},{2,1},{3,0},{4,7},{5,6},{6,5},{7,4},{8,11},{9,10},{10,... | collective-permute-start | bytes 2433032 | tf_op jit(solution)/shard_map/ppermute | solution.py:310
  166.8 26.3 %copy-start.1 = (f32[256,512]{1,0:T(8,128)S(1)}, f32[256,512]{1,0:T(8,128)}, u32[]{:S(2)}) copy-start(f32[256,512]{1,0:T(8,128)} %fusion.9.base_ref) | copy-start | bytes 1572868
  166.8 26.3 %copy-start.4 = (s32[1,256]{1,0:T(1,128)S(1)}, s32[1,256]{1,0:T(1,128)}, u32[]{:S(2)}) copy-start(s32[1,256]{1,0:T(1,128)} %copy-done.3) | copy-start | bytes 3076
  166.8 28.0 %copy-start.2 = (bf16[16,16,512]{2,1,0:T(8,128)(2,1)S(1)}, bf16[16,16,512]{2,1,0:T(8,128)(2,1)}, u32[]{:S(2)}) copy-start(bf16[16,16,512]{2,1,0:T(8,128)(2,1)} %param.11) | copy-start | bytes 786436
  166.8 28.0 %copy-start.5 = (s32[256,1]{0,1:T(1,128)S(1)}, s32[256,1]{0,1:T(1,128)}, u32[]{:S(2)}) copy-start(s32[256,1]{0,1:T(1,128)} %param.12) | copy-start | bytes 3076
  166.9 28.0 %copy-start.6 = (s32[256]{0:T(256)S(1)}, s32[256]{0:T(256)}, u32[]{:S(2)}) copy-start(s32[256]{0:T(256)} %param.13) | copy-start | bytes 3076
  173.4 8.8 %collective-permute-start.9 = (bf16[64,512]{1,0:T(8,128)(2,1)S(1)}, bf16[64,512]{1,0:T(8,128)(2,1)S(1)}, u32[]{:S(2)}, u32[]{:S(2)}) collective-permute-start(bf16[64,512]{1,0:T(8,128)(2,1)S(1)} %get-tuple-element.83), channel_id=1, source_target_pairs={{0,3},{1,2},{2,1},{3,0},{4,7},{5,6},{6,5},{7,4},{8,11},{9,10},{10,... | collective-permute-start | bytes 196616 | tf_op jit(solution)/shard_map/ppermute | solution.py:310
  174.8 7.4 %collective-permute-start.8 = (bf16[64,512]{1,0:T(8,128)(2,1)S(1)}, bf16[64,512]{1,0:T(8,128)(2,1)S(1)}, u32[]{:S(2)}, u32[]{:S(2)}) collective-permute-start(bf16[64,512]{1,0:T(8,128)(2,1)S(1)} %get-tuple-element.82), channel_id=1, source_target_pairs={{0,2},{1,3},{2,0},{3,1},{4,6},{5,7},{6,4},{7,5},{8,10},{9,11},{10,... | collective-permute-start | bytes 196616 | tf_op jit(solution)/shard_map/ppermute | solution.py:310
  175.4 6.8 %collective-permute-start.7 = (bf16[64,512]{1,0:T(8,128)(2,1)S(1)}, bf16[64,512]{1,0:T(8,128)(2,1)S(1)}, u32[]{:S(2)}, u32[]{:S(2)}) collective-permute-start(bf16[64,512]{1,0:T(8,128)(2,1)S(1)} %get-tuple-element.81), channel_id=1, source_target_pairs={{0,1},{1,0},{2,3},{3,2},{4,5},{5,4},{6,7},{7,6},{8,9},{9,8},{10,11... | collective-permute-start | bytes 196616 | tf_op jit(solution)/shard_map/ppermute | solution.py:310
  175.4 17.7 %all-to-all-start.4 = ((bf16[16,16,512]{2,1,0:T(8,128)(2,1)}), bf16[16,16,512]{2,1,0:T(8,128)(2,1)S(1)}, u32[]{:S(2)}, u32[]{:S(2)}) async-start(bf16[16,16,512]{2,1,0:T(8,128)(2,1)} %bitcast.22), calls=%async_computation.4 | async-start | bytes 524288 | tf_op jit(solution)/shard_map/all_to_all | solution.py:399
  182.3 6.3 %collective-permute-start.10 = (bf16[16,512]{1,0:T(8,128)(2,1)S(1)}, bf16[16,512]{1,0:T(8,128)(2,1)S(1)}, u32[]{:S(2)}, u32[]{:S(2)}) collective-permute-start(bf16[16,512]{1,0:T(8,128)(2,1)S(1)} %get-tuple-element.91), channel_id=1, source_target_pairs={{0,4},{1,5},{2,6},{3,7},{4,0},{5,1},{6,2},{7,3},{8,12},{9,13},{10,... | collective-permute-start | bytes 49160 | tf_op jit(solution)/shard_map/ppermute | solution.py:310
  184.3 8.8 %collective-permute-start.11 = (bf16[16,512]{1,0:T(8,128)(2,1)S(1)}, bf16[16,512]{1,0:T(8,128)(2,1)S(1)}, u32[]{:S(2)}, u32[]{:S(2)}) collective-permute-start(bf16[16,512]{1,0:T(8,128)(2,1)S(1)} %get-tuple-element.90), channel_id=1, source_target_pairs={{0,8},{1,9},{2,10},{3,11},{4,12},{5,13},{6,14},{7,15},{8,0},{9,1},... | collective-permute-start | bytes 49160 | tf_op jit(solution)/shard_map/ppermute | solution.py:310
  186.6 6.5 %collective-permute-start.12 = (bf16[16,512]{1,0:T(8,128)(2,1)S(1)}, bf16[16,512]{1,0:T(8,128)(2,1)S(1)}, u32[]{:S(2)}, u32[]{:S(2)}) collective-permute-start(bf16[16,512]{1,0:T(8,128)(2,1)S(1)} %get-tuple-element.89), channel_id=1, source_target_pairs={{0,12},{1,13},{2,14},{3,15},{4,8},{5,9},{6,10},{7,11},{8,4},{9,5},... | collective-permute-start | bytes 49160 | tf_op jit(solution)/shard_map/ppermute | solution.py:310

commit v8 on v7

--- a/solution.py
+++ b/solution.py
@@ -360,14 +360,13 @@
 
     blocks = pack(main_rows, at, note, tokens)
 
+    along = jnp.concatenate(along, axis=0)
+    along, left = lax.optimization_barrier((along, left))
     groups = lax.axis_size("grp")
     flag = left
     for g in range(1, groups):
         other = lax.ppermute(left, "grp", [(s, (s + g) % groups) for s in range(groups)])
         flag = jnp.maximum(flag, other)
-
-
-    along = jnp.concatenate(along, axis=0)
     shared = [along] + [swap(along, a) for a in range(1, PLANE)]
 
     got = lax.all_to_all(
@@ -383,11 +382,11 @@
         [(16 * planes, width)] * PLANE,
         (first, down, up, flag, *shared),
         [SMEM, ANY] + [VMEM] * 6,
-        10**12,
+        2 * 384 * depth * local * rank,
         6 * 2**20,
         [pltpu.VMEM(down.shape, jnp.bfloat16), pltpu.SemaphoreType.DMA((depth // STEP,))],
     )
-    got, base_value = lax.optimization_barrier((got, base_value))
+    got, base_value, *over_delta = lax.optimization_barrier((got, base_value, *over_delta))
     delta = adapt(rank, first, down, up, got)
     delta, *over_delta = lax.optimization_barrier((delta, *over_delta))
     over_sum = over_delta[0]

time: 195 us -> 196 us (level)
  waiting for transfers between devices: 137 us -> 141 us
  starting transfers between devices: 28.5 us -> 25.5 us
    ppermute x12, waiting for transfers between devices: 137 us -> 141 us  [swap(): return lax.ppermute(x, 'ad', [(s, s ^ k) for s in range(count)])]
    all_to_all x1, starting transfers between devices: 6.79 us -> 3.75 us  [on_device(): lax.all_to_all(delta.reshape(count, room, width), 'ad', split_axis=0, con...]
  transfers between devices with their start and end apart: 15 -> 15, of which waited for: 6 -> 7; matrix products, arithmetic and copies ran while one was open for 4% -> 4% of each run, Pallas kernels for 3% -> 3%
where the time goes in v8:
time: 196 us
  waiting for transfers between devices  141 us (72%)
  starting transfers between devices  25.5 us (13%)
  Pallas kernels  20.4 us (10%)
  matrix products  7.87 us (4%)
    ppermute x12, waiting for transfers between devices, swap(): return lax.ppermute(x, 'ad', [(s, s ^ k) for s in range(count)])  141 us
    ppermute x12, starting transfers between devices, swap(): return lax.ppermute(x, 'ad', [(s, s ^ k) for s in range(count)])  12.8 us
    dot_general x1, matrix products, on_device(): jnp.dot(tokens, value_weight, preferred_element_type=jnp.float32)  7.87 us
    all_to_all x1, starting transfers between devices, on_device(): lax.all_to_all(blocks.reshape(count, room, depth + NOTE), 'ad', split_axi...  7.45 us
    pallas_call x1, Pallas kernels, adapt(): pl.pallas_call(functools.partial(adapt_body, rank), in_specs=[SMEM, ANY,...  6.56 us
    pallas_call x1, Pallas kernels, call(): pl.pallas_call(body, in_specs=specs, out_specs=[VMEM] * len(outs), out_sh...  4.89 us
    pallas_call x1, Pallas kernels, pack(): pl.pallas_call(pack_body, in_specs=[VMEM, VMEM, ANY], out_specs=pl.BlockS...  4.08 us
  transfers between devices with their start and end apart: 15, of which 7 were waited for; matrix products, arithmetic and copies ran while one was open for 4% of the time, Pallas kernels for 3%

profile of v8, /device:TPU:0, one launch (start us, length us, event | category | flops | bytes accessed | tf_op | source)
XLA Modules:
  0.0 195.6 jit_solution(11618769232803807054)
XLA Ops:
  0.0 3.8 %shard_map.66 = (bf16[24,4224]{1,0:T(8,128)(2,1)S(1)}, bf16[24,4224]{1,0:T(8,128)(2,1)S(1)}, bf16[24,4224]{1,0:T(8,128)(2,1)S(1)}, bf16[24,4224]{1,0:T(8,128)(2,...) custom-call(s32[1]{0:T(128)} %bitcast.12.me_ref, s32[1,256]{1,0:T(1,128)} %bitcast.52, ...), custom_call_target="tpu_custom_call" | custom-call | flops 805306368 | bytes 6291456 | tf_op jit(solution)/shard_map/pallas_call | solution.py:339
  3.9 4.1 %shard_map.67 = bf16[256,8320]{1,0:T(8,128)(2,1)} custom-call(s32[1,256]{1,0:T(1,128)S(1)} %get-tuple-element.72.at_ref, bf16[128,256]{1,0:T(8,128)(2,1)S(1)} %get-tuple-element.73.note_ref, bf16[256,8192]{1,0:T(8,128)(2,1)S(1)} %copy-done), custom_call_target="tpu_custom_call" | custom-call | flops 1073741824 | bytes 8388608 | tf_op jit(solution)/shard_map/pallas_call | solution.py:159
  8.0 7.4 %all-to-all-start.3 = ((bf16[16,16,8320]{2,1,0:T(8,128)(2,1)}), bf16[16,16,8320]{2,1,0:T(8,128)(2,1)}, u32[]{:S(2)}, u32[]{:S(2)}) async-start(bf16[16,16,8320]{2,1,0:T(8,128)(2,1)} %bitcast.36), calls=%async_computation.3 | async-start | bytes 8519680 | tf_op jit(solution)/shard_map/all_to_all | solution.py:372
  15.4 3.7 %collective-permute-start.2 = (bf16[24,4224]{1,0:T(8,128)(2,1)S(1)}, bf16[24,4224]{1,0:T(8,128)(2,1)S(1)}, u32[]{:S(2)}, u32[]{:S(2)}) collective-permute-start(bf16[24,4224]{1,0:T(8,128)(2,1)S(1)} %get-tuple-element.77), channel_id=1, source_target_pairs={{0,12},{1,13},{2,14},{3,15},{4,8},{5,9},{6,10},{7,11},{8,4},{9,5},... | collective-permute-start | bytes 608264 | tf_op jit(solution)/shard_map/ppermute | solution.py:310
  19.1 0.8 collective-permute-start
  19.9 74.0 %collective-permute-done.2 = bf16[24,4224]{1,0:T(8,128)(2,1)S(1)} collective-permute-done((bf16[24,4224]{1,0:T(8,128)(2,1)S(1)}, bf16[24,4224]{1,0:T(8,128)(2,1)S(1)}, u32[]{:S(2)}, u32[]{:S(2)}) %collective-permute-start.2) | collective-permute-done | bytes 202784 | tf_op jit(solution)/shard_map/ppermute | solution.py:310
  93.9 34.3 %collective-permute-done.1 = bf16[24,4224]{1,0:T(8,128)(2,1)S(1)} collective-permute-done((bf16[24,4224]{1,0:T(8,128)(2,1)S(1)}, bf16[24,4224]{1,0:T(8,128)(2,1)S(1)}, u32[]{:S(2)}, u32[]{:S(2)}) %collective-permute-start.1) | collective-permute-done | bytes 202784 | tf_op jit(solution)/shard_map/ppermute | solution.py:310
  128.3 1.5 collective-permute-start.5
  129.9 0.3 collective-permute-start.6
  130.2 1.5 collective-permute-start.3
  131.7 7.9 %fusion.9.base_ref = f32[256,512]{1,0:T(8,128)} fusion(bf16[256,8192]{1,0:T(8,128)(2,1)} %tokens_hbm.3, bf16[8192,512]{1,0:T(8,128)(2,1)} %param.9), kind=kOutput, calls=%fused_computation.36 | convolution fusion | flops 2147483648 | bytes 13107200 | tf_op jit(solution)/shard_map/dot_general | solution.py:330
  139.6 9.7 %collective-permute-done.5.refs_2_ = bf16[96,4224]{1,0:T(8,128)(2,1)S(1)} collective-permute-done((bf16[96,4224]{1,0:T(8,128)(2,1)S(1)}, bf16[96,4224]{1,0:T(8,128)(2,1)S(1)}, u32[]{:S(2)}, u32[]{:S(2)}) %collective-permute-start.5) | collective-permute-done | bytes 811040 | tf_op jit(solution)/shard_map/ppermute | solution.py:310
  149.3 16.5 %collective-permute-done.6.refs_3_ = bf16[96,4224]{1,0:T(8,128)(2,1)S(1)} collective-permute-done((bf16[96,4224]{1,0:T(8,128)(2,1)S(1)}, bf16[96,4224]{1,0:T(8,128)(2,1)S(1)}, u32[]{:S(2)}, u32[]{:S(2)}) %collective-permute-start.6) | collective-permute-done | bytes 811040 | tf_op jit(solution)/shard_map/ppermute | solution.py:310
  165.8 4.9 %shard_map.68 = (bf16[64,512]{1,0:T(8,128)(2,1)S(1)}, bf16[64,512]{1,0:T(8,128)(2,1)S(1)}, bf16[64,512]{1,0:T(8,128)(2,1)S(1)}, bf16[64,512]{1,0:T(8,128)(2,1)S(1)}) custom-call(s32[1]{0:T(128)} %bitcast.17.first_ref, bf16[256,8192]{1,0:T(8,128)(2,1)} %bitcast.38, bf16[256,512]{1,0:T(8,128)(2,1)} %bitcast.43, s32[1,128]{1,0:T(1,128)S(1)} %max.3.flag_ref, ...), custom_call_target="tpu_custom_call" | custom-call | flops 1610612736 | bytes 6291456 | tf_op jit(solution)/shard_map/pallas_call | solution.py:297
  170.7 6.6 %shard_map.69 = bf16[256,512]{1,0:T(8,128)(2,1)} custom-call(s32[1]{0:T(128)} %bitcast.17.first_ref, bf16[256,8192]{1,0:T(8,128)(2,1)} %bitcast.39, bf16[256,512]{1,0:T(8,128)(2,1)} %bitcast.44, bf16[256,8320]{1,0:T(8,128)(2,1)} %bitcast.16.rows_hbm), custom_call_target="tpu_custom_call" | custom-call | flops 1073741824 | bytes 8388608 | tf_op jit(solution)/shard_map/pallas_call | solution.py:216
  177.3 1.4 collective-permute-start.9
  178.7 0.6 collective-permute-start.8
  179.3 3.8 %all-to-all-start.4 = ((bf16[16,16,512]{2,1,0:T(8,128)(2,1)}), bf16[16,16,512]{2,1,0:T(8,128)(2,1)S(1)}, u32[]{:S(2)}, u32[]{:S(2)}) async-start(bf16[16,16,512]{2,1,0:T(8,128)(2,1)} %bitcast.22), calls=%async_computation.4 | async-start | bytes 524288 | tf_op jit(solution)/shard_map/all_to_all | solution.py:398
  183.2 1.9 collective-permute-start.10
  185.1 2.4 %collective-permute-start.11 = (bf16[16,512]{1,0:T(8,128)(2,1)S(1)}, bf16[16,512]{1,0:T(8,128)(2,1)S(1)}, u32[]{:S(2)}, u32[]{:S(2)}) collective-permute-start(bf16[16,512]{1,0:T(8,128)(2,1)S(1)} %get-tuple-element.102), channel_id=1, source_target_pairs={{0,8},{1,9},{2,10},{3,11},{4,12},{5,13},{6,14},{7,15},{8,0},{9,1},... | collective-permute-start | bytes 49160 | tf_op jit(solution)/shard_map/ppermute | solution.py:310
  187.5 0.2 collective-permute-start.12
  187.6 1.8 collective-permute-done.10.refs_1_
  189.4 4.5 %collective-permute-done.11.refs_2_ = bf16[16,512]{1,0:T(8,128)(2,1)S(1)} collective-permute-done((bf16[16,512]{1,0:T(8,128)(2,1)S(1)}, bf16[16,512]{1,0:T(8,128)(2,1)S(1)}, u32[]{:S(2)}, u32[]{:S(2)}) %collective-permute-start.11) | collective-permute-done | bytes 16416 | tf_op jit(solution)/shard_map/ppermute | solution.py:310
  193.9 1.0 shard_map.70
  (27 shorter events, 0.3 us)
Async XLA Ops:
  0.0 3.9 %copy-start = (bf16[256,8192]{1,0:T(8,128)(2,1)S(1)}, bf16[256,8192]{1,0:T(8,128)(2,1)}, u32[]{:S(2)}) copy-start(bf16[256,8192]{1,0:T(8,128)(2,1)} %tokens_hbm.3) | copy-start | bytes 12582916
  8.0 162.7 %all-to-all-start.3 = ((bf16[16,16,8320]{2,1,0:T(8,128)(2,1)}), bf16[16,16,8320]{2,1,0:T(8,128)(2,1)}, u32[]{:S(2)}, u32[]{:S(2)}) async-start(bf16[16,16,8320]{2,1,0:T(8,128)(2,1)} %bitcast.36), calls=%async_computation.3 | async-start | bytes 8519680 | tf_op jit(solution)/shard_map/all_to_all | solution.py:372
  15.4 78.5 %collective-permute-start.2 = (bf16[24,4224]{1,0:T(8,128)(2,1)S(1)}, bf16[24,4224]{1,0:T(8,128)(2,1)S(1)}, u32[]{:S(2)}, u32[]{:S(2)}) collective-permute-start(bf16[24,4224]{1,0:T(8,128)(2,1)S(1)} %get-tuple-element.77), channel_id=1, source_target_pairs={{0,12},{1,13},{2,14},{3,15},{4,8},{5,9},{6,10},{7,11},{8,4},{9,5},... | collective-permute-start | bytes 608264 | tf_op jit(solution)/shard_map/ppermute | solution.py:310
  19.1 109.1 %collective-permute-start.1 = (bf16[24,4224]{1,0:T(8,128)(2,1)S(1)}, bf16[24,4224]{1,0:T(8,128)(2,1)S(1)}, u32[]{:S(2)}, u32[]{:S(2)}) collective-permute-start(bf16[24,4224]{1,0:T(8,128)(2,1)S(1)} %get-tuple-element.76), channel_id=1, source_target_pairs={{0,8},{1,9},{2,10},{3,11},{4,12},{5,13},{6,14},{7,15},{8,0},{9,1},... | collective-permute-start | bytes 608264 | tf_op jit(solution)/shard_map/ppermute | solution.py:310
  19.1 109.1 %collective-permute-start = (bf16[24,4224]{1,0:T(8,128)(2,1)S(1)}, bf16[24,4224]{1,0:T(8,128)(2,1)S(1)}, u32[]{:S(2)}, u32[]{:S(2)}) collective-permute-start(bf16[24,4224]{1,0:T(8,128)(2,1)S(1)} %get-tuple-element.75), channel_id=1, source_target_pairs={{0,4},{1,5},{2,6},{3,7},{4,0},{5,1},{6,2},{7,3},{8,12},{9,13},{10,... | collective-permute-start | bytes 608264 | tf_op jit(solution)/shard_map/ppermute | solution.py:310
  128.3 11.3 %collective-permute-start.4 = (bf16[96,4224]{1,0:T(8,128)(2,1)S(1)}, bf16[96,4224]{1,0:T(8,128)(2,1)S(1)}, u32[]{:S(2)}, u32[]{:S(2)}) collective-permute-start(bf16[96,4224]{1,0:T(8,128)(2,1)S(1)} %pad_maximum_fusion.refs_0_), channel_id=1, source_target_pairs={{0,1},{1,0},{2,3},{3,2},{4,5},{5,4},{6,7},{7,6},{8,9},{9,8},{10,11... | collective-permute-start | bytes 2433032 | tf_op jit(solution)/shard_map/ppermute | solution.py:310
  128.3 20.9 %collective-permute-start.5 = (bf16[96,4224]{1,0:T(8,128)(2,1)S(1)}, bf16[96,4224]{1,0:T(8,128)(2,1)S(1)}, u32[]{:S(2)}, u32[]{:S(2)}) collective-permute-start(bf16[96,4224]{1,0:T(8,128)(2,1)S(1)} %pad_maximum_fusion.refs_0_), channel_id=1, source_target_pairs={{0,2},{1,3},{2,0},{3,1},{4,6},{5,7},{6,4},{7,5},{8,10},{9,11},{10,... | collective-permute-start | bytes 2433032 | tf_op jit(solution)/shard_map/ppermute | solution.py:310
  129.9 35.9 %collective-permute-start.6 = (bf16[96,4224]{1,0:T(8,128)(2,1)S(1)}, bf16[96,4224]{1,0:T(8,128)(2,1)S(1)}, u32[]{:S(2)}, u32[]{:S(2)}) collective-permute-start(bf16[96,4224]{1,0:T(8,128)(2,1)S(1)} %pad_maximum_fusion.refs_0_), channel_id=1, source_target_pairs={{0,3},{1,2},{2,1},{3,0},{4,7},{5,6},{6,5},{7,4},{8,11},{9,10},{10,... | collective-permute-start | bytes 2433032 | tf_op jit(solution)/shard_map/ppermute | solution.py:310
  130.2 9.4 %collective-permute-start.3 = (s32[1,128]{1,0:T(1,128)S(1)}, s32[1,128]{1,0:T(1,128)S(1)}, u32[]{:S(2)}, u32[]{:S(2)}) collective-permute-start(s32[1,128]{1,0:T(1,128)S(1)} %get-tuple-element.79), channel_id=1, source_target_pairs={{0,16},{16,0},{1,17},{17,1},{2,18},{18,2},{3,19},{19,3},{4,20},{20... | collective-permute-start | bytes 1544 | tf_op jit(solution)/shard_map/ppermute | solution.py:368
  170.7 23.2 %copy-start.1 = (f32[256,512]{1,0:T(8,128)S(1)}, f32[256,512]{1,0:T(8,128)}, u32[]{:S(2)}) copy-start(f32[256,512]{1,0:T(8,128)} %fusion.9.base_ref) | copy-start | bytes 1572868
  170.7 24.9 %copy-start.2 = (bf16[16,16,512]{2,1,0:T(8,128)(2,1)S(1)}, bf16[16,16,512]{2,1,0:T(8,128)(2,1)}, u32[]{:S(2)}) copy-start(bf16[16,16,512]{2,1,0:T(8,128)(2,1)} %param.11) | copy-start | bytes 786436
  170.7 24.9 %copy-start.3 = (s32[256,1]{0,1:T(1,128)S(1)}, s32[256,1]{0,1:T(1,128)}, u32[]{:S(2)}) copy-start(s32[256,1]{0,1:T(1,128)} %param.12) | copy-start | bytes 3076
  170.7 24.9 %copy-start.4 = (s32[256]{0:T(256)S(1)}, s32[256]{0:T(256)}, u32[]{:S(2)}) copy-start(s32[256]{0:T(256)} %param.13) | copy-start | bytes 3076
  177.3 5.7 %collective-permute-start.9 = (bf16[64,512]{1,0:T(8,128)(2,1)S(1)}, bf16[64,512]{1,0:T(8,128)(2,1)S(1)}, u32[]{:S(2)}, u32[]{:S(2)}) collective-permute-start(bf16[64,512]{1,0:T(8,128)(2,1)S(1)} %get-tuple-element.95), channel_id=1, source_target_pairs={{0,3},{1,2},{2,1},{3,0},{4,7},{5,6},{6,5},{7,4},{8,11},{9,10},{10,... | collective-permute-start | bytes 196616 | tf_op jit(solution)/shard_map/ppermute | solution.py:310
  178.7 4.5 %collective-permute-start.8 = (bf16[64,512]{1,0:T(8,128)(2,1)S(1)}, bf16[64,512]{1,0:T(8,128)(2,1)S(1)}, u32[]{:S(2)}, u32[]{:S(2)}) collective-permute-start(bf16[64,512]{1,0:T(8,128)(2,1)S(1)} %get-tuple-element.94), channel_id=1, source_target_pairs={{0,2},{1,3},{2,0},{3,1},{4,6},{5,7},{6,4},{7,5},{8,10},{9,11},{10,... | collective-permute-start | bytes 196616 | tf_op jit(solution)/shard_map/ppermute | solution.py:310
  179.3 3.9 %collective-permute-start.7 = (bf16[64,512]{1,0:T(8,128)(2,1)S(1)}, bf16[64,512]{1,0:T(8,128)(2,1)S(1)}, u32[]{:S(2)}, u32[]{:S(2)}) collective-permute-start(bf16[64,512]{1,0:T(8,128)(2,1)S(1)} %get-tuple-element.93), channel_id=1, source_target_pairs={{0,1},{1,0},{2,3},{3,2},{4,5},{5,4},{6,7},{7,6},{8,9},{9,8},{10,11... | collective-permute-start | bytes 196616 | tf_op jit(solution)/shard_map/ppermute | solution.py:310
  179.3 14.6 %all-to-all-start.4 = ((bf16[16,16,512]{2,1,0:T(8,128)(2,1)}), bf16[16,16,512]{2,1,0:T(8,128)(2,1)S(1)}, u32[]{:S(2)}, u32[]{:S(2)}) async-start(bf16[16,16,512]{2,1,0:T(8,128)(2,1)} %bitcast.22), calls=%async_computation.4 | async-start | bytes 524288 | tf_op jit(solution)/shard_map/all_to_all | solution.py:398
  183.2 6.3 %collective-permute-start.10 = (bf16[16,512]{1,0:T(8,128)(2,1)S(1)}, bf16[16,512]{1,0:T(8,128)(2,1)S(1)}, u32[]{:S(2)}, u32[]{:S(2)}) collective-permute-start(bf16[16,512]{1,0:T(8,128)(2,1)S(1)} %get-tuple-element.103), channel_id=1, source_target_pairs={{0,4},{1,5},{2,6},{3,7},{4,0},{5,1},{6,2},{7,3},{8,12},{9,13},{10,... | collective-permute-start | bytes 49160 | tf_op jit(solution)/shard_map/ppermute | solution.py:310
  185.1 8.8 %collective-permute-start.11 = (bf16[16,512]{1,0:T(8,128)(2,1)S(1)}, bf16[16,512]{1,0:T(8,128)(2,1)S(1)}, u32[]{:S(2)}, u32[]{:S(2)}) collective-permute-start(bf16[16,512]{1,0:T(8,128)(2,1)S(1)} %get-tuple-element.102), channel_id=1, source_target_pairs={{0,8},{1,9},{2,10},{3,11},{4,12},{5,13},{6,14},{7,15},{8,0},{9,1},... | collective-permute-start | bytes 49160 | tf_op jit(solution)/shard_map/ppermute | solution.py:310
  187.5 6.5 %collective-permute-start.12 = (bf16[16,512]{1,0:T(8,128)(2,1)S(1)}, bf16[16,512]{1,0:T(8,128)(2,1)S(1)}, u32[]{:S(2)}, u32[]{:S(2)}) collective-permute-start(bf16[16,512]{1,0:T(8,128)(2,1)S(1)} %get-tuple-element.101), channel_id=1, source_target_pairs={{0,12},{1,13},{2,14},{3,15},{4,8},{5,9},{6,10},{7,11},{8,4},{9,5},... | collective-permute-start | bytes 49160 | tf_op jit(solution)/shard_map/ppermute | solution.py:310

commit v9 on v8

--- a/solution.py
+++ b/solution.py
@@ -382,7 +382,7 @@
         [(16 * planes, width)] * PLANE,
         (first, down, up, flag, *shared),
         [SMEM, ANY] + [VMEM] * 6,
-        2 * 384 * depth * local * rank,
+        10**12,
         6 * 2**20,
         [pltpu.VMEM(down.shape, jnp.bfloat16), pltpu.SemaphoreType.DMA((depth // STEP,))],
     )

time: 196 us -> 144 us (0.73)
  waiting for transfers between devices: 141 us -> 85.6 us
  starting transfers between devices: 25.5 us -> 28.5 us
    ppermute x12, waiting for transfers between devices: 141 us -> 85.6 us  [swap(): return lax.ppermute(x, 'ad', [(s, s ^ k) for s in range(count)])]
    all_to_all x1, starting transfers between devices: 3.75 us -> 6.78 us  [on_device(): lax.all_to_all(delta.reshape(count, room, width), 'ad', split_axis=0, con...]
  transfers between devices with their start and end apart: 15 -> 15, of which waited for: 7 -> 5; matrix products, arithmetic and copies ran while one was open for 4% -> 6% of each run, Pallas kernels for 3% -> 6%
where the time goes in v9:
time: 144 us; the launch traced here: 143 us
  waiting for transfers between devices  85.6 us (59%)
  starting transfers between devices  28.5 us (20%)
  Pallas kernels  20.4 us (14%)
  matrix products  7.85 us (5%)
    ppermute x12, waiting for transfers between devices, swap(): return lax.ppermute(x, 'ad', [(s, s ^ k) for s in range(count)])  85.6 us
    ppermute x12, starting transfers between devices, swap(): return lax.ppermute(x, 'ad', [(s, s ^ k) for s in range(count)])  14.1 us
    dot_general x1, matrix products, on_device(): jnp.dot(tokens, value_weight, preferred_element_type=jnp.float32)  7.85 us
    all_to_all x1, starting transfers between devices, on_device(): lax.all_to_all(delta.reshape(count, room, width), 'ad', split_axis=0, con...  6.78 us
    pallas_call x1, Pallas kernels, adapt(): pl.pallas_call(functools.partial(adapt_body, rank), in_specs=[SMEM, ANY,...  6.55 us
    all_to_all x1, starting transfers between devices, on_device(): lax.all_to_all(blocks.reshape(count, room, depth + NOTE), 'ad', split_axi...  6.13 us
    pallas_call x1, Pallas kernels, call(): pl.pallas_call(body, in_specs=specs, out_specs=[VMEM] * len(outs), out_sh...  4.89 us
    pallas_call x1, Pallas kernels, pack(): pl.pallas_call(pack_body, in_specs=[VMEM, VMEM, ANY], out_specs=pl.BlockS...  4.09 us
  transfers between devices with their start and end apart: 15, of which 5 were waited for; matrix products, arithmetic and copies ran while one was open for 6% of the time, Pallas kernels for 6%

profile of v9, /device:TPU:0, one launch (start us, length us, event | category | flops | bytes accessed | tf_op | source)
XLA Modules:
  0.0 143.3 jit_solution(5470195968963698195)
XLA Ops:
  0.0 3.8 %shard_map.66 = (bf16[24,4224]{1,0:T(8,128)(2,1)S(1)}, bf16[24,4224]{1,0:T(8,128)(2,1)S(1)}, bf16[24,4224]{1,0:T(8,128)(2,1)S(1)}, bf16[24,4224]{1,0:T(8,128)(2,...) custom-call(s32[1]{0:T(128)} %bitcast.12.me_ref, s32[1,256]{1,0:T(1,128)} %bitcast.52, ...), custom_call_target="tpu_custom_call" | custom-call | flops 805306368 | bytes 6291456 | tf_op jit(solution)/shard_map/pallas_call | solution.py:339
  3.9 5.1 %collective-permute-start.2 = (bf16[24,4224]{1,0:T(8,128)(2,1)S(1)}, bf16[24,4224]{1,0:T(8,128)(2,1)S(1)}, u32[]{:S(2)}, u32[]{:S(2)}) collective-permute-start(bf16[24,4224]{1,0:T(8,128)(2,1)S(1)} %get-tuple-element.77), channel_id=1, source_target_pairs={{0,12},{1,13},{2,14},{3,15},{4,8},{5,9},{6,10},{7,11},{8,4},{9,5},... | collective-permute-start | bytes 608264 | tf_op jit(solution)/shard_map/ppermute | solution.py:310
  9.0 0.6 collective-permute-start
  9.6 4.1 %shard_map.67 = bf16[256,8320]{1,0:T(8,128)(2,1)} custom-call(s32[1,256]{1,0:T(1,128)S(1)} %get-tuple-element.72.at_ref, bf16[128,256]{1,0:T(8,128)(2,1)S(1)} %get-tuple-element.73.note_ref, bf16[256,8192]{1,0:T(8,128)(2,1)S(1)} %copy-done), custom_call_target="tpu_custom_call" | custom-call | flops 1073741824 | bytes 8388608 | tf_op jit(solution)/shard_map/pallas_call | solution.py:159
  13.7 6.1 %all-to-all-start.3 = ((bf16[16,16,8320]{2,1,0:T(8,128)(2,1)}), bf16[16,16,8320]{2,1,0:T(8,128)(2,1)}, u32[]{:S(2)}, u32[]{:S(2)}) async-start(bf16[16,16,8320]{2,1,0:T(8,128)(2,1)} %bitcast.36), calls=%async_computation.3 | async-start | bytes 8519680 | tf_op jit(solution)/shard_map/all_to_all | solution.py:372
  19.9 30.3 %collective-permute-done.1 = bf16[24,4224]{1,0:T(8,128)(2,1)S(1)} collective-permute-done((bf16[24,4224]{1,0:T(8,128)(2,1)S(1)}, bf16[24,4224]{1,0:T(8,128)(2,1)S(1)}, u32[]{:S(2)}, u32[]{:S(2)}) %collective-permute-start.1) | collective-permute-done | bytes 202784 | tf_op jit(solution)/shard_map/ppermute | solution.py:310
  50.2 0.1 collective-permute-start.4
  50.3 0.1 collective-permute-start.5
  50.4 1.8 %collective-permute-start.6 = (bf16[96,4224]{1,0:T(8,128)(2,1)S(1)}, bf16[96,4224]{1,0:T(8,128)(2,1)S(1)}, u32[]{:S(2)}, u32[]{:S(2)}) collective-permute-start(bf16[96,4224]{1,0:T(8,128)(2,1)S(1)} %pad_maximum_fusion.refs_0_), channel_id=1, source_target_pairs={{0,3},{1,2},{2,1},{3,0},{4,7},{5,6},{6,5},{7,4},{8,11},{9,10},{10,... | collective-permute-start | bytes 2433032 | tf_op jit(solution)/shard_map/ppermute | solution.py:310
  52.2 1.5 %collective-permute-start.3 = (s32[1,128]{1,0:T(1,128)S(1)}, s32[1,128]{1,0:T(1,128)S(1)}, u32[]{:S(2)}, u32[]{:S(2)}) collective-permute-start(s32[1,128]{1,0:T(1,128)S(1)} %get-tuple-element.79), channel_id=1, source_target_pairs={{0,16},{16,0},{1,17},{17,1},{2,18},{18,2},{3,19},{19,3},{4,20},{20... | collective-permute-start | bytes 1544 | tf_op jit(solution)/shard_map/ppermute | solution.py:368
  53.7 7.8 %fusion.9.base_ref = f32[256,512]{1,0:T(8,128)} fusion(bf16[256,8192]{1,0:T(8,128)(2,1)} %tokens_hbm.3, bf16[8192,512]{1,0:T(8,128)(2,1)} %param.9), kind=kOutput, calls=%fused_computation.36 | convolution fusion | flops 2147483648 | bytes 13107200 | tf_op jit(solution)/shard_map/dot_general | solution.py:330
  61.5 24.4 %collective-permute-done.5.refs_2_ = bf16[96,4224]{1,0:T(8,128)(2,1)S(1)} collective-permute-done((bf16[96,4224]{1,0:T(8,128)(2,1)S(1)}, bf16[96,4224]{1,0:T(8,128)(2,1)S(1)}, u32[]{:S(2)}, u32[]{:S(2)}) %collective-permute-start.5) | collective-permute-done | bytes 811040 | tf_op jit(solution)/shard_map/ppermute | solution.py:310
  86.0 24.5 %collective-permute-done.6.refs_3_ = bf16[96,4224]{1,0:T(8,128)(2,1)S(1)} collective-permute-done((bf16[96,4224]{1,0:T(8,128)(2,1)S(1)}, bf16[96,4224]{1,0:T(8,128)(2,1)S(1)}, u32[]{:S(2)}, u32[]{:S(2)}) %collective-permute-start.6) | collective-permute-done | bytes 811040 | tf_op jit(solution)/shard_map/ppermute | solution.py:310
  110.4 4.9 %shard_map.68 = (bf16[64,512]{1,0:T(8,128)(2,1)S(1)}, bf16[64,512]{1,0:T(8,128)(2,1)S(1)}, bf16[64,512]{1,0:T(8,128)(2,1)S(1)}, bf16[64,512]{1,0:T(8,128)(2,1)S(1)}) custom-call(s32[1]{0:T(128)} %bitcast.17.first_ref, bf16[256,8192]{1,0:T(8,128)(2,1)} %bitcast.38, bf16[256,512]{1,0:T(8,128)(2,1)} %bitcast.44, s32[1,128]{1,0:T(1,128)S(1)} %max.3.flag_ref, ...), custom_call_target="tpu_custom_call" | custom-call | flops 999999995904 | bytes 6291456 | tf_op jit(solution)/shard_map/pallas_call | solution.py:297
  115.4 6.6 %shard_map.69 = bf16[256,512]{1,0:T(8,128)(2,1)} custom-call(s32[1]{0:T(128)} %bitcast.17.first_ref, bf16[256,8192]{1,0:T(8,128)(2,1)} %bitcast.39, bf16[256,512]{1,0:T(8,128)(2,1)} %bitcast.45, bf16[256,8320]{1,0:T(8,128)(2,1)} %bitcast.16.rows_hbm), custom_call_target="tpu_custom_call" | custom-call | flops 1073741824 | bytes 8388608 | tf_op jit(solution)/shard_map/pallas_call | solution.py:216
  122.0 0.4 collective-permute-start.9
  122.3 1.6 %collective-permute-start.8 = (bf16[64,512]{1,0:T(8,128)(2,1)S(1)}, bf16[64,512]{1,0:T(8,128)(2,1)S(1)}, u32[]{:S(2)}, u32[]{:S(2)}) collective-permute-start(bf16[64,512]{1,0:T(8,128)(2,1)S(1)} %get-tuple-element.94), channel_id=1, source_target_pairs={{0,2},{1,3},{2,0},{3,1},{4,6},{5,7},{6,4},{7,5},{8,10},{9,11},{10,... | collective-permute-start | bytes 196616 | tf_op jit(solution)/shard_map/ppermute | solution.py:310
  123.9 6.8 %all-to-all-start.4 = ((bf16[16,16,512]{2,1,0:T(8,128)(2,1)}), bf16[16,16,512]{2,1,0:T(8,128)(2,1)S(1)}, u32[]{:S(2)}, u32[]{:S(2)}) async-start(bf16[16,16,512]{2,1,0:T(8,128)(2,1)} %bitcast.22), calls=%async_computation.4 | async-start | bytes 524288 | tf_op jit(solution)/shard_map/all_to_all | solution.py:398
  130.8 2.0 %collective-permute-start.10 = (bf16[16,512]{1,0:T(8,128)(2,1)S(1)}, bf16[16,512]{1,0:T(8,128)(2,1)S(1)}, u32[]{:S(2)}, u32[]{:S(2)}) collective-permute-start(bf16[16,512]{1,0:T(8,128)(2,1)S(1)} %get-tuple-element.103), channel_id=1, source_target_pairs={{0,4},{1,5},{2,6},{3,7},{4,0},{5,1},{6,2},{7,3},{8,12},{9,13},{10,... | collective-permute-start | bytes 49160 | tf_op jit(solution)/shard_map/ppermute | solution.py:310
  132.8 2.4 %collective-permute-start.11 = (bf16[16,512]{1,0:T(8,128)(2,1)S(1)}, bf16[16,512]{1,0:T(8,128)(2,1)S(1)}, u32[]{:S(2)}, u32[]{:S(2)}) collective-permute-start(bf16[16,512]{1,0:T(8,128)(2,1)S(1)} %get-tuple-element.102), channel_id=1, source_target_pairs={{0,8},{1,9},{2,10},{3,11},{4,12},{5,13},{6,14},{7,15},{8,0},{9,1},... | collective-permute-start | bytes 49160 | tf_op jit(solution)/shard_map/ppermute | solution.py:310
  135.1 0.1 collective-permute-start.12
  135.2 1.9 %collective-permute-done.10.refs_1_ = bf16[16,512]{1,0:T(8,128)(2,1)S(1)} collective-permute-done((bf16[16,512]{1,0:T(8,128)(2,1)S(1)}, bf16[16,512]{1,0:T(8,128)(2,1)S(1)}, u32[]{:S(2)}, u32[]{:S(2)}) %collective-permute-start.10) | collective-permute-done | bytes 16416 | tf_op jit(solution)/shard_map/ppermute | solution.py:310
  137.1 4.5 %collective-permute-done.11.refs_2_ = bf16[16,512]{1,0:T(8,128)(2,1)S(1)} collective-permute-done((bf16[16,512]{1,0:T(8,128)(2,1)S(1)}, bf16[16,512]{1,0:T(8,128)(2,1)S(1)}, u32[]{:S(2)}, u32[]{:S(2)}) %collective-permute-start.11) | collective-permute-done | bytes 16416 | tf_op jit(solution)/shard_map/ppermute | solution.py:310
  141.6 1.0 shard_map.70
  (31 shorter events, 0.2 us)
Async XLA Ops:
  0.0 9.6 %copy-start = (bf16[256,8192]{1,0:T(8,128)(2,1)S(1)}, bf16[256,8192]{1,0:T(8,128)(2,1)}, u32[]{:S(2)}) copy-start(bf16[256,8192]{1,0:T(8,128)(2,1)} %tokens_hbm.3) | copy-start | bytes 12582916
  3.9 9.9 %copy-start.3 = (s32[1,256]{1,0:T(1,128)}, s32[1,256]{1,0:T(1,128)S(1)}, u32[]{:S(2)}) copy-start(s32[1,256]{1,0:T(1,128)S(1)} %get-tuple-element.72.at_ref) | copy-start | bytes 3076
  3.9 16.0 %collective-permute-start.2 = (bf16[24,4224]{1,0:T(8,128)(2,1)S(1)}, bf16[24,4224]{1,0:T(8,128)(2,1)S(1)}, u32[]{:S(2)}, u32[]{:S(2)}) collective-permute-start(bf16[24,4224]{1,0:T(8,128)(2,1)S(1)} %get-tuple-element.77), channel_id=1, source_target_pairs={{0,12},{1,13},{2,14},{3,15},{4,8},{5,9},{6,10},{7,11},{8,4},{9,5},... | collective-permute-start | bytes 608264 | tf_op jit(solution)/shard_map/ppermute | solution.py:310
  9.0 41.2 %collective-permute-start.1 = (bf16[24,4224]{1,0:T(8,128)(2,1)S(1)}, bf16[24,4224]{1,0:T(8,128)(2,1)S(1)}, u32[]{:S(2)}, u32[]{:S(2)}) collective-permute-start(bf16[24,4224]{1,0:T(8,128)(2,1)S(1)} %get-tuple-element.76), channel_id=1, source_target_pairs={{0,8},{1,9},{2,10},{3,11},{4,12},{5,13},{6,14},{7,15},{8,0},{9,1},... | collective-permute-start | bytes 608264 | tf_op jit(solution)/shard_map/ppermute | solution.py:310
  9.0 41.2 %collective-permute-start = (bf16[24,4224]{1,0:T(8,128)(2,1)S(1)}, bf16[24,4224]{1,0:T(8,128)(2,1)S(1)}, u32[]{:S(2)}, u32[]{:S(2)}) collective-permute-start(bf16[24,4224]{1,0:T(8,128)(2,1)S(1)} %get-tuple-element.75), channel_id=1, source_target_pairs={{0,4},{1,5},{2,6},{3,7},{4,0},{5,1},{6,2},{7,3},{8,12},{9,13},{10,... | collective-permute-start | bytes 608264 | tf_op jit(solution)/shard_map/ppermute | solution.py:310
  13.7 101.6 %all-to-all-start.3 = ((bf16[16,16,8320]{2,1,0:T(8,128)(2,1)}), bf16[16,16,8320]{2,1,0:T(8,128)(2,1)}, u32[]{:S(2)}, u32[]{:S(2)}) async-start(bf16[16,16,8320]{2,1,0:T(8,128)(2,1)} %bitcast.36), calls=%async_computation.3 | async-start | bytes 8519680 | tf_op jit(solution)/shard_map/all_to_all | solution.py:372
  50.2 11.3 %collective-permute-start.4 = (bf16[96,4224]{1,0:T(8,128)(2,1)S(1)}, bf16[96,4224]{1,0:T(8,128)(2,1)S(1)}, u32[]{:S(2)}, u32[]{:S(2)}) collective-permute-start(bf16[96,4224]{1,0:T(8,128)(2,1)S(1)} %pad_maximum_fusion.refs_0_), channel_id=1, source_target_pairs={{0,1},{1,0},{2,3},{3,2},{4,5},{5,4},{6,7},{7,6},{8,9},{9,8},{10,11... | collective-permute-start | bytes 2433032 | tf_op jit(solution)/shard_map/ppermute | solution.py:310
  50.3 35.6 %collective-permute-start.5 = (bf16[96,4224]{1,0:T(8,128)(2,1)S(1)}, bf16[96,4224]{1,0:T(8,128)(2,1)S(1)}, u32[]{:S(2)}, u32[]{:S(2)}) collective-permute-start(bf16[96,4224]{1,0:T(8,128)(2,1)S(1)} %pad_maximum_fusion.refs_0_), channel_id=1, source_target_pairs={{0,2},{1,3},{2,0},{3,1},{4,6},{5,7},{6,4},{7,5},{8,10},{9,11},{10,... | collective-permute-start | bytes 2433032 | tf_op jit(solution)/shard_map/ppermute | solution.py:310
  50.4 60.0 %collective-permute-start.6 = (bf16[96,4224]{1,0:T(8,128)(2,1)S(1)}, bf16[96,4224]{1,0:T(8,128)(2,1)S(1)}, u32[]{:S(2)}, u32[]{:S(2)}) collective-permute-start(bf16[96,4224]{1,0:T(8,128)(2,1)S(1)} %pad_maximum_fusion.refs_0_), channel_id=1, source_target_pairs={{0,3},{1,2},{2,1},{3,0},{4,7},{5,6},{6,5},{7,4},{8,11},{9,10},{10,... | collective-permute-start | bytes 2433032 | tf_op jit(solution)/shard_map/ppermute | solution.py:310
  52.2 9.3 %collective-permute-start.3 = (s32[1,128]{1,0:T(1,128)S(1)}, s32[1,128]{1,0:T(1,128)S(1)}, u32[]{:S(2)}, u32[]{:S(2)}) collective-permute-start(s32[1,128]{1,0:T(1,128)S(1)} %get-tuple-element.79), channel_id=1, source_target_pairs={{0,16},{16,0},{1,17},{17,1},{2,18},{18,2},{3,19},{19,3},{4,20},{20... | collective-permute-start | bytes 1544 | tf_op jit(solution)/shard_map/ppermute | solution.py:368
  115.4 26.2 %copy-start.1 = (f32[256,512]{1,0:T(8,128)S(1)}, f32[256,512]{1,0:T(8,128)}, u32[]{:S(2)}) copy-start(f32[256,512]{1,0:T(8,128)} %fusion.9.base_ref) | copy-start | bytes 1572868
  115.4 26.2 %copy-start.4 = (s32[1,256]{1,0:T(1,128)S(1)}, s32[1,256]{1,0:T(1,128)}, u32[]{:S(2)}) copy-start(s32[1,256]{1,0:T(1,128)} %copy-done.3) | copy-start | bytes 3076
  115.4 27.9 %copy-start.2 = (bf16[16,16,512]{2,1,0:T(8,128)(2,1)S(1)}, bf16[16,16,512]{2,1,0:T(8,128)(2,1)}, u32[]{:S(2)}) copy-start(bf16[16,16,512]{2,1,0:T(8,128)(2,1)} %param.11) | copy-start | bytes 786436
  115.4 27.9 %copy-start.5 = (s32[256,1]{0,1:T(1,128)S(1)}, s32[256,1]{0,1:T(1,128)}, u32[]{:S(2)}) copy-start(s32[256,1]{0,1:T(1,128)} %param.12) | copy-start | bytes 3076
  115.4 27.9 %copy-start.6 = (s32[256]{0:T(256)S(1)}, s32[256]{0:T(256)}, u32[]{:S(2)}) copy-start(s32[256]{0:T(256)} %param.13) | copy-start | bytes 3076
  122.0 8.7 %collective-permute-start.9 = (bf16[64,512]{1,0:T(8,128)(2,1)S(1)}, bf16[64,512]{1,0:T(8,128)(2,1)S(1)}, u32[]{:S(2)}, u32[]{:S(2)}) collective-permute-start(bf16[64,512]{1,0:T(8,128)(2,1)S(1)} %get-tuple-element.95), channel_id=1, source_target_pairs={{0,3},{1,2},{2,1},{3,0},{4,7},{5,6},{6,5},{7,4},{8,11},{9,10},{10,... | collective-permute-start | bytes 196616 | tf_op jit(solution)/shard_map/ppermute | solution.py:310
  122.3 8.4 %collective-permute-start.8 = (bf16[64,512]{1,0:T(8,128)(2,1)S(1)}, bf16[64,512]{1,0:T(8,128)(2,1)S(1)}, u32[]{:S(2)}, u32[]{:S(2)}) collective-permute-start(bf16[64,512]{1,0:T(8,128)(2,1)S(1)} %get-tuple-element.94), channel_id=1, source_target_pairs={{0,2},{1,3},{2,0},{3,1},{4,6},{5,7},{6,4},{7,5},{8,10},{9,11},{10,... | collective-permute-start | bytes 196616 | tf_op jit(solution)/shard_map/ppermute | solution.py:310
  123.9 6.8 %collective-permute-start.7 = (bf16[64,512]{1,0:T(8,128)(2,1)S(1)}, bf16[64,512]{1,0:T(8,128)(2,1)S(1)}, u32[]{:S(2)}, u32[]{:S(2)}) collective-permute-start(bf16[64,512]{1,0:T(8,128)(2,1)S(1)} %get-tuple-element.93), channel_id=1, source_target_pairs={{0,1},{1,0},{2,3},{3,2},{4,5},{5,4},{6,7},{7,6},{8,9},{9,8},{10,11... | collective-permute-start | bytes 196616 | tf_op jit(solution)/shard_map/ppermute | solution.py:310
  123.9 17.7 %all-to-all-start.4 = ((bf16[16,16,512]{2,1,0:T(8,128)(2,1)}), bf16[16,16,512]{2,1,0:T(8,128)(2,1)S(1)}, u32[]{:S(2)}, u32[]{:S(2)}) async-start(bf16[16,16,512]{2,1,0:T(8,128)(2,1)} %bitcast.22), calls=%async_computation.4 | async-start | bytes 524288 | tf_op jit(solution)/shard_map/all_to_all | solution.py:398
  130.8 6.3 %collective-permute-start.10 = (bf16[16,512]{1,0:T(8,128)(2,1)S(1)}, bf16[16,512]{1,0:T(8,128)(2,1)S(1)}, u32[]{:S(2)}, u32[]{:S(2)}) collective-permute-start(bf16[16,512]{1,0:T(8,128)(2,1)S(1)} %get-tuple-element.103), channel_id=1, source_target_pairs={{0,4},{1,5},{2,6},{3,7},{4,0},{5,1},{6,2},{7,3},{8,12},{9,13},{10,... | collective-permute-start | bytes 49160 | tf_op jit(solution)/shard_map/ppermute | solution.py:310
  132.8 8.8 %collective-permute-start.11 = (bf16[16,512]{1,0:T(8,128)(2,1)S(1)}, bf16[16,512]{1,0:T(8,128)(2,1)S(1)}, u32[]{:S(2)}, u32[]{:S(2)}) collective-permute-start(bf16[16,512]{1,0:T(8,128)(2,1)S(1)} %get-tuple-element.102), channel_id=1, source_target_pairs={{0,8},{1,9},{2,10},{3,11},{4,12},{5,13},{6,14},{7,15},{8,0},{9,1},... | collective-permute-start | bytes 49160 | tf_op jit(solution)/shard_map/ppermute | solution.py:310
  135.1 6.5 %collective-permute-start.12 = (bf16[16,512]{1,0:T(8,128)(2,1)S(1)}, bf16[16,512]{1,0:T(8,128)(2,1)S(1)}, u32[]{:S(2)}, u32[]{:S(2)}) collective-permute-start(bf16[16,512]{1,0:T(8,128)(2,1)S(1)} %get-tuple-element.101), channel_id=1, source_target_pairs={{0,12},{1,13},{2,14},{3,15},{4,8},{5,9},{6,10},{7,11},{8,4},{9,5},... | collective-permute-start | bytes 49160 | tf_op jit(solution)/shard_map/ppermute | solution.py:310

commit v10 on v9

--- a/solution.py
+++ b/solution.py
@@ -13,7 +13,7 @@
 SPARE = 12
 NOTE = 128
 STEP = 1024
-WIDE = 1664
+PARTS = 8
 VMEM = pl.BlockSpec(memory_space=pltpu.VMEM)
 ANY = pl.BlockSpec(memory_space=pl.ANY)
 SMEM = pl.BlockSpec(memory_space=pltpu.SMEM)
@@ -50,6 +50,16 @@
     )
 
 
+def row_copies(source, target, sems, parts):
+    rows = target.shape[0] // parts
+    return [
+        pltpu.make_async_copy(
+            source.at[i * rows : (i + 1) * rows], target.at[i * rows : (i + 1) * rows], sems.at[i]
+        )
+        for i in range(parts)
+    ]
+
+
 def one_hot(hit):
     return hit.astype(jnp.float32).astype(jnp.bfloat16)
 
@@ -62,11 +72,7 @@
 def route_body(room, local, me_ref, tenant_ref, slot_ref, tokens_hbm, *refs):
     *outs, at_ref, note_ref, left_ref, tokens_ref, sems = refs
     half = tokens_ref.shape[1] // 2
-    spans = [slice(h + c, h + c + STEP) for c in range(0, half, STEP) for h in (0, half)]
-    copies = [
-        pltpu.make_async_copy(tokens_hbm.at[:, span], tokens_ref.at[:, span], sems.at[i])
-        for i, span in enumerate(spans)
-    ]
+    copies = row_copies(tokens_hbm, tokens_ref, sems, PARTS)
     for copy in copies:
         copy.start()
     tenant = tenant_ref[...]
@@ -107,9 +113,9 @@
             outs[b][:, columns] = value[2 * SPARE * b : 2 * SPARE * (b + 1)].astype(jnp.bfloat16)
 
     put(notes_of(one_hot(hit), note), slice(half, half + NOTE))
-    for i, c in enumerate(range(0, half, STEP)):
-        copies[2 * i].wait()
-        copies[2 * i + 1].wait()
+    for copy in copies:
+        copy.wait()
+    for c in range(0, half, STEP):
         put(
             jnp.dot(first, tokens_ref[:, c : c + STEP], preferred_element_type=jnp.float32)
             + jnp.dot(
@@ -127,28 +133,21 @@
     )
 
 
-def pack_body(at_ref, note_ref, tokens_hbm, out_hbm, tokens_ref, out_ref, sems, out_sems):
+def pack_body(at_ref, note_ref, tokens_ref, out_hbm, out_ref, sems):
     depth = tokens_ref.shape[1]
-    spans = [slice(c, c + STEP) for c in range(0, depth, STEP)]
-    loads = [
-        pltpu.make_async_copy(tokens_hbm.at[:, span], tokens_ref.at[:, span], sems.at[i])
-        for i, span in enumerate(spans)
-    ]
-    for load in loads:
-        load.start()
-    pick = lax.broadcasted_iota(jnp.int32, (out_ref.shape[0], at_ref.shape[1]), 0) == at_ref[...]
-    pick = one_hot(pick)
-    out_ref[:, depth:] = notes_of(pick, note_ref[...]).astype(jnp.bfloat16)
-    stores = []
-    for i, span in enumerate(spans):
-        loads[i].wait()
-        out_ref[:, span] = jnp.dot(
-            pick, tokens_ref[:, span], preferred_element_type=jnp.float32
-        ).astype(jnp.bfloat16)
-        ready = slice(span.start, span.stop if i + 1 < len(spans) else depth + NOTE)
-        store = pltpu.make_async_copy(out_ref.at[:, ready], out_hbm.at[:, ready], out_sems.at[i])
-        store.start()
-        stores.append(store)
+    stores = row_copies(out_ref, out_hbm, sems, PARTS)
+    half = out_ref.shape[0] // 2
+    row = lax.broadcasted_iota(jnp.int32, (half, at_ref.shape[1]), 0)
+    for h in range(2):
+        own = slice(h * half, (h + 1) * half)
+        pick = one_hot(row + h * half == at_ref[...])
+        for c in range(0, depth, STEP):
+            out_ref[own, c : c + STEP] = jnp.dot(
+                pick, tokens_ref[:, c : c + STEP], preferred_element_type=jnp.float32
+            ).astype(jnp.bfloat16)
+        out_ref[own, depth:] = notes_of(pick, note_ref[...]).astype(jnp.bfloat16)
+        for store in stores[h * PARTS // 2 : (h + 1) * PARTS // 2]:
+            store.start()
     for store in stores:
         store.wait()
 
@@ -158,14 +157,12 @@
     out = jax.ShapeDtypeStruct((main_rows, depth + NOTE), jnp.bfloat16)
     return pl.pallas_call(
         pack_body,
-        in_specs=[VMEM, VMEM, ANY],
+        in_specs=[VMEM, VMEM, VMEM],
         out_specs=pl.BlockSpec(memory_space=pltpu.HBM),
         out_shape=out,
         scratch_shapes=[
-            pltpu.VMEM(tokens.shape, jnp.bfloat16),
             pltpu.VMEM(out.shape, jnp.bfloat16),
-            pltpu.SemaphoreType.DMA((depth // STEP,)),
-            pltpu.SemaphoreType.DMA((depth // STEP,)),
+            pltpu.SemaphoreType.DMA((PARTS,)),
         ],
         compiler_params=pltpu.CompilerParams(vmem_limit_bytes=52 * 2**20),
         cost_estimate=pl.CostEstimate(
@@ -183,32 +180,27 @@
 def adapt_body(rank, first_ref, down_hbm, up_ref, rows_hbm, out, *scratch):
     down_ref, rows_ref, down_sems, sems = scratch
     depth = down_ref.shape[1]
-    spans = [slice(c, min(c + WIDE, depth + NOTE)) for c in range(0, depth + NOTE, WIDE)]
-    copies = []
-    for i, span in enumerate(spans):
-        kept = slice(span.start, min(span.stop, depth))
-        copies.append(
-            (
-                pltpu.make_async_copy(rows_hbm.at[:, span], rows_ref.at[:, span], sems.at[i]),
-                pltpu.make_async_copy(down_hbm.at[:, kept], down_ref.at[:, kept], down_sems.at[i]),
+    factors = row_copies(down_hbm, down_ref, down_sems, PARTS)
+    copies = row_copies(rows_hbm, rows_ref, sems, PARTS)
+    for copy in factors + copies:
+        copy.start()
+    for copy in factors:
+        copy.wait()
+    half = rows_ref.shape[0] // 2
+    for h in range(2):
+        for copy in copies[h * PARTS // 2 : (h + 1) * PARTS // 2]:
+            copy.wait()
+        own = slice(h * half, (h + 1) * half)
+        low = jnp.zeros((half, down_ref.shape[0]), jnp.float32)
+        for c in range(0, depth, STEP):
+            low += lax.dot_general(
+                rows_ref[own, c : c + STEP],
+                down_ref[:, c : c + STEP],
+                (((1,), (1,)), ((), ())),
+                preferred_element_type=jnp.float32,
             )
-        )
-    for pair in copies:
-        pair[0].start()
-        pair[1].start()
-    low = jnp.zeros((rows_ref.shape[0], down_ref.shape[0]), jnp.float32)
-    for pair, span in zip(copies, spans, strict=True):
-        pair[0].wait()
-        pair[1].wait()
-        span = slice(span.start, min(span.stop, depth))
-        low += lax.dot_general(
-            rows_ref[:, span],
-            down_ref[:, span],
-            (((1,), (1,)), ((), ())),
-            preferred_element_type=jnp.float32,
-        )
-    note = rows_ref[:, depth:].astype(jnp.float32)
-    out[...] = low_delta(low, note[:, :1], first_ref[0], rank, up_ref[...]).astype(jnp.bfloat16)
+        note = rows_ref[own, depth:].astype(jnp.float32)[:, :1]
+        out[own] = low_delta(low, note, first_ref[0], rank, up_ref[...]).astype(jnp.bfloat16)
 
 
 def adapt(rank, first, down, up, got):
@@ -221,8 +213,8 @@
         scratch_shapes=[
             pltpu.VMEM(down.shape, jnp.bfloat16),
             pltpu.VMEM(got.shape, jnp.bfloat16),
-            pltpu.SemaphoreType.DMA((pl.cdiv(got.shape[1], WIDE),)),
-            pltpu.SemaphoreType.DMA((pl.cdiv(got.shape[1], WIDE),)),
+            pltpu.SemaphoreType.DMA((PARTS,)),
+            pltpu.SemaphoreType.DMA((PARTS,)),
         ],
         compiler_params=pltpu.CompilerParams(vmem_limit_bytes=24 * 2**20),
         cost_estimate=pl.CostEstimate(
@@ -235,20 +227,16 @@
     rows_refs, outs = refs[:PLANE], refs[PLANE : 2 * PLANE]
     down_ref, sems = refs[2 * PLANE :]
     half = down_ref.shape[1] // 2
-    spans = [slice(h + c, h + c + STEP) for c in range(0, half, STEP) for h in (0, half)]
-    copies = [
-        pltpu.make_async_copy(down_hbm.at[:, span], down_ref.at[:, span], sems.at[i])
-        for i, span in enumerate(spans)
-    ]
+    copies = row_copies(down_hbm, down_ref, sems, PARTS)
     for copy in copies:
         copy.start()
     each = rows_refs[0].shape[0]
     shape = (PLANE * each, down_ref.shape[0])
     dims = (((1,), (1,)), ((), ()))
     low0, low1 = jnp.zeros(shape, jnp.float32), jnp.zeros(shape, jnp.float32)
-    for i, c in enumerate(range(0, half, STEP)):
-        copies[2 * i].wait()
-        copies[2 * i + 1].wait()
+    for copy in copies:
+        copy.wait()
+    for c in range(0, half, STEP):
         rows = jnp.concatenate([r[:, c : c + STEP] for r in rows_refs], axis=0)
         low0 += lax.dot_general(
             rows, down_ref[:, c : c + STEP], dims, preferred_element_type=jnp.float32
@@ -330,7 +318,7 @@
     base_value = jnp.dot(tokens, value_weight, preferred_element_type=jnp.float32)
     room = row_count // count
     planes = count // PLANE
-    if count != 16 or room != 16 or (depth + NOTE) % WIDE or depth % (2 * STEP):
+    if count != 16 or room != 16 or depth % (2 * STEP):
         slot, owner, place = route(tenant_ids, tenant_slot, local)
         delta = exchange(tokens, slot, owner, place, CAP * local, adapt_down, adapt_up)
         return (base_value + delta).astype(jnp.bfloat16)
@@ -348,7 +336,7 @@
         ],
         scratch_shapes=[
             pltpu.VMEM(tokens.shape, jnp.bfloat16),
-            pltpu.SemaphoreType.DMA((depth // STEP,)),
+            pltpu.SemaphoreType.DMA((PARTS,)),
         ],
         compiler_params=pltpu.CompilerParams(vmem_limit_bytes=24 * 2**20),
         cost_estimate=pl.CostEstimate(
@@ -377,6 +365,7 @@
     down = adapt_down.transpose(0, 2, 1).reshape(local * rank, depth)
     up = adapt_up.reshape(local * rank, width)
 
+    flag, base_value = lax.optimization_barrier((flag, base_value))
     over_delta = call(
         functools.partial(adapt_over_body, planes, rank),
         [(16 * planes, width)] * PLANE,
@@ -384,14 +373,14 @@
         [SMEM, ANY] + [VMEM] * 6,
         10**12,
         6 * 2**20,
-        [pltpu.VMEM(down.shape, jnp.bfloat16), pltpu.SemaphoreType.DMA((depth // STEP,))],
-    )
-    got, base_value, *over_delta = lax.optimization_barrier((got, base_value, *over_delta))
-    delta = adapt(rank, first, down, up, got)
-    delta, *over_delta = lax.optimization_barrier((delta, *over_delta))
+        [pltpu.VMEM(down.shape, jnp.bfloat16), pltpu.SemaphoreType.DMA((PARTS,))],
+    )
     over_sum = over_delta[0]
     for a in range(1, PLANE):
         over_sum = over_sum + swap(over_delta[a], a)
+    got, over_sum = lax.optimization_barrier((got, over_sum))
+    delta = adapt(rank, first, down, up, got)
+    delta, over_sum = lax.optimization_barrier((delta, over_sum))
     over_back = [over_sum[:16]]
     for b in range(1, planes):
         over_back.append(swap(over_sum[16 * b : 16 * (b + 1)], b * PLANE))

time: 144 us -> 152 us (1.056)
  starting transfers between devices: 28.5 us -> 34.5 us
  Pallas kernels: 20.4 us -> 23.4 us
    all_to_all x1, starting transfers between devices: 6.78 us -> 12.9 us  [on_device(): lax.all_to_all(delta.reshape(count, room, width), 'ad', split_axis=0, con...]
    pallas_call x1, Pallas kernels: 6.55 us -> 10.2 us  [adapt(): pl.pallas_call(functools.partial(adapt_body, rank), in_specs=[SMEM, ANY,...]
  transfers between devices with their start and end apart: 15 -> 15, of which waited for: 5 -> 6; matrix products, arithmetic and copies ran while one was open for 6% -> 5% of each run, Pallas kernels for 6% -> 5%
where the time goes in v10:
time: 152 us; the launch traced here: 151 us
  waiting for transfers between devices  84.6 us (56%)
  starting transfers between devices  34.5 us (23%)
  Pallas kernels  23.4 us (15%)
  matrix products  7.85 us (5%)
    ppermute x12, waiting for transfers between devices, swap(): return lax.ppermute(x, 'ad', [(s, s ^ k) for s in range(count)])  84.6 us
    ppermute x12, starting transfers between devices, swap(): return lax.ppermute(x, 'ad', [(s, s ^ k) for s in range(count)])  14 us
    all_to_all x1, starting transfers between devices, on_device(): lax.all_to_all(delta.reshape(count, room, width), 'ad', split_axis=0, con...  12.9 us
    pallas_call x1, Pallas kernels, adapt(): pl.pallas_call(functools.partial(adapt_body, rank), in_specs=[SMEM, ANY,...  10.2 us
    dot_general x1, matrix products, on_device(): jnp.dot(tokens, value_weight, preferred_element_type=jnp.float32)  7.85 us
    all_to_all x1, starting transfers between devices, on_device(): lax.all_to_all(blocks.reshape(count, room, depth + NOTE), 'ad', split_axi...  6.21 us
    pallas_call x1, Pallas kernels, call(): pl.pallas_call(body, in_specs=specs, out_specs=[VMEM] * len(outs), out_sh...  5.14 us
    pallas_call x1, Pallas kernels, on_device(): pl.pallas_call(functools.partial(route_body, room, local), in_specs=[SMEM...  4.12 us
  transfers between devices with their start and end apart: 15, of which 6 were waited for; matrix products, arithmetic and copies ran while one was open for 5% of the time, Pallas kernels for 5%

profile of v10, /device:TPU:0, one launch (start us, length us, event | category | flops | bytes accessed | tf_op | source)
XLA Modules:
  0.0 151.3 jit_solution(574520896518771860)
XLA Ops:
  0.0 4.1 %shard_map.66 = (bf16[24,4224]{1,0:T(8,128)(2,1)S(1)}, bf16[24,4224]{1,0:T(8,128)(2,1)S(1)}, bf16[24,4224]{1,0:T(8,128)(2,1)S(1)}, bf16[24,4224]{1,0:T(8,128)(2,...) custom-call(s32[1]{0:T(128)} %bitcast.12.me_ref, s32[1,256]{1,0:T(1,128)} %bitcast.52, ...), custom_call_target="tpu_custom_call" | custom-call | flops 805306368 | bytes 6291456 | tf_op jit(solution)/shard_map/pallas_call | solution.py:327
  4.1 3.1 %collective-permute-start = (bf16[24,4224]{1,0:T(8,128)(2,1)S(1)}, bf16[24,4224]{1,0:T(8,128)(2,1)S(1)}, u32[]{:S(2)}, u32[]{:S(2)}) collective-permute-start(bf16[24,4224]{1,0:T(8,128)(2,1)S(1)} %get-tuple-element.69), channel_id=1, source_target_pairs={{0,4},{1,5},{2,6},{3,7},{4,0},{5,1},{6,2},{7,3},{8,12},{9,13},{10,... | collective-permute-start | bytes 608264 | tf_op jit(solution)/shard_map/ppermute | solution.py:298
  7.2 2.6 %collective-permute-start.1 = (bf16[24,4224]{1,0:T(8,128)(2,1)S(1)}, bf16[24,4224]{1,0:T(8,128)(2,1)S(1)}, u32[]{:S(2)}, u32[]{:S(2)}) collective-permute-start(bf16[24,4224]{1,0:T(8,128)(2,1)S(1)} %get-tuple-element.70), channel_id=1, source_target_pairs={{0,8},{1,9},{2,10},{3,11},{4,12},{5,13},{6,14},{7,15},{8,0},{9,1},... | collective-permute-start | bytes 608264 | tf_op jit(solution)/shard_map/ppermute | solution.py:298
  9.8 2.9 %shard_map.67 = bf16[256,8320]{1,0:T(8,128)(2,1)} custom-call(s32[1,256]{1,0:T(1,128)S(1)} %get-tuple-element.67.at_ref, bf16[128,256]{1,0:T(8,128)(2,1)S(1)} %get-tuple-element.75.note_ref, bf16[256,8192]{1,0:T(8,128)(2,1)S(1)} %copy-done), custom_call_target="tpu_custom_call" | custom-call | flops 1073741824 | bytes 8388608 | tf_op jit(solution)/shard_map/pallas_call | solution.py:158
  12.7 6.2 %all-to-all-start.3 = ((bf16[16,16,8320]{2,1,0:T(8,128)(2,1)}), bf16[16,16,8320]{2,1,0:T(8,128)(2,1)}, u32[]{:S(2)}, u32[]{:S(2)}) async-start(bf16[16,16,8320]{2,1,0:T(8,128)(2,1)} %bitcast.36), calls=%async_computation.3 | async-start | bytes 8519680 | tf_op jit(solution)/shard_map/all_to_all | solution.py:360
  18.9 28.7 %collective-permute-done.1 = bf16[24,4224]{1,0:T(8,128)(2,1)S(1)} collective-permute-done((bf16[24,4224]{1,0:T(8,128)(2,1)S(1)}, bf16[24,4224]{1,0:T(8,128)(2,1)S(1)}, u32[]{:S(2)}, u32[]{:S(2)}) %collective-permute-start.1) | collective-permute-done | bytes 202784 | tf_op jit(solution)/shard_map/ppermute | solution.py:298
  47.7 0.1 collective-permute-start.6
  47.8 0.1 collective-permute-start.5
  47.9 1.8 %collective-permute-start.4 = (bf16[96,4224]{1,0:T(8,128)(2,1)S(1)}, bf16[96,4224]{1,0:T(8,128)(2,1)S(1)}, u32[]{:S(2)}, u32[]{:S(2)}) collective-permute-start(bf16[96,4224]{1,0:T(8,128)(2,1)S(1)} %pad_maximum_fusion.refs_0_), channel_id=1, source_target_pairs={{0,1},{1,0},{2,3},{3,2},{4,5},{5,4},{6,7},{7,6},{8,9},{9,8},{10,11... | collective-permute-start | bytes 2433032 | tf_op jit(solution)/shard_map/ppermute | solution.py:298
  49.6 1.5 collective-permute-start.3
  51.1 7.8 %fusion.9.base_ref = f32[256,512]{1,0:T(8,128)} fusion(bf16[256,8192]{1,0:T(8,128)(2,1)} %tokens_ref.1, bf16[8192,512]{1,0:T(8,128)(2,1)} %param.9), kind=kOutput, calls=%fused_computation.36 | convolution fusion | flops 2147483648 | bytes 13107200 | tf_op jit(solution)/shard_map/dot_general | solution.py:318
  59.0 20.8 %collective-permute-done.6.refs_3_ = bf16[96,4224]{1,0:T(8,128)(2,1)S(1)} collective-permute-done((bf16[96,4224]{1,0:T(8,128)(2,1)S(1)}, bf16[96,4224]{1,0:T(8,128)(2,1)S(1)}, u32[]{:S(2)}, u32[]{:S(2)}) %collective-permute-start.6) | collective-permute-done | bytes 811040 | tf_op jit(solution)/shard_map/ppermute | solution.py:298
  79.8 25.2 %collective-permute-done.5.refs_2_ = bf16[96,4224]{1,0:T(8,128)(2,1)S(1)} collective-permute-done((bf16[96,4224]{1,0:T(8,128)(2,1)S(1)}, bf16[96,4224]{1,0:T(8,128)(2,1)S(1)}, u32[]{:S(2)}, u32[]{:S(2)}) %collective-permute-start.5) | collective-permute-done | bytes 811040 | tf_op jit(solution)/shard_map/ppermute | solution.py:298
  104.9 5.1 %shard_map.68 = (bf16[64,512]{1,0:T(8,128)(2,1)S(1)}, bf16[64,512]{1,0:T(8,128)(2,1)S(1)}, bf16[64,512]{1,0:T(8,128)(2,1)S(1)}, bf16[64,512]{1,0:T(8,128)(2,1)S(1)}) custom-call(s32[1]{0:T(128)} %bitcast.15.first_ref, bf16[256,8192]{1,0:T(8,128)(2,1)} %bitcast.38, bf16[256,512]{1,0:T(8,128)(2,1)} %bitcast.44, s32[1,128]{1,0:T(1,128)S(1)} %max.3.flag_ref, ...), custom_call_target="tpu_custom_call" | custom-call | flops 999999995904 | bytes 6291456 | tf_op jit(solution)/shard_map/pallas_call | solution.py:285
  110.1 0.4 collective-permute-start.7
  110.4 1.6 %collective-permute-start.9 = (bf16[64,512]{1,0:T(8,128)(2,1)S(1)}, bf16[64,512]{1,0:T(8,128)(2,1)S(1)}, u32[]{:S(2)}, u32[]{:S(2)}) collective-permute-start(bf16[64,512]{1,0:T(8,128)(2,1)S(1)} %get-tuple-element.81), channel_id=1, source_target_pairs={{0,3},{1,2},{2,1},{3,0},{4,7},{5,6},{6,5},{7,4},{8,11},{9,10},{10,... | collective-permute-start | bytes 196616 | tf_op jit(solution)/shard_map/ppermute | solution.py:298
  112.0 3.3 %collective-permute-done.8 = bf16[64,512]{1,0:T(8,128)(2,1)S(1)} collective-permute-done((bf16[64,512]{1,0:T(8,128)(2,1)S(1)}, bf16[64,512]{1,0:T(8,128)(2,1)S(1)}, u32[]{:S(2)}, u32[]{:S(2)}) %collective-permute-start.8) | collective-permute-done | bytes 65568 | tf_op jit(solution)/shard_map/ppermute | solution.py:298
  115.4 10.2 %shard_map.69 = bf16[256,512]{1,0:T(8,128)(2,1)} custom-call(s32[1]{0:T(128)} %bitcast.15.first_ref, bf16[256,8192]{1,0:T(8,128)(2,1)} %bitcast.39, bf16[256,512]{1,0:T(8,128)(2,1)} %bitcast.45, bf16[256,8320]{1,0:T(8,128)(2,1)} %bitcast.20.rows_hbm), custom_call_target="tpu_custom_call" | custom-call | flops 1073741824 | bytes 8388608 | tf_op jit(solution)/shard_map/pallas_call | solution.py:208
  125.6 12.9 %all-to-all-start.4 = ((bf16[16,16,512]{2,1,0:T(8,128)(2,1)}), bf16[16,16,512]{2,1,0:T(8,128)(2,1)S(1)}, u32[]{:S(2)}, u32[]{:S(2)}) async-start(bf16[16,16,512]{2,1,0:T(8,128)(2,1)} %bitcast.22), calls=%async_computation.4 | async-start | bytes 524288 | tf_op jit(solution)/shard_map/all_to_all | solution.py:387
  138.5 3.8 %collective-permute-start.12 = (bf16[16,512]{1,0:T(8,128)(2,1)S(1)}, bf16[16,512]{1,0:T(8,128)(2,1)S(1)}, u32[]{:S(2)}, u32[]{:S(2)}) collective-permute-start(bf16[16,512]{1,0:T(8,128)(2,1)S(1)} %get-tuple-element.91), channel_id=1, source_target_pairs={{0,12},{1,13},{2,14},{3,15},{4,8},{5,9},{6,10},{7,11},{8,4},{9,5},... | collective-permute-start | bytes 49160 | tf_op jit(solution)/shard_map/ppermute | solution.py:298
  142.3 0.7 collective-permute-start.10
  143.0 5.4 %collective-permute-done.12.refs_3_ = bf16[16,512]{1,0:T(8,128)(2,1)S(1)} collective-permute-done((bf16[16,512]{1,0:T(8,128)(2,1)S(1)}, bf16[16,512]{1,0:T(8,128)(2,1)S(1)}, u32[]{:S(2)}, u32[]{:S(2)}) %collective-permute-start.12) | collective-permute-done | bytes 16416 | tf_op jit(solution)/shard_map/ppermute | solution.py:298
  148.4 1.2 collective-permute-done.11.refs_2_
  149.6 1.1 shard_map.70
  (31 shorter events, 0.2 us)
Async XLA Ops:
  0.0 9.8 %copy-start = (bf16[256,8192]{1,0:T(8,128)(2,1)S(1)}, bf16[256,8192]{1,0:T(8,128)(2,1)}, u32[]{:S(2)}) copy-start(bf16[256,8192]{1,0:T(8,128)(2,1)} %tokens_ref.1) | copy-start | bytes 12582916
  4.1 8.6 %copy-start.3 = (s32[1,256]{1,0:T(1,128)}, s32[1,256]{1,0:T(1,128)S(1)}, u32[]{:S(2)}) copy-start(s32[1,256]{1,0:T(1,128)S(1)} %get-tuple-element.67.at_ref) | copy-start | bytes 3076
  4.1 14.8 %collective-permute-start = (bf16[24,4224]{1,0:T(8,128)(2,1)S(1)}, bf16[24,4224]{1,0:T(8,128)(2,1)S(1)}, u32[]{:S(2)}, u32[]{:S(2)}) collective-permute-start(bf16[24,4224]{1,0:T(8,128)(2,1)S(1)} %get-tuple-element.69), channel_id=1, source_target_pairs={{0,4},{1,5},{2,6},{3,7},{4,0},{5,1},{6,2},{7,3},{8,12},{9,13},{10,... | collective-permute-start | bytes 608264 | tf_op jit(solution)/shard_map/ppermute | solution.py:298
  7.2 40.4 %collective-permute-start.1 = (bf16[24,4224]{1,0:T(8,128)(2,1)S(1)}, bf16[24,4224]{1,0:T(8,128)(2,1)S(1)}, u32[]{:S(2)}, u32[]{:S(2)}) collective-permute-start(bf16[24,4224]{1,0:T(8,128)(2,1)S(1)} %get-tuple-element.70), channel_id=1, source_target_pairs={{0,8},{1,9},{2,10},{3,11},{4,12},{5,13},{6,14},{7,15},{8,0},{9,1},... | collective-permute-start | bytes 608264 | tf_op jit(solution)/shard_map/ppermute | solution.py:298
  9.8 37.8 %collective-permute-start.2 = (bf16[24,4224]{1,0:T(8,128)(2,1)S(1)}, bf16[24,4224]{1,0:T(8,128)(2,1)S(1)}, u32[]{:S(2)}, u32[]{:S(2)}) collective-permute-start(bf16[24,4224]{1,0:T(8,128)(2,1)S(1)} %get-tuple-element.71), channel_id=1, source_target_pairs={{0,12},{1,13},{2,14},{3,15},{4,8},{5,9},{6,10},{7,11},{8,4},{9,5},... | collective-permute-start | bytes 608264 | tf_op jit(solution)/shard_map/ppermute | solution.py:298
  12.7 102.7 %all-to-all-start.3 = ((bf16[16,16,8320]{2,1,0:T(8,128)(2,1)}), bf16[16,16,8320]{2,1,0:T(8,128)(2,1)}, u32[]{:S(2)}, u32[]{:S(2)}) async-start(bf16[16,16,8320]{2,1,0:T(8,128)(2,1)} %bitcast.36), calls=%async_computation.3 | async-start | bytes 8519680 | tf_op jit(solution)/shard_map/all_to_all | solution.py:360
  47.7 32.0 %collective-permute-start.6 = (bf16[96,4224]{1,0:T(8,128)(2,1)S(1)}, bf16[96,4224]{1,0:T(8,128)(2,1)S(1)}, u32[]{:S(2)}, u32[]{:S(2)}) collective-permute-start(bf16[96,4224]{1,0:T(8,128)(2,1)S(1)} %pad_maximum_fusion.refs_0_), channel_id=1, source_target_pairs={{0,3},{1,2},{2,1},{3,0},{4,7},{5,6},{6,5},{7,4},{8,11},{9,10},{10,... | collective-permute-start | bytes 2433032 | tf_op jit(solution)/shard_map/ppermute | solution.py:298
  47.8 57.1 %collective-permute-start.5 = (bf16[96,4224]{1,0:T(8,128)(2,1)S(1)}, bf16[96,4224]{1,0:T(8,128)(2,1)S(1)}, u32[]{:S(2)}, u32[]{:S(2)}) collective-permute-start(bf16[96,4224]{1,0:T(8,128)(2,1)S(1)} %pad_maximum_fusion.refs_0_), channel_id=1, source_target_pairs={{0,2},{1,3},{2,0},{3,1},{4,6},{5,7},{6,4},{7,5},{8,10},{9,11},{10,... | collective-permute-start | bytes 2433032 | tf_op jit(solution)/shard_map/ppermute | solution.py:298
  47.9 57.1 %collective-permute-start.4 = (bf16[96,4224]{1,0:T(8,128)(2,1)S(1)}, bf16[96,4224]{1,0:T(8,128)(2,1)S(1)}, u32[]{:S(2)}, u32[]{:S(2)}) collective-permute-start(bf16[96,4224]{1,0:T(8,128)(2,1)S(1)} %pad_maximum_fusion.refs_0_), channel_id=1, source_target_pairs={{0,1},{1,0},{2,3},{3,2},{4,5},{5,4},{6,7},{7,6},{8,9},{9,8},{10,11... | collective-permute-start | bytes 2433032 | tf_op jit(solution)/shard_map/ppermute | solution.py:298
  49.6 9.3 %collective-permute-start.3 = (s32[1,128]{1,0:T(1,128)S(1)}, s32[1,128]{1,0:T(1,128)S(1)}, u32[]{:S(2)}, u32[]{:S(2)}) collective-permute-start(s32[1,128]{1,0:T(1,128)S(1)} %get-tuple-element.73), channel_id=1, source_target_pairs={{0,16},{16,0},{1,17},{17,1},{2,18},{18,2},{3,19},{19,3},{4,20},{20... | collective-permute-start | bytes 1544 | tf_op jit(solution)/shard_map/ppermute | solution.py:356
  110.1 1.9 %collective-permute-start.7 = (bf16[64,512]{1,0:T(8,128)(2,1)S(1)}, bf16[64,512]{1,0:T(8,128)(2,1)S(1)}, u32[]{:S(2)}, u32[]{:S(2)}) collective-permute-start(bf16[64,512]{1,0:T(8,128)(2,1)S(1)} %get-tuple-element.79), channel_id=1, source_target_pairs={{0,1},{1,0},{2,3},{3,2},{4,5},{5,4},{6,7},{7,6},{8,9},{9,8},{10,11... | collective-permute-start | bytes 196616 | tf_op jit(solution)/shard_map/ppermute | solution.py:298
  110.4 4.9 %collective-permute-start.8 = (bf16[64,512]{1,0:T(8,128)(2,1)S(1)}, bf16[64,512]{1,0:T(8,128)(2,1)S(1)}, u32[]{:S(2)}, u32[]{:S(2)}) collective-permute-start(bf16[64,512]{1,0:T(8,128)(2,1)S(1)} %get-tuple-element.80), channel_id=1, source_target_pairs={{0,2},{1,3},{2,0},{3,1},{4,6},{5,7},{6,4},{7,5},{8,10},{9,11},{10,... | collective-permute-start | bytes 196616 | tf_op jit(solution)/shard_map/ppermute | solution.py:298
  110.4 4.9 %collective-permute-start.9 = (bf16[64,512]{1,0:T(8,128)(2,1)S(1)}, bf16[64,512]{1,0:T(8,128)(2,1)S(1)}, u32[]{:S(2)}, u32[]{:S(2)}) collective-permute-start(bf16[64,512]{1,0:T(8,128)(2,1)S(1)} %get-tuple-element.81), channel_id=1, source_target_pairs={{0,3},{1,2},{2,1},{3,0},{4,7},{5,6},{6,5},{7,4},{8,11},{9,10},{10,... | collective-permute-start | bytes 196616 | tf_op jit(solution)/shard_map/ppermute | solution.py:298
  115.4 34.2 %copy-start.1 = (f32[256,512]{1,0:T(8,128)S(1)}, f32[256,512]{1,0:T(8,128)}, u32[]{:S(2)}) copy-start(f32[256,512]{1,0:T(8,128)} %fusion.9.base_ref) | copy-start | bytes 1572868
  115.4 34.2 %copy-start.4 = (s32[1,256]{1,0:T(1,128)S(1)}, s32[1,256]{1,0:T(1,128)}, u32[]{:S(2)}) copy-start(s32[1,256]{1,0:T(1,128)} %copy-done.3) | copy-start | bytes 3076
  115.4 35.8 %copy-start.2 = (bf16[16,16,512]{2,1,0:T(8,128)(2,1)S(1)}, bf16[16,16,512]{2,1,0:T(8,128)(2,1)}, u32[]{:S(2)}) copy-start(bf16[16,16,512]{2,1,0:T(8,128)(2,1)} %param.11) | copy-start | bytes 786436
  115.4 35.8 %copy-start.5 = (s32[256,1]{0,1:T(1,128)S(1)}, s32[256,1]{0,1:T(1,128)}, u32[]{:S(2)}) copy-start(s32[256,1]{0,1:T(1,128)} %param.12) | copy-start | bytes 3076
  115.4 35.8 %copy-start.6 = (s32[256]{0:T(256)S(1)}, s32[256]{0:T(256)}, u32[]{:S(2)}) copy-start(s32[256]{0:T(256)} %param.13) | copy-start | bytes 3076
  125.6 23.9 %all-to-all-start.4 = ((bf16[16,16,512]{2,1,0:T(8,128)(2,1)}), bf16[16,16,512]{2,1,0:T(8,128)(2,1)S(1)}, u32[]{:S(2)}, u32[]{:S(2)}) async-start(bf16[16,16,512]{2,1,0:T(8,128)(2,1)} %bitcast.22), calls=%async_computation.4 | async-start | bytes 524288 | tf_op jit(solution)/shard_map/all_to_all | solution.py:387
  138.5 9.8 %collective-permute-start.12 = (bf16[16,512]{1,0:T(8,128)(2,1)S(1)}, bf16[16,512]{1,0:T(8,128)(2,1)S(1)}, u32[]{:S(2)}, u32[]{:S(2)}) collective-permute-start(bf16[16,512]{1,0:T(8,128)(2,1)S(1)} %get-tuple-element.91), channel_id=1, source_target_pairs={{0,12},{1,13},{2,14},{3,15},{4,8},{5,9},{6,10},{7,11},{8,4},{9,5},... | collective-permute-start | bytes 49160 | tf_op jit(solution)/shard_map/ppermute | solution.py:298
  142.3 7.2 %collective-permute-start.11 = (bf16[16,512]{1,0:T(8,128)(2,1)S(1)}, bf16[16,512]{1,0:T(8,128)(2,1)S(1)}, u32[]{:S(2)}, u32[]{:S(2)}) collective-permute-start(bf16[16,512]{1,0:T(8,128)(2,1)S(1)} %get-tuple-element.92), channel_id=1, source_target_pairs={{0,8},{1,9},{2,10},{3,11},{4,12},{5,13},{6,14},{7,15},{8,0},{9,1},... | collective-permute-start | bytes 49160 | tf_op jit(solution)/shard_map/ppermute | solution.py:298
  142.3 7.2 %collective-permute-start.10 = (bf16[16,512]{1,0:T(8,128)(2,1)S(1)}, bf16[16,512]{1,0:T(8,128)(2,1)S(1)}, u32[]{:S(2)}, u32[]{:S(2)}) collective-permute-start(bf16[16,512]{1,0:T(8,128)(2,1)S(1)} %get-tuple-element.93), channel_id=1, source_target_pairs={{0,4},{1,5},{2,6},{3,7},{4,0},{5,1},{6,2},{7,3},{8,12},{9,13},{10,... | collective-permute-start | bytes 49160 | tf_op jit(solution)/shard_map/ppermute | solution.py:298

commit v11 on v10

--- a/solution.py
+++ b/solution.py
@@ -11,8 +11,10 @@
 CAP = 2
 PLANE = 4
 SPARE = 12
+EXTRA = 8
 NOTE = 128
 STEP = 1024
+WIDE = 1664
 PARTS = 8
 VMEM = pl.BlockSpec(memory_space=pltpu.VMEM)
 ANY = pl.BlockSpec(memory_space=pl.ANY)
@@ -70,7 +72,7 @@
 
 
 def route_body(room, local, me_ref, tenant_ref, slot_ref, tokens_hbm, *refs):
-    *outs, at_ref, note_ref, left_ref, tokens_ref, sems = refs
+    *outs, at_ref, back_ref, note_ref, tokens_ref, sems = refs
     half = tokens_ref.shape[1] // 2
     copies = row_copies(tokens_hbm, tokens_ref, sems, PARTS)
     for copy in copies:
@@ -91,14 +93,15 @@
     plane = (owner ^ me_ref[0]) // PLANE
     over = place >= room
     over_place = earlier((iota(16) == plane) & over, until)
-    left = over & (over_place >= SPARE)
+    left = over & ((over_place >= SPARE) | (place >= room + EXTRA))
     at = jnp.where(over, main_rows + plane * SPARE + over_place, owner * room + place)
     at = jnp.where(left, -1, at)
     at_ref[...] = at
-    most = jnp.max(left.astype(jnp.float32), axis=1, keepdims=True).astype(jnp.int32)
-    left_ref[...] = jnp.broadcast_to(most, left_ref.shape)
-    note = jnp.where(iota(NOTE) == 0, slot + 1.0, 0.0).astype(jnp.bfloat16)
+    back_ref[...] = jnp.where(left, -1, owner * (room + EXTRA) + place)
+    note = jnp.where(iota(NOTE) == 0, slot + 1.0, 0.0)
+    note = jnp.where(iota(NOTE) == 1, place.astype(jnp.float32), note).astype(jnp.bfloat16)
     note_ref[...] = note
+    most = jnp.max(left.astype(jnp.float32), axis=1, keepdims=True)
 
     row = iota(2 * SPARE)
     upper = row >= SPARE
@@ -112,7 +115,9 @@
         for b in range(planes):
             outs[b][:, columns] = value[2 * SPARE * b : 2 * SPARE * (b + 1)].astype(jnp.bfloat16)
 
-    put(notes_of(one_hot(hit), note), slice(half, half + NOTE))
+    notes = notes_of(one_hot(hit), note)
+    flag = lax.broadcasted_iota(jnp.int32, notes.shape, 1) == 2
+    put(jnp.where(flag, most, notes), slice(half, half + NOTE))
     for copy in copies:
         copy.wait()
     for c in range(0, half, STEP):
@@ -177,55 +182,69 @@
     return jnp.dot(low.astype(jnp.bfloat16), up, preferred_element_type=jnp.float32)
 
 
-def adapt_body(rank, first_ref, down_hbm, up_ref, rows_hbm, out, *scratch):
+def adapt_body(rank, me_ref, down_hbm, up_ref, rows_hbm, extra_ref, out, *scratch):
     down_ref, rows_ref, down_sems, sems = scratch
     depth = down_ref.shape[1]
-    factors = row_copies(down_hbm, down_ref, down_sems, PARTS)
-    copies = row_copies(rows_hbm, rows_ref, sems, PARTS)
-    for copy in factors + copies:
-        copy.start()
-    for copy in factors:
-        copy.wait()
-    half = rows_ref.shape[0] // 2
-    for h in range(2):
-        for copy in copies[h * PARTS // 2 : (h + 1) * PARTS // 2]:
-            copy.wait()
-        own = slice(h * half, (h + 1) * half)
-        low = jnp.zeros((half, down_ref.shape[0]), jnp.float32)
-        for c in range(0, depth, STEP):
-            low += lax.dot_general(
-                rows_ref[own, c : c + STEP],
-                down_ref[:, c : c + STEP],
-                (((1,), (1,)), ((), ())),
-                preferred_element_type=jnp.float32,
+    spans = [slice(c, min(c + WIDE, depth + NOTE)) for c in range(0, depth + NOTE, WIDE)]
+    copies = []
+    for i, span in enumerate(spans):
+        kept = slice(span.start, min(span.stop, depth))
+        copies.append(
+            (
+                pltpu.make_async_copy(rows_hbm.at[:, span], rows_ref.at[:, span], sems.at[i]),
+                pltpu.make_async_copy(down_hbm.at[:, kept], down_ref.at[:, kept], down_sems.at[i]),
             )
-        note = rows_ref[own, depth:].astype(jnp.float32)[:, :1]
-        out[own] = low_delta(low, note, first_ref[0], rank, up_ref[...]).astype(jnp.bfloat16)
-
-
-def adapt(rank, first, down, up, got):
+        )
+    for pair in copies:
+        pair[0].start()
+        pair[1].start()
+    low = jnp.zeros((rows_ref.shape[0], down_ref.shape[0]), jnp.float32)
+    for pair, span in zip(copies, spans, strict=True):
+        pair[0].wait()
+        pair[1].wait()
+        span = slice(span.start, min(span.stop, depth))
+        low += lax.dot_general(
+            rows_ref[:, span],
+            down_ref[:, span],
+            (((1,), (1,)), ((), ())),
+            preferred_element_type=jnp.float32,
+        )
+    note = rows_ref[:, depth:].astype(jnp.float32)
+    sources = out.shape[0]
+    first = me_ref[0] * (down_ref.shape[0] // rank)
+    delta = low_delta(low, note[:, :1], first, rank, up_ref[...])
+    room = delta.shape[0] // sources
+    for s in range(sources):
+        k = me_ref[0] ^ s
+        extra = extra_ref[(k % PLANE) * (sources // PLANE) + k // PLANE]
+        rows = jnp.concatenate([delta[s * room : (s + 1) * room], extra], axis=0)
+        out[s] = rows.astype(jnp.bfloat16)
+
+
+def adapt(rank, me, down, up, got, extra):
     rows, width = got.shape[0], up.shape[1]
+    count = extra.shape[0]
     return pl.pallas_call(
         functools.partial(adapt_body, rank),
-        in_specs=[SMEM, ANY, VMEM, ANY],
+        in_specs=[SMEM, ANY, VMEM, ANY, VMEM],
         out_specs=VMEM,
-        out_shape=jax.ShapeDtypeStruct((rows, width), jnp.bfloat16),
+        out_shape=jax.ShapeDtypeStruct((count, rows // count + EXTRA, width), jnp.bfloat16),
         scratch_shapes=[
             pltpu.VMEM(down.shape, jnp.bfloat16),
             pltpu.VMEM(got.shape, jnp.bfloat16),
-            pltpu.SemaphoreType.DMA((PARTS,)),
-            pltpu.SemaphoreType.DMA((PARTS,)),
+            pltpu.SemaphoreType.DMA((pl.cdiv(got.shape[1], WIDE),)),
+            pltpu.SemaphoreType.DMA((pl.cdiv(got.shape[1], WIDE),)),
         ],
         compiler_params=pltpu.CompilerParams(vmem_limit_bytes=24 * 2**20),
         cost_estimate=pl.CostEstimate(
             flops=2 * rows * down.size, bytes_accessed=8 * 2**20, transcendentals=0
         ),
-    )(first, down, up, got)
-
-
-def adapt_over_body(planes, rank, first_ref, down_hbm, up_ref, flag_ref, *refs):
-    rows_refs, outs = refs[:PLANE], refs[PLANE : 2 * PLANE]
-    down_ref, sems = refs[2 * PLANE :]
+    )(me, down, up, got, extra)
+
+
+def adapt_over_body(planes, rank, first_ref, down_hbm, up_ref, *refs):
+    rows_refs = refs[:PLANE]
+    out, flag_out, down_ref, sems = refs[PLANE:]
     half = down_ref.shape[1] // 2
     copies = row_copies(down_hbm, down_ref, sems, PARTS)
     for copy in copies:
@@ -255,42 +274,34 @@
             lows += [low0[m : m + SPARE] + low1[m + SPARE : m + 2 * SPARE], zeros]
             notes += [note[s : s + SPARE], no_note]
     low = jnp.concatenate(lows, axis=0)
-    note = jnp.concatenate(notes, axis=0)[:, :1]
-    delta = low_delta(low, note, first_ref[0], rank, up_ref[...])
-    row = lax.broadcasted_iota(jnp.int32, delta.shape, 0) % 16
-    flag = flag_ref[...][:, :1].astype(jnp.float32)
-    delta = jnp.where(row == SPARE, flag, delta).astype(jnp.bfloat16)
-    for a, out in enumerate(outs):
-        out[...] = delta[16 * planes * a : 16 * planes * (a + 1)]
-
-
-def final_body(at_ref, base_ref, back_ref, *refs):
-    *overs, out, seen_ref = refs
-    seen = sum(o[...][SPARE:, :1].astype(jnp.float32) for o in overs)
-    seen_ref[0] = jnp.max(seen).astype(jnp.int32)
-    back = jnp.concatenate([back_ref[...]] + [o[...] for o in overs], axis=0)
-    main_rows, size = back_ref.shape[0], overs[0].shape[0]
-    row = lax.broadcasted_iota(jnp.int32, (back.shape[0], at_ref.shape[1]), 0)
-    b, i = (row - main_rows) // size, (row - main_rows) % size
-    spare = jnp.where(i < SPARE, main_rows + b * SPARE + i, -2)
-    pick = jnp.where(row < main_rows, row, spare) == at_ref[...]
-    pick = pick.astype(jnp.float32).astype(jnp.bfloat16)
+    note = jnp.concatenate(notes, axis=0)
+    delta = low_delta(low, note[:, :1], first_ref[0], rank, up_ref[...]).astype(jnp.bfloat16)
+    shape = (delta.shape[0], PLANE * planes * EXTRA)
+    row, column = (lax.broadcasted_iota(jnp.int32, shape, axis) for axis in (0, 1))
+    own = (note[:, :1].astype(jnp.int32) - 1) // (down_ref.shape[0] // rank) == first_ref[
+        0
+    ] // (down_ref.shape[0] // rank)
+    own = own & (note[:, :1] > 0)
+    put = (note[:, 1:2].astype(jnp.int32) == 16 + column % EXTRA) & (row // 16 == column // EXTRA)
+    extra = lax.dot_general(
+        one_hot(put & own), delta, (((0,), (0,)), ((), ())), preferred_element_type=jnp.float32
+    )
+    for g in range(PLANE * planes):
+        out[g] = extra[g * EXTRA : (g + 1) * EXTRA]
+    flags = [jnp.max(r[:, half : half + NOTE].astype(jnp.float32), axis=0) for r in rows_refs]
+    most = functools.reduce(jnp.maximum, flags).reshape(1, NOTE)
+    flag_out[...] = most.astype(jnp.int32)
+
+
+def final_body(at_ref, base_ref, back_ref, out):
+    row = lax.broadcasted_iota(jnp.int32, (back_ref.shape[0], at_ref.shape[1]), 0)
     delta = lax.dot_general(
-        pick, back, (((0,), (0,)), ((), ())), preferred_element_type=jnp.float32
+        one_hot(row == at_ref[...]),
+        back_ref[...],
+        (((0,), (0,)), ((), ())),
+        preferred_element_type=jnp.float32,
     )
     out[...] = (base_ref[...] + delta).astype(jnp.bfloat16)
-
-
-def call(body, outs, args, specs, flops, moved, scratch=()):
-    return pl.pallas_call(
-        body,
-        in_specs=specs,
-        out_specs=[VMEM] * len(outs),
-        out_shape=[jax.ShapeDtypeStruct(s, jnp.bfloat16) for s in outs],
-        scratch_shapes=list(scratch),
-        compiler_params=pltpu.CompilerParams(vmem_limit_bytes=40 * 2**20),
-        cost_estimate=pl.CostEstimate(flops=flops, bytes_accessed=moved, transcendentals=0),
-    )(*args)
 
 
 def swap(x, k):
@@ -324,15 +335,15 @@
         return (base_value + delta).astype(jnp.bfloat16)
 
     main_rows = count * room
-    *spare, at, note, left = pl.pallas_call(
+    *spare, at, at_back, note = pl.pallas_call(
         functools.partial(route_body, room, local),
         in_specs=[SMEM, VMEM, VMEM, ANY],
         out_specs=[VMEM] * (planes + 3),
         out_shape=[jax.ShapeDtypeStruct((2 * SPARE, depth // 2 + NOTE), jnp.bfloat16)] * planes
         + [
             jax.ShapeDtypeStruct((1, row_count), jnp.int32),
+            jax.ShapeDtypeStruct((1, row_count), jnp.int32),
             jax.ShapeDtypeStruct((NOTE, row_count), jnp.bfloat16),
-            jax.ShapeDtypeStruct((1, NOTE), jnp.int32),
         ],
         scratch_shapes=[
             pltpu.VMEM(tokens.shape, jnp.bfloat16),
@@ -349,12 +360,6 @@
     blocks = pack(main_rows, at, note, tokens)
 
     along = jnp.concatenate(along, axis=0)
-    along, left = lax.optimization_barrier((along, left))
-    groups = lax.axis_size("grp")
-    flag = left
-    for g in range(1, groups):
-        other = lax.ppermute(left, "grp", [(s, (s + g) % groups) for s in range(groups)])
-        flag = jnp.maximum(flag, other)
     shared = [along] + [swap(along, a) for a in range(1, PLANE)]
 
     got = lax.all_to_all(
@@ -365,41 +370,42 @@
     down = adapt_down.transpose(0, 2, 1).reshape(local * rank, depth)
     up = adapt_up.reshape(local * rank, width)
 
-    flag, base_value = lax.optimization_barrier((flag, base_value))
-    over_delta = call(
+    shared[0], base_value = lax.optimization_barrier((shared[0], base_value))
+    extra, flag = pl.pallas_call(
         functools.partial(adapt_over_body, planes, rank),
-        [(16 * planes, width)] * PLANE,
-        (first, down, up, flag, *shared),
-        [SMEM, ANY] + [VMEM] * 6,
-        10**12,
-        6 * 2**20,
-        [pltpu.VMEM(down.shape, jnp.bfloat16), pltpu.SemaphoreType.DMA((PARTS,))],
-    )
-    over_sum = over_delta[0]
-    for a in range(1, PLANE):
-        over_sum = over_sum + swap(over_delta[a], a)
-    got, over_sum = lax.optimization_barrier((got, over_sum))
-    delta = adapt(rank, first, down, up, got)
-    delta, over_sum = lax.optimization_barrier((delta, over_sum))
-    over_back = [over_sum[:16]]
-    for b in range(1, planes):
-        over_back.append(swap(over_sum[16 * b : 16 * (b + 1)], b * PLANE))
-    back = lax.all_to_all(
-        delta.reshape(count, room, width), "ad", split_axis=0, concat_axis=0, tiled=True
-    ).reshape(main_rows, width)
+        in_specs=[SMEM, ANY] + [VMEM] * (1 + PLANE),
+        out_specs=[VMEM, VMEM],
+        out_shape=[
+            jax.ShapeDtypeStruct((count, EXTRA, width), jnp.float32),
+            jax.ShapeDtypeStruct((1, NOTE), jnp.int32),
+        ],
+        scratch_shapes=[pltpu.VMEM(down.shape, jnp.bfloat16), pltpu.SemaphoreType.DMA((PARTS,))],
+        compiler_params=pltpu.CompilerParams(vmem_limit_bytes=40 * 2**20),
+        cost_estimate=pl.CostEstimate(
+            flops=10**12,
+            bytes_accessed=6 * 2**20,
+            transcendentals=0,
+        ),
+    )(first, down, up, *shared)
+
+    groups = lax.axis_size("grp")
+    own = flag[0, 2]
+    seen = own
+    for g in range(1, groups):
+        other = lax.ppermute(own, "grp", [(s, (s + g) % groups) for s in range(groups)])
+        seen = jnp.maximum(seen, other)
+    got, extra, seen = lax.optimization_barrier((got, extra, seen))
+    delta = adapt(rank, me.reshape(1), down, up, got, extra)
+    back = lax.all_to_all(delta, "ad", split_axis=0, concat_axis=0, tiled=True)
+    back = back.reshape(count * (room + EXTRA), width)
 
     def finish(base):
         return pl.pallas_call(
             final_body,
-            in_specs=[VMEM] * (3 + planes),
-            out_specs=[VMEM, SMEM],
-            out_shape=[
-                jax.ShapeDtypeStruct((row_count, width), jnp.bfloat16),
-                jax.ShapeDtypeStruct((1,), jnp.int32),
-            ],
-        )(at, base, back, *over_back)
-
-    out, seen = finish(base_value)
+            in_specs=[VMEM] * 3,
+            out_specs=VMEM,
+            out_shape=jax.ShapeDtypeStruct((row_count, width), jnp.bfloat16),
+        )(at_back, base, back)
 
     def more():
         slot, owner, place = route(tenant_ids, tenant_slot, local)
@@ -412,9 +418,9 @@
             adapt_down,
             adapt_up,
         )
-        return finish(base_value + extra)[0]
-
-    return lax.cond(seen[0] > 0, more, lambda: out)
+        return finish(base_value + extra)
+
+    return lax.cond(seen > 0, more, lambda: finish(base_value))
 
 
 def solution(mesh):

time: 152 us -> 145 us (0.954)
  Pallas kernels: 23.4 us -> 15.5 us
  starting transfers between devices: 34.5 us -> 28 us
  waiting for transfers between devices: 84.6 us -> 90.3 us
    all_to_all x1, waiting for transfers between devices: 0.01 us -> 12.2 us  [on_device(): back = lax.all_to_all(delta, 'ad', split_axis=0, concat_axis=0, tiled=True)]
    ppermute x12 -> x6, waiting for transfers between devices: 84.6 us -> 76.1 us  [swap(): return lax.ppermute(x, 'ad', [(s, s ^ k) for s in range(count)])]
    ppermute x12 -> x6, starting transfers between devices: 14 us -> 7.59 us  [swap(): return lax.ppermute(x, 'ad', [(s, s ^ k) for s in range(count)])]
    pallas_call x1, Pallas kernels: 10.2 us -> 5.64 us  [adapt(): pl.pallas_call(functools.partial(adapt_body, rank), in_specs=[SMEM, ANY,...]
    pallas_call x2, Pallas kernels: 6.19 us -> 2.86 us  [the longest x1 2.54 us: on_device(): pl.pallas_call(functools.partial(adapt_over_body, planes, rank), in_specs...]
    ppermute x1, waiting for transfers between devices: 0.01 us -> 2.06 us  [on_device(): lax.ppermute(own, 'grp', [(s, (s + g) % groups) for s in range(groups)])]
  transfers between devices with their start and end apart: 15 -> 9, of which waited for: 6 -> 5; matrix products, arithmetic and copies ran while one was open for 5% -> 6% of each run, Pallas kernels for 5% -> 4%
where the time goes in v11:
time: 145 us
  waiting for transfers between devices  90.3 us (62%)
  starting transfers between devices  28 us (19%)
  Pallas kernels  15.5 us (11%)
  matrix products  7.85 us (5%)
  between operations  1.53 us (1%)
  local copies, waits for them, and re-layouts  1.48 us (1%)
    ppermute x6, waiting for transfers between devices, swap(): return lax.ppermute(x, 'ad', [(s, s ^ k) for s in range(count)])  76.1 us
    all_to_all x1, starting transfers between devices, on_device(): back = lax.all_to_all(delta, 'ad', split_axis=0, concat_axis=0, tiled=True)  12.7 us
    all_to_all x1, waiting for transfers between devices, on_device(): back = lax.all_to_all(delta, 'ad', split_axis=0, concat_axis=0, tiled=True)  12.2 us
    dot_general x1, matrix products, on_device(): jnp.dot(tokens, value_weight, preferred_element_type=jnp.float32)  7.85 us
    ppermute x6, starting transfers between devices, swap(): return lax.ppermute(x, 'ad', [(s, s ^ k) for s in range(count)])  7.59 us
    all_to_all x1, starting transfers between devices, on_device(): lax.all_to_all(blocks.reshape(count, room, depth + NOTE), 'ad', split_axi...  6.22 us
    pallas_call x1, Pallas kernels, adapt(): pl.pallas_call(functools.partial(adapt_body, rank), in_specs=[SMEM, ANY,...  5.64 us
    pallas_call x1, Pallas kernels, on_device(): pl.pallas_call(functools.partial(route_body, room, local), in_specs=[SMEM...  4.1 us
  transfers between devices with their start and end apart: 9, of which 5 were waited for; matrix products, arithmetic and copies ran while one was open for 6% of the time, Pallas kernels for 4%

profile of v11, /device:TPU:0, one launch (start us, length us, event | category | flops | bytes accessed | tf_op | source)
XLA Modules:
  0.0 144.7 jit_solution(14732216493254736808)
XLA Ops:
  0.0 4.1 %shard_map.66 = (bf16[24,4224]{1,0:T(8,128)(2,1)S(1)}, bf16[24,4224]{1,0:T(8,128)(2,1)S(1)}, bf16[24,4224]{1,0:T(8,128)(2,1)S(1)}, bf16[24,4224]{1,0:T(8,128)(2,...) custom-call(s32[1]{0:T(128)} %bitcast.12.me_ref, s32[1,256]{1,0:T(1,128)} %bitcast.51, ...), custom_call_target="tpu_custom_call" | custom-call | flops 805306368 | bytes 6291456 | tf_op jit(solution)/shard_map/pallas_call | solution.py:338
  4.1 3.1 %collective-permute-start = (bf16[24,4224]{1,0:T(8,128)(2,1)S(1)}, bf16[24,4224]{1,0:T(8,128)(2,1)S(1)}, u32[]{:S(2)}, u32[]{:S(2)}) collective-permute-start(bf16[24,4224]{1,0:T(8,128)(2,1)S(1)} %get-tuple-element.61), channel_id=1, source_target_pairs={{0,4},{1,5},{2,6},{3,7},{4,0},{5,1},{6,2},{7,3},{8,12},{9,13},{10,... | collective-permute-start | bytes 608264 | tf_op jit(solution)/shard_map/ppermute | solution.py:309
  7.2 2.6 %collective-permute-start.1 = (bf16[24,4224]{1,0:T(8,128)(2,1)S(1)}, bf16[24,4224]{1,0:T(8,128)(2,1)S(1)}, u32[]{:S(2)}, u32[]{:S(2)}) collective-permute-start(bf16[24,4224]{1,0:T(8,128)(2,1)S(1)} %get-tuple-element.62), channel_id=1, source_target_pairs={{0,8},{1,9},{2,10},{3,11},{4,12},{5,13},{6,14},{7,15},{8,0},{9,1},... | collective-permute-start | bytes 608264 | tf_op jit(solution)/shard_map/ppermute | solution.py:309
  9.8 2.9 %shard_map.67 = bf16[256,8320]{1,0:T(8,128)(2,1)} custom-call(s32[1,256]{1,0:T(1,128)S(1)} %get-tuple-element.58.at_ref, bf16[128,256]{1,0:T(8,128)(2,1)S(1)} %get-tuple-element.59.note_ref, bf16[256,8192]{1,0:T(8,128)(2,1)S(1)} %copy-done), custom_call_target="tpu_custom_call" | custom-call | flops 1073741824 | bytes 8388608 | tf_op jit(solution)/shard_map/pallas_call | solution.py:163
  12.7 6.2 %all-to-all-start.3 = ((bf16[16,16,8320]{2,1,0:T(8,128)(2,1)}), bf16[16,16,8320]{2,1,0:T(8,128)(2,1)}, u32[]{:S(2)}, u32[]{:S(2)}) async-start(bf16[16,16,8320]{2,1,0:T(8,128)(2,1)} %bitcast.35), calls=%async_computation.3 | async-start | bytes 8519680 | tf_op jit(solution)/shard_map/all_to_all | solution.py:365
  19.0 28.7 %collective-permute-done.1 = bf16[24,4224]{1,0:T(8,128)(2,1)S(1)} collective-permute-done((bf16[24,4224]{1,0:T(8,128)(2,1)S(1)}, bf16[24,4224]{1,0:T(8,128)(2,1)S(1)}, u32[]{:S(2)}, u32[]{:S(2)}) %collective-permute-start.1) | collective-permute-done | bytes 202784 | tf_op jit(solution)/shard_map/ppermute | solution.py:309
  47.7 0.0 copy-start.1
  47.7 0.1 collective-permute-start.5
  47.8 0.1 collective-permute-start.4
  47.9 1.8 %collective-permute-start.3 = (bf16[96,4224]{1,0:T(8,128)(2,1)S(1)}, bf16[96,4224]{1,0:T(8,128)(2,1)S(1)}, u32[]{:S(2)}, u32[]{:S(2)}) collective-permute-start(bf16[96,4224]{1,0:T(8,128)(2,1)S(1)} %constant_dynamic-update-slice_fusion.refs_0_), channel_id=1, source_target_pairs={{0,1},{1,0},{2,3},{3,2},{4,5},{5,4},{6,7},{7,6},{8,9},{9,8},{10,11... | collective-permute-start | bytes 2433032 | tf_op jit(solution)/shard_map/ppermute | solution.py:309
  49.6 7.9 %fusion.8 = f32[256,512]{1,0:T(8,128)} fusion(bf16[256,8192]{1,0:T(8,128)(2,1)} %tokens_ref.1, bf16[8192,512]{1,0:T(8,128)(2,1)} %param.9), kind=kOutput, calls=%fused_computation.37 | convolution fusion | flops 2147483648 | bytes 13107200 | tf_op jit(solution)/shard_map/dot_general | solution.py:329
  57.5 22.3 %collective-permute-done.5.refs_3_ = bf16[96,4224]{1,0:T(8,128)(2,1)S(1)} collective-permute-done((bf16[96,4224]{1,0:T(8,128)(2,1)S(1)}, bf16[96,4224]{1,0:T(8,128)(2,1)S(1)}, u32[]{:S(2)}, u32[]{:S(2)}) %collective-permute-start.5) | collective-permute-done | bytes 811040 | tf_op jit(solution)/shard_map/ppermute | solution.py:309
  79.8 25.1 %collective-permute-done.4.refs_2_ = bf16[96,4224]{1,0:T(8,128)(2,1)S(1)} collective-permute-done((bf16[96,4224]{1,0:T(8,128)(2,1)S(1)}, bf16[96,4224]{1,0:T(8,128)(2,1)S(1)}, u32[]{:S(2)}, u32[]{:S(2)}) %collective-permute-start.4) | collective-permute-done | bytes 811040 | tf_op jit(solution)/shard_map/ppermute | solution.py:309
  104.9 2.5 %shard_map.68 = (f32[16,8,512]{2,1,0:T(8,128)S(1)}, s32[1,128]{1,0:T(1,128)S(1)}) custom-call(s32[1]{0:T(128)} %bitcast.17.first_ref, bf16[256,8192]{1,0:T(8,128)(2,1)S(1)} %bitcast.38, bf16[256,512]{1,0:T(8,128)(2,1)S(1)} %bitcast.43, bf16[96,4224]{1,0:T(8,128)(2,1)S(1)} %constant_dynamic-update-slice_fusion.refs_0_, ...), custom_call_target="tpu_custom_call" | custom-call | flops 999999995904 | bytes 6291456 | tf_op jit(solution)/shard_map/pallas_call | solution.py:374
  107.5 0.7 slice.3
  108.1 1.5 %collective-permute-start.6 = (s32[]{:T(128)}, s32[]{:T(128)}, u32[]{:S(2)}, u32[]{:S(2)}) collective-permute-start(s32[]{:T(128)} %bitcast.21), channel_id=1, source_target_pairs={{0,16},{16,0},{1,17},{17,1},{2,18},{18,2},{3,19},{19,3},{4,20},{20... | collective-permute-start | bytes 20 | tf_op jit(solution)/shard_map/ppermute | solution.py:395
  109.6 2.1 %collective-permute-done.6 = s32[]{:T(128)} collective-permute-done((s32[]{:T(128)}, s32[]{:T(128)}, u32[]{:S(2)}, u32[]{:S(2)}) %collective-permute-start.6) | collective-permute-done | bytes 36 | tf_op jit(solution)/shard_map/ppermute | solution.py:395
  113.0 0.0 copy-start.7
  113.0 5.6 %shard_map.69 = bf16[16,24,512]{2,1,0:T(8,128)(2,1)} custom-call(s32[1]{0:T(128)} %bitcast.12.me_ref, bf16[256,8192]{1,0:T(8,128)(2,1)} %bitcast.37, bf16[256,512]{1,0:T(8,128)(2,1)S(1)} %bitcast.44, bf16[256,8320]{1,0:T(8,128)(2,1)} %bitcast.16.rows_hbm, f32[16,8,512]{2,1,0:T(8,128)S(1)} %get-tuple-element.71.extra_ref), custom_call_target="tpu_custom_call" | custom-call | flops 1073741824 | bytes 8388608 | tf_op jit(solution)/shard_map/pallas_call | solution.py:227
  118.7 12.7 %all-to-all-start.4 = ((bf16[16,24,512]{2,1,0:T(8,128)(2,1)}), bf16[16,24,512]{2,1,0:T(8,128)(2,1)S(1)}, u32[]{:S(2)}, u32[]{:S(2)}) async-start(bf16[16,24,512]{2,1,0:T(8,128)(2,1)} %shard_map.69), calls=%async_computation.4 | async-start | bytes 786432 | tf_op jit(solution)/shard_map/all_to_all | solution.py:399
  131.4 12.2 %all-to-all-done.4 = bf16[16,24,512]{2,1,0:T(8,128)(2,1)S(1)} async-done(((bf16[16,24,512]{2,1,0:T(8,128)(2,1)}), bf16[16,24,512]{2,1,0:T(8,128)(2,1)S(1)}, u32[]{:S(2)}, u32[]{:S(2)}) %all-to-all-start.4) | async-done | bytes 393248 | tf_op jit(solution)/shard_map/all_to_all | solution.py:399
  143.6 0.3 conditional.1
  143.6 0.3 branch_0_fun.1
  144.0 0.7 copy-done.4
  (26 shorter events, 0.1 us)
Async XLA Ops:
  0.0 9.8 %copy-start = (bf16[256,8192]{1,0:T(8,128)(2,1)S(1)}, bf16[256,8192]{1,0:T(8,128)(2,1)}, u32[]{:S(2)}) copy-start(bf16[256,8192]{1,0:T(8,128)(2,1)} %tokens_ref.1) | copy-start | bytes 12582916
  4.1 8.6 %copy-start.5 = (s32[1,256]{1,0:T(1,128)}, s32[1,256]{1,0:T(1,128)S(1)}, u32[]{:S(2)}) copy-start(s32[1,256]{1,0:T(1,128)S(1)} %get-tuple-element.58.at_ref) | copy-start | bytes 3076
  4.1 14.8 %collective-permute-start = (bf16[24,4224]{1,0:T(8,128)(2,1)S(1)}, bf16[24,4224]{1,0:T(8,128)(2,1)S(1)}, u32[]{:S(2)}, u32[]{:S(2)}) collective-permute-start(bf16[24,4224]{1,0:T(8,128)(2,1)S(1)} %get-tuple-element.61), channel_id=1, source_target_pairs={{0,4},{1,5},{2,6},{3,7},{4,0},{5,1},{6,2},{7,3},{8,12},{9,13},{10,... | collective-permute-start | bytes 608264 | tf_op jit(solution)/shard_map/ppermute | solution.py:309
  7.2 40.4 %collective-permute-start.1 = (bf16[24,4224]{1,0:T(8,128)(2,1)S(1)}, bf16[24,4224]{1,0:T(8,128)(2,1)S(1)}, u32[]{:S(2)}, u32[]{:S(2)}) collective-permute-start(bf16[24,4224]{1,0:T(8,128)(2,1)S(1)} %get-tuple-element.62), channel_id=1, source_target_pairs={{0,8},{1,9},{2,10},{3,11},{4,12},{5,13},{6,14},{7,15},{8,0},{9,1},... | collective-permute-start | bytes 608264 | tf_op jit(solution)/shard_map/ppermute | solution.py:309
  9.8 37.9 %collective-permute-start.2 = (bf16[24,4224]{1,0:T(8,128)(2,1)S(1)}, bf16[24,4224]{1,0:T(8,128)(2,1)S(1)}, u32[]{:S(2)}, u32[]{:S(2)}) collective-permute-start(bf16[24,4224]{1,0:T(8,128)(2,1)S(1)} %get-tuple-element.63), channel_id=1, source_target_pairs={{0,12},{1,13},{2,14},{3,15},{4,8},{5,9},{6,10},{7,11},{8,4},{9,5},... | collective-permute-start | bytes 608264 | tf_op jit(solution)/shard_map/ppermute | solution.py:309
  12.7 100.3 %all-to-all-start.3 = ((bf16[16,16,8320]{2,1,0:T(8,128)(2,1)}), bf16[16,16,8320]{2,1,0:T(8,128)(2,1)}, u32[]{:S(2)}, u32[]{:S(2)}) async-start(bf16[16,16,8320]{2,1,0:T(8,128)(2,1)} %bitcast.35), calls=%async_computation.3 | async-start | bytes 8519680 | tf_op jit(solution)/shard_map/all_to_all | solution.py:365
  47.7 57.2 %copy-start.1 = (bf16[16,8192,16]{1,2,0:T(8,128)(2,1)S(1)}, bf16[16,8192,16]{1,2,0:T(8,128)(2,1)}, u32[]{:S(2)}) copy-start(bf16[16,8192,16]{1,2,0:T(8,128)(2,1)} %param.10) | copy-start | bytes 12582916
  47.7 57.2 %copy-start.3 = (bf16[16,16,512]{2,1,0:T(8,128)(2,1)S(1)}, bf16[16,16,512]{2,1,0:T(8,128)(2,1)}, u32[]{:S(2)}) copy-start(bf16[16,16,512]{2,1,0:T(8,128)(2,1)} %param.11) | copy-start | bytes 786436
  47.7 32.0 %collective-permute-start.5 = (bf16[96,4224]{1,0:T(8,128)(2,1)S(1)}, bf16[96,4224]{1,0:T(8,128)(2,1)S(1)}, u32[]{:S(2)}, u32[]{:S(2)}) collective-permute-start(bf16[96,4224]{1,0:T(8,128)(2,1)S(1)} %constant_dynamic-update-slice_fusion.refs_0_), channel_id=1, source_target_pairs={{0,3},{1,2},{2,1},{3,0},{4,7},{5,6},{6,5},{7,4},{8,11},{9,10},{10,... | collective-permute-start | bytes 2433032 | tf_op jit(solution)/shard_map/ppermute | solution.py:309
  47.8 57.1 %collective-permute-start.4 = (bf16[96,4224]{1,0:T(8,128)(2,1)S(1)}, bf16[96,4224]{1,0:T(8,128)(2,1)S(1)}, u32[]{:S(2)}, u32[]{:S(2)}) collective-permute-start(bf16[96,4224]{1,0:T(8,128)(2,1)S(1)} %constant_dynamic-update-slice_fusion.refs_0_), channel_id=1, source_target_pairs={{0,2},{1,3},{2,0},{3,1},{4,6},{5,7},{6,4},{7,5},{8,10},{9,11},{10,... | collective-permute-start | bytes 2433032 | tf_op jit(solution)/shard_map/ppermute | solution.py:309
  47.9 57.0 %collective-permute-start.3 = (bf16[96,4224]{1,0:T(8,128)(2,1)S(1)}, bf16[96,4224]{1,0:T(8,128)(2,1)S(1)}, u32[]{:S(2)}, u32[]{:S(2)}) collective-permute-start(bf16[96,4224]{1,0:T(8,128)(2,1)S(1)} %constant_dynamic-update-slice_fusion.refs_0_), channel_id=1, source_target_pairs={{0,1},{1,0},{2,3},{3,2},{4,5},{5,4},{6,7},{7,6},{8,9},{9,8},{10,11... | collective-permute-start | bytes 2433032 | tf_op jit(solution)/shard_map/ppermute | solution.py:309
  108.1 3.6 %collective-permute-start.6 = (s32[]{:T(128)}, s32[]{:T(128)}, u32[]{:S(2)}, u32[]{:S(2)}) collective-permute-start(s32[]{:T(128)} %bitcast.21), channel_id=1, source_target_pairs={{0,16},{16,0},{1,17},{17,1},{2,18},{18,2},{3,19},{19,3},{4,20},{20... | collective-permute-start | bytes 20 | tf_op jit(solution)/shard_map/ppermute | solution.py:395
  113.0 30.6 %copy-start.2 = (f32[256,512]{1,0:T(8,128)S(1)}, f32[256,512]{1,0:T(8,128)}, u32[]{:S(2)}) copy-start(f32[256,512]{1,0:T(8,128)} %fusion.8) | copy-start | bytes 1572868
  113.0 30.6 %copy-start.6 = (s32[1,256]{1,0:T(1,128)S(1)}, s32[1,256]{1,0:T(1,128)}, u32[]{:S(2)}) copy-start(s32[1,256]{1,0:T(1,128)} %copy-done.5) | copy-start | bytes 3076
  113.0 30.6 %copy-start.7 = (s32[1,256]{1,0:T(1,128)S(1)}, s32[1,256]{1,0:T(1,128)}, u32[]{:S(2)}) copy-start(s32[1,256]{1,0:T(1,128)} %get-tuple-element.68) | copy-start | bytes 3076
  113.0 30.6 %copy-start.8 = (s32[256,1]{0,1:T(1,128)S(1)}, s32[256,1]{0,1:T(1,128)}, u32[]{:S(2)}) copy-start(s32[256,1]{0,1:T(1,128)} %param.12) | copy-start | bytes 3076
  113.0 30.6 %copy-start.9 = (s32[256]{0:T(256)S(1)}, s32[256]{0:T(256)}, u32[]{:S(2)}) copy-start(s32[256]{0:T(256)} %param.13) | copy-start | bytes 3076
  118.7 24.9 %all-to-all-start.4 = ((bf16[16,24,512]{2,1,0:T(8,128)(2,1)}), bf16[16,24,512]{2,1,0:T(8,128)(2,1)S(1)}, u32[]{:S(2)}, u32[]{:S(2)}) async-start(bf16[16,24,512]{2,1,0:T(8,128)(2,1)} %shard_map.69), calls=%async_computation.4 | async-start | bytes 786432 | tf_op jit(solution)/shard_map/all_to_all | solution.py:399
  144.0 0.7 copy-start.4

commit v12 on v11

--- a/solution.py
+++ b/solution.py
@@ -355,11 +355,11 @@
         ),
     )(me.reshape(1), tenant_ids.reshape(1, row_count), tenant_slot.reshape(1, TENANTS), tokens)
 
-    along = [spare[0]] + [swap(spare[b], b * PLANE) for b in range(1, planes)]
-
+    along = [swap(spare[b], b * PLANE) for b in range(planes - 1, 0, -1)]
+    along = list(lax.optimization_barrier(tuple(along)))
     blocks = pack(main_rows, at, note, tokens)
 
-    along = jnp.concatenate(along, axis=0)
+    along = jnp.concatenate([spare[0]] + along[::-1], axis=0)
     shared = [along] + [swap(along, a) for a in range(1, PLANE)]
 
     got = lax.all_to_all(
@@ -388,16 +388,18 @@
         ),
     )(first, down, up, *shared)
 
+    got, extra = lax.optimization_barrier((got, extra))
+    delta = adapt(rank, me.reshape(1), down, up, got, extra)
+    delta, flag = lax.optimization_barrier((delta, flag))
+    back = lax.all_to_all(delta, "ad", split_axis=0, concat_axis=0, tiled=True)
+    back = back.reshape(count * (room + EXTRA), width)
+
     groups = lax.axis_size("grp")
     own = flag[0, 2]
     seen = own
     for g in range(1, groups):
         other = lax.ppermute(own, "grp", [(s, (s + g) % groups) for s in range(groups)])
         seen = jnp.maximum(seen, other)
-    got, extra, seen = lax.optimization_barrier((got, extra, seen))
-    delta = adapt(rank, me.reshape(1), down, up, got, extra)
-    back = lax.all_to_all(delta, "ad", split_axis=0, concat_axis=0, tiled=True)
-    back = back.reshape(count * (room + EXTRA), width)
 
     def finish(base):
         return pl.pallas_call(

time: 145 us -> 141 us (0.972)
  waiting for transfers between devices: 90.3 us -> 87.6 us
    all_to_all x1, waiting for transfers between devices: 12.2 us -> 6.66 us  [on_device(): back = lax.all_to_all(delta, 'ad', split_axis=0, concat_axis=0, tiled=True)]
    ppermute x6, waiting for transfers between devices: 76.1 us -> 78.7 us  [swap(): return lax.ppermute(x, 'ad', [(s, s ^ k) for s in range(count)])]
where the time goes in v12:
time: 141 us
  waiting for transfers between devices  87.6 us (62%)
  starting transfers between devices  27.3 us (19%)
  Pallas kernels  15.5 us (11%)
  matrix products  7.85 us (6%)
  between operations  1.46 us (1%)
  local copies, waits for them, and re-layouts  1.41 us (1%)
    ppermute x6, waiting for transfers between devices, swap(): return lax.ppermute(x, 'ad', [(s, s ^ k) for s in range(count)])  78.7 us
    all_to_all x1, starting transfers between devices, on_device(): back = lax.all_to_all(delta, 'ad', split_axis=0, concat_axis=0, tiled=True)  12 us
    dot_general x1, matrix products, on_device(): jnp.dot(tokens, value_weight, preferred_element_type=jnp.float32)  7.85 us
    ppermute x6, starting transfers between devices, swap(): return lax.ppermute(x, 'ad', [(s, s ^ k) for s in range(count)])  7.67 us
    all_to_all x1, waiting for transfers between devices, on_device(): back = lax.all_to_all(delta, 'ad', split_axis=0, concat_axis=0, tiled=True)  6.66 us
    all_to_all x1, starting transfers between devices, on_device(): lax.all_to_all(blocks.reshape(count, room, depth + NOTE), 'ad', split_axi...  6.14 us
    pallas_call x1, Pallas kernels, adapt(): pl.pallas_call(functools.partial(adapt_body, rank), in_specs=[SMEM, ANY,...  5.63 us
    pallas_call x1, Pallas kernels, on_device(): pl.pallas_call(functools.partial(route_body, room, local), in_specs=[SMEM...  4.1 us
  transfers between devices with their start and end apart: 9, of which 5 were waited for; matrix products, arithmetic and copies ran while one was open for 6% of the time, Pallas kernels for 4%

profile of v12, /device:TPU:0, one launch (start us, length us, event | category | flops | bytes accessed | tf_op | source)
XLA Modules:
  0.0 141.1 jit_solution(12789905115317180333)
XLA Ops:
  0.0 4.1 %shard_map.66 = (bf16[24,4224]{1,0:T(8,128)(2,1)S(1)}, bf16[24,4224]{1,0:T(8,128)(2,1)S(1)}, bf16[24,4224]{1,0:T(8,128)(2,1)S(1)}, bf16[24,4224]{1,0:T(8,128)(2,...) custom-call(s32[1]{0:T(128)} %bitcast.12.me_ref, s32[1,256]{1,0:T(1,128)} %bitcast.51, ...), custom_call_target="tpu_custom_call" | custom-call | flops 805306368 | bytes 6291456 | tf_op jit(solution)/shard_map/pallas_call | solution.py:338
  4.1 5.1 %collective-permute-start = (bf16[24,4224]{1,0:T(8,128)(2,1)S(1)}, bf16[24,4224]{1,0:T(8,128)(2,1)S(1)}, u32[]{:S(2)}, u32[]{:S(2)}) collective-permute-start(bf16[24,4224]{1,0:T(8,128)(2,1)S(1)} %get-tuple-element.65), channel_id=1, source_target_pairs={{0,12},{1,13},{2,14},{3,15},{4,8},{5,9},{6,10},{7,11},{8,4},{9,5},... | collective-permute-start | bytes 608264 | tf_op jit(solution)/shard_map/ppermute | solution.py:309
  9.2 0.6 collective-permute-start.2
  9.9 2.9 %shard_map.67 = bf16[256,8320]{1,0:T(8,128)(2,1)} custom-call(s32[1,256]{1,0:T(1,128)S(1)} %get-tuple-element.62.at_ref, bf16[128,256]{1,0:T(8,128)(2,1)S(1)} %get-tuple-element.63.note_ref, bf16[256,8192]{1,0:T(8,128)(2,1)S(1)} %copy-done), custom_call_target="tpu_custom_call" | custom-call | flops 1073741824 | bytes 8388608 | tf_op jit(solution)/shard_map/pallas_call | solution.py:163
  12.8 6.1 %all-to-all-start.3 = ((bf16[16,16,8320]{2,1,0:T(8,128)(2,1)}), bf16[16,16,8320]{2,1,0:T(8,128)(2,1)}, u32[]{:S(2)}, u32[]{:S(2)}) async-start(bf16[16,16,8320]{2,1,0:T(8,128)(2,1)} %bitcast.35), calls=%async_computation.3 | async-start | bytes 8519680 | tf_op jit(solution)/shard_map/all_to_all | solution.py:365
  19.0 31.5 %collective-permute-done.1 = bf16[24,4224]{1,0:T(8,128)(2,1)S(1)} collective-permute-done((bf16[24,4224]{1,0:T(8,128)(2,1)S(1)}, bf16[24,4224]{1,0:T(8,128)(2,1)S(1)}, u32[]{:S(2)}, u32[]{:S(2)}) %collective-permute-start.1) | collective-permute-done | bytes 202784 | tf_op jit(solution)/shard_map/ppermute | solution.py:309
  50.5 0.1 collective-permute-start.5
  50.6 0.1 collective-permute-start.4
  50.7 1.8 %collective-permute-start.3 = (bf16[96,4224]{1,0:T(8,128)(2,1)S(1)}, bf16[96,4224]{1,0:T(8,128)(2,1)S(1)}, u32[]{:S(2)}, u32[]{:S(2)}) collective-permute-start(bf16[96,4224]{1,0:T(8,128)(2,1)S(1)} %constant_dynamic-update-slice_fusion.refs_0_), channel_id=1, source_target_pairs={{0,1},{1,0},{2,3},{3,2},{4,5},{5,4},{6,7},{7,6},{8,9},{9,8},{10,11... | collective-permute-start | bytes 2433032 | tf_op jit(solution)/shard_map/ppermute | solution.py:309
  52.5 7.9 %fusion.8 = f32[256,512]{1,0:T(8,128)} fusion(bf16[256,8192]{1,0:T(8,128)(2,1)} %tokens_ref.1, bf16[8192,512]{1,0:T(8,128)(2,1)} %param.9), kind=kOutput, calls=%fused_computation.37 | convolution fusion | flops 2147483648 | bytes 13107200 | tf_op jit(solution)/shard_map/dot_general | solution.py:329
  60.3 25.9 %collective-permute-done.5.refs_3_ = bf16[96,4224]{1,0:T(8,128)(2,1)S(1)} collective-permute-done((bf16[96,4224]{1,0:T(8,128)(2,1)S(1)}, bf16[96,4224]{1,0:T(8,128)(2,1)S(1)}, u32[]{:S(2)}, u32[]{:S(2)}) %collective-permute-start.5) | collective-permute-done | bytes 811040 | tf_op jit(solution)/shard_map/ppermute | solution.py:309
  86.2 21.3 %collective-permute-done.4.refs_2_ = bf16[96,4224]{1,0:T(8,128)(2,1)S(1)} collective-permute-done((bf16[96,4224]{1,0:T(8,128)(2,1)S(1)}, bf16[96,4224]{1,0:T(8,128)(2,1)S(1)}, u32[]{:S(2)}, u32[]{:S(2)}) %collective-permute-start.4) | collective-permute-done | bytes 811040 | tf_op jit(solution)/shard_map/ppermute | solution.py:309
  107.6 2.5 %shard_map.68 = (f32[16,8,512]{2,1,0:T(8,128)S(1)}, s32[1,128]{1,0:T(1,128)S(1)}) custom-call(s32[1]{0:T(128)} %bitcast.20.first_ref, bf16[256,8192]{1,0:T(8,128)(2,1)S(1)} %bitcast.38, bf16[256,512]{1,0:T(8,128)(2,1)S(1)} %bitcast.43, bf16[96,4224]{1,0:T(8,128)(2,1)S(1)} %constant_dynamic-update-slice_fusion.refs_0_, ...), custom_call_target="tpu_custom_call" | custom-call | flops 999999995904 | bytes 6291456 | tf_op jit(solution)/shard_map/pallas_call | solution.py:374
  110.1 0.0 copy-start.8
  110.2 0.0 copy-start.9
  110.2 5.6 %shard_map.69 = bf16[16,24,512]{2,1,0:T(8,128)(2,1)} custom-call(s32[1]{0:T(128)} %bitcast.12.me_ref, bf16[256,8192]{1,0:T(8,128)(2,1)} %bitcast.37, bf16[256,512]{1,0:T(8,128)(2,1)S(1)} %bitcast.44, bf16[256,8320]{1,0:T(8,128)(2,1)} %bitcast.19.rows_hbm, f32[16,8,512]{2,1,0:T(8,128)S(1)} %get-tuple-element.74.extra_ref), custom_call_target="tpu_custom_call" | custom-call | flops 1073741824 | bytes 8388608 | tf_op jit(solution)/shard_map/pallas_call | solution.py:227
  115.8 12.0 %all-to-all-start.4 = ((bf16[16,24,512]{2,1,0:T(8,128)(2,1)}), bf16[16,24,512]{2,1,0:T(8,128)(2,1)S(1)}, u32[]{:S(2)}, u32[]{:S(2)}) async-start(bf16[16,24,512]{2,1,0:T(8,128)(2,1)} %shard_map.69), calls=%async_computation.4 | async-start | bytes 786432 | tf_op jit(solution)/shard_map/all_to_all | solution.py:394
  127.9 0.6 slice.3
  128.5 1.5 %collective-permute-start.6 = (s32[]{:T(128)}, s32[]{:T(128)}, u32[]{:S(2)}, u32[]{:S(2)}) collective-permute-start(s32[]{:T(128)} %bitcast.22), channel_id=1, source_target_pairs={{0,16},{16,0},{1,17},{17,1},{2,18},{18,2},{3,19},{19,3},{4,20},{20... | collective-permute-start | bytes 20 | tf_op jit(solution)/shard_map/ppermute | solution.py:401
  129.9 2.2 %collective-permute-done.6 = s32[]{:T(128)} collective-permute-done((s32[]{:T(128)}, s32[]{:T(128)}, u32[]{:S(2)}, u32[]{:S(2)}) %collective-permute-start.6) | collective-permute-done | bytes 36 | tf_op jit(solution)/shard_map/ppermute | solution.py:401
  133.4 6.7 %all-to-all-done.4 = bf16[16,24,512]{2,1,0:T(8,128)(2,1)S(1)} async-done(((bf16[16,24,512]{2,1,0:T(8,128)(2,1)}), bf16[16,24,512]{2,1,0:T(8,128)(2,1)S(1)}, u32[]{:S(2)}, u32[]{:S(2)}) %all-to-all-start.4) | async-done | bytes 393248 | tf_op jit(solution)/shard_map/all_to_all | solution.py:394
  140.1 0.3 conditional.1
  140.1 0.3 branch_0_fun.1
  140.5 0.7 copy-done.4
  (26 shorter events, 0.1 us)
Async XLA Ops:
  0.0 9.9 %copy-start = (bf16[256,8192]{1,0:T(8,128)(2,1)S(1)}, bf16[256,8192]{1,0:T(8,128)(2,1)}, u32[]{:S(2)}) copy-start(bf16[256,8192]{1,0:T(8,128)(2,1)} %tokens_ref.1) | copy-start | bytes 12582916
  4.1 8.7 %copy-start.5 = (s32[1,256]{1,0:T(1,128)}, s32[1,256]{1,0:T(1,128)S(1)}, u32[]{:S(2)}) copy-start(s32[1,256]{1,0:T(1,128)S(1)} %get-tuple-element.62.at_ref) | copy-start | bytes 3076
  4.1 14.8 %collective-permute-start = (bf16[24,4224]{1,0:T(8,128)(2,1)S(1)}, bf16[24,4224]{1,0:T(8,128)(2,1)S(1)}, u32[]{:S(2)}, u32[]{:S(2)}) collective-permute-start(bf16[24,4224]{1,0:T(8,128)(2,1)S(1)} %get-tuple-element.65), channel_id=1, source_target_pairs={{0,12},{1,13},{2,14},{3,15},{4,8},{5,9},{6,10},{7,11},{8,4},{9,5},... | collective-permute-start | bytes 608264 | tf_op jit(solution)/shard_map/ppermute | solution.py:309
  9.2 41.2 %collective-permute-start.1 = (bf16[24,4224]{1,0:T(8,128)(2,1)S(1)}, bf16[24,4224]{1,0:T(8,128)(2,1)S(1)}, u32[]{:S(2)}, u32[]{:S(2)}) collective-permute-start(bf16[24,4224]{1,0:T(8,128)(2,1)S(1)} %get-tuple-element.66), channel_id=1, source_target_pairs={{0,8},{1,9},{2,10},{3,11},{4,12},{5,13},{6,14},{7,15},{8,0},{9,1},... | collective-permute-start | bytes 608264 | tf_op jit(solution)/shard_map/ppermute | solution.py:309
  9.2 41.2 %collective-permute-start.2 = (bf16[24,4224]{1,0:T(8,128)(2,1)S(1)}, bf16[24,4224]{1,0:T(8,128)(2,1)S(1)}, u32[]{:S(2)}, u32[]{:S(2)}) collective-permute-start(bf16[24,4224]{1,0:T(8,128)(2,1)S(1)} %get-tuple-element.67), channel_id=1, source_target_pairs={{0,4},{1,5},{2,6},{3,7},{4,0},{5,1},{6,2},{7,3},{8,12},{9,13},{10,... | collective-permute-start | bytes 608264 | tf_op jit(solution)/shard_map/ppermute | solution.py:309
  12.8 97.3 %all-to-all-start.3 = ((bf16[16,16,8320]{2,1,0:T(8,128)(2,1)}), bf16[16,16,8320]{2,1,0:T(8,128)(2,1)}, u32[]{:S(2)}, u32[]{:S(2)}) async-start(bf16[16,16,8320]{2,1,0:T(8,128)(2,1)} %bitcast.35), calls=%async_computation.3 | async-start | bytes 8519680 | tf_op jit(solution)/shard_map/all_to_all | solution.py:365
  50.5 57.0 %copy-start.1 = (bf16[16,8192,16]{1,2,0:T(8,128)(2,1)S(1)}, bf16[16,8192,16]{1,2,0:T(8,128)(2,1)}, u32[]{:S(2)}) copy-start(bf16[16,8192,16]{1,2,0:T(8,128)(2,1)} %param.10) | copy-start | bytes 12582916
  50.5 57.0 %copy-start.3 = (bf16[16,16,512]{2,1,0:T(8,128)(2,1)S(1)}, bf16[16,16,512]{2,1,0:T(8,128)(2,1)}, u32[]{:S(2)}) copy-start(bf16[16,16,512]{2,1,0:T(8,128)(2,1)} %param.11) | copy-start | bytes 786436
  50.5 35.7 %collective-permute-start.5 = (bf16[96,4224]{1,0:T(8,128)(2,1)S(1)}, bf16[96,4224]{1,0:T(8,128)(2,1)S(1)}, u32[]{:S(2)}, u32[]{:S(2)}) collective-permute-start(bf16[96,4224]{1,0:T(8,128)(2,1)S(1)} %constant_dynamic-update-slice_fusion.refs_0_), channel_id=1, source_target_pairs={{0,3},{1,2},{2,1},{3,0},{4,7},{5,6},{6,5},{7,4},{8,11},{9,10},{10,... | collective-permute-start | bytes 2433032 | tf_op jit(solution)/shard_map/ppermute | solution.py:309
  50.6 56.9 %collective-permute-start.4 = (bf16[96,4224]{1,0:T(8,128)(2,1)S(1)}, bf16[96,4224]{1,0:T(8,128)(2,1)S(1)}, u32[]{:S(2)}, u32[]{:S(2)}) collective-permute-start(bf16[96,4224]{1,0:T(8,128)(2,1)S(1)} %constant_dynamic-update-slice_fusion.refs_0_), channel_id=1, source_target_pairs={{0,2},{1,3},{2,0},{3,1},{4,6},{5,7},{6,4},{7,5},{8,10},{9,11},{10,... | collective-permute-start | bytes 2433032 | tf_op jit(solution)/shard_map/ppermute | solution.py:309
  50.7 56.9 %collective-permute-start.3 = (bf16[96,4224]{1,0:T(8,128)(2,1)S(1)}, bf16[96,4224]{1,0:T(8,128)(2,1)S(1)}, u32[]{:S(2)}, u32[]{:S(2)}) collective-permute-start(bf16[96,4224]{1,0:T(8,128)(2,1)S(1)} %constant_dynamic-update-slice_fusion.refs_0_), channel_id=1, source_target_pairs={{0,1},{1,0},{2,3},{3,2},{4,5},{5,4},{6,7},{7,6},{8,9},{9,8},{10,11... | collective-permute-start | bytes 2433032 | tf_op jit(solution)/shard_map/ppermute | solution.py:309
  110.1 30.0 %copy-start.2 = (f32[256,512]{1,0:T(8,128)S(1)}, f32[256,512]{1,0:T(8,128)}, u32[]{:S(2)}) copy-start(f32[256,512]{1,0:T(8,128)} %fusion.8) | copy-start | bytes 1572868
  110.1 29.9 %copy-start.6 = (s32[1,256]{1,0:T(1,128)S(1)}, s32[1,256]{1,0:T(1,128)}, u32[]{:S(2)}) copy-start(s32[1,256]{1,0:T(1,128)} %copy-done.5) | copy-start | bytes 3076
  110.1 29.9 %copy-start.7 = (s32[1,256]{1,0:T(1,128)S(1)}, s32[1,256]{1,0:T(1,128)}, u32[]{:S(2)}) copy-start(s32[1,256]{1,0:T(1,128)} %get-tuple-element.77) | copy-start | bytes 3076
  110.1 29.9 %copy-start.8 = (s32[256,1]{0,1:T(1,128)S(1)}, s32[256,1]{0,1:T(1,128)}, u32[]{:S(2)}) copy-start(s32[256,1]{0,1:T(1,128)} %param.12) | copy-start | bytes 3076
  110.2 29.9 %copy-start.9 = (s32[256]{0:T(256)S(1)}, s32[256]{0:T(256)}, u32[]{:S(2)}) copy-start(s32[256]{0:T(256)} %param.13) | copy-start | bytes 3076
  115.8 24.3 %all-to-all-start.4 = ((bf16[16,24,512]{2,1,0:T(8,128)(2,1)}), bf16[16,24,512]{2,1,0:T(8,128)(2,1)S(1)}, u32[]{:S(2)}, u32[]{:S(2)}) async-start(bf16[16,24,512]{2,1,0:T(8,128)(2,1)} %shard_map.69), calls=%async_computation.4 | async-start | bytes 786432 | tf_op jit(solution)/shard_map/all_to_all | solution.py:394
  128.5 3.7 %collective-permute-start.6 = (s32[]{:T(128)}, s32[]{:T(128)}, u32[]{:S(2)}, u32[]{:S(2)}) collective-permute-start(s32[]{:T(128)} %bitcast.22), channel_id=1, source_target_pairs={{0,16},{16,0},{1,17},{17,1},{2,18},{18,2},{3,19},{19,3},{4,20},{20... | collective-permute-start | bytes 20 | tf_op jit(solution)/shard_map/ppermute | solution.py:401
  140.4 0.7 copy-start.4

commit v13 on v12

--- a/solution.py
+++ b/solution.py
@@ -169,7 +169,7 @@
             pltpu.VMEM(out.shape, jnp.bfloat16),
             pltpu.SemaphoreType.DMA((PARTS,)),
         ],
-        compiler_params=pltpu.CompilerParams(vmem_limit_bytes=52 * 2**20),
+        compiler_params=pltpu.CompilerParams(vmem_limit_bytes=48 * 2**20),
         cost_estimate=pl.CostEstimate(
             flops=2 * main_rows * rows * depth, bytes_accessed=8 * 2**20, transcendentals=0
         ),
@@ -335,18 +335,18 @@
         return (base_value + delta).astype(jnp.bfloat16)
 
     main_rows = count * room
-    *spare, at, at_back, note = pl.pallas_call(
+    *spare, at, at_back, note, near = pl.pallas_call(
         functools.partial(route_body, room, local),
         in_specs=[SMEM, VMEM, VMEM, ANY],
-        out_specs=[VMEM] * (planes + 3),
+        out_specs=[VMEM] * (planes + 4),
         out_shape=[jax.ShapeDtypeStruct((2 * SPARE, depth // 2 + NOTE), jnp.bfloat16)] * planes
         + [
             jax.ShapeDtypeStruct((1, row_count), jnp.int32),
             jax.ShapeDtypeStruct((1, row_count), jnp.int32),
             jax.ShapeDtypeStruct((NOTE, row_count), jnp.bfloat16),
+            jax.ShapeDtypeStruct(tokens.shape, jnp.bfloat16),
         ],
         scratch_shapes=[
-            pltpu.VMEM(tokens.shape, jnp.bfloat16),
             pltpu.SemaphoreType.DMA((PARTS,)),
         ],
         compiler_params=pltpu.CompilerParams(vmem_limit_bytes=24 * 2**20),
@@ -357,7 +357,7 @@
 
     along = [swap(spare[b], b * PLANE) for b in range(planes - 1, 0, -1)]
     along = list(lax.optimization_barrier(tuple(along)))
-    blocks = pack(main_rows, at, note, tokens)
+    blocks = pack(main_rows, at, note, near)
 
     along = jnp.concatenate([spare[0]] + along[::-1], axis=0)
     shared = [along] + [swap(along, a) for a in range(1, PLANE)]

time: 141 us -> 141 us (level)
  waiting for transfers between devices: 87.6 us -> 90 us
  starting transfers between devices: 27.3 us -> 24.9 us
    ppermute x6, waiting for transfers between devices: 78.7 us -> 81.2 us  [swap(): return lax.ppermute(x, 'ad', [(s, s ^ k) for s in range(count)])]
    all_to_all x1, starting transfers between devices: 12 us -> 9.61 us  [on_device(): back = lax.all_to_all(delta, 'ad', split_axis=0, concat_axis=0, tiled=True)]
where the time goes in v13:
time: 141 us
  waiting for transfers between devices  90 us (64%)
  starting transfers between devices  24.9 us (18%)
  Pallas kernels  15.2 us (11%)
  matrix products  7.84 us (6%)
  local copies, waits for them, and re-layouts  1.47 us (1%)
  between operations  1.47 us (1%)
    ppermute x6, waiting for transfers between devices, swap(): return lax.ppermute(x, 'ad', [(s, s ^ k) for s in range(count)])  81.2 us
    all_to_all x1, starting transfers between devices, on_device(): back = lax.all_to_all(delta, 'ad', split_axis=0, concat_axis=0, tiled=True)  9.61 us
    dot_general x1, matrix products, on_device(): jnp.dot(tokens, value_weight, preferred_element_type=jnp.float32)  7.84 us
    ppermute x6, starting transfers between devices, swap(): return lax.ppermute(x, 'ad', [(s, s ^ k) for s in range(count)])  7.68 us
    all_to_all x1, waiting for transfers between devices, on_device(): back = lax.all_to_all(delta, 'ad', split_axis=0, concat_axis=0, tiled=True)  6.59 us
    all_to_all x1, starting transfers between devices, on_device(): lax.all_to_all(blocks.reshape(count, room, depth + NOTE), 'ad', split_axi...  6.14 us
    pallas_call x1, Pallas kernels, adapt(): pl.pallas_call(functools.partial(adapt_body, rank), in_specs=[SMEM, ANY,...  5.65 us
    pallas_call x1, Pallas kernels, on_device(): pl.pallas_call(functools.partial(route_body, room, local), in_specs=[SMEM...  3.84 us
  transfers between devices with their start and end apart: 9, of which 5 were waited for; matrix products, arithmetic and copies ran while one was open for 6% of the time, Pallas kernels for 4%

profile of v13, /device:TPU:0, one launch (start us, length us, event | category | flops | bytes accessed | tf_op | source)
XLA Modules:
  0.0 140.9 jit_solution(6877789740998827168)
XLA Ops:
  0.0 3.8 %shard_map.66 = (bf16[24,4224]{1,0:T(8,128)(2,1)S(1)}, bf16[24,4224]{1,0:T(8,128)(2,1)S(1)}, bf16[24,4224]{1,0:T(8,128)(2,1)S(1)}, bf16[24,4224]{1,0:T(8,128)(2,...) custom-call(s32[1]{0:T(128)} %bitcast.12.me_ref, ...), custom_call_target="tpu_custom_call" | custom-call | flops 805306368 | bytes 6291456 | tf_op jit(solution)/shard_map/pallas_call | solution.py:338
  3.9 5.1 %collective-permute-start = (bf16[24,4224]{1,0:T(8,128)(2,1)S(1)}, bf16[24,4224]{1,0:T(8,128)(2,1)S(1)}, u32[]{:S(2)}, u32[]{:S(2)}) collective-permute-start(bf16[24,4224]{1,0:T(8,128)(2,1)S(1)} %get-tuple-element.67), channel_id=1, source_target_pairs={{0,12},{1,13},{2,14},{3,15},{4,8},{5,9},{6,10},{7,11},{8,4},{9,5},... | collective-permute-start | bytes 608264 | tf_op jit(solution)/shard_map/ppermute | solution.py:309
  9.0 0.6 collective-permute-start.2
  9.6 2.9 %shard_map.67 = bf16[256,8320]{1,0:T(8,128)(2,1)} custom-call(s32[1,256]{1,0:T(1,128)S(1)} %get-tuple-element.63.at_ref, bf16[128,256]{1,0:T(8,128)(2,1)S(1)} %get-tuple-element.64.note_ref, bf16[256,8192]{1,0:T(8,128)(2,1)S(1)} %get-tuple-element.65.tokens_ref), custom_call_target="tpu_custom_call" | custom-call | flops 1073741824 | bytes 8388608 | tf_op jit(solution)/shard_map/pallas_call | solution.py:163
  12.5 6.1 %all-to-all-start.3 = ((bf16[16,16,8320]{2,1,0:T(8,128)(2,1)}), bf16[16,16,8320]{2,1,0:T(8,128)(2,1)}, u32[]{:S(2)}, u32[]{:S(2)}) async-start(bf16[16,16,8320]{2,1,0:T(8,128)(2,1)} %bitcast.35), calls=%async_computation.3 | async-start | bytes 8519680 | tf_op jit(solution)/shard_map/all_to_all | solution.py:365
  18.7 31.5 %collective-permute-done.1 = bf16[24,4224]{1,0:T(8,128)(2,1)S(1)} collective-permute-done((bf16[24,4224]{1,0:T(8,128)(2,1)S(1)}, bf16[24,4224]{1,0:T(8,128)(2,1)S(1)}, u32[]{:S(2)}, u32[]{:S(2)}) %collective-permute-start.1) | collective-permute-done | bytes 202784 | tf_op jit(solution)/shard_map/ppermute | solution.py:309
  50.2 0.0 copy-start
  50.3 0.0 copy-start.2
  50.3 0.1 collective-permute-start.3
  50.3 0.1 collective-permute-start.4
  50.4 1.8 %collective-permute-start.5 = (bf16[96,4224]{1,0:T(8,128)(2,1)S(1)}, bf16[96,4224]{1,0:T(8,128)(2,1)S(1)}, u32[]{:S(2)}, u32[]{:S(2)}) collective-permute-start(bf16[96,4224]{1,0:T(8,128)(2,1)S(1)} %constant_dynamic-update-slice_fusion.refs_0_), channel_id=1, source_target_pairs={{0,3},{1,2},{2,1},{3,0},{4,7},{5,6},{6,5},{7,4},{8,11},{9,10},{10,... | collective-permute-start | bytes 2433032 | tf_op jit(solution)/shard_map/ppermute | solution.py:309
  52.2 7.8 %fusion.8 = f32[256,512]{1,0:T(8,128)} fusion(bf16[256,8192]{1,0:T(8,128)(2,1)} %tokens_hbm.1, bf16[8192,512]{1,0:T(8,128)(2,1)} %param.9), kind=kOutput, calls=%fused_computation.37 | convolution fusion | flops 2147483648 | bytes 13107200 | tf_op jit(solution)/shard_map/dot_general | solution.py:329
  60.1 25.9 %collective-permute-done.4.refs_2_ = bf16[96,4224]{1,0:T(8,128)(2,1)S(1)} collective-permute-done((bf16[96,4224]{1,0:T(8,128)(2,1)S(1)}, bf16[96,4224]{1,0:T(8,128)(2,1)S(1)}, u32[]{:S(2)}, u32[]{:S(2)}) %collective-permute-start.4) | collective-permute-done | bytes 811040 | tf_op jit(solution)/shard_map/ppermute | solution.py:309
  86.0 23.7 %collective-permute-done.5.refs_3_ = bf16[96,4224]{1,0:T(8,128)(2,1)S(1)} collective-permute-done((bf16[96,4224]{1,0:T(8,128)(2,1)S(1)}, bf16[96,4224]{1,0:T(8,128)(2,1)S(1)}, u32[]{:S(2)}, u32[]{:S(2)}) %collective-permute-start.5) | collective-permute-done | bytes 811040 | tf_op jit(solution)/shard_map/ppermute | solution.py:309
  109.7 2.5 %shard_map.68 = (f32[16,8,512]{2,1,0:T(8,128)S(1)}, s32[1,128]{1,0:T(1,128)S(1)}) custom-call(s32[1]{0:T(128)} %bitcast.20.first_ref, bf16[256,8192]{1,0:T(8,128)(2,1)S(1)} %bitcast.38, bf16[256,512]{1,0:T(8,128)(2,1)S(1)} %bitcast.43, bf16[96,4224]{1,0:T(8,128)(2,1)S(1)} %constant_dynamic-update-slice_fusion.refs_0_, ...), custom_call_target="tpu_custom_call" | custom-call | flops 999999995904 | bytes 6291456 | tf_op jit(solution)/shard_map/pallas_call | solution.py:374
  112.3 5.7 %shard_map.69 = bf16[16,24,512]{2,1,0:T(8,128)(2,1)} custom-call(s32[1]{0:T(128)} %bitcast.12.me_ref, bf16[256,8192]{1,0:T(8,128)(2,1)} %bitcast.37, bf16[256,512]{1,0:T(8,128)(2,1)S(1)} %bitcast.44, bf16[256,8320]{1,0:T(8,128)(2,1)} %bitcast.19.rows_hbm, f32[16,8,512]{2,1,0:T(8,128)S(1)} %get-tuple-element.76.extra_ref), custom_call_target="tpu_custom_call" | custom-call | flops 1073741824 | bytes 8388608 | tf_op jit(solution)/shard_map/pallas_call | solution.py:227
  118.0 9.6 %all-to-all-start.4 = ((bf16[16,24,512]{2,1,0:T(8,128)(2,1)}), bf16[16,24,512]{2,1,0:T(8,128)(2,1)S(1)}, u32[]{:S(2)}, u32[]{:S(2)}) async-start(bf16[16,24,512]{2,1,0:T(8,128)(2,1)} %shard_map.69), calls=%async_computation.4 | async-start | bytes 786432 | tf_op jit(solution)/shard_map/all_to_all | solution.py:394
  127.6 0.6 slice.3
  128.3 1.5 %collective-permute-start.6 = (s32[]{:T(128)}, s32[]{:T(128)}, u32[]{:S(2)}, u32[]{:S(2)}) collective-permute-start(s32[]{:T(128)} %bitcast.22), channel_id=1, source_target_pairs={{0,16},{16,0},{1,17},{17,1},{2,18},{18,2},{3,19},{19,3},{4,20},{20... | collective-permute-start | bytes 20 | tf_op jit(solution)/shard_map/ppermute | solution.py:401
  129.7 2.2 %collective-permute-done.6 = s32[]{:T(128)} collective-permute-done((s32[]{:T(128)}, s32[]{:T(128)}, u32[]{:S(2)}, u32[]{:S(2)}) %collective-permute-start.6) | collective-permute-done | bytes 36 | tf_op jit(solution)/shard_map/ppermute | solution.py:401
  133.2 6.6 %all-to-all-done.4 = bf16[16,24,512]{2,1,0:T(8,128)(2,1)S(1)} async-done(((bf16[16,24,512]{2,1,0:T(8,128)(2,1)}), bf16[16,24,512]{2,1,0:T(8,128)(2,1)S(1)}, u32[]{:S(2)}, u32[]{:S(2)}) %all-to-all-start.4) | async-done | bytes 393248 | tf_op jit(solution)/shard_map/all_to_all | solution.py:394
  139.8 0.3 conditional.1
  139.9 0.3 branch_0_fun.1
  140.2 0.7 copy-done.3
  (24 shorter events, 0.1 us)
Async XLA Ops:
  3.9 8.6 %copy-start.4 = (s32[1,256]{1,0:T(1,128)}, s32[1,256]{1,0:T(1,128)S(1)}, u32[]{:S(2)}) copy-start(s32[1,256]{1,0:T(1,128)S(1)} %get-tuple-element.63.at_ref) | copy-start | bytes 3076
  3.9 14.8 %collective-permute-start = (bf16[24,4224]{1,0:T(8,128)(2,1)S(1)}, bf16[24,4224]{1,0:T(8,128)(2,1)S(1)}, u32[]{:S(2)}, u32[]{:S(2)}) collective-permute-start(bf16[24,4224]{1,0:T(8,128)(2,1)S(1)} %get-tuple-element.67), channel_id=1, source_target_pairs={{0,12},{1,13},{2,14},{3,15},{4,8},{5,9},{6,10},{7,11},{8,4},{9,5},... | collective-permute-start | bytes 608264 | tf_op jit(solution)/shard_map/ppermute | solution.py:309
  9.0 41.2 %collective-permute-start.1 = (bf16[24,4224]{1,0:T(8,128)(2,1)S(1)}, bf16[24,4224]{1,0:T(8,128)(2,1)S(1)}, u32[]{:S(2)}, u32[]{:S(2)}) collective-permute-start(bf16[24,4224]{1,0:T(8,128)(2,1)S(1)} %get-tuple-element.68), channel_id=1, source_target_pairs={{0,8},{1,9},{2,10},{3,11},{4,12},{5,13},{6,14},{7,15},{8,0},{9,1},... | collective-permute-start | bytes 608264 | tf_op jit(solution)/shard_map/ppermute | solution.py:309
  9.0 41.2 %collective-permute-start.2 = (bf16[24,4224]{1,0:T(8,128)(2,1)S(1)}, bf16[24,4224]{1,0:T(8,128)(2,1)S(1)}, u32[]{:S(2)}, u32[]{:S(2)}) collective-permute-start(bf16[24,4224]{1,0:T(8,128)(2,1)S(1)} %get-tuple-element.69), channel_id=1, source_target_pairs={{0,4},{1,5},{2,6},{3,7},{4,0},{5,1},{6,2},{7,3},{8,12},{9,13},{10,... | collective-permute-start | bytes 608264 | tf_op jit(solution)/shard_map/ppermute | solution.py:309
  12.5 99.8 %all-to-all-start.3 = ((bf16[16,16,8320]{2,1,0:T(8,128)(2,1)}), bf16[16,16,8320]{2,1,0:T(8,128)(2,1)}, u32[]{:S(2)}, u32[]{:S(2)}) async-start(bf16[16,16,8320]{2,1,0:T(8,128)(2,1)} %bitcast.35), calls=%async_computation.3 | async-start | bytes 8519680 | tf_op jit(solution)/shard_map/all_to_all | solution.py:365
  50.2 59.5 %copy-start = (bf16[16,8192,16]{1,2,0:T(8,128)(2,1)S(1)}, bf16[16,8192,16]{1,2,0:T(8,128)(2,1)}, u32[]{:S(2)}) copy-start(bf16[16,8192,16]{1,2,0:T(8,128)(2,1)} %param.10) | copy-start | bytes 12582916
  50.3 59.5 %copy-start.2 = (bf16[16,16,512]{2,1,0:T(8,128)(2,1)S(1)}, bf16[16,16,512]{2,1,0:T(8,128)(2,1)}, u32[]{:S(2)}) copy-start(bf16[16,16,512]{2,1,0:T(8,128)(2,1)} %param.11) | copy-start | bytes 786436
  50.3 9.8 %collective-permute-start.3 = (bf16[96,4224]{1,0:T(8,128)(2,1)S(1)}, bf16[96,4224]{1,0:T(8,128)(2,1)S(1)}, u32[]{:S(2)}, u32[]{:S(2)}) collective-permute-start(bf16[96,4224]{1,0:T(8,128)(2,1)S(1)} %constant_dynamic-update-slice_fusion.refs_0_), channel_id=1, source_target_pairs={{0,1},{1,0},{2,3},{3,2},{4,5},{5,4},{6,7},{7,6},{8,9},{9,8},{10,11... | collective-permute-start | bytes 2433032 | tf_op jit(solution)/shard_map/ppermute | solution.py:309
  50.3 35.6 %collective-permute-start.4 = (bf16[96,4224]{1,0:T(8,128)(2,1)S(1)}, bf16[96,4224]{1,0:T(8,128)(2,1)S(1)}, u32[]{:S(2)}, u32[]{:S(2)}) collective-permute-start(bf16[96,4224]{1,0:T(8,128)(2,1)S(1)} %constant_dynamic-update-slice_fusion.refs_0_), channel_id=1, source_target_pairs={{0,2},{1,3},{2,0},{3,1},{4,6},{5,7},{6,4},{7,5},{8,10},{9,11},{10,... | collective-permute-start | bytes 2433032 | tf_op jit(solution)/shard_map/ppermute | solution.py:309
  50.4 59.3 %collective-permute-start.5 = (bf16[96,4224]{1,0:T(8,128)(2,1)S(1)}, bf16[96,4224]{1,0:T(8,128)(2,1)S(1)}, u32[]{:S(2)}, u32[]{:S(2)}) collective-permute-start(bf16[96,4224]{1,0:T(8,128)(2,1)S(1)} %constant_dynamic-update-slice_fusion.refs_0_), channel_id=1, source_target_pairs={{0,3},{1,2},{2,1},{3,0},{4,7},{5,6},{6,5},{7,4},{8,11},{9,10},{10,... | collective-permute-start | bytes 2433032 | tf_op jit(solution)/shard_map/ppermute | solution.py:309
  112.3 27.5 %copy-start.1 = (f32[256,512]{1,0:T(8,128)S(1)}, f32[256,512]{1,0:T(8,128)}, u32[]{:S(2)}) copy-start(f32[256,512]{1,0:T(8,128)} %fusion.8) | copy-start | bytes 1572868
  112.3 27.5 %copy-start.5 = (s32[1,256]{1,0:T(1,128)S(1)}, s32[1,256]{1,0:T(1,128)}, u32[]{:S(2)}) copy-start(s32[1,256]{1,0:T(1,128)} %copy-done.4) | copy-start | bytes 3076
  112.3 27.5 %copy-start.6 = (s32[1,256]{1,0:T(1,128)S(1)}, s32[1,256]{1,0:T(1,128)}, u32[]{:S(2)}) copy-start(s32[1,256]{1,0:T(1,128)} %get-tuple-element.79) | copy-start | bytes 3076
  112.3 27.5 %copy-start.7 = (s32[256,1]{0,1:T(1,128)S(1)}, s32[256,1]{0,1:T(1,128)}, u32[]{:S(2)}) copy-start(s32[256,1]{0,1:T(1,128)} %param.12) | copy-start | bytes 3076
  112.3 27.5 %copy-start.8 = (s32[256]{0:T(256)S(1)}, s32[256]{0:T(256)}, u32[]{:S(2)}) copy-start(s32[256]{0:T(256)} %param.13) | copy-start | bytes 3076
  118.0 21.8 %all-to-all-start.4 = ((bf16[16,24,512]{2,1,0:T(8,128)(2,1)}), bf16[16,24,512]{2,1,0:T(8,128)(2,1)S(1)}, u32[]{:S(2)}, u32[]{:S(2)}) async-start(bf16[16,24,512]{2,1,0:T(8,128)(2,1)} %shard_map.69), calls=%async_computation.4 | async-start | bytes 786432 | tf_op jit(solution)/shard_map/all_to_all | solution.py:394
  128.3 3.7 %collective-permute-start.6 = (s32[]{:T(128)}, s32[]{:T(128)}, u32[]{:S(2)}, u32[]{:S(2)}) collective-permute-start(s32[]{:T(128)} %bitcast.22), channel_id=1, source_target_pairs={{0,16},{16,0},{1,17},{17,1},{2,18},{18,2},{3,19},{19,3},{4,20},{20... | collective-permute-start | bytes 20 | tf_op jit(solution)/shard_map/ppermute | solution.py:401
  140.2 0.7 copy-start.3

commit v14 on v12

--- a/solution.py
+++ b/solution.py
@@ -14,7 +14,6 @@
 EXTRA = 8
 NOTE = 128
 STEP = 1024
-WIDE = 1664
 PARTS = 8
 VMEM = pl.BlockSpec(memory_space=pltpu.VMEM)
 ANY = pl.BlockSpec(memory_space=pl.ANY)
@@ -185,27 +184,17 @@
 def adapt_body(rank, me_ref, down_hbm, up_ref, rows_hbm, extra_ref, out, *scratch):
     down_ref, rows_ref, down_sems, sems = scratch
     depth = down_ref.shape[1]
-    spans = [slice(c, min(c + WIDE, depth + NOTE)) for c in range(0, depth + NOTE, WIDE)]
-    copies = []
-    for i, span in enumerate(spans):
-        kept = slice(span.start, min(span.stop, depth))
-        copies.append(
-            (
-                pltpu.make_async_copy(rows_hbm.at[:, span], rows_ref.at[:, span], sems.at[i]),
-                pltpu.make_async_copy(down_hbm.at[:, kept], down_ref.at[:, kept], down_sems.at[i]),
-            )
-        )
-    for pair in copies:
-        pair[0].start()
-        pair[1].start()
+    copies = row_copies(down_hbm, down_ref, down_sems, PARTS)
+    copies += row_copies(rows_hbm, rows_ref, sems, PARTS)
+    for copy in copies:
+        copy.start()
+    for copy in copies:
+        copy.wait()
     low = jnp.zeros((rows_ref.shape[0], down_ref.shape[0]), jnp.float32)
-    for pair, span in zip(copies, spans, strict=True):
-        pair[0].wait()
-        pair[1].wait()
-        span = slice(span.start, min(span.stop, depth))
+    for c in range(0, depth, STEP):
         low += lax.dot_general(
-            rows_ref[:, span],
-            down_ref[:, span],
+            rows_ref[:, c : c + STEP],
+            down_ref[:, c : c + STEP],
             (((1,), (1,)), ((), ())),
             preferred_element_type=jnp.float32,
         )
@@ -232,8 +221,8 @@
         scratch_shapes=[
             pltpu.VMEM(down.shape, jnp.bfloat16),
             pltpu.VMEM(got.shape, jnp.bfloat16),
-            pltpu.SemaphoreType.DMA((pl.cdiv(got.shape[1], WIDE),)),
-            pltpu.SemaphoreType.DMA((pl.cdiv(got.shape[1], WIDE),)),
+            pltpu.SemaphoreType.DMA((PARTS,)),
+            pltpu.SemaphoreType.DMA((PARTS,)),
         ],
         compiler_params=pltpu.CompilerParams(vmem_limit_bytes=24 * 2**20),
         cost_estimate=pl.CostEstimate(

time: 141 us -> 142 us (level)
  no operation moved by 1% of the time
where the time goes in v14:
time: 142 us; the launch traced here: 141 us
  waiting for transfers between devices  87.6 us (62%)
  starting transfers between devices  27.3 us (19%)
  Pallas kernels  15.7 us (11%)
  matrix products  7.85 us (6%)
  between operations  1.46 us (1%)
    ppermute x6, waiting for transfers between devices, swap(): return lax.ppermute(x, 'ad', [(s, s ^ k) for s in range(count)])  78.7 us
    all_to_all x1, starting transfers between devices, on_device(): back = lax.all_to_all(delta, 'ad', split_axis=0, concat_axis=0, tiled=True)  12 us
    dot_general x1, matrix products, on_device(): jnp.dot(tokens, value_weight, preferred_element_type=jnp.float32)  7.85 us
    ppermute x6, starting transfers between devices, swap(): return lax.ppermute(x, 'ad', [(s, s ^ k) for s in range(count)])  7.67 us
    all_to_all x1, waiting for transfers between devices, on_device(): back = lax.all_to_all(delta, 'ad', split_axis=0, concat_axis=0, tiled=True)  6.66 us
    all_to_all x1, starting transfers between devices, on_device(): lax.all_to_all(blocks.reshape(count, room, depth + NOTE), 'ad', split_axi...  6.14 us
    pallas_call x1, Pallas kernels, adapt(): pl.pallas_call(functools.partial(adapt_body, rank), in_specs=[SMEM, ANY,...  5.87 us
    pallas_call x1, Pallas kernels, on_device(): pl.pallas_call(functools.partial(route_body, room, local), in_specs=[SMEM...  4.1 us
  transfers between devices with their start and end apart: 9, of which 5 were waited for; matrix products, arithmetic and copies ran while one was open for 6% of the time, Pallas kernels for 4%

profile of v14, /device:TPU:0, one launch (start us, length us, event | category | flops | bytes accessed | tf_op | source)
XLA Modules:
  0.0 141.4 jit_solution(12347445020228060199)
XLA Ops:
  0.0 4.1 %shard_map.66 = (bf16[24,4224]{1,0:T(8,128)(2,1)S(1)}, bf16[24,4224]{1,0:T(8,128)(2,1)S(1)}, bf16[24,4224]{1,0:T(8,128)(2,1)S(1)}, bf16[24,4224]{1,0:T(8,128)(2,...) custom-call(s32[1]{0:T(128)} %bitcast.12.me_ref, s32[1,256]{1,0:T(1,128)} %bitcast.51, ...), custom_call_target="tpu_custom_call" | custom-call | flops 805306368 | bytes 6291456 | tf_op jit(solution)/shard_map/pallas_call | solution.py:327
  4.1 5.1 %collective-permute-start = (bf16[24,4224]{1,0:T(8,128)(2,1)S(1)}, bf16[24,4224]{1,0:T(8,128)(2,1)S(1)}, u32[]{:S(2)}, u32[]{:S(2)}) collective-permute-start(bf16[24,4224]{1,0:T(8,128)(2,1)S(1)} %get-tuple-element.65), channel_id=1, source_target_pairs={{0,12},{1,13},{2,14},{3,15},{4,8},{5,9},{6,10},{7,11},{8,4},{9,5},... | collective-permute-start | bytes 608264 | tf_op jit(solution)/shard_map/ppermute | solution.py:298
  9.2 0.6 collective-permute-start.2
  9.9 2.9 %shard_map.67 = bf16[256,8320]{1,0:T(8,128)(2,1)} custom-call(s32[1,256]{1,0:T(1,128)S(1)} %get-tuple-element.62.at_ref, bf16[128,256]{1,0:T(8,128)(2,1)S(1)} %get-tuple-element.63.note_ref, bf16[256,8192]{1,0:T(8,128)(2,1)S(1)} %copy-done), custom_call_target="tpu_custom_call" | custom-call | flops 1073741824 | bytes 8388608 | tf_op jit(solution)/shard_map/pallas_call | solution.py:162
  12.8 6.1 %all-to-all-start.3 = ((bf16[16,16,8320]{2,1,0:T(8,128)(2,1)}), bf16[16,16,8320]{2,1,0:T(8,128)(2,1)}, u32[]{:S(2)}, u32[]{:S(2)}) async-start(bf16[16,16,8320]{2,1,0:T(8,128)(2,1)} %bitcast.35), calls=%async_computation.3 | async-start | bytes 8519680 | tf_op jit(solution)/shard_map/all_to_all | solution.py:354
  19.0 31.5 %collective-permute-done.1 = bf16[24,4224]{1,0:T(8,128)(2,1)S(1)} collective-permute-done((bf16[24,4224]{1,0:T(8,128)(2,1)S(1)}, bf16[24,4224]{1,0:T(8,128)(2,1)S(1)}, u32[]{:S(2)}, u32[]{:S(2)}) %collective-permute-start.1) | collective-permute-done | bytes 202784 | tf_op jit(solution)/shard_map/ppermute | solution.py:298
  50.5 0.0 copy-start.1
  50.5 0.1 collective-permute-start.5
  50.6 0.1 collective-permute-start.4
  50.7 1.8 %collective-permute-start.3 = (bf16[96,4224]{1,0:T(8,128)(2,1)S(1)}, bf16[96,4224]{1,0:T(8,128)(2,1)S(1)}, u32[]{:S(2)}, u32[]{:S(2)}) collective-permute-start(bf16[96,4224]{1,0:T(8,128)(2,1)S(1)} %constant_dynamic-update-slice_fusion.refs_0_), channel_id=1, source_target_pairs={{0,1},{1,0},{2,3},{3,2},{4,5},{5,4},{6,7},{7,6},{8,9},{9,8},{10,11... | collective-permute-start | bytes 2433032 | tf_op jit(solution)/shard_map/ppermute | solution.py:298
  52.5 7.9 %fusion.8 = f32[256,512]{1,0:T(8,128)} fusion(bf16[256,8192]{1,0:T(8,128)(2,1)} %tokens_ref.1, bf16[8192,512]{1,0:T(8,128)(2,1)} %param.9), kind=kOutput, calls=%fused_computation.37 | convolution fusion | flops 2147483648 | bytes 13107200 | tf_op jit(solution)/shard_map/dot_general | solution.py:318
  60.3 25.9 %collective-permute-done.5.refs_3_ = bf16[96,4224]{1,0:T(8,128)(2,1)S(1)} collective-permute-done((bf16[96,4224]{1,0:T(8,128)(2,1)S(1)}, bf16[96,4224]{1,0:T(8,128)(2,1)S(1)}, u32[]{:S(2)}, u32[]{:S(2)}) %collective-permute-start.5) | collective-permute-done | bytes 811040 | tf_op jit(solution)/shard_map/ppermute | solution.py:298
  86.2 21.3 %collective-permute-done.4.refs_2_ = bf16[96,4224]{1,0:T(8,128)(2,1)S(1)} collective-permute-done((bf16[96,4224]{1,0:T(8,128)(2,1)S(1)}, bf16[96,4224]{1,0:T(8,128)(2,1)S(1)}, u32[]{:S(2)}, u32[]{:S(2)}) %collective-permute-start.4) | collective-permute-done | bytes 811040 | tf_op jit(solution)/shard_map/ppermute | solution.py:298
  107.6 2.5 %shard_map.68 = (f32[16,8,512]{2,1,0:T(8,128)S(1)}, s32[1,128]{1,0:T(1,128)S(1)}) custom-call(s32[1]{0:T(128)} %bitcast.20.first_ref, bf16[256,8192]{1,0:T(8,128)(2,1)S(1)} %bitcast.38, bf16[256,512]{1,0:T(8,128)(2,1)S(1)} %bitcast.43, bf16[96,4224]{1,0:T(8,128)(2,1)S(1)} %constant_dynamic-update-slice_fusion.refs_0_, ...), custom_call_target="tpu_custom_call" | custom-call | flops 999999995904 | bytes 6291456 | tf_op jit(solution)/shard_map/pallas_call | solution.py:363
  110.1 0.0 copy-start.7
  110.2 5.9 %shard_map.69 = bf16[16,24,512]{2,1,0:T(8,128)(2,1)} custom-call(s32[1]{0:T(128)} %bitcast.12.me_ref, bf16[256,8192]{1,0:T(8,128)(2,1)} %bitcast.37, bf16[256,512]{1,0:T(8,128)(2,1)S(1)} %bitcast.44, bf16[256,8320]{1,0:T(8,128)(2,1)} %bitcast.19.rows_hbm, f32[16,8,512]{2,1,0:T(8,128)S(1)} %get-tuple-element.74.extra_ref), custom_call_target="tpu_custom_call" | custom-call | flops 1073741824 | bytes 8388608 | tf_op jit(solution)/shard_map/pallas_call | solution.py:216
  116.0 12.0 %all-to-all-start.4 = ((bf16[16,24,512]{2,1,0:T(8,128)(2,1)}), bf16[16,24,512]{2,1,0:T(8,128)(2,1)S(1)}, u32[]{:S(2)}, u32[]{:S(2)}) async-start(bf16[16,24,512]{2,1,0:T(8,128)(2,1)} %shard_map.69), calls=%async_computation.4 | async-start | bytes 786432 | tf_op jit(solution)/shard_map/all_to_all | solution.py:383
  128.1 0.6 slice.3
  128.7 1.5 %collective-permute-start.6 = (s32[]{:T(128)}, s32[]{:T(128)}, u32[]{:S(2)}, u32[]{:S(2)}) collective-permute-start(s32[]{:T(128)} %bitcast.22), channel_id=1, source_target_pairs={{0,16},{16,0},{1,17},{17,1},{2,18},{18,2},{3,19},{19,3},{4,20},{20... | collective-permute-start | bytes 20 | tf_op jit(solution)/shard_map/ppermute | solution.py:390
  130.2 2.2 %collective-permute-done.6 = s32[]{:T(128)} collective-permute-done((s32[]{:T(128)}, s32[]{:T(128)}, u32[]{:S(2)}, u32[]{:S(2)}) %collective-permute-start.6) | collective-permute-done | bytes 36 | tf_op jit(solution)/shard_map/ppermute | solution.py:390
  133.6 6.7 %all-to-all-done.4 = bf16[16,24,512]{2,1,0:T(8,128)(2,1)S(1)} async-done(((bf16[16,24,512]{2,1,0:T(8,128)(2,1)}), bf16[16,24,512]{2,1,0:T(8,128)(2,1)S(1)}, u32[]{:S(2)}, u32[]{:S(2)}) %all-to-all-start.4) | async-done | bytes 393248 | tf_op jit(solution)/shard_map/all_to_all | solution.py:383
  140.3 0.3 conditional.1
  140.3 0.3 branch_0_fun.1
  140.7 0.7 copy-done.4
  (26 shorter events, 0.1 us)
Async XLA Ops:
  0.0 9.9 %copy-start = (bf16[256,8192]{1,0:T(8,128)(2,1)S(1)}, bf16[256,8192]{1,0:T(8,128)(2,1)}, u32[]{:S(2)}) copy-start(bf16[256,8192]{1,0:T(8,128)(2,1)} %tokens_ref.1) | copy-start | bytes 12582916
  4.1 8.7 %copy-start.5 = (s32[1,256]{1,0:T(1,128)}, s32[1,256]{1,0:T(1,128)S(1)}, u32[]{:S(2)}) copy-start(s32[1,256]{1,0:T(1,128)S(1)} %get-tuple-element.62.at_ref) | copy-start | bytes 3076
  4.1 14.8 %collective-permute-start = (bf16[24,4224]{1,0:T(8,128)(2,1)S(1)}, bf16[24,4224]{1,0:T(8,128)(2,1)S(1)}, u32[]{:S(2)}, u32[]{:S(2)}) collective-permute-start(bf16[24,4224]{1,0:T(8,128)(2,1)S(1)} %get-tuple-element.65), channel_id=1, source_target_pairs={{0,12},{1,13},{2,14},{3,15},{4,8},{5,9},{6,10},{7,11},{8,4},{9,5},... | collective-permute-start | bytes 608264 | tf_op jit(solution)/shard_map/ppermute | solution.py:298
  9.2 41.2 %collective-permute-start.1 = (bf16[24,4224]{1,0:T(8,128)(2,1)S(1)}, bf16[24,4224]{1,0:T(8,128)(2,1)S(1)}, u32[]{:S(2)}, u32[]{:S(2)}) collective-permute-start(bf16[24,4224]{1,0:T(8,128)(2,1)S(1)} %get-tuple-element.66), channel_id=1, source_target_pairs={{0,8},{1,9},{2,10},{3,11},{4,12},{5,13},{6,14},{7,15},{8,0},{9,1},... | collective-permute-start | bytes 608264 | tf_op jit(solution)/shard_map/ppermute | solution.py:298
  9.2 41.2 %collective-permute-start.2 = (bf16[24,4224]{1,0:T(8,128)(2,1)S(1)}, bf16[24,4224]{1,0:T(8,128)(2,1)S(1)}, u32[]{:S(2)}, u32[]{:S(2)}) collective-permute-start(bf16[24,4224]{1,0:T(8,128)(2,1)S(1)} %get-tuple-element.67), channel_id=1, source_target_pairs={{0,4},{1,5},{2,6},{3,7},{4,0},{5,1},{6,2},{7,3},{8,12},{9,13},{10,... | collective-permute-start | bytes 608264 | tf_op jit(solution)/shard_map/ppermute | solution.py:298
  12.8 97.3 %all-to-all-start.3 = ((bf16[16,16,8320]{2,1,0:T(8,128)(2,1)}), bf16[16,16,8320]{2,1,0:T(8,128)(2,1)}, u32[]{:S(2)}, u32[]{:S(2)}) async-start(bf16[16,16,8320]{2,1,0:T(8,128)(2,1)} %bitcast.35), calls=%async_computation.3 | async-start | bytes 8519680 | tf_op jit(solution)/shard_map/all_to_all | solution.py:354
  50.5 57.0 %copy-start.1 = (bf16[16,8192,16]{1,2,0:T(8,128)(2,1)S(1)}, bf16[16,8192,16]{1,2,0:T(8,128)(2,1)}, u32[]{:S(2)}) copy-start(bf16[16,8192,16]{1,2,0:T(8,128)(2,1)} %param.10) | copy-start | bytes 12582916
  50.5 57.0 %copy-start.3 = (bf16[16,16,512]{2,1,0:T(8,128)(2,1)S(1)}, bf16[16,16,512]{2,1,0:T(8,128)(2,1)}, u32[]{:S(2)}) copy-start(bf16[16,16,512]{2,1,0:T(8,128)(2,1)} %param.11) | copy-start | bytes 786436
  50.5 35.7 %collective-permute-start.5 = (bf16[96,4224]{1,0:T(8,128)(2,1)S(1)}, bf16[96,4224]{1,0:T(8,128)(2,1)S(1)}, u32[]{:S(2)}, u32[]{:S(2)}) collective-permute-start(bf16[96,4224]{1,0:T(8,128)(2,1)S(1)} %constant_dynamic-update-slice_fusion.refs_0_), channel_id=1, source_target_pairs={{0,3},{1,2},{2,1},{3,0},{4,7},{5,6},{6,5},{7,4},{8,11},{9,10},{10,... | collective-permute-start | bytes 2433032 | tf_op jit(solution)/shard_map/ppermute | solution.py:298
  50.6 56.9 %collective-permute-start.4 = (bf16[96,4224]{1,0:T(8,128)(2,1)S(1)}, bf16[96,4224]{1,0:T(8,128)(2,1)S(1)}, u32[]{:S(2)}, u32[]{:S(2)}) collective-permute-start(bf16[96,4224]{1,0:T(8,128)(2,1)S(1)} %constant_dynamic-update-slice_fusion.refs_0_), channel_id=1, source_target_pairs={{0,2},{1,3},{2,0},{3,1},{4,6},{5,7},{6,4},{7,5},{8,10},{9,11},{10,... | collective-permute-start | bytes 2433032 | tf_op jit(solution)/shard_map/ppermute | solution.py:298
  50.7 56.9 %collective-permute-start.3 = (bf16[96,4224]{1,0:T(8,128)(2,1)S(1)}, bf16[96,4224]{1,0:T(8,128)(2,1)S(1)}, u32[]{:S(2)}, u32[]{:S(2)}) collective-permute-start(bf16[96,4224]{1,0:T(8,128)(2,1)S(1)} %constant_dynamic-update-slice_fusion.refs_0_), channel_id=1, source_target_pairs={{0,1},{1,0},{2,3},{3,2},{4,5},{5,4},{6,7},{7,6},{8,9},{9,8},{10,11... | collective-permute-start | bytes 2433032 | tf_op jit(solution)/shard_map/ppermute | solution.py:298
  110.1 30.2 %copy-start.2 = (f32[256,512]{1,0:T(8,128)S(1)}, f32[256,512]{1,0:T(8,128)}, u32[]{:S(2)}) copy-start(f32[256,512]{1,0:T(8,128)} %fusion.8) | copy-start | bytes 1572868
  110.1 30.2 %copy-start.6 = (s32[1,256]{1,0:T(1,128)S(1)}, s32[1,256]{1,0:T(1,128)}, u32[]{:S(2)}) copy-start(s32[1,256]{1,0:T(1,128)} %copy-done.5) | copy-start | bytes 3076
  110.1 30.2 %copy-start.7 = (s32[1,256]{1,0:T(1,128)S(1)}, s32[1,256]{1,0:T(1,128)}, u32[]{:S(2)}) copy-start(s32[1,256]{1,0:T(1,128)} %get-tuple-element.77) | copy-start | bytes 3076
  110.1 30.2 %copy-start.8 = (s32[256,1]{0,1:T(1,128)S(1)}, s32[256,1]{0,1:T(1,128)}, u32[]{:S(2)}) copy-start(s32[256,1]{0,1:T(1,128)} %param.12) | copy-start | bytes 3076
  110.2 30.2 %copy-start.9 = (s32[256]{0:T(256)S(1)}, s32[256]{0:T(256)}, u32[]{:S(2)}) copy-start(s32[256]{0:T(256)} %param.13) | copy-start | bytes 3076
  116.0 24.2 %all-to-all-start.4 = ((bf16[16,24,512]{2,1,0:T(8,128)(2,1)}), bf16[16,24,512]{2,1,0:T(8,128)(2,1)S(1)}, u32[]{:S(2)}, u32[]{:S(2)}) async-start(bf16[16,24,512]{2,1,0:T(8,128)(2,1)} %shard_map.69), calls=%async_computation.4 | async-start | bytes 786432 | tf_op jit(solution)/shard_map/all_to_all | solution.py:383
  128.7 3.7 %collective-permute-start.6 = (s32[]{:T(128)}, s32[]{:T(128)}, u32[]{:S(2)}, u32[]{:S(2)}) collective-permute-start(s32[]{:T(128)} %bitcast.22), channel_id=1, source_target_pairs={{0,16},{16,0},{1,17},{17,1},{2,18},{18,2},{3,19},{19,3},{4,20},{20... | collective-permute-start | bytes 20 | tf_op jit(solution)/shard_map/ppermute | solution.py:390
  140.7 0.7 copy-start.4

commit v15 on v12

--- a/solution.py
+++ b/solution.py
@@ -195,13 +195,15 @@
                 pltpu.make_async_copy(down_hbm.at[:, kept], down_ref.at[:, kept], down_sems.at[i]),
             )
         )
-    for pair in copies:
-        pair[0].start()
-        pair[1].start()
+    for copy in copies[0] + copies[1]:
+        copy.start()
     low = jnp.zeros((rows_ref.shape[0], down_ref.shape[0]), jnp.float32)
-    for pair, span in zip(copies, spans, strict=True):
-        pair[0].wait()
-        pair[1].wait()
+    for i, span in enumerate(spans):
+        for copy in copies[i]:
+            copy.wait()
+        if i + 2 < len(spans):
+            for copy in copies[i + 2]:
+                copy.start()
         span = slice(span.start, min(span.stop, depth))
         low += lax.dot_general(
             rows_ref[:, span],

time: 141 us -> 142 us (level)
  no operation moved by 1% of the time
where the time goes in v15:
time: 142 us
  waiting for transfers between devices  87.6 us (62%)
  starting transfers between devices  27.3 us (19%)
  Pallas kernels  16 us (11%)
  matrix products  7.85 us (6%)
  between operations  1.46 us (1%)
    ppermute x6, waiting for transfers between devices, swap(): return lax.ppermute(x, 'ad', [(s, s ^ k) for s in range(count)])  78.7 us
    all_to_all x1, starting transfers between devices, on_device(): back = lax.all_to_all(delta, 'ad', split_axis=0, concat_axis=0, tiled=True)  12 us
    dot_general x1, matrix products, on_device(): jnp.dot(tokens, value_weight, preferred_element_type=jnp.float32)  7.85 us
    ppermute x6, starting transfers between devices, swap(): return lax.ppermute(x, 'ad', [(s, s ^ k) for s in range(count)])  7.67 us
    all_to_all x1, waiting for transfers between devices, on_device(): back = lax.all_to_all(delta, 'ad', split_axis=0, concat_axis=0, tiled=True)  6.66 us
    pallas_call x1, Pallas kernels, adapt(): pl.pallas_call(functools.partial(adapt_body, rank), in_specs=[SMEM, ANY,...  6.17 us
    all_to_all x1, starting transfers between devices, on_device(): lax.all_to_all(blocks.reshape(count, room, depth + NOTE), 'ad', split_axi...  6.14 us
    pallas_call x1, Pallas kernels, on_device(): pl.pallas_call(functools.partial(route_body, room, local), in_specs=[SMEM...  4.1 us
  transfers between devices with their start and end apart: 9, of which 5 were waited for; matrix products, arithmetic and copies ran while one was open for 6% of the time, Pallas kernels for 4%

profile of v15, /device:TPU:0, one launch (start us, length us, event | category | flops | bytes accessed | tf_op | source)
XLA Modules:
  0.0 141.7 jit_solution(1152772005055353275)
XLA Ops:
  0.0 4.1 %shard_map.66 = (bf16[24,4224]{1,0:T(8,128)(2,1)S(1)}, bf16[24,4224]{1,0:T(8,128)(2,1)S(1)}, bf16[24,4224]{1,0:T(8,128)(2,1)S(1)}, bf16[24,4224]{1,0:T(8,128)(2,...) custom-call(s32[1]{0:T(128)} %bitcast.12.me_ref, s32[1,256]{1,0:T(1,128)} %bitcast.51, ...), custom_call_target="tpu_custom_call" | custom-call | flops 805306368 | bytes 6291456 | tf_op jit(solution)/shard_map/pallas_call | solution.py:340
  4.1 5.1 %collective-permute-start = (bf16[24,4224]{1,0:T(8,128)(2,1)S(1)}, bf16[24,4224]{1,0:T(8,128)(2,1)S(1)}, u32[]{:S(2)}, u32[]{:S(2)}) collective-permute-start(bf16[24,4224]{1,0:T(8,128)(2,1)S(1)} %get-tuple-element.65), channel_id=1, source_target_pairs={{0,12},{1,13},{2,14},{3,15},{4,8},{5,9},{6,10},{7,11},{8,4},{9,5},... | collective-permute-start | bytes 608264 | tf_op jit(solution)/shard_map/ppermute | solution.py:311
  9.2 0.6 collective-permute-start.2
  9.9 2.9 %shard_map.67 = bf16[256,8320]{1,0:T(8,128)(2,1)} custom-call(s32[1,256]{1,0:T(1,128)S(1)} %get-tuple-element.62.at_ref, bf16[128,256]{1,0:T(8,128)(2,1)S(1)} %get-tuple-element.63.note_ref, bf16[256,8192]{1,0:T(8,128)(2,1)S(1)} %copy-done), custom_call_target="tpu_custom_call" | custom-call | flops 1073741824 | bytes 8388608 | tf_op jit(solution)/shard_map/pallas_call | solution.py:163
  12.8 6.1 %all-to-all-start.3 = ((bf16[16,16,8320]{2,1,0:T(8,128)(2,1)}), bf16[16,16,8320]{2,1,0:T(8,128)(2,1)}, u32[]{:S(2)}, u32[]{:S(2)}) async-start(bf16[16,16,8320]{2,1,0:T(8,128)(2,1)} %bitcast.35), calls=%async_computation.3 | async-start | bytes 8519680 | tf_op jit(solution)/shard_map/all_to_all | solution.py:367
  19.0 31.5 %collective-permute-done.1 = bf16[24,4224]{1,0:T(8,128)(2,1)S(1)} collective-permute-done((bf16[24,4224]{1,0:T(8,128)(2,1)S(1)}, bf16[24,4224]{1,0:T(8,128)(2,1)S(1)}, u32[]{:S(2)}, u32[]{:S(2)}) %collective-permute-start.1) | collective-permute-done | bytes 202784 | tf_op jit(solution)/shard_map/ppermute | solution.py:311
  50.5 0.0 copy-start.3
  50.5 0.1 collective-permute-start.5
  50.6 0.1 collective-permute-start.4
  50.7 1.8 %collective-permute-start.3 = (bf16[96,4224]{1,0:T(8,128)(2,1)S(1)}, bf16[96,4224]{1,0:T(8,128)(2,1)S(1)}, u32[]{:S(2)}, u32[]{:S(2)}) collective-permute-start(bf16[96,4224]{1,0:T(8,128)(2,1)S(1)} %constant_dynamic-update-slice_fusion.refs_0_), channel_id=1, source_target_pairs={{0,1},{1,0},{2,3},{3,2},{4,5},{5,4},{6,7},{7,6},{8,9},{9,8},{10,11... | collective-permute-start | bytes 2433032 | tf_op jit(solution)/shard_map/ppermute | solution.py:311
  52.5 7.9 %fusion.8 = f32[256,512]{1,0:T(8,128)} fusion(bf16[256,8192]{1,0:T(8,128)(2,1)} %tokens_ref.1, bf16[8192,512]{1,0:T(8,128)(2,1)} %param.9), kind=kOutput, calls=%fused_computation.37 | convolution fusion | flops 2147483648 | bytes 13107200 | tf_op jit(solution)/shard_map/dot_general | solution.py:331
  60.3 25.9 %collective-permute-done.5.refs_3_ = bf16[96,4224]{1,0:T(8,128)(2,1)S(1)} collective-permute-done((bf16[96,4224]{1,0:T(8,128)(2,1)S(1)}, bf16[96,4224]{1,0:T(8,128)(2,1)S(1)}, u32[]{:S(2)}, u32[]{:S(2)}) %collective-permute-start.5) | collective-permute-done | bytes 811040 | tf_op jit(solution)/shard_map/ppermute | solution.py:311
  86.2 21.3 %collective-permute-done.4.refs_2_ = bf16[96,4224]{1,0:T(8,128)(2,1)S(1)} collective-permute-done((bf16[96,4224]{1,0:T(8,128)(2,1)S(1)}, bf16[96,4224]{1,0:T(8,128)(2,1)S(1)}, u32[]{:S(2)}, u32[]{:S(2)}) %collective-permute-start.4) | collective-permute-done | bytes 811040 | tf_op jit(solution)/shard_map/ppermute | solution.py:311
  107.6 2.5 %shard_map.68 = (f32[16,8,512]{2,1,0:T(8,128)S(1)}, s32[1,128]{1,0:T(1,128)S(1)}) custom-call(s32[1]{0:T(128)} %bitcast.20.first_ref, bf16[256,8192]{1,0:T(8,128)(2,1)S(1)} %bitcast.38, bf16[256,512]{1,0:T(8,128)(2,1)S(1)} %bitcast.43, bf16[96,4224]{1,0:T(8,128)(2,1)S(1)} %constant_dynamic-update-slice_fusion.refs_0_, ...), custom_call_target="tpu_custom_call" | custom-call | flops 999999995904 | bytes 6291456 | tf_op jit(solution)/shard_map/pallas_call | solution.py:376
  110.1 0.0 copy-start.8
  110.2 6.2 %shard_map.69 = bf16[16,24,512]{2,1,0:T(8,128)(2,1)} custom-call(s32[1]{0:T(128)} %bitcast.12.me_ref, bf16[256,8192]{1,0:T(8,128)(2,1)} %bitcast.37, bf16[256,512]{1,0:T(8,128)(2,1)S(1)} %bitcast.44, bf16[256,8320]{1,0:T(8,128)(2,1)} %bitcast.19.rows_hbm, f32[16,8,512]{2,1,0:T(8,128)S(1)} %get-tuple-element.74.extra_ref), custom_call_target="tpu_custom_call" | custom-call | flops 1073741824 | bytes 8388608 | tf_op jit(solution)/shard_map/pallas_call | solution.py:229
  116.3 12.0 %all-to-all-start.4 = ((bf16[16,24,512]{2,1,0:T(8,128)(2,1)}), bf16[16,24,512]{2,1,0:T(8,128)(2,1)S(1)}, u32[]{:S(2)}, u32[]{:S(2)}) async-start(bf16[16,24,512]{2,1,0:T(8,128)(2,1)} %shard_map.69), calls=%async_computation.4 | async-start | bytes 786432 | tf_op jit(solution)/shard_map/all_to_all | solution.py:396
  128.4 0.6 slice.3
  129.0 1.5 %collective-permute-start.6 = (s32[]{:T(128)}, s32[]{:T(128)}, u32[]{:S(2)}, u32[]{:S(2)}) collective-permute-start(s32[]{:T(128)} %bitcast.22), channel_id=1, source_target_pairs={{0,16},{16,0},{1,17},{17,1},{2,18},{18,2},{3,19},{19,3},{4,20},{20... | collective-permute-start | bytes 20 | tf_op jit(solution)/shard_map/ppermute | solution.py:403
  130.5 2.2 %collective-permute-done.6 = s32[]{:T(128)} collective-permute-done((s32[]{:T(128)}, s32[]{:T(128)}, u32[]{:S(2)}, u32[]{:S(2)}) %collective-permute-start.6) | collective-permute-done | bytes 36 | tf_op jit(solution)/shard_map/ppermute | solution.py:403
  133.9 6.7 %all-to-all-done.4 = bf16[16,24,512]{2,1,0:T(8,128)(2,1)S(1)} async-done(((bf16[16,24,512]{2,1,0:T(8,128)(2,1)}), bf16[16,24,512]{2,1,0:T(8,128)(2,1)S(1)}, u32[]{:S(2)}, u32[]{:S(2)}) %all-to-all-start.4) | async-done | bytes 393248 | tf_op jit(solution)/shard_map/all_to_all | solution.py:396
  140.6 0.3 conditional.1
  140.6 0.3 branch_0_fun.1
  141.0 0.7 copy-done.4
  (26 shorter events, 0.1 us)
Async XLA Ops:
  0.0 9.9 %copy-start = (bf16[256,8192]{1,0:T(8,128)(2,1)S(1)}, bf16[256,8192]{1,0:T(8,128)(2,1)}, u32[]{:S(2)}) copy-start(bf16[256,8192]{1,0:T(8,128)(2,1)} %tokens_ref.1) | copy-start | bytes 12582916
  4.1 8.7 %copy-start.5 = (s32[1,256]{1,0:T(1,128)}, s32[1,256]{1,0:T(1,128)S(1)}, u32[]{:S(2)}) copy-start(s32[1,256]{1,0:T(1,128)S(1)} %get-tuple-element.62.at_ref) | copy-start | bytes 3076
  4.1 14.8 %collective-permute-start = (bf16[24,4224]{1,0:T(8,128)(2,1)S(1)}, bf16[24,4224]{1,0:T(8,128)(2,1)S(1)}, u32[]{:S(2)}, u32[]{:S(2)}) collective-permute-start(bf16[24,4224]{1,0:T(8,128)(2,1)S(1)} %get-tuple-element.65), channel_id=1, source_target_pairs={{0,12},{1,13},{2,14},{3,15},{4,8},{5,9},{6,10},{7,11},{8,4},{9,5},... | collective-permute-start | bytes 608264 | tf_op jit(solution)/shard_map/ppermute | solution.py:311
  9.2 41.2 %collective-permute-start.1 = (bf16[24,4224]{1,0:T(8,128)(2,1)S(1)}, bf16[24,4224]{1,0:T(8,128)(2,1)S(1)}, u32[]{:S(2)}, u32[]{:S(2)}) collective-permute-start(bf16[24,4224]{1,0:T(8,128)(2,1)S(1)} %get-tuple-element.66), channel_id=1, source_target_pairs={{0,8},{1,9},{2,10},{3,11},{4,12},{5,13},{6,14},{7,15},{8,0},{9,1},... | collective-permute-start | bytes 608264 | tf_op jit(solution)/shard_map/ppermute | solution.py:311
  9.2 41.2 %collective-permute-start.2 = (bf16[24,4224]{1,0:T(8,128)(2,1)S(1)}, bf16[24,4224]{1,0:T(8,128)(2,1)S(1)}, u32[]{:S(2)}, u32[]{:S(2)}) collective-permute-start(bf16[24,4224]{1,0:T(8,128)(2,1)S(1)} %get-tuple-element.67), channel_id=1, source_target_pairs={{0,4},{1,5},{2,6},{3,7},{4,0},{5,1},{6,2},{7,3},{8,12},{9,13},{10,... | collective-permute-start | bytes 608264 | tf_op jit(solution)/shard_map/ppermute | solution.py:311
  12.8 97.3 %all-to-all-start.3 = ((bf16[16,16,8320]{2,1,0:T(8,128)(2,1)}), bf16[16,16,8320]{2,1,0:T(8,128)(2,1)}, u32[]{:S(2)}, u32[]{:S(2)}) async-start(bf16[16,16,8320]{2,1,0:T(8,128)(2,1)} %bitcast.35), calls=%async_computation.3 | async-start | bytes 8519680 | tf_op jit(solution)/shard_map/all_to_all | solution.py:367
  50.5 57.0 %copy-start.1 = (bf16[16,8192,16]{1,2,0:T(8,128)(2,1)S(1)}, bf16[16,8192,16]{1,2,0:T(8,128)(2,1)}, u32[]{:S(2)}) copy-start(bf16[16,8192,16]{1,2,0:T(8,128)(2,1)} %param.10) | copy-start | bytes 12582916
  50.5 57.0 %copy-start.3 = (bf16[16,16,512]{2,1,0:T(8,128)(2,1)S(1)}, bf16[16,16,512]{2,1,0:T(8,128)(2,1)}, u32[]{:S(2)}) copy-start(bf16[16,16,512]{2,1,0:T(8,128)(2,1)} %param.11) | copy-start | bytes 786436
  50.5 35.7 %collective-permute-start.5 = (bf16[96,4224]{1,0:T(8,128)(2,1)S(1)}, bf16[96,4224]{1,0:T(8,128)(2,1)S(1)}, u32[]{:S(2)}, u32[]{:S(2)}) collective-permute-start(bf16[96,4224]{1,0:T(8,128)(2,1)S(1)} %constant_dynamic-update-slice_fusion.refs_0_), channel_id=1, source_target_pairs={{0,3},{1,2},{2,1},{3,0},{4,7},{5,6},{6,5},{7,4},{8,11},{9,10},{10,... | collective-permute-start | bytes 2433032 | tf_op jit(solution)/shard_map/ppermute | solution.py:311
  50.6 56.9 %collective-permute-start.4 = (bf16[96,4224]{1,0:T(8,128)(2,1)S(1)}, bf16[96,4224]{1,0:T(8,128)(2,1)S(1)}, u32[]{:S(2)}, u32[]{:S(2)}) collective-permute-start(bf16[96,4224]{1,0:T(8,128)(2,1)S(1)} %constant_dynamic-update-slice_fusion.refs_0_), channel_id=1, source_target_pairs={{0,2},{1,3},{2,0},{3,1},{4,6},{5,7},{6,4},{7,5},{8,10},{9,11},{10,... | collective-permute-start | bytes 2433032 | tf_op jit(solution)/shard_map/ppermute | solution.py:311
  50.7 56.9 %collective-permute-start.3 = (bf16[96,4224]{1,0:T(8,128)(2,1)S(1)}, bf16[96,4224]{1,0:T(8,128)(2,1)S(1)}, u32[]{:S(2)}, u32[]{:S(2)}) collective-permute-start(bf16[96,4224]{1,0:T(8,128)(2,1)S(1)} %constant_dynamic-update-slice_fusion.refs_0_), channel_id=1, source_target_pairs={{0,1},{1,0},{2,3},{3,2},{4,5},{5,4},{6,7},{7,6},{8,9},{9,8},{10,11... | collective-permute-start | bytes 2433032 | tf_op jit(solution)/shard_map/ppermute | solution.py:311
  110.1 30.5 %copy-start.2 = (f32[256,512]{1,0:T(8,128)S(1)}, f32[256,512]{1,0:T(8,128)}, u32[]{:S(2)}) copy-start(f32[256,512]{1,0:T(8,128)} %fusion.8) | copy-start | bytes 1572868
  110.1 30.5 %copy-start.6 = (s32[1,256]{1,0:T(1,128)S(1)}, s32[1,256]{1,0:T(1,128)}, u32[]{:S(2)}) copy-start(s32[1,256]{1,0:T(1,128)} %copy-done.5) | copy-start | bytes 3076
  110.1 30.5 %copy-start.7 = (s32[1,256]{1,0:T(1,128)S(1)}, s32[1,256]{1,0:T(1,128)}, u32[]{:S(2)}) copy-start(s32[1,256]{1,0:T(1,128)} %get-tuple-element.77) | copy-start | bytes 3076
  110.1 30.5 %copy-start.8 = (s32[256,1]{0,1:T(1,128)S(1)}, s32[256,1]{0,1:T(1,128)}, u32[]{:S(2)}) copy-start(s32[256,1]{0,1:T(1,128)} %param.12) | copy-start | bytes 3076
  110.2 30.5 %copy-start.9 = (s32[256]{0:T(256)S(1)}, s32[256]{0:T(256)}, u32[]{:S(2)}) copy-start(s32[256]{0:T(256)} %param.13) | copy-start | bytes 3076
  116.3 24.2 %all-to-all-start.4 = ((bf16[16,24,512]{2,1,0:T(8,128)(2,1)}), bf16[16,24,512]{2,1,0:T(8,128)(2,1)S(1)}, u32[]{:S(2)}, u32[]{:S(2)}) async-start(bf16[16,24,512]{2,1,0:T(8,128)(2,1)} %shard_map.69), calls=%async_computation.4 | async-start | bytes 786432 | tf_op jit(solution)/shard_map/all_to_all | solution.py:396
  129.0 3.7 %collective-permute-start.6 = (s32[]{:T(128)}, s32[]{:T(128)}, u32[]{:S(2)}, u32[]{:S(2)}) collective-permute-start(s32[]{:T(128)} %bitcast.22), channel_id=1, source_target_pairs={{0,16},{16,0},{1,17},{17,1},{2,18},{18,2},{3,19},{19,3},{4,20},{20... | collective-permute-start | bytes 20 | tf_op jit(solution)/shard_map/ppermute | solution.py:403
  141.0 0.7 copy-start.4

commit v16 on v12

--- a/solution.py
+++ b/solution.py
@@ -329,7 +329,7 @@
     base_value = jnp.dot(tokens, value_weight, preferred_element_type=jnp.float32)
     room = row_count // count
     planes = count // PLANE
-    if count != 16 or room != 16 or depth % (2 * STEP):
+    if count != 16 or planes != 4 or room != 16 or depth % (2 * STEP):
         slot, owner, place = route(tenant_ids, tenant_slot, local)
         delta = exchange(tokens, slot, owner, place, CAP * local, adapt_down, adapt_up)
         return (base_value + delta).astype(jnp.bfloat16)
@@ -355,11 +355,11 @@
         ),
     )(me.reshape(1), tenant_ids.reshape(1, row_count), tenant_slot.reshape(1, TENANTS), tokens)
 
-    along = [swap(spare[b], b * PLANE) for b in range(planes - 1, 0, -1)]
+    along = [swap(spare[b], b * PLANE) for b in (2, 3, 1)]
     along = list(lax.optimization_barrier(tuple(along)))
     blocks = pack(main_rows, at, note, tokens)
 
-    along = jnp.concatenate([spare[0]] + along[::-1], axis=0)
+    along = jnp.concatenate([spare[0], along[2], along[0], along[1]], axis=0)
     shared = [along] + [swap(along, a) for a in range(1, PLANE)]
 
     got = lax.all_to_all(

time: 141 us -> 143 us (1.014)
  starting transfers between devices: 27.3 us -> 37.4 us
  waiting for transfers between devices: 87.6 us -> 78.9 us
    ppermute x6, waiting for transfers between devices: 78.7 us -> 67 us  [swap(): return lax.ppermute(x, 'ad', [(s, s ^ k) for s in range(count)])]
    all_to_all x1, starting transfers between devices: 12 us -> 23 us  [on_device(): back = lax.all_to_all(delta, 'ad', split_axis=0, concat_axis=0, tiled=True)]
    all_to_all x1, waiting for transfers between devices: 0.01 us -> 3.08 us  [on_device(): lax.all_to_all(blocks.reshape(count, room, depth + NOTE), 'ad', split_axi...]
  transfers between devices with their start and end apart: 9 -> 9, of which waited for: 5 -> 7; matrix products, arithmetic and copies ran while one was open for 6% -> 6% of each run, Pallas kernels for 4% -> 4%
where the time goes in v16:
time: 143 us; the launch traced here: 142 us
  waiting for transfers between devices  78.9 us (55%)
  starting transfers between devices  37.4 us (26%)
  Pallas kernels  15.5 us (11%)
  matrix products  7.85 us (5%)
    ppermute x6, waiting for transfers between devices, swap(): return lax.ppermute(x, 'ad', [(s, s ^ k) for s in range(count)])  67 us
    all_to_all x1, starting transfers between devices, on_device(): back = lax.all_to_all(delta, 'ad', split_axis=0, concat_axis=0, tiled=True)  23 us
    dot_general x1, matrix products, on_device(): jnp.dot(tokens, value_weight, preferred_element_type=jnp.float32)  7.85 us
    ppermute x6, starting transfers between devices, swap(): return lax.ppermute(x, 'ad', [(s, s ^ k) for s in range(count)])  7.59 us
    all_to_all x1, waiting for transfers between devices, on_device(): back = lax.all_to_all(delta, 'ad', split_axis=0, concat_axis=0, tiled=True)  6.66 us
    pallas_call x1, Pallas kernels, adapt(): pl.pallas_call(functools.partial(adapt_body, rank), in_specs=[SMEM, ANY,...  5.64 us
    all_to_all x1, starting transfers between devices, on_device(): lax.all_to_all(blocks.reshape(count, room, depth + NOTE), 'ad', split_axi...  5.31 us
    pallas_call x1, Pallas kernels, on_device(): pl.pallas_call(functools.partial(route_body, room, local), in_specs=[SMEM...  4.1 us
  transfers between devices with their start and end apart: 9, of which 7 were waited for; matrix products, arithmetic and copies ran while one was open for 6% of the time, Pallas kernels for 4%

profile of v16, /device:TPU:0, one launch (start us, length us, event | category | flops | bytes accessed | tf_op | source)
XLA Modules:
  0.0 142.5 jit_solution(13918363585344438758)
XLA Ops:
  0.0 4.1 %shard_map.66 = (bf16[24,4224]{1,0:T(8,128)(2,1)S(1)}, bf16[24,4224]{1,0:T(8,128)(2,1)S(1)}, bf16[24,4224]{1,0:T(8,128)(2,1)S(1)}, bf16[24,4224]{1,0:T(8,128)(2,...) custom-call(s32[1]{0:T(128)} %bitcast.12.me_ref, s32[1,256]{1,0:T(1,128)} %bitcast.51, ...), custom_call_target="tpu_custom_call" | custom-call | flops 805306368 | bytes 6291456 | tf_op jit(solution)/shard_map/pallas_call | solution.py:338
  4.1 4.1 %collective-permute-start = (bf16[24,4224]{1,0:T(8,128)(2,1)S(1)}, bf16[24,4224]{1,0:T(8,128)(2,1)S(1)}, u32[]{:S(2)}, u32[]{:S(2)}) collective-permute-start(bf16[24,4224]{1,0:T(8,128)(2,1)S(1)} %get-tuple-element.65), channel_id=1, source_target_pairs={{0,8},{1,9},{2,10},{3,11},{4,12},{5,13},{6,14},{7,15},{8,0},{9,1},... | collective-permute-start | bytes 608264 | tf_op jit(solution)/shard_map/ppermute | solution.py:309
  8.2 1.3 collective-permute-start.1
  9.6 0.2 collective-permute-start.2
  9.8 2.9 %shard_map.67 = bf16[256,8320]{1,0:T(8,128)(2,1)} custom-call(s32[1,256]{1,0:T(1,128)S(1)} %get-tuple-element.62.at_ref, bf16[128,256]{1,0:T(8,128)(2,1)S(1)} %get-tuple-element.63.note_ref, bf16[256,8192]{1,0:T(8,128)(2,1)S(1)} %copy-done), custom_call_target="tpu_custom_call" | custom-call | flops 1073741824 | bytes 8388608 | tf_op jit(solution)/shard_map/pallas_call | solution.py:163
  12.7 5.3 %all-to-all-start.3 = ((bf16[16,16,8320]{2,1,0:T(8,128)(2,1)}), bf16[16,16,8320]{2,1,0:T(8,128)(2,1)}, u32[]{:S(2)}, u32[]{:S(2)}) async-start(bf16[16,16,8320]{2,1,0:T(8,128)(2,1)} %bitcast.35), calls=%async_computation.3 | async-start | bytes 8519680 | tf_op jit(solution)/shard_map/all_to_all | solution.py:365
  18.0 4.8 %collective-permute-done = bf16[24,4224]{1,0:T(8,128)(2,1)S(1)} collective-permute-done((bf16[24,4224]{1,0:T(8,128)(2,1)S(1)}, bf16[24,4224]{1,0:T(8,128)(2,1)S(1)}, u32[]{:S(2)}, u32[]{:S(2)}) %collective-permute-start) | collective-permute-done | bytes 202784 | tf_op jit(solution)/shard_map/ppermute | solution.py:309
  22.8 13.1 %collective-permute-done.2 = bf16[24,4224]{1,0:T(8,128)(2,1)S(1)} collective-permute-done((bf16[24,4224]{1,0:T(8,128)(2,1)S(1)}, bf16[24,4224]{1,0:T(8,128)(2,1)S(1)}, u32[]{:S(2)}, u32[]{:S(2)}) %collective-permute-start.2) | collective-permute-done | bytes 202784 | tf_op jit(solution)/shard_map/ppermute | solution.py:309
  36.1 0.1 collective-permute-start.5
  36.2 1.8 %collective-permute-start.3 = (bf16[96,4224]{1,0:T(8,128)(2,1)S(1)}, bf16[96,4224]{1,0:T(8,128)(2,1)S(1)}, u32[]{:S(2)}, u32[]{:S(2)}) collective-permute-start(bf16[96,4224]{1,0:T(8,128)(2,1)S(1)} %constant_dynamic-update-slice_fusion.refs_0_), channel_id=1, source_target_pairs={{0,1},{1,0},{2,3},{3,2},{4,5},{5,4},{6,7},{7,6},{8,9},{9,8},{10,11... | collective-permute-start | bytes 2433032 | tf_op jit(solution)/shard_map/ppermute | solution.py:309
  38.0 7.9 %fusion.8 = f32[256,512]{1,0:T(8,128)} fusion(bf16[256,8192]{1,0:T(8,128)(2,1)} %tokens_ref.1, bf16[8192,512]{1,0:T(8,128)(2,1)} %param.9), kind=kOutput, calls=%fused_computation.37 | convolution fusion | flops 2147483648 | bytes 13107200 | tf_op jit(solution)/shard_map/dot_general | solution.py:329
  45.8 27.8 %collective-permute-done.5.refs_3_ = bf16[96,4224]{1,0:T(8,128)(2,1)S(1)} collective-permute-done((bf16[96,4224]{1,0:T(8,128)(2,1)S(1)}, bf16[96,4224]{1,0:T(8,128)(2,1)S(1)}, u32[]{:S(2)}, u32[]{:S(2)}) %collective-permute-start.5) | collective-permute-done | bytes 811040 | tf_op jit(solution)/shard_map/ppermute | solution.py:309
  73.7 21.2 %collective-permute-done.4.refs_2_ = bf16[96,4224]{1,0:T(8,128)(2,1)S(1)} collective-permute-done((bf16[96,4224]{1,0:T(8,128)(2,1)S(1)}, bf16[96,4224]{1,0:T(8,128)(2,1)S(1)}, u32[]{:S(2)}, u32[]{:S(2)}) %collective-permute-start.4) | collective-permute-done | bytes 811040 | tf_op jit(solution)/shard_map/ppermute | solution.py:309
  94.9 2.5 %shard_map.68 = (f32[16,8,512]{2,1,0:T(8,128)S(1)}, s32[1,128]{1,0:T(1,128)S(1)}) custom-call(s32[1]{0:T(128)} %bitcast.20.first_ref, bf16[256,8192]{1,0:T(8,128)(2,1)S(1)} %bitcast.38, bf16[256,512]{1,0:T(8,128)(2,1)S(1)} %bitcast.43, bf16[96,4224]{1,0:T(8,128)(2,1)S(1)} %constant_dynamic-update-slice_fusion.refs_0_, ...), custom_call_target="tpu_custom_call" | custom-call | flops 999999995904 | bytes 6291456 | tf_op jit(solution)/shard_map/pallas_call | solution.py:374
  97.5 3.1 %all-to-all-done.3 = bf16[16,16,8320]{2,1,0:T(8,128)(2,1)} async-done(((bf16[16,16,8320]{2,1,0:T(8,128)(2,1)}), bf16[16,16,8320]{2,1,0:T(8,128)(2,1)}, u32[]{:S(2)}, u32[]{:S(2)}) %all-to-all-start.3) | async-done | bytes 4259872 | tf_op jit(solution)/shard_map/all_to_all | solution.py:365
  100.6 5.6 %shard_map.69 = bf16[16,24,512]{2,1,0:T(8,128)(2,1)} custom-call(s32[1]{0:T(128)} %bitcast.12.me_ref, bf16[256,8192]{1,0:T(8,128)(2,1)} %bitcast.37, bf16[256,512]{1,0:T(8,128)(2,1)S(1)} %bitcast.44, bf16[256,8320]{1,0:T(8,128)(2,1)} %bitcast.19.rows_hbm, f32[16,8,512]{2,1,0:T(8,128)S(1)} %get-tuple-element.74.extra_ref), custom_call_target="tpu_custom_call" | custom-call | flops 1073741824 | bytes 8388608 | tf_op jit(solution)/shard_map/pallas_call | solution.py:227
  106.2 23.0 %all-to-all-start.4 = ((bf16[16,24,512]{2,1,0:T(8,128)(2,1)}), bf16[16,24,512]{2,1,0:T(8,128)(2,1)S(1)}, u32[]{:S(2)}, u32[]{:S(2)}) async-start(bf16[16,24,512]{2,1,0:T(8,128)(2,1)} %shard_map.69), calls=%async_computation.4 | async-start | bytes 786432 | tf_op jit(solution)/shard_map/all_to_all | solution.py:394
  129.2 0.6 slice.3
  129.8 1.5 %collective-permute-start.6 = (s32[]{:T(128)}, s32[]{:T(128)}, u32[]{:S(2)}, u32[]{:S(2)}) collective-permute-start(s32[]{:T(128)} %bitcast.22), channel_id=1, source_target_pairs={{0,16},{16,0},{1,17},{17,1},{2,18},{18,2},{3,19},{19,3},{4,20},{20... | collective-permute-start | bytes 20 | tf_op jit(solution)/shard_map/ppermute | solution.py:401
  131.3 2.2 %collective-permute-done.6 = s32[]{:T(128)} collective-permute-done((s32[]{:T(128)}, s32[]{:T(128)}, u32[]{:S(2)}, u32[]{:S(2)}) %collective-permute-start.6) | collective-permute-done | bytes 36 | tf_op jit(solution)/shard_map/ppermute | solution.py:401
  134.7 6.7 %all-to-all-done.4 = bf16[16,24,512]{2,1,0:T(8,128)(2,1)S(1)} async-done(((bf16[16,24,512]{2,1,0:T(8,128)(2,1)}), bf16[16,24,512]{2,1,0:T(8,128)(2,1)S(1)}, u32[]{:S(2)}, u32[]{:S(2)}) %all-to-all-start.4) | async-done | bytes 393248 | tf_op jit(solution)/shard_map/all_to_all | solution.py:394
  141.4 0.3 conditional.1
  141.4 0.3 branch_0_fun.1
  141.8 0.7 copy-done.4
  (26 shorter events, 0.2 us)
Async XLA Ops:
  0.0 9.8 %copy-start = (bf16[256,8192]{1,0:T(8,128)(2,1)S(1)}, bf16[256,8192]{1,0:T(8,128)(2,1)}, u32[]{:S(2)}) copy-start(bf16[256,8192]{1,0:T(8,128)(2,1)} %tokens_ref.1) | copy-start | bytes 12582916
  4.1 8.6 %copy-start.5 = (s32[1,256]{1,0:T(1,128)}, s32[1,256]{1,0:T(1,128)S(1)}, u32[]{:S(2)}) copy-start(s32[1,256]{1,0:T(1,128)S(1)} %get-tuple-element.62.at_ref) | copy-start | bytes 3076
  4.1 18.7 %collective-permute-start = (bf16[24,4224]{1,0:T(8,128)(2,1)S(1)}, bf16[24,4224]{1,0:T(8,128)(2,1)S(1)}, u32[]{:S(2)}, u32[]{:S(2)}) collective-permute-start(bf16[24,4224]{1,0:T(8,128)(2,1)S(1)} %get-tuple-element.65), channel_id=1, source_target_pairs={{0,8},{1,9},{2,10},{3,11},{4,12},{5,13},{6,14},{7,15},{8,0},{9,1},... | collective-permute-start | bytes 608264 | tf_op jit(solution)/shard_map/ppermute | solution.py:309
  8.2 14.6 %collective-permute-start.1 = (bf16[24,4224]{1,0:T(8,128)(2,1)S(1)}, bf16[24,4224]{1,0:T(8,128)(2,1)S(1)}, u32[]{:S(2)}, u32[]{:S(2)}) collective-permute-start(bf16[24,4224]{1,0:T(8,128)(2,1)S(1)} %get-tuple-element.66), channel_id=1, source_target_pairs={{0,12},{1,13},{2,14},{3,15},{4,8},{5,9},{6,10},{7,11},{8,4},{9,5},... | collective-permute-start | bytes 608264 | tf_op jit(solution)/shard_map/ppermute | solution.py:309
  9.6 26.4 %collective-permute-start.2 = (bf16[24,4224]{1,0:T(8,128)(2,1)S(1)}, bf16[24,4224]{1,0:T(8,128)(2,1)S(1)}, u32[]{:S(2)}, u32[]{:S(2)}) collective-permute-start(bf16[24,4224]{1,0:T(8,128)(2,1)S(1)} %get-tuple-element.67), channel_id=1, source_target_pairs={{0,4},{1,5},{2,6},{3,7},{4,0},{5,1},{6,2},{7,3},{8,12},{9,13},{10,... | collective-permute-start | bytes 608264 | tf_op jit(solution)/shard_map/ppermute | solution.py:309
  12.7 87.8 %all-to-all-start.3 = ((bf16[16,16,8320]{2,1,0:T(8,128)(2,1)}), bf16[16,16,8320]{2,1,0:T(8,128)(2,1)}, u32[]{:S(2)}, u32[]{:S(2)}) async-start(bf16[16,16,8320]{2,1,0:T(8,128)(2,1)} %bitcast.35), calls=%async_computation.3 | async-start | bytes 8519680 | tf_op jit(solution)/shard_map/all_to_all | solution.py:365
  36.0 58.9 %copy-start.1 = (bf16[16,8192,16]{1,2,0:T(8,128)(2,1)S(1)}, bf16[16,8192,16]{1,2,0:T(8,128)(2,1)}, u32[]{:S(2)}) copy-start(bf16[16,8192,16]{1,2,0:T(8,128)(2,1)} %param.10) | copy-start | bytes 12582916
  36.1 58.9 %copy-start.3 = (bf16[16,16,512]{2,1,0:T(8,128)(2,1)S(1)}, bf16[16,16,512]{2,1,0:T(8,128)(2,1)}, u32[]{:S(2)}) copy-start(bf16[16,16,512]{2,1,0:T(8,128)(2,1)} %param.11) | copy-start | bytes 786436
  36.1 37.6 %collective-permute-start.5 = (bf16[96,4224]{1,0:T(8,128)(2,1)S(1)}, bf16[96,4224]{1,0:T(8,128)(2,1)S(1)}, u32[]{:S(2)}, u32[]{:S(2)}) collective-permute-start(bf16[96,4224]{1,0:T(8,128)(2,1)S(1)} %constant_dynamic-update-slice_fusion.refs_0_), channel_id=1, source_target_pairs={{0,3},{1,2},{2,1},{3,0},{4,7},{5,6},{6,5},{7,4},{8,11},{9,10},{10,... | collective-permute-start | bytes 2433032 | tf_op jit(solution)/shard_map/ppermute | solution.py:309
  36.1 58.8 %collective-permute-start.4 = (bf16[96,4224]{1,0:T(8,128)(2,1)S(1)}, bf16[96,4224]{1,0:T(8,128)(2,1)S(1)}, u32[]{:S(2)}, u32[]{:S(2)}) collective-permute-start(bf16[96,4224]{1,0:T(8,128)(2,1)S(1)} %constant_dynamic-update-slice_fusion.refs_0_), channel_id=1, source_target_pairs={{0,2},{1,3},{2,0},{3,1},{4,6},{5,7},{6,4},{7,5},{8,10},{9,11},{10,... | collective-permute-start | bytes 2433032 | tf_op jit(solution)/shard_map/ppermute | solution.py:309
  36.2 58.7 %collective-permute-start.3 = (bf16[96,4224]{1,0:T(8,128)(2,1)S(1)}, bf16[96,4224]{1,0:T(8,128)(2,1)S(1)}, u32[]{:S(2)}, u32[]{:S(2)}) collective-permute-start(bf16[96,4224]{1,0:T(8,128)(2,1)S(1)} %constant_dynamic-update-slice_fusion.refs_0_), channel_id=1, source_target_pairs={{0,1},{1,0},{2,3},{3,2},{4,5},{5,4},{6,7},{7,6},{8,9},{9,8},{10,11... | collective-permute-start | bytes 2433032 | tf_op jit(solution)/shard_map/ppermute | solution.py:309
  100.5 40.9 %copy-start.2 = (f32[256,512]{1,0:T(8,128)S(1)}, f32[256,512]{1,0:T(8,128)}, u32[]{:S(2)}) copy-start(f32[256,512]{1,0:T(8,128)} %fusion.8) | copy-start | bytes 1572868
  100.5 40.9 %copy-start.6 = (s32[1,256]{1,0:T(1,128)S(1)}, s32[1,256]{1,0:T(1,128)}, u32[]{:S(2)}) copy-start(s32[1,256]{1,0:T(1,128)} %copy-done.5) | copy-start | bytes 3076
  100.5 40.9 %copy-start.7 = (s32[1,256]{1,0:T(1,128)S(1)}, s32[1,256]{1,0:T(1,128)}, u32[]{:S(2)}) copy-start(s32[1,256]{1,0:T(1,128)} %get-tuple-element.77) | copy-start | bytes 3076
  100.5 40.9 %copy-start.8 = (s32[256,1]{0,1:T(1,128)S(1)}, s32[256,1]{0,1:T(1,128)}, u32[]{:S(2)}) copy-start(s32[256,1]{0,1:T(1,128)} %param.12) | copy-start | bytes 3076
  100.5 40.9 %copy-start.9 = (s32[256]{0:T(256)S(1)}, s32[256]{0:T(256)}, u32[]{:S(2)}) copy-start(s32[256]{0:T(256)} %param.13) | copy-start | bytes 3076
  106.2 35.2 %all-to-all-start.4 = ((bf16[16,24,512]{2,1,0:T(8,128)(2,1)}), bf16[16,24,512]{2,1,0:T(8,128)(2,1)S(1)}, u32[]{:S(2)}, u32[]{:S(2)}) async-start(bf16[16,24,512]{2,1,0:T(8,128)(2,1)} %shard_map.69), calls=%async_computation.4 | async-start | bytes 786432 | tf_op jit(solution)/shard_map/all_to_all | solution.py:394
  129.8 3.7 %collective-permute-start.6 = (s32[]{:T(128)}, s32[]{:T(128)}, u32[]{:S(2)}, u32[]{:S(2)}) collective-permute-start(s32[]{:T(128)} %bitcast.22), channel_id=1, source_target_pairs={{0,16},{16,0},{1,17},{17,1},{2,18},{18,2},{3,19},{19,3},{4,20},{20... | collective-permute-start | bytes 20 | tf_op jit(solution)/shard_map/ppermute | solution.py:401
  141.8 0.7 copy-start.4

commit v17 on v12

--- a/solution.py
+++ b/solution.py
@@ -14,7 +14,7 @@
 EXTRA = 8
 NOTE = 128
 STEP = 1024
-WIDE = 1664
+WIDE = 2816
 PARTS = 8
 VMEM = pl.BlockSpec(memory_space=pltpu.VMEM)
 ANY = pl.BlockSpec(memory_space=pl.ANY)

time: 141 us -> 142 us (level)
  no operation moved by 1% of the time
where the time goes in v17:
time: 142 us; the launch traced here: 141 us
  waiting for transfers between devices  87.6 us (62%)
  starting transfers between devices  27.3 us (19%)
  Pallas kernels  15.6 us (11%)
  matrix products  7.85 us (6%)
  between operations  1.46 us (1%)
    ppermute x6, waiting for transfers between devices, swap(): return lax.ppermute(x, 'ad', [(s, s ^ k) for s in range(count)])  78.7 us
    all_to_all x1, starting transfers between devices, on_device(): back = lax.all_to_all(delta, 'ad', split_axis=0, concat_axis=0, tiled=True)  12 us
    dot_general x1, matrix products, on_device(): jnp.dot(tokens, value_weight, preferred_element_type=jnp.float32)  7.85 us
    ppermute x6, starting transfers between devices, swap(): return lax.ppermute(x, 'ad', [(s, s ^ k) for s in range(count)])  7.67 us
    all_to_all x1, waiting for transfers between devices, on_device(): back = lax.all_to_all(delta, 'ad', split_axis=0, concat_axis=0, tiled=True)  6.66 us
    all_to_all x1, starting transfers between devices, on_device(): lax.all_to_all(blocks.reshape(count, room, depth + NOTE), 'ad', split_axi...  6.14 us
    pallas_call x1, Pallas kernels, adapt(): pl.pallas_call(functools.partial(adapt_body, rank), in_specs=[SMEM, ANY,...  5.77 us
    pallas_call x1, Pallas kernels, on_device(): pl.pallas_call(functools.partial(route_body, room, local), in_specs=[SMEM...  4.1 us
  transfers between devices with their start and end apart: 9, of which 5 were waited for; matrix products, arithmetic and copies ran while one was open for 6% of the time, Pallas kernels for 4%

profile of v17, /device:TPU:0, one launch (start us, length us, event | category | flops | bytes accessed | tf_op | source)
XLA Modules:
  0.0 141.3 jit_solution(4042916707550635114)
XLA Ops:
  0.0 4.1 %shard_map.66 = (bf16[24,4224]{1,0:T(8,128)(2,1)S(1)}, bf16[24,4224]{1,0:T(8,128)(2,1)S(1)}, bf16[24,4224]{1,0:T(8,128)(2,1)S(1)}, bf16[24,4224]{1,0:T(8,128)(2,...) custom-call(s32[1]{0:T(128)} %bitcast.12.me_ref, s32[1,256]{1,0:T(1,128)} %bitcast.51, ...), custom_call_target="tpu_custom_call" | custom-call | flops 805306368 | bytes 6291456 | tf_op jit(solution)/shard_map/pallas_call | solution.py:338
  4.1 5.1 %collective-permute-start = (bf16[24,4224]{1,0:T(8,128)(2,1)S(1)}, bf16[24,4224]{1,0:T(8,128)(2,1)S(1)}, u32[]{:S(2)}, u32[]{:S(2)}) collective-permute-start(bf16[24,4224]{1,0:T(8,128)(2,1)S(1)} %get-tuple-element.65), channel_id=1, source_target_pairs={{0,12},{1,13},{2,14},{3,15},{4,8},{5,9},{6,10},{7,11},{8,4},{9,5},... | collective-permute-start | bytes 608264 | tf_op jit(solution)/shard_map/ppermute | solution.py:309
  9.2 0.6 collective-permute-start.2
  9.9 2.9 %shard_map.67 = bf16[256,8320]{1,0:T(8,128)(2,1)} custom-call(s32[1,256]{1,0:T(1,128)S(1)} %get-tuple-element.62.at_ref, bf16[128,256]{1,0:T(8,128)(2,1)S(1)} %get-tuple-element.63.note_ref, bf16[256,8192]{1,0:T(8,128)(2,1)S(1)} %copy-done), custom_call_target="tpu_custom_call" | custom-call | flops 1073741824 | bytes 8388608 | tf_op jit(solution)/shard_map/pallas_call | solution.py:163
  12.8 6.1 %all-to-all-start.3 = ((bf16[16,16,8320]{2,1,0:T(8,128)(2,1)}), bf16[16,16,8320]{2,1,0:T(8,128)(2,1)}, u32[]{:S(2)}, u32[]{:S(2)}) async-start(bf16[16,16,8320]{2,1,0:T(8,128)(2,1)} %bitcast.35), calls=%async_computation.3 | async-start | bytes 8519680 | tf_op jit(solution)/shard_map/all_to_all | solution.py:365
  19.0 31.5 %collective-permute-done.1 = bf16[24,4224]{1,0:T(8,128)(2,1)S(1)} collective-permute-done((bf16[24,4224]{1,0:T(8,128)(2,1)S(1)}, bf16[24,4224]{1,0:T(8,128)(2,1)S(1)}, u32[]{:S(2)}, u32[]{:S(2)}) %collective-permute-start.1) | collective-permute-done | bytes 202784 | tf_op jit(solution)/shard_map/ppermute | solution.py:309
  50.5 0.0 copy-start.1
  50.5 0.1 collective-permute-start.5
  50.6 0.1 collective-permute-start.4
  50.7 1.8 %collective-permute-start.3 = (bf16[96,4224]{1,0:T(8,128)(2,1)S(1)}, bf16[96,4224]{1,0:T(8,128)(2,1)S(1)}, u32[]{:S(2)}, u32[]{:S(2)}) collective-permute-start(bf16[96,4224]{1,0:T(8,128)(2,1)S(1)} %constant_dynamic-update-slice_fusion.refs_0_), channel_id=1, source_target_pairs={{0,1},{1,0},{2,3},{3,2},{4,5},{5,4},{6,7},{7,6},{8,9},{9,8},{10,11... | collective-permute-start | bytes 2433032 | tf_op jit(solution)/shard_map/ppermute | solution.py:309
  52.5 7.9 %fusion.8 = f32[256,512]{1,0:T(8,128)} fusion(bf16[256,8192]{1,0:T(8,128)(2,1)} %tokens_ref.1, bf16[8192,512]{1,0:T(8,128)(2,1)} %param.9), kind=kOutput, calls=%fused_computation.37 | convolution fusion | flops 2147483648 | bytes 13107200 | tf_op jit(solution)/shard_map/dot_general | solution.py:329
  60.3 25.9 %collective-permute-done.5.refs_3_ = bf16[96,4224]{1,0:T(8,128)(2,1)S(1)} collective-permute-done((bf16[96,4224]{1,0:T(8,128)(2,1)S(1)}, bf16[96,4224]{1,0:T(8,128)(2,1)S(1)}, u32[]{:S(2)}, u32[]{:S(2)}) %collective-permute-start.5) | collective-permute-done | bytes 811040 | tf_op jit(solution)/shard_map/ppermute | solution.py:309
  86.2 21.3 %collective-permute-done.4.refs_2_ = bf16[96,4224]{1,0:T(8,128)(2,1)S(1)} collective-permute-done((bf16[96,4224]{1,0:T(8,128)(2,1)S(1)}, bf16[96,4224]{1,0:T(8,128)(2,1)S(1)}, u32[]{:S(2)}, u32[]{:S(2)}) %collective-permute-start.4) | collective-permute-done | bytes 811040 | tf_op jit(solution)/shard_map/ppermute | solution.py:309
  107.6 2.5 %shard_map.68 = (f32[16,8,512]{2,1,0:T(8,128)S(1)}, s32[1,128]{1,0:T(1,128)S(1)}) custom-call(s32[1]{0:T(128)} %bitcast.20.first_ref, bf16[256,8192]{1,0:T(8,128)(2,1)S(1)} %bitcast.38, bf16[256,512]{1,0:T(8,128)(2,1)S(1)} %bitcast.43, bf16[96,4224]{1,0:T(8,128)(2,1)S(1)} %constant_dynamic-update-slice_fusion.refs_0_, ...), custom_call_target="tpu_custom_call" | custom-call | flops 999999995904 | bytes 6291456 | tf_op jit(solution)/shard_map/pallas_call | solution.py:374
  110.2 0.0 copy-start.9
  110.2 5.8 %shard_map.69 = bf16[16,24,512]{2,1,0:T(8,128)(2,1)} custom-call(s32[1]{0:T(128)} %bitcast.12.me_ref, bf16[256,8192]{1,0:T(8,128)(2,1)} %bitcast.37, bf16[256,512]{1,0:T(8,128)(2,1)S(1)} %bitcast.44, bf16[256,8320]{1,0:T(8,128)(2,1)} %bitcast.19.rows_hbm, f32[16,8,512]{2,1,0:T(8,128)S(1)} %get-tuple-element.74.extra_ref), custom_call_target="tpu_custom_call" | custom-call | flops 1073741824 | bytes 8388608 | tf_op jit(solution)/shard_map/pallas_call | solution.py:227
  115.9 12.0 %all-to-all-start.4 = ((bf16[16,24,512]{2,1,0:T(8,128)(2,1)}), bf16[16,24,512]{2,1,0:T(8,128)(2,1)S(1)}, u32[]{:S(2)}, u32[]{:S(2)}) async-start(bf16[16,24,512]{2,1,0:T(8,128)(2,1)} %shard_map.69), calls=%async_computation.4 | async-start | bytes 786432 | tf_op jit(solution)/shard_map/all_to_all | solution.py:394
  128.0 0.6 slice.3
  128.6 1.5 %collective-permute-start.6 = (s32[]{:T(128)}, s32[]{:T(128)}, u32[]{:S(2)}, u32[]{:S(2)}) collective-permute-start(s32[]{:T(128)} %bitcast.22), channel_id=1, source_target_pairs={{0,16},{16,0},{1,17},{17,1},{2,18},{18,2},{3,19},{19,3},{4,20},{20... | collective-permute-start | bytes 20 | tf_op jit(solution)/shard_map/ppermute | solution.py:401
  130.1 2.2 %collective-permute-done.6 = s32[]{:T(128)} collective-permute-done((s32[]{:T(128)}, s32[]{:T(128)}, u32[]{:S(2)}, u32[]{:S(2)}) %collective-permute-start.6) | collective-permute-done | bytes 36 | tf_op jit(solution)/shard_map/ppermute | solution.py:401
  133.5 6.7 %all-to-all-done.4 = bf16[16,24,512]{2,1,0:T(8,128)(2,1)S(1)} async-done(((bf16[16,24,512]{2,1,0:T(8,128)(2,1)}), bf16[16,24,512]{2,1,0:T(8,128)(2,1)S(1)}, u32[]{:S(2)}, u32[]{:S(2)}) %all-to-all-start.4) | async-done | bytes 393248 | tf_op jit(solution)/shard_map/all_to_all | solution.py:394
  140.2 0.3 conditional.1
  140.2 0.3 branch_0_fun.1
  140.6 0.7 copy-done.4
  (26 shorter events, 0.1 us)
Async XLA Ops:
  0.0 9.9 %copy-start = (bf16[256,8192]{1,0:T(8,128)(2,1)S(1)}, bf16[256,8192]{1,0:T(8,128)(2,1)}, u32[]{:S(2)}) copy-start(bf16[256,8192]{1,0:T(8,128)(2,1)} %tokens_ref.1) | copy-start | bytes 12582916
  4.1 8.7 %copy-start.5 = (s32[1,256]{1,0:T(1,128)}, s32[1,256]{1,0:T(1,128)S(1)}, u32[]{:S(2)}) copy-start(s32[1,256]{1,0:T(1,128)S(1)} %get-tuple-element.62.at_ref) | copy-start | bytes 3076
  4.1 14.8 %collective-permute-start = (bf16[24,4224]{1,0:T(8,128)(2,1)S(1)}, bf16[24,4224]{1,0:T(8,128)(2,1)S(1)}, u32[]{:S(2)}, u32[]{:S(2)}) collective-permute-start(bf16[24,4224]{1,0:T(8,128)(2,1)S(1)} %get-tuple-element.65), channel_id=1, source_target_pairs={{0,12},{1,13},{2,14},{3,15},{4,8},{5,9},{6,10},{7,11},{8,4},{9,5},... | collective-permute-start | bytes 608264 | tf_op jit(solution)/shard_map/ppermute | solution.py:309
  9.2 41.2 %collective-permute-start.1 = (bf16[24,4224]{1,0:T(8,128)(2,1)S(1)}, bf16[24,4224]{1,0:T(8,128)(2,1)S(1)}, u32[]{:S(2)}, u32[]{:S(2)}) collective-permute-start(bf16[24,4224]{1,0:T(8,128)(2,1)S(1)} %get-tuple-element.66), channel_id=1, source_target_pairs={{0,8},{1,9},{2,10},{3,11},{4,12},{5,13},{6,14},{7,15},{8,0},{9,1},... | collective-permute-start | bytes 608264 | tf_op jit(solution)/shard_map/ppermute | solution.py:309
  9.2 41.2 %collective-permute-start.2 = (bf16[24,4224]{1,0:T(8,128)(2,1)S(1)}, bf16[24,4224]{1,0:T(8,128)(2,1)S(1)}, u32[]{:S(2)}, u32[]{:S(2)}) collective-permute-start(bf16[24,4224]{1,0:T(8,128)(2,1)S(1)} %get-tuple-element.67), channel_id=1, source_target_pairs={{0,4},{1,5},{2,6},{3,7},{4,0},{5,1},{6,2},{7,3},{8,12},{9,13},{10,... | collective-permute-start | bytes 608264 | tf_op jit(solution)/shard_map/ppermute | solution.py:309
  12.8 97.3 %all-to-all-start.3 = ((bf16[16,16,8320]{2,1,0:T(8,128)(2,1)}), bf16[16,16,8320]{2,1,0:T(8,128)(2,1)}, u32[]{:S(2)}, u32[]{:S(2)}) async-start(bf16[16,16,8320]{2,1,0:T(8,128)(2,1)} %bitcast.35), calls=%async_computation.3 | async-start | bytes 8519680 | tf_op jit(solution)/shard_map/all_to_all | solution.py:365
  50.5 57.0 %copy-start.1 = (bf16[16,8192,16]{1,2,0:T(8,128)(2,1)S(1)}, bf16[16,8192,16]{1,2,0:T(8,128)(2,1)}, u32[]{:S(2)}) copy-start(bf16[16,8192,16]{1,2,0:T(8,128)(2,1)} %param.10) | copy-start | bytes 12582916
  50.5 57.0 %copy-start.3 = (bf16[16,16,512]{2,1,0:T(8,128)(2,1)S(1)}, bf16[16,16,512]{2,1,0:T(8,128)(2,1)}, u32[]{:S(2)}) copy-start(bf16[16,16,512]{2,1,0:T(8,128)(2,1)} %param.11) | copy-start | bytes 786436
  50.5 35.7 %collective-permute-start.5 = (bf16[96,4224]{1,0:T(8,128)(2,1)S(1)}, bf16[96,4224]{1,0:T(8,128)(2,1)S(1)}, u32[]{:S(2)}, u32[]{:S(2)}) collective-permute-start(bf16[96,4224]{1,0:T(8,128)(2,1)S(1)} %constant_dynamic-update-slice_fusion.refs_0_), channel_id=1, source_target_pairs={{0,3},{1,2},{2,1},{3,0},{4,7},{5,6},{6,5},{7,4},{8,11},{9,10},{10,... | collective-permute-start | bytes 2433032 | tf_op jit(solution)/shard_map/ppermute | solution.py:309
  50.6 56.9 %collective-permute-start.4 = (bf16[96,4224]{1,0:T(8,128)(2,1)S(1)}, bf16[96,4224]{1,0:T(8,128)(2,1)S(1)}, u32[]{:S(2)}, u32[]{:S(2)}) collective-permute-start(bf16[96,4224]{1,0:T(8,128)(2,1)S(1)} %constant_dynamic-update-slice_fusion.refs_0_), channel_id=1, source_target_pairs={{0,2},{1,3},{2,0},{3,1},{4,6},{5,7},{6,4},{7,5},{8,10},{9,11},{10,... | collective-permute-start | bytes 2433032 | tf_op jit(solution)/shard_map/ppermute | solution.py:309
  50.7 56.9 %collective-permute-start.3 = (bf16[96,4224]{1,0:T(8,128)(2,1)S(1)}, bf16[96,4224]{1,0:T(8,128)(2,1)S(1)}, u32[]{:S(2)}, u32[]{:S(2)}) collective-permute-start(bf16[96,4224]{1,0:T(8,128)(2,1)S(1)} %constant_dynamic-update-slice_fusion.refs_0_), channel_id=1, source_target_pairs={{0,1},{1,0},{2,3},{3,2},{4,5},{5,4},{6,7},{7,6},{8,9},{9,8},{10,11... | collective-permute-start | bytes 2433032 | tf_op jit(solution)/shard_map/ppermute | solution.py:309
  110.1 30.1 %copy-start.2 = (f32[256,512]{1,0:T(8,128)S(1)}, f32[256,512]{1,0:T(8,128)}, u32[]{:S(2)}) copy-start(f32[256,512]{1,0:T(8,128)} %fusion.8) | copy-start | bytes 1572868
  110.1 30.1 %copy-start.6 = (s32[1,256]{1,0:T(1,128)S(1)}, s32[1,256]{1,0:T(1,128)}, u32[]{:S(2)}) copy-start(s32[1,256]{1,0:T(1,128)} %copy-done.5) | copy-start | bytes 3076
  110.1 30.1 %copy-start.7 = (s32[1,256]{1,0:T(1,128)S(1)}, s32[1,256]{1,0:T(1,128)}, u32[]{:S(2)}) copy-start(s32[1,256]{1,0:T(1,128)} %get-tuple-element.77) | copy-start | bytes 3076
  110.1 30.1 %copy-start.8 = (s32[256,1]{0,1:T(1,128)S(1)}, s32[256,1]{0,1:T(1,128)}, u32[]{:S(2)}) copy-start(s32[256,1]{0,1:T(1,128)} %param.12) | copy-start | bytes 3076
  110.2 30.1 %copy-start.9 = (s32[256]{0:T(256)S(1)}, s32[256]{0:T(256)}, u32[]{:S(2)}) copy-start(s32[256]{0:T(256)} %param.13) | copy-start | bytes 3076
  115.9 24.2 %all-to-all-start.4 = ((bf16[16,24,512]{2,1,0:T(8,128)(2,1)}), bf16[16,24,512]{2,1,0:T(8,128)(2,1)S(1)}, u32[]{:S(2)}, u32[]{:S(2)}) async-start(bf16[16,24,512]{2,1,0:T(8,128)(2,1)} %shard_map.69), calls=%async_computation.4 | async-start | bytes 786432 | tf_op jit(solution)/shard_map/all_to_all | solution.py:394
  128.6 3.7 %collective-permute-start.6 = (s32[]{:T(128)}, s32[]{:T(128)}, u32[]{:S(2)}, u32[]{:S(2)}) collective-permute-start(s32[]{:T(128)} %bitcast.22), channel_id=1, source_target_pairs={{0,16},{16,0},{1,17},{17,1},{2,18},{18,2},{3,19},{19,3},{4,20},{20... | collective-permute-start | bytes 20 | tf_op jit(solution)/shard_map/ppermute | solution.py:401
  140.6 0.7 copy-start.4

commit v18 on v13

--- a/solution.py
+++ b/solution.py
@@ -14,7 +14,7 @@
 EXTRA = 8
 NOTE = 128
 STEP = 1024
-WIDE = 1664
+WIDE = 2816
 PARTS = 8
 VMEM = pl.BlockSpec(memory_space=pltpu.VMEM)
 ANY = pl.BlockSpec(memory_space=pl.ANY)

time: 141 us -> 141 us (level)
  no operation moved by 1% of the time
where the time goes in v18:
time: 141 us
  waiting for transfers between devices  90 us (64%)
  starting transfers between devices  24.9 us (18%)
  Pallas kernels  15.3 us (11%)
  matrix products  7.84 us (6%)
  local copies, waits for them, and re-layouts  1.47 us (1%)
  between operations  1.47 us (1%)
    ppermute x6, waiting for transfers between devices, swap(): return lax.ppermute(x, 'ad', [(s, s ^ k) for s in range(count)])  81.2 us
    all_to_all x1, starting transfers between devices, on_device(): back = lax.all_to_all(delta, 'ad', split_axis=0, concat_axis=0, tiled=True)  9.61 us
    dot_general x1, matrix products, on_device(): jnp.dot(tokens, value_weight, preferred_element_type=jnp.float32)  7.84 us
    ppermute x6, starting transfers between devices, swap(): return lax.ppermute(x, 'ad', [(s, s ^ k) for s in range(count)])  7.68 us
    all_to_all x1, waiting for transfers between devices, on_device(): back = lax.all_to_all(delta, 'ad', split_axis=0, concat_axis=0, tiled=True)  6.59 us
    all_to_all x1, starting transfers between devices, on_device(): lax.all_to_all(blocks.reshape(count, room, depth + NOTE), 'ad', split_axi...  6.14 us
    pallas_call x1, Pallas kernels, adapt(): pl.pallas_call(functools.partial(adapt_body, rank), in_specs=[SMEM, ANY,...  5.77 us
    pallas_call x1, Pallas kernels, on_device(): pl.pallas_call(functools.partial(route_body, room, local), in_specs=[SMEM...  3.84 us
  transfers between devices with their start and end apart: 9, of which 5 were waited for; matrix products, arithmetic and copies ran while one was open for 6% of the time, Pallas kernels for 4%

profile of v18, /device:TPU:0, one launch (start us, length us, event | category | flops | bytes accessed | tf_op | source)
XLA Modules:
  0.0 141.0 jit_solution(9101059728911409772)
XLA Ops:
  0.0 3.8 %shard_map.66 = (bf16[24,4224]{1,0:T(8,128)(2,1)S(1)}, bf16[24,4224]{1,0:T(8,128)(2,1)S(1)}, bf16[24,4224]{1,0:T(8,128)(2,1)S(1)}, bf16[24,4224]{1,0:T(8,128)(2,...) custom-call(s32[1]{0:T(128)} %bitcast.12.me_ref, ...), custom_call_target="tpu_custom_call" | custom-call | flops 805306368 | bytes 6291456 | tf_op jit(solution)/shard_map/pallas_call | solution.py:338
  3.9 5.1 %collective-permute-start = (bf16[24,4224]{1,0:T(8,128)(2,1)S(1)}, bf16[24,4224]{1,0:T(8,128)(2,1)S(1)}, u32[]{:S(2)}, u32[]{:S(2)}) collective-permute-start(bf16[24,4224]{1,0:T(8,128)(2,1)S(1)} %get-tuple-element.67), channel_id=1, source_target_pairs={{0,12},{1,13},{2,14},{3,15},{4,8},{5,9},{6,10},{7,11},{8,4},{9,5},... | collective-permute-start | bytes 608264 | tf_op jit(solution)/shard_map/ppermute | solution.py:309
  9.0 0.6 collective-permute-start.2
  9.6 2.9 %shard_map.67 = bf16[256,8320]{1,0:T(8,128)(2,1)} custom-call(s32[1,256]{1,0:T(1,128)S(1)} %get-tuple-element.63.at_ref, bf16[128,256]{1,0:T(8,128)(2,1)S(1)} %get-tuple-element.64.note_ref, bf16[256,8192]{1,0:T(8,128)(2,1)S(1)} %get-tuple-element.65.tokens_ref), custom_call_target="tpu_custom_call" | custom-call | flops 1073741824 | bytes 8388608 | tf_op jit(solution)/shard_map/pallas_call | solution.py:163
  12.5 6.1 %all-to-all-start.3 = ((bf16[16,16,8320]{2,1,0:T(8,128)(2,1)}), bf16[16,16,8320]{2,1,0:T(8,128)(2,1)}, u32[]{:S(2)}, u32[]{:S(2)}) async-start(bf16[16,16,8320]{2,1,0:T(8,128)(2,1)} %bitcast.35), calls=%async_computation.3 | async-start | bytes 8519680 | tf_op jit(solution)/shard_map/all_to_all | solution.py:365
  18.7 31.5 %collective-permute-done.1 = bf16[24,4224]{1,0:T(8,128)(2,1)S(1)} collective-permute-done((bf16[24,4224]{1,0:T(8,128)(2,1)S(1)}, bf16[24,4224]{1,0:T(8,128)(2,1)S(1)}, u32[]{:S(2)}, u32[]{:S(2)}) %collective-permute-start.1) | collective-permute-done | bytes 202784 | tf_op jit(solution)/shard_map/ppermute | solution.py:309
  50.2 0.0 copy-start
  50.3 0.1 collective-permute-start.3
  50.3 0.1 collective-permute-start.4
  50.4 1.8 %collective-permute-start.5 = (bf16[96,4224]{1,0:T(8,128)(2,1)S(1)}, bf16[96,4224]{1,0:T(8,128)(2,1)S(1)}, u32[]{:S(2)}, u32[]{:S(2)}) collective-permute-start(bf16[96,4224]{1,0:T(8,128)(2,1)S(1)} %constant_dynamic-update-slice_fusion.refs_0_), channel_id=1, source_target_pairs={{0,3},{1,2},{2,1},{3,0},{4,7},{5,6},{6,5},{7,4},{8,11},{9,10},{10,... | collective-permute-start | bytes 2433032 | tf_op jit(solution)/shard_map/ppermute | solution.py:309
  52.2 7.8 %fusion.8 = f32[256,512]{1,0:T(8,128)} fusion(bf16[256,8192]{1,0:T(8,128)(2,1)} %tokens_hbm.1, bf16[8192,512]{1,0:T(8,128)(2,1)} %param.9), kind=kOutput, calls=%fused_computation.37 | convolution fusion | flops 2147483648 | bytes 13107200 | tf_op jit(solution)/shard_map/dot_general | solution.py:329
  60.1 25.9 %collective-permute-done.4.refs_2_ = bf16[96,4224]{1,0:T(8,128)(2,1)S(1)} collective-permute-done((bf16[96,4224]{1,0:T(8,128)(2,1)S(1)}, bf16[96,4224]{1,0:T(8,128)(2,1)S(1)}, u32[]{:S(2)}, u32[]{:S(2)}) %collective-permute-start.4) | collective-permute-done | bytes 811040 | tf_op jit(solution)/shard_map/ppermute | solution.py:309
  86.0 23.7 %collective-permute-done.5.refs_3_ = bf16[96,4224]{1,0:T(8,128)(2,1)S(1)} collective-permute-done((bf16[96,4224]{1,0:T(8,128)(2,1)S(1)}, bf16[96,4224]{1,0:T(8,128)(2,1)S(1)}, u32[]{:S(2)}, u32[]{:S(2)}) %collective-permute-start.5) | collective-permute-done | bytes 811040 | tf_op jit(solution)/shard_map/ppermute | solution.py:309
  109.7 2.5 %shard_map.68 = (f32[16,8,512]{2,1,0:T(8,128)S(1)}, s32[1,128]{1,0:T(1,128)S(1)}) custom-call(s32[1]{0:T(128)} %bitcast.20.first_ref, bf16[256,8192]{1,0:T(8,128)(2,1)S(1)} %bitcast.38, bf16[256,512]{1,0:T(8,128)(2,1)S(1)} %bitcast.43, bf16[96,4224]{1,0:T(8,128)(2,1)S(1)} %constant_dynamic-update-slice_fusion.refs_0_, ...), custom_call_target="tpu_custom_call" | custom-call | flops 999999995904 | bytes 6291456 | tf_op jit(solution)/shard_map/pallas_call | solution.py:374
  112.3 0.0 copy-start.7
  112.3 5.8 %shard_map.69 = bf16[16,24,512]{2,1,0:T(8,128)(2,1)} custom-call(s32[1]{0:T(128)} %bitcast.12.me_ref, bf16[256,8192]{1,0:T(8,128)(2,1)} %bitcast.37, bf16[256,512]{1,0:T(8,128)(2,1)S(1)} %bitcast.44, bf16[256,8320]{1,0:T(8,128)(2,1)} %bitcast.19.rows_hbm, f32[16,8,512]{2,1,0:T(8,128)S(1)} %get-tuple-element.76.extra_ref), custom_call_target="tpu_custom_call" | custom-call | flops 1073741824 | bytes 8388608 | tf_op jit(solution)/shard_map/pallas_call | solution.py:227
  118.1 9.6 %all-to-all-start.4 = ((bf16[16,24,512]{2,1,0:T(8,128)(2,1)}), bf16[16,24,512]{2,1,0:T(8,128)(2,1)S(1)}, u32[]{:S(2)}, u32[]{:S(2)}) async-start(bf16[16,24,512]{2,1,0:T(8,128)(2,1)} %shard_map.69), calls=%async_computation.4 | async-start | bytes 786432 | tf_op jit(solution)/shard_map/all_to_all | solution.py:394
  127.7 0.6 slice.3
  128.4 1.5 %collective-permute-start.6 = (s32[]{:T(128)}, s32[]{:T(128)}, u32[]{:S(2)}, u32[]{:S(2)}) collective-permute-start(s32[]{:T(128)} %bitcast.22), channel_id=1, source_target_pairs={{0,16},{16,0},{1,17},{17,1},{2,18},{18,2},{3,19},{19,3},{4,20},{20... | collective-permute-start | bytes 20 | tf_op jit(solution)/shard_map/ppermute | solution.py:401
  129.9 2.2 %collective-permute-done.6 = s32[]{:T(128)} collective-permute-done((s32[]{:T(128)}, s32[]{:T(128)}, u32[]{:S(2)}, u32[]{:S(2)}) %collective-permute-start.6) | collective-permute-done | bytes 36 | tf_op jit(solution)/shard_map/ppermute | solution.py:401
  133.3 6.6 %all-to-all-done.4 = bf16[16,24,512]{2,1,0:T(8,128)(2,1)S(1)} async-done(((bf16[16,24,512]{2,1,0:T(8,128)(2,1)}), bf16[16,24,512]{2,1,0:T(8,128)(2,1)S(1)}, u32[]{:S(2)}, u32[]{:S(2)}) %all-to-all-start.4) | async-done | bytes 393248 | tf_op jit(solution)/shard_map/all_to_all | solution.py:394
  140.0 0.3 conditional.1
  140.0 0.3 branch_0_fun.1
  140.3 0.7 copy-done.3
  (24 shorter events, 0.1 us)
Async XLA Ops:
  3.9 8.6 %copy-start.4 = (s32[1,256]{1,0:T(1,128)}, s32[1,256]{1,0:T(1,128)S(1)}, u32[]{:S(2)}) copy-start(s32[1,256]{1,0:T(1,128)S(1)} %get-tuple-element.63.at_ref) | copy-start | bytes 3076
  3.9 14.8 %collective-permute-start = (bf16[24,4224]{1,0:T(8,128)(2,1)S(1)}, bf16[24,4224]{1,0:T(8,128)(2,1)S(1)}, u32[]{:S(2)}, u32[]{:S(2)}) collective-permute-start(bf16[24,4224]{1,0:T(8,128)(2,1)S(1)} %get-tuple-element.67), channel_id=1, source_target_pairs={{0,12},{1,13},{2,14},{3,15},{4,8},{5,9},{6,10},{7,11},{8,4},{9,5},... | collective-permute-start | bytes 608264 | tf_op jit(solution)/shard_map/ppermute | solution.py:309
  9.0 41.2 %collective-permute-start.1 = (bf16[24,4224]{1,0:T(8,128)(2,1)S(1)}, bf16[24,4224]{1,0:T(8,128)(2,1)S(1)}, u32[]{:S(2)}, u32[]{:S(2)}) collective-permute-start(bf16[24,4224]{1,0:T(8,128)(2,1)S(1)} %get-tuple-element.68), channel_id=1, source_target_pairs={{0,8},{1,9},{2,10},{3,11},{4,12},{5,13},{6,14},{7,15},{8,0},{9,1},... | collective-permute-start | bytes 608264 | tf_op jit(solution)/shard_map/ppermute | solution.py:309
  9.0 41.2 %collective-permute-start.2 = (bf16[24,4224]{1,0:T(8,128)(2,1)S(1)}, bf16[24,4224]{1,0:T(8,128)(2,1)S(1)}, u32[]{:S(2)}, u32[]{:S(2)}) collective-permute-start(bf16[24,4224]{1,0:T(8,128)(2,1)S(1)} %get-tuple-element.69), channel_id=1, source_target_pairs={{0,4},{1,5},{2,6},{3,7},{4,0},{5,1},{6,2},{7,3},{8,12},{9,13},{10,... | collective-permute-start | bytes 608264 | tf_op jit(solution)/shard_map/ppermute | solution.py:309
  12.5 99.8 %all-to-all-start.3 = ((bf16[16,16,8320]{2,1,0:T(8,128)(2,1)}), bf16[16,16,8320]{2,1,0:T(8,128)(2,1)}, u32[]{:S(2)}, u32[]{:S(2)}) async-start(bf16[16,16,8320]{2,1,0:T(8,128)(2,1)} %bitcast.35), calls=%async_computation.3 | async-start | bytes 8519680 | tf_op jit(solution)/shard_map/all_to_all | solution.py:365
  50.2 59.5 %copy-start = (bf16[16,8192,16]{1,2,0:T(8,128)(2,1)S(1)}, bf16[16,8192,16]{1,2,0:T(8,128)(2,1)}, u32[]{:S(2)}) copy-start(bf16[16,8192,16]{1,2,0:T(8,128)(2,1)} %param.10) | copy-start | bytes 12582916
  50.3 59.5 %copy-start.2 = (bf16[16,16,512]{2,1,0:T(8,128)(2,1)S(1)}, bf16[16,16,512]{2,1,0:T(8,128)(2,1)}, u32[]{:S(2)}) copy-start(bf16[16,16,512]{2,1,0:T(8,128)(2,1)} %param.11) | copy-start | bytes 786436
  50.3 9.8 %collective-permute-start.3 = (bf16[96,4224]{1,0:T(8,128)(2,1)S(1)}, bf16[96,4224]{1,0:T(8,128)(2,1)S(1)}, u32[]{:S(2)}, u32[]{:S(2)}) collective-permute-start(bf16[96,4224]{1,0:T(8,128)(2,1)S(1)} %constant_dynamic-update-slice_fusion.refs_0_), channel_id=1, source_target_pairs={{0,1},{1,0},{2,3},{3,2},{4,5},{5,4},{6,7},{7,6},{8,9},{9,8},{10,11... | collective-permute-start | bytes 2433032 | tf_op jit(solution)/shard_map/ppermute | solution.py:309
  50.3 35.6 %collective-permute-start.4 = (bf16[96,4224]{1,0:T(8,128)(2,1)S(1)}, bf16[96,4224]{1,0:T(8,128)(2,1)S(1)}, u32[]{:S(2)}, u32[]{:S(2)}) collective-permute-start(bf16[96,4224]{1,0:T(8,128)(2,1)S(1)} %constant_dynamic-update-slice_fusion.refs_0_), channel_id=1, source_target_pairs={{0,2},{1,3},{2,0},{3,1},{4,6},{5,7},{6,4},{7,5},{8,10},{9,11},{10,... | collective-permute-start | bytes 2433032 | tf_op jit(solution)/shard_map/ppermute | solution.py:309
  50.4 59.3 %collective-permute-start.5 = (bf16[96,4224]{1,0:T(8,128)(2,1)S(1)}, bf16[96,4224]{1,0:T(8,128)(2,1)S(1)}, u32[]{:S(2)}, u32[]{:S(2)}) collective-permute-start(bf16[96,4224]{1,0:T(8,128)(2,1)S(1)} %constant_dynamic-update-slice_fusion.refs_0_), channel_id=1, source_target_pairs={{0,3},{1,2},{2,1},{3,0},{4,7},{5,6},{6,5},{7,4},{8,11},{9,10},{10,... | collective-permute-start | bytes 2433032 | tf_op jit(solution)/shard_map/ppermute | solution.py:309
  112.3 27.7 %copy-start.1 = (f32[256,512]{1,0:T(8,128)S(1)}, f32[256,512]{1,0:T(8,128)}, u32[]{:S(2)}) copy-start(f32[256,512]{1,0:T(8,128)} %fusion.8) | copy-start | bytes 1572868
  112.3 27.7 %copy-start.5 = (s32[1,256]{1,0:T(1,128)S(1)}, s32[1,256]{1,0:T(1,128)}, u32[]{:S(2)}) copy-start(s32[1,256]{1,0:T(1,128)} %copy-done.4) | copy-start | bytes 3076
  112.3 27.6 %copy-start.6 = (s32[1,256]{1,0:T(1,128)S(1)}, s32[1,256]{1,0:T(1,128)}, u32[]{:S(2)}) copy-start(s32[1,256]{1,0:T(1,128)} %get-tuple-element.79) | copy-start | bytes 3076
  112.3 27.6 %copy-start.7 = (s32[256,1]{0,1:T(1,128)S(1)}, s32[256,1]{0,1:T(1,128)}, u32[]{:S(2)}) copy-start(s32[256,1]{0,1:T(1,128)} %param.12) | copy-start | bytes 3076
  112.3 27.6 %copy-start.8 = (s32[256]{0:T(256)S(1)}, s32[256]{0:T(256)}, u32[]{:S(2)}) copy-start(s32[256]{0:T(256)} %param.13) | copy-start | bytes 3076
  118.1 21.8 %all-to-all-start.4 = ((bf16[16,24,512]{2,1,0:T(8,128)(2,1)}), bf16[16,24,512]{2,1,0:T(8,128)(2,1)S(1)}, u32[]{:S(2)}, u32[]{:S(2)}) async-start(bf16[16,24,512]{2,1,0:T(8,128)(2,1)} %shard_map.69), calls=%async_computation.4 | async-start | bytes 786432 | tf_op jit(solution)/shard_map/all_to_all | solution.py:394
  128.4 3.7 %collective-permute-start.6 = (s32[]{:T(128)}, s32[]{:T(128)}, u32[]{:S(2)}, u32[]{:S(2)}) collective-permute-start(s32[]{:T(128)} %bitcast.22), channel_id=1, source_target_pairs={{0,16},{16,0},{1,17},{17,1},{2,18},{18,2},{3,19},{19,3},{4,20},{20... | collective-permute-start | bytes 20 | tf_op jit(solution)/shard_map/ppermute | solution.py:401
  140.3 0.7 copy-start.3
